TPU v7x, 32 devices: a whole 2x2x4 slice. The times are simulated.
32 devices in a mesh: ctx: 8 (over z, core), shard: 4 (over y, x).
Axes of the slice: x: 2, y: 2, z: 4, core: 2. Of those that a mesh axis runs over, the one named last changes fastest.
Arguments:
- tokens: float32 [8, 1024, 1536], P('shard', 'ctx'), may hold values from -6 to 6
- cotangent: float32 [8, 1024, 1536], P('shard', 'ctx'), may hold values from -6 to 6
- norm_gains: float32 [2, 1536], replicated, may hold values from 0.5 to 1.5
- router: float32 [1536, 4], replicated, may hold values from -0.15625 to 0.15625
- dense_weight: float32 [128, 192, 256], P(('ctx', 'shard')), may hold values from -0.15625 to 0.15625
- expert_weight: float32 [4, 96, 192, 256], P('shard', 'ctx'), may hold values from -0.15625 to 0.15625
- routes: int32 [8, 1024, 2], P('shard', 'ctx'), may hold values from 0 to 3, all different within a row; in each aligned block of 128 rows (0 to 127, 128 to 255, ..., all dimensions but the last counted through in order) at most 128 rows name the same one
- assign: int32 [8, 2], replicated, may hold values from 0 to 15, as said below
- dense_order: int32 [128], replicated, may hold values from 0 to 127, each once
- expert_order: int32 [96], replicated, may hold values from 0 to 95, each once
- dense_moment: float32 [128, 192, 256], P(('ctx', 'shard')), may hold values from -6 to 6
- dense_second: float32 [128, 192, 256], P(('ctx', 'shard')), may hold values from 1 to 30
- dense_left: float32 [128, 192, 192], P(('ctx', 'shard'))
- dense_right: float32 [128, 256, 256], P(('ctx', 'shard'))
- expert_moment: float32 [4, 96, 192, 256], P('shard', 'ctx'), may hold values from -18 to 18
- expert_second: float32 [4, 96, 192, 256], P('shard', 'ctx'), may hold values from 10 to 300
- expert_left: float32 [4, 96, 192, 192], P('shard', 'ctx')
- expert_right: float32 [4, 96, 256, 256], P('shard', 'ctx')
- gains_moment: float32 [2, 1536], replicated, may hold values from -30 to 30
- gains_second: float32 [2, 1536], replicated, may hold values from 10 to 1000
- router_moment: float32 [1536, 4], replicated, may hold values from -30 to 30
- router_second: float32 [1536, 4], replicated, may hold values from 10 to 1000
Outputs:
- output: float32 [8, 1024, 1536], P('shard', 'ctx')
- input_grad: float32 [8, 1024, 1536], P('shard', 'ctx')
- dense_grad: float32 [128, 192, 256], P(('ctx', 'shard'))
- dense_new: float32 [128, 192, 256], P(('ctx', 'shard'))
- dense_moment_new: float32 [128, 192, 256], P(('ctx', 'shard'))
- dense_second_new: float32 [128, 192, 256], P(('ctx', 'shard'))
- expert_grad: float32 [4, 96, 192, 256], P('shard', 'ctx')
- expert_new: float32 [4, 96, 192, 256], P('shard', 'ctx')
- expert_moment_new: float32 [4, 96, 192, 256], P('shard', 'ctx')
- expert_second_new: float32 [4, 96, 192, 256], P('shard', 'ctx')
- gains_grad: float32 [2, 1536], replicated
- gains_new: float32 [2, 1536], replicated
- gains_moment_new: float32 [2, 1536], replicated
- gains_second_new: float32 [2, 1536], replicated
- router_grad: float32 [1536, 4], replicated
- router_new: float32 [1536, 4], replicated
- router_moment_new: float32 [1536, 4], replicated
- router_second_new: float32 [1536, 4], replicated
Inputs may be any that keep to these rules, and one draw needn't show every extreme that they name: `assign`: row c names causal blocks b and 15 - b; every causal block is named once. `routes`: in each aligned block of 128 rows of a sequence, no expert is named more than 128 times. `dense_order`: each block number once. `expert_order`: each block number once.
All inputs are finite; a program needn't handle non-finite values.
Results may differ from a plain program's by a relative error of at most 0.015.
Values may be sent and summed in bfloat16 or wider, within the bound.
No kernel may reach another device: no remote copies, remote signals or barrier semaphores. Data moves between devices by JAX's collectives and lax.ppermute only.
A program may use at most 192 MiB of HBM per device.

v0:
```python
import jax
import jax.numpy as jnp
from jax import lax
from jax.sharding import PartitionSpec as P

HEADS = 24
KVH = 8
HD = 64
FF = 1024
BR = 192
BC = 256


norm_eps = 1e-06
beta_one = 0.9
beta_two = 0.95
rate = 0.01
gain_rate = 0.5
adam_eps = 1e-08
masked_score = -1e30
highest = lax.Precision.HIGHEST


def rms_parts(inputs, gain):
    inverse = lax.rsqrt(jnp.mean(inputs * inputs, axis=-1, keepdims=True) + norm_eps)
    return (inputs * inverse * gain, inverse)


def rms_back(inputs, gain, inverse, gradient):
    unit = inputs * inverse
    scaled = gradient * gain
    inner_mean = jnp.mean(scaled * unit, axis=-1, keepdims=True)
    return (inverse * (scaled - unit * inner_mean), jnp.sum(gradient * unit, axis=0))


def soft_max(scores):
    largest = jnp.max(scores, axis=-1, keepdims=True)
    raised = jnp.exp(scores - largest)
    return raised / jnp.sum(raised, axis=-1, keepdims=True)


def inverse_order(slot_order):
    count = slot_order.shape[0]
    return jnp.zeros((count,), jnp.int32).at[slot_order].set(jnp.arange(count, dtype=jnp.int32))


def forward_map(rows_mat, blocks):
    grouped = rows_mat.reshape(rows_mat.shape[0], blocks.shape[0], blocks.shape[2])
    result = jnp.einsum("rai,abij->rbj", grouped, blocks, preferred_element_type=jnp.float32)
    return result.reshape(rows_mat.shape[0], blocks.shape[1] * blocks.shape[3])


def backward_map(rows_mat, blocks):
    grouped = rows_mat.reshape(rows_mat.shape[0], blocks.shape[1], blocks.shape[3])
    result = jnp.einsum("rbj,abij->rai", grouped, blocks, preferred_element_type=jnp.float32)
    return result.reshape(rows_mat.shape[0], blocks.shape[0] * blocks.shape[2])


def outer_blocks(left_rows, right_rows, block_rows, block_cols):
    count = left_rows.shape[0]
    left_grouped = left_rows.reshape(count, left_rows.shape[1] // block_rows, block_rows)
    right_grouped = right_rows.reshape(count, right_rows.shape[1] // block_cols, block_cols)
    return jnp.einsum(
        "rai,rbj->abij", left_grouped, right_grouped, preferred_element_type=jnp.float32
    )


def head_view(rows_mat):
    return rows_mat.reshape(rows_mat.shape[0], KVH, HEADS // KVH, HD)


def masked_scores(query_heads, key_block, rows_pos, key_pos):
    scores = jnp.einsum(
        "rkgd,nkd->kgrn", query_heads, key_block, preferred_element_type=jnp.float32
    ) * HD ** (-0.5)
    return jnp.where(
        key_pos[None, None, None, :] <= rows_pos[None, None, :, None], scores, masked_score
    )


def attend(query_heads, all_keys, all_values, rows_pos, key_pos, key_span):
    block_count = all_keys.shape[0] // key_span
    key_blocks = all_keys.reshape(block_count, key_span, KVH, HD)
    value_blocks = all_values.reshape(block_count, key_span, KVH, HD)
    pos_blocks = key_pos.reshape(block_count, key_span)
    stat_shape = (KVH, HEADS // KVH, query_heads.shape[0])

    def running(carried, pieces):
        largest, summed = carried
        key_block, pos_block = pieces
        scores = masked_scores(query_heads, key_block, rows_pos, pos_block)
        new_largest = jnp.maximum(largest, jnp.max(scores, axis=-1))
        summed = summed * jnp.exp(largest - new_largest) + jnp.sum(
            jnp.exp(scores - new_largest[..., None]), axis=-1
        )
        return ((new_largest, summed), None)

    start = (jnp.full(stat_shape, masked_score, jnp.float32), jnp.zeros(stat_shape, jnp.float32))
    (largest, summed), _ = lax.scan(running, start, (key_blocks, pos_blocks))
    log_total = largest + jnp.log(summed)

    def weighted(running_sum, pieces):
        key_block, value_block, pos_block = pieces
        chance = jnp.exp(
            masked_scores(query_heads, key_block, rows_pos, pos_block) - log_total[..., None]
        ).astype(jnp.bfloat16)
        return (
            running_sum
            + jnp.einsum("kgrn,nkd->rkgd", chance, value_block, preferred_element_type=jnp.float32),
            None,
        )

    mixture, _ = lax.scan(
        weighted, jnp.zeros(query_heads.shape, jnp.float32), (key_blocks, value_blocks, pos_blocks)
    )
    return (mixture, log_total)


def attend_back(
    query_heads, grad_heads, log_total, delta, all_keys, all_values, rows_pos, key_pos, key_span
):
    block_count = all_keys.shape[0] // key_span
    key_blocks = all_keys.reshape(block_count, key_span, KVH, HD)
    value_blocks = all_values.reshape(block_count, key_span, KVH, HD)
    pos_blocks = key_pos.reshape(block_count, key_span)
    score_scale = HD ** (-0.5)

    def one_block(query_grad, pieces):
        key_block, value_block, pos_block = pieces
        chance = jnp.exp(
            masked_scores(query_heads, key_block, rows_pos, pos_block) - log_total[..., None]
        )
        chance_low = chance.astype(jnp.bfloat16)
        value_grad = jnp.einsum(
            "kgrn,rkgd->nkd", chance_low, grad_heads, preferred_element_type=jnp.float32
        )
        prob_grad = jnp.einsum(
            "rkgd,nkd->kgrn", grad_heads, value_block, preferred_element_type=jnp.float32
        )
        score_grad = (chance * (prob_grad - delta[..., None])).astype(jnp.bfloat16)
        query_grad = query_grad + jnp.einsum(
            "kgrn,nkd->rkgd", score_grad, key_block, preferred_element_type=jnp.float32
        )
        key_grad = (
            jnp.einsum(
                "kgrn,rkgd->nkd", score_grad, query_heads, preferred_element_type=jnp.float32
            )
            * score_scale
        )
        return (query_grad, (key_grad, value_grad))

    query_grad, (key_grads, value_grads) = lax.scan(
        one_block, jnp.zeros(query_heads.shape, jnp.float32), (key_blocks, value_blocks, pos_blocks)
    )
    return (
        query_grad * score_scale,
        key_grads.reshape(-1, KVH * HD),
        value_grads.reshape(-1, KVH * HD),
    )


def soap(weight, gradient, moment, second, left_basis, right_basis):
    rotated = jnp.matmul(
        jnp.matmul(jnp.swapaxes(left_basis, -1, -2), gradient, precision=highest),
        right_basis,
        precision=highest,
    )
    moment_new = beta_one * moment + (1.0 - beta_one) * rotated
    second_new = beta_two * second + (1.0 - beta_two) * rotated * rotated
    direction = moment_new / (jnp.sqrt(second_new) + adam_eps)
    rotated_back = jnp.matmul(
        jnp.matmul(left_basis, direction, precision=highest),
        jnp.swapaxes(right_basis, -1, -2),
        precision=highest,
    )
    return (weight - rate * rotated_back, moment_new, second_new)


def adam(weight, gradient, moment, second, step_rate):
    moment_new = beta_one * moment + (1.0 - beta_one) * gradient
    second_new = beta_two * second + (1.0 - beta_two) * gradient * gradient
    return (
        weight - step_rate * moment_new / (jnp.sqrt(second_new) + adam_eps),
        moment_new,
        second_new,
    )


def shards(
    tokens,
    cotangent,
    norm_gains,
    router,
    dense_weight,
    expert_weight,
    routes,
    assign,
    dense_order,
    expert_order,
    dense_moment,
    dense_second,
    dense_left,
    dense_right,
    expert_moment,
    expert_second,
    expert_left,
    expert_right,
    gains_moment,
    gains_second,
    router_moment,
    router_second,
):
    ctx_count = lax.axis_size("ctx")
    shard_count = lax.axis_size("shard")
    micro_count = tokens.shape[0]
    row_count = tokens.shape[1]
    model_width = tokens.shape[2]
    causal_len = row_count // 2
    length = row_count * ctx_count
    capacity = 8 * causal_len // shard_count
    key_span = min(512, length)
    query_width = HEADS * HD
    pair_width = KVH * HD
    in_width = query_width + 2 * pair_width
    dense_cols = in_width + query_width
    row_groups = model_width // BR
    col_groups = dense_cols // BC
    in_groups = in_width // BC
    ff_groups = FF // BC
    dense_inverse = inverse_order(dense_order)
    expert_inverse = inverse_order(expert_order)
    row_ids = jnp.arange(row_count, dtype=jnp.int32)
    all_pos = (assign[:, row_ids // causal_len] * causal_len + row_ids % causal_len).reshape(length)
    rows_pos = lax.dynamic_slice_in_dim(all_pos, lax.axis_index("ctx") * row_count, row_count)
    expert_ids = jnp.arange(shard_count, dtype=jnp.int32)
    gain_one = norm_gains[0]
    gain_two = norm_gains[1]
    router_low = router.astype(jnp.bfloat16)
    dense_total = jnp.zeros(dense_weight.shape, jnp.float32)
    expert_total = jnp.zeros(expert_weight.shape[1:], jnp.float32)
    router_total = jnp.zeros(router.shape, jnp.float32)
    gains_total = jnp.zeros(norm_gains.shape, jnp.float32)
    output_rows = []
    input_rows = []
    for micro_batch in range(micro_count):
        gathered = lax.all_gather(
            dense_weight.astype(jnp.bfloat16), ("ctx", "shard"), axis=0, tiled=True
        )
        dense_four = gathered[dense_inverse].reshape(row_groups, col_groups, BR, BC)
        in_maps = dense_four[:, :in_groups]
        out_maps = dense_four[:, in_groups:]
        expert_pieces = lax.all_gather(
            expert_weight[0].astype(jnp.bfloat16), "ctx", axis=0, tiled=True
        )
        expert_five = expert_pieces[expert_inverse].reshape(3, row_groups, ff_groups, BR, BC)
        inputs = tokens[micro_batch]
        normed, inverse_one = rms_parts(inputs, gain_one)
        normed_one = normed.astype(jnp.bfloat16)
        projected = forward_map(normed_one, in_maps).astype(jnp.bfloat16)
        query_rows = projected[:, :query_width]
        key_rows = projected[:, query_width : query_width + pair_width]
        value_rows = projected[:, query_width + pair_width :]
        all_keys, all_values = (
            lax.all_gather(key_rows, "ctx", axis=0, tiled=True),
            lax.all_gather(value_rows, "ctx", axis=0, tiled=True),
        )
        query_heads = head_view(query_rows)
        mixture, log_total = attend(query_heads, all_keys, all_values, rows_pos, all_pos, key_span)
        attended = mixture.reshape(row_count, query_width).astype(jnp.bfloat16)
        after_attn = inputs + backward_map(attended, out_maps)
        normed, inverse_two = rms_parts(after_attn, gain_two)
        normed_two = normed.astype(jnp.bfloat16)
        router_probs = soft_max(jnp.dot(normed_two, router_low, preferred_element_type=jnp.float32))
        route_flat = routes[micro_batch].reshape(-1)
        route_hits = (route_flat[:, None] == expert_ids[None, :]).astype(jnp.int32)
        earlier = jnp.cumsum(route_hits, axis=0) - route_hits
        slot_flat = jnp.sum(earlier * route_hits, axis=1)
        hits_float = route_hits.astype(jnp.float32).reshape(row_count, 2, shard_count)
        mix_weight = jnp.sum(hits_float * router_probs[:, None, :], axis=-1)
        empty_slots = jnp.zeros((shard_count, capacity, model_width), jnp.bfloat16)
        outgoing = empty_slots.at[route_flat, slot_flat].set(jnp.repeat(normed_two, 2, axis=0))
        incoming = lax.all_to_all(
            outgoing, "shard", split_axis=0, concat_axis=0, tiled=True
        ).reshape(-1, model_width)
        gate_pre = forward_map(incoming, expert_five[0])
        up_pre = forward_map(incoming, expert_five[1])
        gate_sig = jax.nn.sigmoid(gate_pre)
        hidden = (gate_pre * gate_sig * up_pre).astype(jnp.bfloat16)
        produced = backward_map(hidden, expert_five[2]).astype(jnp.bfloat16)
        returned = lax.all_to_all(
            produced.reshape(shard_count, capacity, model_width),
            "shard",
            split_axis=0,
            concat_axis=0,
            tiled=True,
        )
        arrived = (
            returned[route_flat, slot_flat].astype(jnp.float32).reshape(row_count, 2, model_width)
        )
        output_rows.append(after_attn + jnp.sum(mix_weight[:, :, None] * arrived, axis=1))
        out_grad = cotangent[micro_batch]
        route_grad = jnp.sum(out_grad[:, None, :] * arrived, axis=-1)
        sent_grad = (
            (mix_weight[:, :, None] * out_grad[:, None, :])
            .reshape(-1, model_width)
            .astype(jnp.bfloat16)
        )
        outgoing_grad = empty_slots.at[route_flat, slot_flat].set(sent_grad)
        incoming_grad = lax.all_to_all(
            outgoing_grad, "shard", split_axis=0, concat_axis=0, tiled=True
        ).reshape(-1, model_width)
        hidden_grad = forward_map(incoming_grad, expert_five[2])
        gate_grad = (hidden_grad * up_pre * gate_sig * (1.0 + gate_pre * (1.0 - gate_sig))).astype(
            jnp.bfloat16
        )
        up_grad = (hidden_grad * gate_pre * gate_sig).astype(jnp.bfloat16)
        rows_grad = backward_map(gate_grad, expert_five[0]) + backward_map(up_grad, expert_five[1])
        expert_term = jnp.stack(
            [
                outer_blocks(incoming, gate_grad, BR, BC),
                outer_blocks(incoming, up_grad, BR, BC),
                outer_blocks(incoming_grad, hidden, BR, BC),
            ]
        )
        returned_grad = lax.all_to_all(
            rows_grad.astype(jnp.bfloat16).reshape(shard_count, capacity, model_width),
            "shard",
            split_axis=0,
            concat_axis=0,
            tiled=True,
        )
        normed_two_grad = jnp.sum(
            returned_grad[route_flat, slot_flat]
            .astype(jnp.float32)
            .reshape(row_count, 2, model_width),
            axis=1,
        )
        prob_grad = jnp.sum(hits_float * route_grad[:, :, None], axis=1)
        logit_grad = router_probs * (
            prob_grad - jnp.sum(router_probs * prob_grad, axis=-1, keepdims=True)
        )
        router_total = router_total + jnp.einsum(
            "rd,re->de", normed_two, logit_grad, preferred_element_type=jnp.float32
        )
        normed_two_grad = normed_two_grad + jnp.einsum(
            "re,de->rd", logit_grad, router_low, preferred_element_type=jnp.float32
        )
        moe_input_grad, gain_two_grad = rms_back(after_attn, gain_two, inverse_two, normed_two_grad)
        after_grad = out_grad + moe_input_grad
        attn_grad = after_grad.astype(jnp.bfloat16)
        out_map_grad = outer_blocks(attn_grad, attended, BR, BC)
        mixture_grad = forward_map(attn_grad, out_maps).astype(jnp.bfloat16)
        grad_heads = head_view(mixture_grad)
        delta = jnp.einsum("rkgd,rkgd->kgr", grad_heads.astype(jnp.float32), mixture)
        query_grad, key_terms, value_terms = attend_back(
            query_heads,
            grad_heads,
            log_total,
            delta,
            all_keys,
            all_values,
            rows_pos,
            all_pos,
            key_span,
        )
        key_grad, value_grad = (
            lax.psum_scatter(
                key_terms.astype(jnp.bfloat16), "ctx", scatter_dimension=0, tiled=True
            ).astype(jnp.float32),
            lax.psum_scatter(
                value_terms.astype(jnp.bfloat16), "ctx", scatter_dimension=0, tiled=True
            ).astype(jnp.float32),
        )
        proj_grad = jnp.concatenate(
            [
                query_grad.reshape(row_count, query_width).astype(jnp.bfloat16),
                key_grad.astype(jnp.bfloat16),
                value_grad.astype(jnp.bfloat16),
            ],
            axis=1,
        )
        in_map_grad = outer_blocks(normed_one, proj_grad, BR, BC)
        normed_one_grad = backward_map(proj_grad, in_maps)
        attn_input_grad, gain_one_grad = rms_back(inputs, gain_one, inverse_one, normed_one_grad)
        input_rows.append(after_grad + attn_input_grad)
        gains_total = gains_total + jnp.stack([gain_one_grad, gain_two_grad])
        dense_term = jnp.concatenate([in_map_grad, out_map_grad], axis=1)
        dense_slots = dense_term.reshape(-1, BR, BC)[dense_order]
        expert_slots = expert_term.reshape(-1, BR, BC)[expert_order]
        dense_total = dense_total + lax.psum_scatter(
            dense_slots, ("ctx", "shard"), scatter_dimension=0, tiled=True
        )
        expert_total = expert_total + lax.psum_scatter(
            expert_slots.astype(jnp.bfloat16), "ctx", scatter_dimension=0, tiled=True
        ).astype(jnp.float32)
    expert_grad = expert_total[None]
    router_grad, gains_grad = lax.psum((router_total, gains_total), ("ctx", "shard"))
    dense_new, dense_moment_new, dense_second_new = soap(
        dense_weight, dense_total, dense_moment, dense_second, dense_left, dense_right
    )
    expert_new, expert_moment_new, expert_second_new = soap(
        expert_weight, expert_grad, expert_moment, expert_second, expert_left, expert_right
    )
    gains_new, gains_moment_new, gains_second_new = adam(
        norm_gains, gains_grad, gains_moment, gains_second, gain_rate
    )
    router_new, router_moment_new, router_second_new = adam(
        router, router_grad, router_moment, router_second, rate
    )
    return (
        jnp.stack(output_rows),
        jnp.stack(input_rows),
        dense_total,
        dense_new,
        dense_moment_new,
        dense_second_new,
        expert_grad,
        expert_new,
        expert_moment_new,
        expert_second_new,
        gains_grad,
        gains_new,
        gains_moment_new,
        gains_second_new,
        router_grad,
        router_new,
        router_moment_new,
        router_second_new,
    )


def solution(mesh):
    in_specs = (
        P("shard", "ctx", None),
        P("shard", "ctx", None),
        P(),
        P(),
        P(("ctx", "shard"), None, None),
        P("shard", "ctx", None, None),
        P("shard", "ctx", None),
        P(),
        P(),
        P(),
        P(("ctx", "shard"), None, None),
        P(("ctx", "shard"), None, None),
        P(("ctx", "shard"), None, None),
        P(("ctx", "shard"), None, None),
        P("shard", "ctx", None, None),
        P("shard", "ctx", None, None),
        P("shard", "ctx", None, None),
        P("shard", "ctx", None, None),
        P(),
        P(),
        P(),
        P(),
    )
    out_specs = (
        P("shard", "ctx", None),
        P("shard", "ctx", None),
        P(("ctx", "shard"), None, None),
        P(("ctx", "shard"), None, None),
        P(("ctx", "shard"), None, None),
        P(("ctx", "shard"), None, None),
        P("shard", "ctx", None, None),
        P("shard", "ctx", None, None),
        P("shard", "ctx", None, None),
        P("shard", "ctx", None, None),
        P(),
        P(),
        P(),
        P(),
        P(),
        P(),
        P(),
        P(),
    )
    return jax.shard_map(shards, mesh=mesh, in_specs=in_specs, out_specs=out_specs, check_vma=False)
```

profile of v0, /device:TPU:0, one launch (start us, length us, event | category | flops | bytes accessed | tf_op | source)
XLA Modules:
  0.0 1427.0 jit_solution(12759881883174957300)
XLA Ops:
  23.0 87.3 %all-gather.8.cloned.1.call-done = bf16[128,192,256]{2,1,0:T(8,128)(2,1)} async-done(((bf16[4,192,256]{2,1,0:T(8,128)(2,1)}), bf16[128,192,256]{2,1,0:T(8,128)(2,1)}) %all-gather.8.cloned.1.call-update) | async-done | bytes 12582928 | tf_op jit(solution)/shard_map/all_gather | solution.py:246
  110.3 13.3 gather_fusion
  123.6 11.0 slice_bitcast_fusion.5
  134.6 16.3 %copy.674 = bf16[8,10,192,256]{2,0,3,1:T(8,128)(2,1)} copy(bf16[8,10,192,256]{3,2,1,0:T(8,128)(2,1)} %get-tuple-element.969) | data formatting | bytes 15728640
  150.9 14.0 copy.488
  205.5 11.3 gather_fusion.2
  333.0 43.0 %scatter_fusion = bf16[4,128,1536]{2,1,0:T(8,128)(2,1)} fusion(bf16[4,128,1536]{2,1,0:T(8,128)(2,1)} %broadcast.557.clone, s32[256]{0:T(256)S(1)} %bitcast.893, bf16[256,1536]{1,0:T(8,128)(2,1)} %reshape.920), kind=kCustom, calls=%fused_computation.12 | custom fusion | bytes 2361344 | tf_op jit(solution)/shard_map/scatter | solution.py:281
  389.0 42.8 %scatter_fusion.2 = bf16[4,128,1536]{2,1,0:T(8,128)(2,1)} fusion(bf16[4,128,1536]{2,1,0:T(8,128)(2,1)} %broadcast.557.clone.1, s32[256]{0:T(256)S(1)} %bitcast.894, bf16[256,1536]{1,0:T(8,128)(2,1)} %multiply_convert_fusion.1), kind=kCustom, calls=%fused_computation.15 | custom fusion | bytes 2361344 | tf_op jit(solution)/shard_map/scatter | solution.py:308
  559.4 44.3 %scatter_fusion.1 = bf16[4,128,1536]{2,1,0:T(8,128)(2,1)} fusion(bf16[4,128,1536]{2,1,0:T(8,128)(2,1)} %broadcast.557.clone.2, s32[256]{0:T(256)S(1)} %bitcast.889, bf16[256,1536]{1,0:T(8,128)(2,1)} %reshape.934), kind=kCustom, calls=%fused_computation.14 | custom fusion | bytes 2361344 | tf_op jit(solution)/shard_map/scatter | solution.py:281
  618.3 44.9 %scatter_fusion.3 = bf16[4,128,1536]{2,1,0:T(8,128)(2,1)} fusion(bf16[4,128,1536]{2,1,0:T(8,128)(2,1)} %broadcast.557.clone.3, s32[256]{0:T(256)S(1)} %bitcast.890, bf16[256,1536]{1,0:T(8,128)(2,1)} %multiply_convert_fusion), kind=kCustom, calls=%fused_computation.16 | custom fusion | bytes 2361344 | tf_op jit(solution)/shard_map/scatter | solution.py:308
  715.1 11.6 all-to-all-done.3
  739.4 10.4 dot_general.259
  798.8 19.5 %while.82 = (s32[]{:T(128)}, f32[128,8,3,64]{0,3,2,1:T(8,128)}, bf16[2,512,8,64]{1,3,2,0:T(8,128)(2,1)}, bf16[2,512,8,64]{1,3,2,0:T(8,128)(2,1)}, bf16[2,512,8,6...) while((s32[]{:T(128)}, f32[128,8,3,64]{0,3,2,1:T(8,128)}, ...), condition=%wide.region_41.42_spmd.clone, body=%wide.region_40.41_spmd.clone.sunk | while | flops 1023082496 | bytes 70081536 | solution.py:152
  845.9 19.0 %while.83 = (s32[]{:T(128)}, f32[128,8,3,64]{0,3,2,1:T(8,128)}, bf16[2,512,8,64]{1,3,2,0:T(8,128)(2,1)}, bf16[2,512,8,64]{1,3,2,0:T(8,128)(2,1)}, bf16[2,512,8,6...) while((s32[]{:T(128)}, f32[128,8,3,64]{0,3,2,1:T(8,128)}, ...), condition=%wide.region_52.53_spmd.clone, body=%wide.region_51.52_spmd.clone.sunk | while | flops 1023082496 | bytes 68508640 | solution.py:152
  915.6 11.3 gather_fusion.9
  962.4 11.2 gather_fusion.10
  1005.6 17.8 %copy.558 = f32[8,16,192,256]{3,2,1,0:T(8,128)} copy(f32[8,16,192,256]{3,2,0,1:T(8,128)} %pad_maximum_fusion) | data formatting | bytes 50331648 | tf_op jit(solution)/shard_map/concatenate | solution.py:387
  1031.0 12.7 pad_maximum_fusion.1
  1043.7 17.7 %copy.561 = f32[8,16,192,256]{3,2,1,0:T(8,128)} copy(f32[8,16,192,256]{3,2,0,1:T(8,128)} %pad_maximum_fusion.1) | data formatting | bytes 50331648 | tf_op jit(solution)/shard_map/concatenate | solution.py:387
  1061.3 20.4 %gather_fusion.7 = f32[128,192,256]{2,1,0:T(8,128)} fusion(f32[128,192,256]{2,1,0:T(8,128)} %bitcast.883, s32[1024]{0:T(1024)S(1)} %pad_clamp_fusion.1), kind=kCustom, calls=%fused_computation.7 | custom fusion | bytes 50332160 | tf_op jit(solution)/shard_map/gather | solution.py:388
  1081.8 19.7 %gather_fusion.8 = f32[128,192,256]{2,1,0:T(8,128)} fusion(f32[128,192,256]{2,1,0:T(8,128)} %bitcast.884, s32[1024]{0:T(1024)S(1)} %pad_clamp_fusion.1), kind=kCustom, calls=%fused_computation.8 | custom fusion | bytes 50332160 | tf_op jit(solution)/shard_map/gather | solution.py:388
  1101.5 26.3 %add.390 = f32[128,192,256]{2,1,0:T(8,128)} add(f32[128,192,256]{2,1,0:T(8,128)} %gather_fusion.7, f32[128,192,256]{2,1,0:T(8,128)} %gather_fusion.8) | non-fusion elementwise | flops 6291456 | bytes 75497472 | tf_op jit(solution)/shard_map/add | solution.py:390
  1147.8 44.2 %all-reduce = (f32[2,1536]{1,0:T(2,128)S(1)}, f32[1536,4]{0,1:T(4,128)S(1)}) all-reduce(f32[2,1536]{1,0:T(2,128)S(1)} %maximum_add_fusion, f32[1536,4]{0,1:T(4,128)S(1)} %copy-done.102), channel_id=1, replica_groups=mesh['ctx'=8,'shard'=4] {'ctx','shard'}, use_global_device_ids=true, to_apply=%region_64.65 | all-reduce | flops 9216 | bytes 73728 | tf_op jit(solution)/shard_map/psum | solution.py:397
  1219.2 191.5 %reduce-scatter.20.cloned.1.call-done = f32[4,192,256]{2,1,0:T(8,128)} async-done(((f32[128,192,256]{2,1,0:T(8,128)}), f32[4,192,256]{2,1,0:T(8,128)}) %reduce-scatter.20.cloned.1.call-update) | async-done | bytes 786448 | tf_op jit(solution)/shard_map/reduce_scatter | solution.py:390
  (742 shorter events, 724.3 us)
Async XLA Ops:
  7.2 1200.1 %copy-start = (f32[1,12,256,256]{3,2,1,0:T(8,128)S(1)}, f32[1,12,256,256]{3,2,1,0:T(8,128)}, u32[]{:S(2)}) copy-start(f32[1,12,256,256]{3,2,1,0:T(8,128)} %param.51) | copy-start | bytes 9437188
  7.2 103.0 %all-gather.8.cloned.1.call-start = ((), (), s32[]{:S(2)}) async-start(), calls=%async_computation.15 | async-start | bytes 12976128 | tf_op jit(solution)/shard_map/all_gather | solution.py:246
  9.4 196.1 %all-gather.18.cloned.1.call-start = ((), (), s32[]{:S(2)}) async-start(), calls=%async_computation.22 | async-start | bytes 10616832 | tf_op jit(solution)/shard_map/all_gather | solution.py:252
  12.3 257.3 %all-gather.16.cloned.1.call-start = ((), (), s32[]{:S(2)}) async-start(), calls=%async_computation.19 | async-start | bytes 1179648 | tf_op jit(solution)/shard_map/all_gather | solution.py:264
  20.8 144.2 %copy-start.37 = (bf16[1,128,1536]{1,2,0:T(8,128)(2,1)}, bf16[1,128,1536]{1,2,0:T(8,128)(2,1)S(1)}, u32[]{:S(2)}) copy-start(bf16[1,128,1536]{1,2,0:T(8,128)(2,1)S(1)} %copy.511) | copy-start | bytes 1179652
  171.1 114.3 %all-gather.10.cloned.1.call-start = ((), (), s32[]{:S(2)}) async-start(), calls=%async_computation.16 | async-start | bytes 1179648 | tf_op jit(solution)/shard_map/all_gather | solution.py:265
  187.4 105.2 %all-gather.12.cloned.1.call-start = ((), (), s32[]{:S(2)}) async-start(), calls=%async_computation.17 | async-start | bytes 1179648 | tf_op jit(solution)/shard_map/all_gather | solution.py:264
  190.9 289.3 %all-gather.14.cloned.1.call-start = ((), (), s32[]{:S(2)}) async-start(), calls=%async_computation.18 | async-start | bytes 1179648 | tf_op jit(solution)/shard_map/all_gather | solution.py:265
  376.0 55.8 %all-to-all-start = ((bf16[4,128,1536]{2,1,0:T(8,128)(2,1)}), bf16[4,128,1536]{2,1,0:T(8,128)(2,1)}, u32[]{:S(2)}, u32[]{:S(2)}) async-start(bf16[4,128,1536]{2,1,0:T(8,128)(2,1)} %scatter_fusion), calls=%async_computation | async-start | bytes 3145728 | tf_op jit(solution)/shard_map/all_to_all | solution.py:282
  431.8 24.5 %all-to-all-start.4 = ((bf16[4,128,1536]{2,1,0:T(8,128)(2,1)}), bf16[4,128,1536]{2,1,0:T(8,128)(2,1)}, u32[]{:S(2)}, u32[]{:S(2)}) async-start(bf16[4,128,1536]{2,1,0:T(8,128)(2,1)} %scatter_fusion.2), calls=%async_computation.4 | async-start | bytes 3145728 | tf_op jit(solution)/shard_map/all_to_all | solution.py:309
  474.4 25.3 %all-to-all-start.1 = ((bf16[4,128,1536]{2,1,0:T(8,128)(2,1)}), bf16[4,128,1536]{2,1,0:T(8,128)(2,1)}, u32[]{:S(2)}, u32[]{:S(2)}) async-start(bf16[4,128,1536]{2,1,0:T(8,128)(2,1)} %bitcast.939), calls=%async_computation.1 | async-start | bytes 3145728 | tf_op jit(solution)/shard_map/all_to_all | solution.py:290
  499.6 38.0 %all-to-all-start.5 = ((bf16[4,128,1536]{2,1,0:T(8,128)(2,1)}), bf16[4,128,1536]{2,1,0:T(8,128)(2,1)}, u32[]{:S(2)}, u32[]{:S(2)}) async-start(bf16[4,128,1536]{2,1,0:T(8,128)(2,1)} %bitcast.937), calls=%async_computation.5 | async-start | bytes 3145728 | tf_op jit(solution)/shard_map/all_to_all | solution.py:325
  603.8 59.5 %all-to-all-start.2 = ((bf16[4,128,1536]{2,1,0:T(8,128)(2,1)}), bf16[4,128,1536]{2,1,0:T(8,128)(2,1)}, u32[]{:S(2)}, u32[]{:S(2)}) async-start(bf16[4,128,1536]{2,1,0:T(8,128)(2,1)} %scatter_fusion.1), calls=%async_computation.2 | async-start | bytes 3145728 | tf_op jit(solution)/shard_map/all_to_all | solution.py:282
  610.0 169.6 %copy-start.112 = (f32[128,4]{0,1:T(4,128)}, f32[128,4]{0,1:T(4,128)S(1)}, u32[]{:S(2)}) copy-start(f32[128,4]{0,1:T(4,128)S(1)} %fusion.209) | copy-start | bytes 6148
  663.2 22.2 %all-to-all-start.6 = ((bf16[4,128,1536]{2,1,0:T(8,128)(2,1)}), bf16[4,128,1536]{2,1,0:T(8,128)(2,1)}, u32[]{:S(2)}, u32[]{:S(2)}) async-start(bf16[4,128,1536]{2,1,0:T(8,128)(2,1)} %scatter_fusion.3), calls=%async_computation.6 | async-start | bytes 3145728 | tf_op jit(solution)/shard_map/all_to_all | solution.py:309
  703.5 23.2 %all-to-all-start.3 = ((bf16[4,128,1536]{2,1,0:T(8,128)(2,1)}), bf16[4,128,1536]{2,1,0:T(8,128)(2,1)}, u32[]{:S(2)}, u32[]{:S(2)}) async-start(bf16[4,128,1536]{2,1,0:T(8,128)(2,1)} %bitcast.940), calls=%async_computation.3 | async-start | bytes 3145728 | tf_op jit(solution)/shard_map/all_to_all | solution.py:290
  726.7 40.9 %all-to-all-start.7 = ((bf16[4,128,1536]{2,1,0:T(8,128)(2,1)}), bf16[4,128,1536]{2,1,0:T(8,128)(2,1)}, u32[]{:S(2)}, u32[]{:S(2)}) async-start(bf16[4,128,1536]{2,1,0:T(8,128)(2,1)} %bitcast.938), calls=%async_computation.7 | async-start | bytes 3145728 | tf_op jit(solution)/shard_map/all_to_all | solution.py:325
  731.1 258.3 %reduce-scatter.24.cloned.1.call-start = ((), (), s32[]{:S(2)}) async-start(), calls=%async_computation.25 | async-start | bytes 1179648
  825.9 164.6 %reduce-scatter.22.cloned.1.call-start = ((), (), s32[]{:S(2)}) async-start(), calls=%async_computation.24 | async-start | bytes 1179648
  843.7 179.7 %reduce-scatter.28.cloned.1.call-start = ((), (), s32[]{:S(2)}) async-start(), calls=%async_computation.27 | async-start | bytes 1179648
  872.5 152.6 %reduce-scatter.26.cloned.1.call-start = ((), (), s32[]{:S(2)}) async-start(), calls=%async_computation.26 | async-start | bytes 1179648
  880.1 317.9 %reduce-scatter.16.cloned.1.call-start = ((), (), s32[]{:S(2)}) async-start(), calls=%async_computation.20 | async-start | bytes 10616832 | tf_op jit(solution)/shard_map/reduce_scatter | solution.py:393
  926.9 271.0 %reduce-scatter.18.cloned.1.call-start = ((), (), s32[]{:S(2)}) async-start(), calls=%async_computation.21 | async-start | bytes 10616832 | tf_op jit(solution)/shard_map/reduce_scatter | solution.py:393
  973.6 437.1 %reduce-scatter.20.cloned.1.call-start = ((), (), s32[]{:S(2)}) async-start(), calls=%async_computation.23 | async-start | bytes 25952256 | tf_op jit(solution)/shard_map/reduce_scatter | solution.py:390
  (178 other events, 660.6 us)
Sparse Core Ops, SparseCore 0:
  11.5 98.7 all-gather.7
  112.5 88.9 all-gather.17
  203.1 20.5 all-gather.15
  225.7 21.7 all-gather.9
  249.5 21.8 all-gather.11
  272.8 21.6 all-gather.13
  826.0 34.4 reduce-scatter.23
  862.8 30.3 reduce-scatter.21
  895.5 30.6 reduce-scatter.27
  928.9 30.5 reduce-scatter.25
  961.8 97.9 reduce-scatter.15
  1062.0 97.8 reduce-scatter.17
  1166.9 243.7 reduce-scatter.19
where the time goes:
time: 1450 us; the launch traced here: 1430 us
  local copies, waits for them, and re-layouts  669 us (46%)
  waiting for transfers between devices  300 us (21%)
  matrix products  213 us (15%)
  other arithmetic  145 us (10%)
  blocking collectives  44.2 us (3%)
  starting transfers between devices  38.5 us (3%)
  between operations  15.9 us (1%)
    reduce_scatter x1, waiting for transfers between devices, shards(): lax.psum_scatter(dense_slots, ('ctx', 'shard'), scatter_dimension=0, tile...  191 us
    scatter x2, local copies, waits for them, and re-layouts, shards(): outgoing_grad = empty_slots.at[route_flat, slot_flat].set(sent_grad)  87.7 us
    scatter x2, local copies, waits for them, and re-layouts, shards(): empty_slots.at[route_flat, slot_flat].set(jnp.repeat(normed_two, 2, axis=0))  87.3 us
    all_gather x1, waiting for transfers between devices, shards(): lax.all_gather(dense_weight.astype(jnp.bfloat16), ('ctx', 'shard'), axis=...  87.3 us
    unnamed x262, local copies, waits for them, and re-layouts  83 us
    dot_general x10, matrix products, forward_map(): jnp.einsum('rai,abij->rbj', grouped, blocks, preferred_element_type=jnp.f...  49.9 us
    psum x1, blocking collectives, shards(): lax.psum((router_total, gains_total), ('ctx', 'shard'))  44.2 us
    dot_general x5, local copies, waits for them, and re-layouts, forward_map(): jnp.einsum('rai,abij->rbj', grouped, blocks, preferred_element_type=jnp.f...  42.8 us
  transfers between devices with their start and end apart: 21, of which 6 were waited for; matrix products, arithmetic and copies ran while one was open for 60% of the time, Pallas kernels for 0%

commit v1 on v0

v1 whole, which is shorter than its diff:
```python
import functools

import jax
import jax.numpy as jnp
from jax import lax
from jax.experimental import pallas as pl
from jax.experimental.pallas import tpu as pltpu
from jax.sharding import PartitionSpec as P

HEADS = 24
KVH = 8
HD = 64
FF = 1024
BR = 192
BC = 256
LANES = 128

norm_eps = 1e-06
beta_one = 0.9
beta_two = 0.95
rate = 0.01
gain_rate = 0.5
adam_eps = 1e-08
masked_score = -1e30
low_type = jnp.bfloat16
MIB = 1 << 20

NN = (((1,), (0,)), ((), ()))
NT = (((1,), (1,)), ((), ()))
TN = (((0,), (0,)), ((), ()))

in_vmem = pl.BlockSpec(memory_space=pltpu.VMEM)
in_smem = pl.BlockSpec(memory_space=pltpu.SMEM)
in_any = pl.BlockSpec(memory_space=pl.ANY)


def dot(left_side, right_side, dims=NN):
    return lax.dot_general(left_side, right_side, dims, preferred_element_type=jnp.float32)


def call(kernel, out_shapes, in_specs, out_specs, scratch, flops, moved, limit):
    return pl.pallas_call(
        kernel,
        out_shape=out_shapes,
        in_specs=in_specs,
        out_specs=out_specs,
        scratch_shapes=scratch,
        compiler_params=pltpu.CompilerParams(vmem_limit_bytes=limit * MIB),
        cost_estimate=pl.CostEstimate(flops=flops, bytes_accessed=moved, transcendentals=0),
    )


def shaped(dims, kind):
    return jax.ShapeDtypeStruct(dims, kind)


def inverse_order(slot_order):
    count = slot_order.shape[0]
    numbers = jnp.arange(count, dtype=jnp.int32)
    return jnp.sum(
        jnp.where(slot_order[None, :] == numbers[:, None], numbers[None, :], 0), axis=1
    ).astype(jnp.int32)


def wait_bytes(landed, semaphore):
    pltpu.make_async_copy(landed, landed, semaphore).wait()


def unit_rows(rows, gain):
    inverse = lax.rsqrt(jnp.mean(rows * rows, axis=-1, keepdims=True) + norm_eps)
    return rows * inverse * gain, inverse


def unit_back(rows, gain, inverse, gradient):
    unit = rows * inverse
    scaled = gradient * gain
    inner = jnp.mean(scaled * unit, axis=-1, keepdims=True)
    return inverse * (scaled - unit * inner), jnp.sum(gradient * unit, axis=0, keepdims=True)


def lane_ids(dims):
    return lax.broadcasted_iota(jnp.int32, dims, len(dims) - 1)


def half_turn(tile):
    return pltpu.roll(tile, HD, 1)


def stack_heads(ref, pair, scale=None):
    base = pair * (3 * LANES)
    tiles = [
        ref[:, pl.ds(pl.multiple_of(base + LANES * t, LANES), LANES)].astype(jnp.float32)
        for t in range(3)
    ]
    if scale is not None:
        tiles = [t * scale for t in tiles]
    lower = lane_ids(tiles[0].shape) < HD
    first = [tiles[0], half_turn(tiles[0]), tiles[1]]
    second = [tiles[1], half_turn(tiles[2]), tiles[2]]
    return (
        jnp.concatenate([jnp.where(lower, t, 0.0) for t in first], axis=0),
        jnp.concatenate([jnp.where(lower, 0.0, t) for t in second], axis=0),
    )


def unstack_heads(ref, pair, first, second):
    rows = first.shape[0] // 3
    base = pair * (3 * LANES)
    lower = lane_ids((rows, LANES)) < HD
    tiles = (
        jnp.where(lower, first[:rows], half_turn(first[rows : 2 * rows])),
        jnp.where(lower, first[2 * rows :], second[:rows]),
        jnp.where(lower, half_turn(second[rows : 2 * rows]), second[2 * rows :]),
    )
    for t in range(3):
        ref[:, pl.ds(pl.multiple_of(base + LANES * t, LANES), LANES)] = tiles[t].astype(ref.dtype)


def project_kernel(order_ref, x_ref, gain_ref, w_ref, h_ref, q_ref, kv_ref, held, sems):
    row_groups = x_ref.shape[-1] // BR
    groups = held.shape[0]
    q_groups = q_ref.shape[-1] // BC
    all_groups = w_ref.shape[0] // row_groups
    micros = x_ref.shape[0]
    rows = x_ref.shape[1]

    @pl.loop(0, groups)
    def _(b):
        for a in range(row_groups):
            pltpu.make_async_copy(
                w_ref.at[order_ref[a * all_groups + b]], held.at[b, pl.ds(a * BR, BR)], sems.at[b]
            ).start()

    for m in range(micros):
        h_ref[pl.ds(m * rows, rows), :] = unit_rows(x_ref[m], gain_ref[0:1])[0].astype(low_type)

    @pl.loop(0, q_groups)
    def _(b):
        wait_bytes(held.at[b], sems.at[b])
        made = dot(h_ref[...], held[b]).astype(low_type)
        for m in range(micros):
            q_ref[m, :, pl.ds(pl.multiple_of(b * BC, BC), BC)] = made[m * rows : (m + 1) * rows]

    @pl.loop(q_groups, groups)
    def _(b):
        wait_bytes(held.at[b], sems.at[b])
        made = dot(h_ref[...], held[b]).astype(low_type)
        for m in range(micros):
            kv_ref[m, :, pl.ds(pl.multiple_of((b - q_groups) * BC, BC), BC)] = made[
                m * rows : (m + 1) * rows
            ]


def project(order, x, gains, w):
    micros, rows, width = x.shape
    groups = (HEADS + 2 * KVH) * HD // BC
    return call(
        project_kernel,
        (
            shaped((micros * rows, width), low_type),
            shaped((micros, rows, HEADS * HD), low_type),
            shaped((micros, rows, 2 * KVH * HD), low_type),
        ),
        [in_smem, in_vmem, in_vmem, in_any],
        (in_vmem, in_vmem, in_vmem),
        [pltpu.VMEM((groups, width, BC), low_type), pltpu.SemaphoreType.DMA((groups,))],
        2 * micros * rows * width * groups * BC,
        groups * width * BC * 2,
        24,
    )(order, x, gains, w)


def start_matrix(order_ref, w_ref, held, sem, first_group, all_groups):
    row_groups = held.shape[0] // BR
    groups = held.shape[1] // BC

    @pl.loop(0, row_groups)
    def _(a):
        for b in range(groups):
            pltpu.make_async_copy(
                w_ref.at[order_ref[a * all_groups + first_group + b]],
                held.at[pl.ds(pl.multiple_of(a * BR, 64), BR), pl.ds(b * BC, BC)],
                sem,
            ).start()


def attend_kernel(
    all_groups, order_ref, q_ref, kv_ref, rpos_ref, kpos_ref, x_ref, gain_ref, w_ref,
    ob_ref, log_ref, x2_ref, h2_ref, bias, held, sem,
):
    rows = q_ref.shape[0]
    in_groups = (HEADS + 2 * KVH) * HD // BC
    start_matrix(order_ref, w_ref, held, sem, in_groups, all_groups)
    bias[...] = jnp.where(kpos_ref[...] <= rpos_ref[...], 0.0, masked_score)
    log_ref[...] = jnp.zeros_like(log_ref)
    length = kv_ref.shape[0]

    @pl.loop(0, KVH // 2)
    def _(pair):
        lane = pl.multiple_of(pair * LANES, LANES)
        keys = kv_ref[:, pl.ds(lane, LANES)]
        values = kv_ref[:, pl.ds(pl.multiple_of(lane + KVH * HD, LANES), LANES)]
        stacked = stack_heads(q_ref, pair, HD**-0.5)
        mixed = []
        for part in range(2):
            scores = dot(stacked[part].astype(low_type), keys, NT)
            scores = (scores.reshape(3, rows, length) + bias[...][None]).reshape(3 * rows, length)
            largest = jnp.max(scores, axis=-1, keepdims=True)
            raised = jnp.exp(scores - largest)
            summed = jnp.sum(raised, axis=-1, keepdims=True)
            mixed.append(dot(raised.astype(low_type), values) / summed)
            log_ref[...] = jnp.where(
                lane_ids(log_ref.shape) == 2 * pair + part, largest + jnp.log(summed), log_ref[...]
            )
        unstack_heads(ob_ref, pair, mixed[0], mixed[1])

    wait_bytes(held, sem)
    for n in range(held.shape[0] // BC):
        cut = slice(n * BC, (n + 1) * BC)
        x2_ref[:, cut] = x_ref[:, cut] + dot(ob_ref[...], held[cut, :], NT)
    h2_ref[...] = unit_rows(x2_ref[...], gain_ref[1:2])[0].astype(low_type)


def attend(order, q, kv, rows_pos, key_pos, x, gains, w):
    rows, width = q.shape
    length = kv.shape[0]
    model = x.shape[1]
    return call(
        functools.partial(attend_kernel, w.shape[0] * BR // model),
        (
            shaped((rows, width), low_type),
            shaped((3 * rows, LANES), jnp.float32),
            shaped((rows, model), jnp.float32),
            shaped((rows, model), low_type),
        ),
        [in_smem] + [in_vmem] * 6 + [in_any],
        (in_vmem,) * 4,
        [
            pltpu.VMEM((rows, length), jnp.float32),
            pltpu.VMEM((model, width), low_type),
            pltpu.SemaphoreType.DMA,
        ],
        16 * rows * length * width,
        8 * MIB,
        40,
    )(order, q, kv, rows_pos, key_pos, x, gains, w)


def router_parts(h2, router, experts):
    logits = dot(h2, router)
    logits = jnp.where(lane_ids(logits.shape) < experts, logits, masked_score)
    raised = jnp.exp(logits - jnp.max(logits, axis=-1, keepdims=True))
    return raised / jnp.sum(raised, axis=-1, keepdims=True)


def expert_kernel(sources, micro, order_ref, me_ref, router_ref, *refs):
    h_parts = refs[:sources]
    c_parts = refs[sources : 2 * sources]
    w_ref = refs[2 * sources]
    outs = refs[2 * sources + 1 :]
    back_refs = outs[:sources]
    out_refs = outs[sources : 2 * sources]
    z_ref, dg_ref, du_ref, dy_ref, xs_ref = outs[2 * sources : 2 * sources + 5]
    cs, held, chance, load_sem, w_sems = outs[2 * sources + 5 :]
    rows, width = h_parts[0].shape
    row_groups = width // BR
    col_groups = FF // BC
    for j in range(sources):
        pltpu.make_async_copy(h_parts[j], xs_ref.at[pl.ds(j * rows, rows)], load_sem.at[0]).start()
        pltpu.make_async_copy(
            c_parts[j].at[pl.ds(micro * rows, rows)], cs.at[pl.ds(j * rows, rows)], load_sem.at[1]
        ).start()
    for k in (0, 1, 2):

        @pl.loop(0, row_groups)
        def _(a):
            for b in range(col_groups):
                pltpu.make_async_copy(
                    w_ref.at[order_ref[(k * row_groups + a) * col_groups + b]],
                    held.at[k, pl.ds(pl.multiple_of(a * BR, 64), BR), pl.ds(b * BC, BC)],
                    w_sems.at[k],
                ).start()

    wait_bytes(xs_ref, load_sem.at[0])
    wait_bytes(cs, load_sem.at[1])
    me = me_ref[0]
    probs = router_parts(xs_ref[...], router_ref[...], sources)
    hits = cs[:, width:].astype(jnp.float32)
    mine = lane_ids(hits.shape) == me
    hit = jnp.sum(jnp.where(mine, hits, 0.0), axis=-1, keepdims=True)
    weight = jnp.sum(jnp.where(mine, probs, 0.0), axis=-1, keepdims=True) * hit
    dy_ref[...] = (weight * cs[:, :width].astype(jnp.float32)).astype(low_type)
    chance[...] = jnp.zeros_like(chance)
    for k in (0, 1, 2):
        wait_bytes(held.at[k], w_sems.at[k])

    @pl.loop(0, col_groups)
    def _(b):
        cut = pl.ds(pl.multiple_of(b * BC, BC), BC)
        gate = dot(xs_ref[...], held[0, :, cut])
        up = dot(xs_ref[...], held[1, :, cut])
        down = dot(cs[:, :width], held[2, :, cut])
        sig = jax.nn.sigmoid(gate)
        act = gate * sig
        hidden = act * up
        z_ref[:, cut] = hidden.astype(low_type)
        chance[...] += jnp.sum(down * hidden, axis=-1, keepdims=True)
        down = down * weight
        dg_ref[:, cut] = (down * up * sig * (1.0 + gate * (1.0 - sig))).astype(low_type)
        du_ref[:, cut] = (down * act).astype(low_type)

    for n in range(width // BC):
        cut = slice(n * BC, (n + 1) * BC)
        back = dot(dg_ref[...], held[0, cut, :], NT) + dot(du_ref[...], held[1, cut, :], NT)
        for j in range(sources):
            back_refs[j][:, cut] = back[j * rows : (j + 1) * rows].astype(low_type)
    told = chance[...] * hit
    high_part = told.astype(low_type)
    low_part = (told - high_part.astype(jnp.float32)).astype(low_type)
    lanes = lane_ids((sources * rows, LANES))
    tail = jnp.where(lanes == 0, high_part, jnp.where(lanes == 1, low_part, jnp.zeros_like(low_part)))
    for j in range(sources):
        back_refs[j][:, width:] = tail[j * rows : (j + 1) * rows]
    for n in range(width // BC):
        cut = slice(n * BC, (n + 1) * BC)
        made = dot(z_ref[...], held[2, cut, :], NT) * weight
        for j in range(sources):
            out_refs[j][:, cut] = made[j * rows : (j + 1) * rows].astype(low_type)


def run_expert(micro, order, me, router, h_parts, c_parts, w):
    sources = len(h_parts)
    rows, width = h_parts[0].shape
    total = sources * rows
    return call(
        functools.partial(expert_kernel, sources, micro),
        tuple(
            [shaped((rows, width + LANES), low_type)] * sources
            + [shaped((rows, width), low_type)] * sources
            + [shaped((total, FF), low_type)] * 3
            + [shaped((total, width), low_type)] * 2
        ),
        [in_smem, in_smem, in_vmem] + [in_any] * (2 * sources + 1),
        tuple([in_vmem] * (2 * sources + 5)),
        [
            pltpu.VMEM((total, width + LANES), low_type),
            pltpu.VMEM((3, width, FF), low_type),
            pltpu.VMEM((total, 1), jnp.float32),
            pltpu.SemaphoreType.DMA((2,)),
            pltpu.SemaphoreType.DMA((3,)),
        ],
        12 * total * width * FF,
        20 * MIB,
        56,
    )(order, me, router, *h_parts, *c_parts, w)


def outer_kernel(place, pairs, order_ref, *refs):
    count = len(pairs)
    micros = len(refs[:-3]) // (2 * count)
    lefts = refs[: count * micros]
    rights = refs[count * micros : 2 * count * micros]
    out_ref, stage, sems = refs[-3:]
    span = 2 * BR
    steps = []
    for k in range(count):
        for p in range(lefts[k * micros].shape[-1] // span):
            steps.append((k, p))

    def wait_stage(slot, cols):
        wait_bytes(stage.at[slot, :, pl.ds(0, cols)], sems.at[slot])

    used = [None, None]
    for n, (k, p) in enumerate(steps):
        slot = n % 2
        cols = rights[k * micros].shape[-1]
        if used[slot] is not None:
            wait_stage(slot, used[slot])
        used[slot] = cols
        cut = slice(p * span, (p + 1) * span)
        for c in range(0, cols, 512):
            part = slice(c, c + 512)
            made = sum(
                dot(lefts[k * micros + m][:, cut], rights[k * micros + m][:, part], TN)
                for m in range(micros)
            )
            stage[slot, :, part] = made.astype(low_type)
        first, row_step = place(k)
        for half in range(2):
            for b in range(cols // BC):
                pltpu.make_async_copy(
                    stage.at[slot, pl.ds(half * BR, BR), pl.ds(b * BC, BC)],
                    out_ref.at[order_ref[first + (2 * p + half) * row_step + b]],
                    sems.at[slot],
                ).start()
    for slot in range(2):
        if used[slot] is not None:
            wait_stage(slot, used[slot])


def outer_blocks(order, place, lefts, rights, blocks):
    pairs = [(l[0].shape[-1], r[0].shape[-1]) for l, r in zip(lefts, rights)]
    widest = max(r for _, r in pairs)
    rows = sum(l.shape[0] for l in lefts[0])
    flat = [l for group in lefts for l in group] + [r for group in rights for r in group]
    return call(
        functools.partial(outer_kernel, place, pairs),
        shaped((blocks, BR, BC), low_type),
        [in_smem] + [in_vmem] * len(flat),
        in_any,
        [pltpu.VMEM((2, 2 * BR, widest), low_type), pltpu.SemaphoreType.DMA((2,))],
        2 * rows * blocks * BR * BC,
        blocks * BR * BC * 2 + sum(f.size * 2 for f in flat),
        48,
    )(order, *flat)


def merge_kernel(
    all_groups, sources, order_ref, me_ref, x2_ref, cot_ref, h2_ref, gain_ref, router_ref, w_ref, *refs
):
    back_refs = refs[:sources]
    dx_ref, da_ref, do_ref, stat_ref, held, sem = refs[sources:]
    rows, width = x2_ref.shape
    in_groups = (HEADS + 2 * KVH) * HD // BC
    start_matrix(order_ref, w_ref, held, sem, in_groups, all_groups)
    lanes = lane_ids((rows, LANES))
    prob_grad = jnp.zeros((rows, LANES), jnp.float32)
    gathered = jnp.zeros((rows, width), jnp.float32)
    for j in range(sources):
        tail = back_refs[j][:, width:].astype(jnp.float32)
        told = jnp.sum(tail, axis=-1, keepdims=True)
        expert = jnp.bitwise_xor(me_ref[0], j)
        prob_grad = prob_grad + jnp.where(lanes == expert, told, 0.0)
        gathered = gathered + back_refs[j][:, :width].astype(jnp.float32)
    h2 = h2_ref[...]
    probs = router_parts(h2, router_ref[...], sources)
    logit_grad = probs * (prob_grad - jnp.sum(probs * prob_grad, axis=-1, keepdims=True))
    high_part = logit_grad.astype(low_type)
    low_part = (logit_grad - high_part.astype(jnp.float32)).astype(low_type)
    router_grad = dot(high_part, h2, TN) + dot(low_part, h2, TN)
    gathered = gathered + dot(high_part, router_ref[...], NT) + dot(low_part, router_ref[...], NT)
    x2 = x2_ref[...]
    inverse = lax.rsqrt(jnp.mean(x2 * x2, axis=-1, keepdims=True) + norm_eps)
    moe_grad, gain_grad = unit_back(x2, gain_ref[1:2], inverse, gathered)
    after = cot_ref[...] + moe_grad
    dx_ref[...] = after
    da_ref[...] = after.astype(low_type)
    experts_up = stat_ref.shape[0] - 8
    stat_ref[:experts_up] = router_grad[:experts_up]
    stat_ref[experts_up:] = jnp.broadcast_to(gain_grad, (8, width))
    wait_bytes(held, sem)
    for n in range(held.shape[1] // BC):
        cut = slice(n * BC, (n + 1) * BC)
        do_ref[:, cut] = dot(da_ref[...], held[:, cut]).astype(low_type)


def merge(order, me, x2, cot, h2, gains, router, w, backs):
    rows, width = x2.shape
    sources = len(backs)
    experts_up = -(-sources // 8) * 8
    return call(
        functools.partial(merge_kernel, w.shape[0] * BR // width, sources),
        (
            shaped((rows, width), jnp.float32),
            shaped((rows, width), low_type),
            shaped((rows, HEADS * HD), low_type),
            shaped((experts_up + 8, width), jnp.float32),
        ),
        [in_smem, in_smem] + [in_vmem] * 5 + [in_any] + [in_vmem] * sources,
        (in_vmem,) * 4,
        [pltpu.VMEM((width, HEADS * HD), low_type), pltpu.SemaphoreType.DMA],
        2 * rows * width * HEADS * HD,
        10 * MIB,
        40,
    )(order, me, x2, cot, h2, gains, router, w, *backs)


def attend_back_kernel(
    q_ref, kv_ref, rpos_ref, kpos_ref, ob_ref, log_ref, do_ref, dq_ref, dkv_ref, bias
):
    rows = q_ref.shape[0]
    length = kv_ref.shape[0]
    bias[...] = jnp.where(kpos_ref[...] <= rpos_ref[...], 0.0, masked_score)

    @pl.loop(0, KVH // 2)
    def _(pair):
        lane = pl.multiple_of(pair * LANES, LANES)
        value_lane = pl.multiple_of(lane + KVH * HD, LANES)
        keys = kv_ref[:, pl.ds(lane, LANES)]
        values = kv_ref[:, pl.ds(value_lane, LANES)]
        queries = stack_heads(q_ref, pair, HD**-0.5)
        grads = stack_heads(do_ref, pair)
        mixes = stack_heads(ob_ref, pair)
        query_grads = []
        key_grad = value_grad = None
        for part in range(2):
            query = queries[part].astype(low_type)
            grad = grads[part].astype(low_type)
            log_total = jnp.sum(
                jnp.where(lane_ids(log_ref.shape) == 2 * pair + part, log_ref[...], 0.0),
                axis=-1,
                keepdims=True,
            )
            delta = jnp.sum(grads[part] * mixes[part], axis=-1, keepdims=True)
            scores = dot(query, keys, NT)
            scores = (scores.reshape(3, rows, length) + bias[...][None]).reshape(3 * rows, length)
            chance = jnp.exp(scores - log_total)
            prob_grad = dot(grad, values, NT)
            score_grad = (chance * (prob_grad - delta)).astype(low_type)
            value_term = dot(chance.astype(low_type), grad, TN)
            key_term = dot(score_grad, query, TN)
            key_grad = key_term if part == 0 else key_grad + key_term
            value_grad = value_term if part == 0 else value_grad + value_term
            query_grads.append(dot(score_grad, keys) * HD**-0.5)
        unstack_heads(dq_ref, pair, query_grads[0], query_grads[1])
        dkv_ref[:, pl.ds(lane, LANES)] = key_grad.astype(low_type)
        dkv_ref[:, pl.ds(value_lane, LANES)] = value_grad.astype(low_type)


def attend_back(q, kv, rows_pos, key_pos, ob, log_total, do):
    rows, width = q.shape
    length = kv.shape[0]
    return call(
        attend_back_kernel,
        (shaped((rows, width), low_type), shaped(kv.shape, low_type)),
        [in_vmem] * 7,
        (in_vmem,) * 2,
        [pltpu.VMEM((rows, length), jnp.float32)],
        40 * rows * length * width,
        8 * MIB,
        48,
    )(q, kv, rows_pos, key_pos, ob, log_total, do)


def input_kernel(all_groups, order_ref, x_ref, gain_ref, w_ref, *refs):
    micros = x_ref.shape[0]
    rows = x_ref.shape[1]
    dx_refs = refs[:micros]
    dq_refs = refs[micros : 2 * micros]
    dkv_refs = refs[2 * micros : 3 * micros]
    out_ref, stat_ref, grad, held, sem = refs[3 * micros :]
    start_matrix(order_ref, w_ref, held, sem, 0, all_groups)
    q_width = dq_refs[0].shape[-1]
    wait_bytes(held, sem)
    for n in range(held.shape[0] // BC):
        cut = slice(n * BC, (n + 1) * BC)
        for m in range(micros):
            grad[m, :, cut] = dot(dq_refs[m][...], held[cut, :q_width], NT) + dot(
                dkv_refs[m][...], held[cut, q_width:], NT
            )
    total = jnp.zeros((1, x_ref.shape[-1]), jnp.float32)
    for m in range(micros):
        x = x_ref[m]
        inverse = lax.rsqrt(jnp.mean(x * x, axis=-1, keepdims=True) + norm_eps)
        term, gain_grad = unit_back(x, gain_ref[0:1], inverse, grad[m])
        out_ref[m] = dx_refs[m][...] + term
        total = total + gain_grad
    stat_ref[...] = jnp.broadcast_to(total, stat_ref.shape)


def input_back(order, x, gains, w, dxs, dqs, dkvs):
    micros, rows, width = x.shape
    in_width = (HEADS + 2 * KVH) * HD
    return call(
        functools.partial(input_kernel, w.shape[0] * BR // width),
        (shaped(x.shape, jnp.float32), shaped((8, width), jnp.float32)),
        [in_smem, in_vmem, in_vmem, in_any] + [in_vmem] * (3 * micros),
        (in_vmem,) * 2,
        [
            pltpu.VMEM(x.shape, jnp.float32),
            pltpu.VMEM((width, in_width), low_type),
            pltpu.SemaphoreType.DMA,
        ],
        2 * micros * rows * width * in_width,
        14 * MIB,
        40,
    )(order, x, gains, w, *dxs, *dqs, *dkvs)


def rotate_kernel(
    b_ref, g_ref, m_ref, s_ref, l_ref, r_ref, grad_ref, new_ref, moment_ref, second_ref
):
    gradient = g_ref[0].astype(jnp.float32)
    grad_ref[0] = gradient
    left = l_ref[0].astype(low_type)
    right = r_ref[0].astype(low_type)
    rotated = dot(dot(left, gradient.astype(low_type), TN).astype(low_type), right)
    moment = beta_one * m_ref[0] + (1.0 - beta_one) * rotated
    second = beta_two * s_ref[0] + (1.0 - beta_two) * rotated * rotated
    moment_ref[0] = moment
    second_ref[0] = second
    direction = (moment / (jnp.sqrt(second) + adam_eps)).astype(low_type)
    turned = dot(dot(left, direction).astype(low_type), right, NT)
    new_ref[0] = b_ref[0] - rate * turned


def rotate(weight, gradient, moment, second, left, right):
    count = weight.shape[0]

    def spec(rows, cols):
        return pl.BlockSpec((1, rows, cols), lambda i: (i, 0, 0))

    block = spec(BR, BC)
    return pl.pallas_call(
        rotate_kernel,
        grid=(count,),
        out_shape=(shaped(weight.shape, jnp.float32),) * 4,
        in_specs=[block] * 4 + [spec(BR, BR), spec(BC, BC)],
        out_specs=(block,) * 4,
        compiler_params=pltpu.CompilerParams(vmem_limit_bytes=24 * MIB),
        cost_estimate=pl.CostEstimate(
            flops=4 * count * BR * BC * (BR + BC),
            bytes_accessed=count * 2 * MIB,
            transcendentals=0,
        ),
    )(weight, gradient, moment, second, left, right)


def adam(weight, gradient, moment, second, step_rate):
    moment_new = beta_one * moment + (1.0 - beta_one) * gradient
    second_new = beta_two * second + (1.0 - beta_two) * gradient * gradient
    return (
        weight - step_rate * moment_new / (jnp.sqrt(second_new) + adam_eps),
        moment_new,
        second_new,
    )


def to_partner(array, offset):
    if offset == 0:
        return array
    count = lax.axis_size("shard")
    return lax.ppermute(array, "shard", [(i, i ^ offset) for i in range(count)])


def shards(
    tokens,
    cotangent,
    norm_gains,
    router,
    dense_weight,
    expert_weight,
    routes,
    assign,
    dense_order,
    expert_order,
    dense_moment,
    dense_second,
    dense_left,
    dense_right,
    expert_moment,
    expert_second,
    expert_left,
    expert_right,
    gains_moment,
    gains_second,
    router_moment,
    router_second,
):
    ctx_count = lax.axis_size("ctx")
    shard_count = lax.axis_size("shard")
    micros, rows, width = tokens.shape
    span = rows // 2
    length = rows * ctx_count
    dense_groups = (2 * HEADS + 2 * KVH) * HD // BC
    in_groups = (HEADS + 2 * KVH) * HD // BC
    row_groups = width // BR
    ff_groups = FF // BC
    dense_blocks = row_groups * dense_groups
    expert_blocks = 3 * row_groups * ff_groups

    dense_inverse = inverse_order(dense_order)
    expert_inverse = inverse_order(expert_order)
    row_ids = jnp.arange(rows, dtype=jnp.int32)
    all_pos = (assign[:, row_ids // span] * span + row_ids % span).reshape(length)
    rows_pos = lax.dynamic_slice_in_dim(all_pos, lax.axis_index("ctx") * rows, rows)
    rows_pos = rows_pos.reshape(rows, 1)
    key_pos = all_pos.reshape(1, length)
    me = lax.axis_index("shard").astype(jnp.int32).reshape(1)
    router_pad = jnp.pad(router.astype(low_type), ((0, 0), (0, LANES - shard_count)))

    dense_all = lax.all_gather(dense_weight.astype(low_type), ("ctx", "shard"), axis=0, tiled=True)
    expert_all = lax.all_gather(expert_weight[0].astype(low_type), "ctx", axis=0, tiled=True)

    lanes = jnp.arange(LANES, dtype=jnp.int32)
    hits = jnp.sum((routes[..., None] == lanes).astype(low_type), axis=2)
    cot_rows = jnp.concatenate([cotangent.astype(low_type), hits], axis=2)
    cot_rows = cot_rows.reshape(micros * rows, width + LANES)
    cot_parts = [to_partner(cot_rows, j) for j in range(shard_count)]

    h1, q, kv = project(dense_inverse, tokens, norm_gains, dense_all)
    kv_all = [lax.all_gather(kv[m], "ctx", axis=0, tiled=True) for m in range(micros)]
    obs, logs, x2s, h2s = [], [], [], []
    for m in range(micros):
        ob, log_total, x2, h2 = attend(
            dense_inverse, q[m], kv_all[m], rows_pos, key_pos, tokens[m], norm_gains, dense_all
        )
        obs.append(ob)
        logs.append(log_total)
        x2s.append(x2)
        h2s.append(h2)

    outputs, backs = [], []
    zs, dgs, dus, dys, xs = [], [], [], [], []
    for m in range(micros):
        h_parts = [to_partner(h2s[m], j) for j in range(shard_count)]
        made = run_expert(m, expert_inverse, me, router_pad, h_parts, cot_parts, expert_all)
        back = made[:shard_count]
        out = made[shard_count : 2 * shard_count]
        z, dg, du, dy, x = made[2 * shard_count :]
        zs.append(z)
        dgs.append(dg)
        dus.append(du)
        dys.append(dy)
        xs.append(x)
        backs.append([to_partner(back[j], j) for j in range(shard_count)])
        arrived = [to_partner(out[j], j) for j in range(shard_count)]
        total = x2s[m]
        for part in arrived:
            total = total + part.astype(jnp.float32)
        outputs.append(total)

    expert_slots = inverse_slots = expert_inverse
    expert_term = outer_blocks(
        expert_slots,
        lambda k: (k * row_groups * ff_groups, ff_groups),
        [xs, xs, dys],
        [dgs, dus, zs],
        expert_blocks,
    )
    expert_sum = lax.psum_scatter(expert_term, "ctx", scatter_dimension=0, tiled=True)

    dxs, das, dqs, dkvs, stats = [], [], [], [], []
    for m in range(micros):
        dx, da, do, stat = merge(
            dense_inverse, me, x2s[m], cotangent[m], h2s[m], norm_gains, router_pad, dense_all, backs[m]
        )
        dq, dkv_part = attend_back(q[m], kv_all[m], rows_pos, key_pos, obs[m], logs[m], do)
        dkv = lax.psum_scatter(dkv_part, "ctx", scatter_dimension=0, tiled=True)
        dxs.append(dx)
        das.append(da)
        dqs.append(dq)
        dkvs.append(dkv)
        stats.append(stat)

    h1s = [h1[m * rows : (m + 1) * rows] for m in range(micros)]
    q_groups = HEADS * HD // BC
    starts = (0, q_groups, in_groups)
    dense_term = outer_blocks(
        dense_inverse,
        lambda k: (starts[k], dense_groups),
        [h1s, h1s, das],
        [dqs, dkvs, obs],
        dense_blocks,
    )
    dense_sum = lax.psum_scatter(dense_term, ("ctx", "shard"), scatter_dimension=0, tiled=True)
    input_grad, gain_stat = input_back(
        dense_inverse, tokens, norm_gains, dense_all, dxs, dqs, dkvs
    )
    experts_up = stats[0].shape[0] - 8
    stat_rows = jnp.concatenate(
        [sum(stats)[: experts_up + 1], gain_stat[: 7]], axis=0
    )
    stat_rows = lax.psum(stat_rows, ("ctx", "shard"))
    router_grad = stat_rows[:shard_count].T
    gains_grad = jnp.stack([stat_rows[experts_up + 1], stat_rows[experts_up]])

    expert_grad, expert_new, expert_moment_new, expert_second_new = rotate(
        expert_weight[0], expert_sum, expert_moment[0], expert_second[0], expert_left[0], expert_right[0]
    )
    dense_grad, dense_new, dense_moment_new, dense_second_new = rotate(
        dense_weight, dense_sum, dense_moment, dense_second, dense_left, dense_right
    )
    gains_new, gains_moment_new, gains_second_new = adam(
        norm_gains, gains_grad, gains_moment, gains_second, gain_rate
    )
    router_new, router_moment_new, router_second_new = adam(
        router, router_grad, router_moment, router_second, rate
    )
    return (
        jnp.stack(outputs),
        input_grad,
        dense_grad,
        dense_new,
        dense_moment_new,
        dense_second_new,
        expert_grad[None],
        expert_new[None],
        expert_moment_new[None],
        expert_second_new[None],
        gains_grad,
        gains_new,
        gains_moment_new,
        gains_second_new,
        router_grad,
        router_new,
        router_moment_new,
        router_second_new,
    )


def solution(mesh):
    rows_spec = P("shard", "ctx", None)
    dense_spec = P(("ctx", "shard"), None, None)
    expert_spec = P("shard", "ctx", None, None)
    in_specs = (
        (rows_spec, rows_spec, P(), P(), dense_spec, expert_spec, rows_spec, P(), P(), P())
        + (dense_spec,) * 4
        + (expert_spec,) * 4
        + (P(),) * 4
    )
    out_specs = (rows_spec,) * 2 + (dense_spec,) * 4 + (expert_spec,) * 4 + (P(),) * 8
    return jax.shard_map(shards, mesh=mesh, in_specs=in_specs, out_specs=out_specs, check_vma=False)
```

time: 1450 us -> 870 us (0.60)
  local copies, waits for them, and re-layouts: 669 us -> 66.7 us
  waiting for transfers between devices: 300 us -> 575 us
  matrix products: 213 us -> 0 us
  Pallas kernels: 0 us -> 159 us
  other arithmetic: 145 us -> 16.4 us
  blocking collectives: 44.2 us -> 0 us
    dot_general x72 -> x0, matrix products: 213 us -> none  [the longest x10 49.9 us: forward_map(): jnp.einsum('rai,abij->rbj', grouped, blocks, preferred_element_type=jnp.f...]
    scatter x6 -> x0, local copies, waits for them, and re-layouts: 178 us -> none  [the longest x2 87.7 us: shards(): outgoing_grad = empty_slots.at[route_flat, slot_flat].set(sent_grad)]
    pallas_call x0 -> x14, Pallas kernels: none -> 159 us  [the longest x2 40.2 us: run_expert(): call(functools.partial(expert_kernel, sources, micro), tuple([shaped((row...]
    gather x12 -> x1, local copies, waits for them, and re-layouts: 106 us -> 0.64 us  [shards(): assign[:, row_ids // span] * span + row_ids % span]
    all_gather x6 -> x4, waiting for transfers between devices: 87.3 us -> 185 us  [the longest x1 100 us: shards(): lax.all_gather(dense_weight.astype(low_type), ('ctx', 'shard'), axis=0, t...]
    reduce_scatter x3 -> x4, waiting for transfers between devices: 191 us -> 272 us  [the longest x1 141 us: shards(): lax.psum_scatter(dense_term, ('ctx', 'shard'), scatter_dimension=0, tiled...]
    ppermute x0 -> x21, waiting for transfers between devices: none -> 76 us  [to_partner(): return lax.ppermute(array, 'shard', [(i, i ^ offset) for i in range(count)])]
    dot_general x8 -> x0, local copies, waits for them, and re-layouts: 63.8 us -> none  [the longest x5 42.8 us: forward_map(): jnp.einsum('rai,abij->rbj', grouped, blocks, preferred_element_type=jnp.f...]
  transfers between devices with their start and end apart: 21 -> 30, of which waited for: 6 -> 17; matrix products, arithmetic and copies ran while one was open for 60% -> 2% of each run, Pallas kernels for 0% -> 15%
where the time goes in v1:
time: 870 us; the launch traced here: 859 us
  waiting for transfers between devices  575 us (66%)
  Pallas kernels  159 us (18%)
  local copies, waits for them, and re-layouts  66.7 us (8%)
  starting transfers between devices  26.4 us (3%)
  other arithmetic  16.4 us (2%)
  between operations  14.7 us (2%)
    reduce_scatter x1, waiting for transfers between devices, shards(): lax.psum_scatter(dense_term, ('ctx', 'shard'), scatter_dimension=0, tiled...  141 us
    all_gather x1, waiting for transfers between devices, shards(): lax.all_gather(dense_weight.astype(low_type), ('ctx', 'shard'), axis=0, t...  100 us
    reduce_scatter x1, waiting for transfers between devices, shards(): lax.psum_scatter(expert_term, 'ctx', scatter_dimension=0, tiled=True)  99.7 us
    ppermute x21, waiting for transfers between devices, to_partner(): return lax.ppermute(array, 'shard', [(i, i ^ offset) for i in range(count)])  76 us
    all_gather x1, waiting for transfers between devices, shards(): lax.all_gather(expert_weight[0].astype(low_type), 'ctx', axis=0, tiled=True)  69.7 us
    unnamed x196, local copies, waits for them, and re-layouts  59.5 us
    psum x1, waiting for transfers between devices, shards(): stat_rows = lax.psum(stat_rows, ('ctx', 'shard'))  42.2 us
    pallas_call x2, Pallas kernels, run_expert(): call(functools.partial(expert_kernel, sources, micro), tuple([shaped((row...  40.2 us
  transfers between devices with their start and end apart: 30, of which 17 were waited for; matrix products, arithmetic and copies ran while one was open for 2% of the time, Pallas kernels for 15%

profile of v1, /device:TPU:0, one launch (start us, length us, event | category | flops | bytes accessed | tf_op | source)
XLA Modules:
  0.0 858.6 jit_solution(4558532400058006458)
XLA Ops:
  10.1 100.1 %all-gather.7.cloned.1.call-done.w_ref = bf16[128,192,256]{2,1,0:T(8,128)(2,1)} async-done(((bf16[4,192,256]{2,1,0:T(8,128)(2,1)}), bf16[128,192,256]{2,1,0:T(8,128)(2,1)}) %all-gather.7.cloned.1.call-update) | async-done | bytes 12582928 | tf_op jit(solution)/shard_map/all_gather | solution.py:682
  115.5 15.1 %shard_map.349 = (bf16[256,1536]{1,0:T(8,128)(2,1)S(1)}, bf16[2,128,1536]{2,1,0:T(8,128)(2,1)S(1)}, bf16[2,128,1024]{2,1,0:T(8,128)(2,1)S(1)}) custom-call(s32[128]{0:T(128)S(1)} %select_reduce_fusion.order_ref, f32[2,128,1536]{2,1,0:T(8,128)S(1)} %copy-done.3, f32[2,1536]{1,0:T(2,128)S(1)} %copy-done.44, bf16[128,192,256]{2,1,0:T(8,128)(2,1)S(1)} %copy-done.2), custom_call_target="tpu_custom_call" | custom-call | flops 2013265920 | bytes 7864320 | tf_op jit(solution)/shard_map/pallas_call | solution.py:157
  145.1 14.9 %all-gather.11.cloned.1.call-done = bf16[1,1024,1024]{2,1,0:T(8,128)(2,1)} async-done(((bf16[1,128,1024]{2,1,0:T(8,128)(2,1)}), bf16[1,1024,1024]{2,1,0:T(8,128)(2,1)}) %all-gather.11.cloned.1.call-update) | async-done | bytes 2097168 | tf_op jit(solution)/shard_map/all_gather | solution.py:692
  164.1 10.7 %shard_map.350 = (bf16[128,1536]{1,0:T(8,128)(2,1)S(1)}, f32[384,128]{1,0:T(8,128)S(1)}, f32[128,1536]{1,0:T(8,128)S(1)}, bf16[128,1536]{1,0:T(8,128)(2,1)}) custom-call(s32[128]{0:T(128)S(1)} %copy-done.68, bf16[128,1536]{1,0:T(8,128)(2,1)S(1)} %copy-done.20, bf16[1024,1024]{1,0:T(8,128)(2,1)S(1)} %bitcast.49, s32[128,1]{1,0:T(8,128)S(1)} %copy-done.46, ...), custom_call_target="tpu_custom_call" | custom-call | flops 3221225472 | bytes 8388608 | tf_op jit(solution)/shard_map/pallas_call | solution.py:228
  182.9 69.7 %all-gather.9.cloned.1.call-done.refs_8_ = bf16[96,192,256]{2,1,0:T(8,128)(2,1)} async-done(((bf16[12,192,256]{2,1,0:T(8,128)(2,1)}), bf16[96,192,256]{2,1,0:T(8,128)(2,1)}) %all-gather.9.cloned.1.call-update) | async-done | bytes 9437200 | tf_op jit(solution)/shard_map/all_gather | solution.py:683
  252.5 20.2 %shard_map.351 = (bf16[128,1664]{1,0:T(8,128)(2,1)}, bf16[128,1664]{1,0:T(8,128)(2,1)}, bf16[128,1664]{1,0:T(8,128)(2,1)}, bf16[128,1664]{1,0:T(8,128)(2,1)}, bf...) custom-call(s32[96]{0:T(128)} %select_reduce_fusion.1.order_ref, ...), custom_call_target="tpu_custom_call" | custom-call | flops 9663676416 | bytes 20971520 | tf_op jit(solution)/shard_map/pallas_call | solution.py:335
  277.3 8.4 collective-permute-done.15.refs_1_
  285.7 9.7 %collective-permute-done.16.refs_2_ = bf16[128,1664]{1,0:T(8,128)(2,1)S(1)} collective-permute-done((bf16[128,1664]{1,0:T(8,128)(2,1)}, bf16[128,1664]{1,0:T(8,128)(2,1)S(1)}, u32[]{:S(2)}, u32[]{:S(2)}) %collective-permute-start.16) | collective-permute-done | bytes 426016 | tf_op jit(solution)/shard_map/ppermute | solution.py:633
  302.1 10.8 %shard_map.356 = (bf16[128,1536]{1,0:T(8,128)(2,1)S(1)}, bf16[1024,1024]{1,0:T(8,128)(2,1)S(1)}) custom-call(bf16[128,1536]{1,0:T(8,128)(2,1)S(1)} %copy-done.21, bf16[1024,1024]{1,0:T(8,128)(2,1)S(1)} %bitcast.50, s32[128,1]{1,0:T(8,128)S(1)} %copy-done.47, s32[1,1024]{1,0:T(1,128)S(1)} %bitcast.54, bf16[128,1536]{1,0:T(8,128)(2,1)S(1)} %copy-done.54, ...), custom_call_target="tpu_custom_call" | custom-call | flops 8053063680 | bytes 8388608 | tf_op jit(solution)/shard_map/pallas_call | solution.py:523
  319.4 9.9 %shard_map.352 = (bf16[128,1536]{1,0:T(8,128)(2,1)S(1)}, f32[384,128]{1,0:T(8,128)S(1)}, f32[128,1536]{1,0:T(8,128)S(1)}, bf16[128,1536]{1,0:T(8,128)(2,1)S(1)}) custom-call(s32[128]{0:T(128)S(1)} %copy-done.70, bf16[128,1536]{1,0:T(8,128)(2,1)S(1)} %get-tuple-element.151.q_ref, bf16[1024,1024]{1,0:T(8,128)(2,1)S(1)} %bitcast.47, s32[128,1]{1,0:T(8,128)S(1)} %copy-done.48, ...), custom_call_target="tpu_custom_call" | custom-call | flops 3221225472 | bytes 8388608 | tf_op jit(solution)/shard_map/pallas_call | solution.py:228
  333.6 8.6 collective-permute-done.9.refs_1_
  342.2 7.7 collective-permute-done.10.refs_2_
  351.4 20.0 %shard_map.353 = (bf16[128,1664]{1,0:T(8,128)(2,1)}, bf16[128,1664]{1,0:T(8,128)(2,1)}, bf16[128,1664]{1,0:T(8,128)(2,1)}, bf16[128,1664]{1,0:T(8,128)(2,1)}, bf...) custom-call(s32[96]{0:T(128)} %select_reduce_fusion.1.order_ref, ...), custom_call_target="tpu_custom_call" | custom-call | flops 9663676416 | bytes 20971520 | tf_op jit(solution)/shard_map/pallas_call | solution.py:335
  375.0 9.5 %collective-permute-done.18.refs_1_ = bf16[128,1664]{1,0:T(8,128)(2,1)S(1)} collective-permute-done((bf16[128,1664]{1,0:T(8,128)(2,1)}, bf16[128,1664]{1,0:T(8,128)(2,1)S(1)}, u32[]{:S(2)}, u32[]{:S(2)}) %collective-permute-start.18) | collective-permute-done | bytes 426016 | tf_op jit(solution)/shard_map/ppermute | solution.py:633
  398.5 11.0 %shard_map.357 = (bf16[128,1536]{1,0:T(8,128)(2,1)S(1)}, bf16[1024,1024]{1,0:T(8,128)(2,1)S(1)}) custom-call(bf16[128,1536]{1,0:T(8,128)(2,1)S(1)} %get-tuple-element.151.q_ref, bf16[1024,1024]{1,0:T(8,128)(2,1)S(1)} %bitcast.48, s32[128,1]{1,0:T(8,128)S(1)} %copy-done.49, s32[1,1024]{1,0:T(1,128)S(1)} %bitcast.56, bf16[128,1536]{1,0:T(8,128)(2,1)S(1)} %copy-done.59, ...), custom_call_target="tpu_custom_call" | custom-call | flops 8053063680 | bytes 8388608 | tf_op jit(solution)/shard_map/pallas_call | solution.py:523
  413.3 32.0 %reduce-scatter.7.cloned.1.call-done.refs_5_.refs_9_ = bf16[128,1024]{1,0:T(8,128)(2,1)} async-done(((bf16[1024,1024]{1,0:T(8,128)(2,1)}), bf16[128,1024]{1,0:T(8,128)(2,1)}) %reduce-scatter.7.cloned.1.call-update) | async-done | bytes 262160 | tf_op jit(solution)/shard_map/reduce_scatter | solution.py:739
  450.4 10.7 %shard_map.358 = (f32[2,128,1536]{2,1,0:T(8,128)}, f32[8,1536]{1,0:T(8,128)S(1)}) custom-call(s32[128]{0:T(128)S(1)} %copy-done.71, f32[2,128,1536]{2,1,0:T(8,128)S(1)} %copy-done.3, f32[2,1536]{1,0:T(2,128)S(1)} %copy-done.45, bf16[128,192,256]{2,1,0:T(8,128)(2,1)} %all-gather.7.cloned.1.call-done.w_ref, f32[128,1536]{1,0:T(8,128)S(1)} %copy-done.34, ...), custom_call_target="tpu_custom_call" | custom-call | flops 2013265920 | bytes 14680064 | tf_op jit(solution)/shard_map/pallas_call | solution.py:564
  468.8 17.5 %shard_map.361 = bf16[96,192,256]{2,1,0:T(8,128)(2,1)} custom-call(s32[96]{0:T(128)S(1)} %copy-done.76, bf16[512,1536]{1,0:T(8,128)(2,1)} %get-tuple-element.119.refs_0_.refs_2_, bf16[512,1536]{1,0:T(8,128)(2,1)} %get-tuple-element.120.refs_1_.refs_3_, bf16[512,1536]{1,0:T(8,128)(2,1)} %get-tuple-element.119.refs_0_.refs_2_, ...), custom_call_target="tpu_custom_call" | custom-call | flops 9663676416 | bytes 25165824 | tf_op jit(solution)/shard_map/pallas_call | solution.py:406
  490.9 11.8 %shard_map.359 = bf16[128,192,256]{2,1,0:T(8,128)(2,1)} custom-call(s32[128]{0:T(128)S(1)} %copy-done.71, bf16[128,1536]{1,0:T(8,128)(2,1)S(1)} %get-tuple-element.149.refs_0_.refs_2_, bf16[128,1536]{1,0:T(8,128)(2,1)S(1)} %get-tuple-element.148.refs_1_.refs_3_, bf16[128,1536]{1,0:T(8,128)(2,1)S(1)} %get-tuple-element.149.refs_0_.refs_2_, ...), custom_call_target="tpu_custom_call" | custom-call | flops 3221225472 | bytes 17039360 | tf_op jit(solution)/shard_map/pallas_call | solution.py:406
  517.6 8.2 collective-permute-done.13
  539.2 42.2 %all-reduce.3.cloned.1.call-done = f32[16,1536]{1,0:T(8,128)} async-done(((f32[16,1536]{1,0:T(8,128)}), f32[16,1536]{1,0:T(8,128)}) %all-reduce.3.cloned.1.call-update) | async-done | bytes 98320 | tf_op jit(solution)/shard_map/psum | solution.py:764
  584.4 99.7 %reduce-scatter.11.cloned.1.call-done.g_ref = bf16[12,192,256]{2,1,0:T(8,128)(2,1)} async-done(((bf16[96,192,256]{2,1,0:T(8,128)(2,1)}), bf16[12,192,256]{2,1,0:T(8,128)(2,1)}) %reduce-scatter.11.cloned.1.call-update) | async-done | bytes 1179664 | tf_op jit(solution)/shard_map/reduce_scatter | solution.py:731
  693.9 9.4 %shard_map.362 = (f32[12,192,256]{2,1,0:T(8,128)}, f32[12,192,256]{2,1,0:T(8,128)}, f32[12,192,256]{2,1,0:T(8,128)}, f32[12,192,256]{2,1,0:T(8,128)}) custom-call(f32[12,192,256]{2,1,0:T(8,128)S(1)} %bitcast.42, bf16[12,192,256]{2,1,0:T(8,128)(2,1)S(1)} %copy-done.27, f32[12,192,256]{2,1,0:T(8,128)S(1)} %bitcast.44, f32[12,192,256]{2,1,0:T(8,128)S(1)} %bitcast.45, ...), custom_call_target="tpu_custom_call" | custom-call | flops 1056964608 | bytes 25165824 | tf_op jit(solution)/shard_map/pallas_call | solution.py:604
  703.2 140.6 %reduce-scatter.9.cloned.1.call-done.g_ref = bf16[4,192,256]{2,1,0:T(8,128)(2,1)} async-done(((bf16[128,192,256]{2,1,0:T(8,128)(2,1)}), bf16[4,192,256]{2,1,0:T(8,128)(2,1)}) %reduce-scatter.9.cloned.1.call-update) | async-done | bytes 393232 | tf_op jit(solution)/shard_map/reduce_scatter | solution.py:756
  (286 shorter events, 145.9 us)
Async XLA Ops:
  7.2 103.0 %all-gather.7.cloned.1.call-start = ((), (), s32[]{:S(2)}) async-start(), calls=%async_computation.4 | async-start | bytes 12976128 | tf_op jit(solution)/shard_map/all_gather | solution.py:682
  9.3 150.7 %all-gather.11.cloned.1.call-start = ((), (), s32[]{:S(2)}) async-start(), calls=%async_computation.11 | async-start | bytes 2359296 | tf_op jit(solution)/shard_map/all_gather | solution.py:692
  132.5 120.0 %all-gather.9.cloned.1.call-start = ((), (), s32[]{:S(2)}) async-start(), calls=%async_computation.5 | async-start | bytes 10616832 | tf_op jit(solution)/shard_map/all_gather | solution.py:683
  135.4 179.7 %all-gather.13.cloned.1.call-start = ((), (), s32[]{:S(2)}) async-start(), calls=%async_computation.12 | async-start | bytes 2359296 | tf_op jit(solution)/shard_map/all_gather | solution.py:692
  138.1 41.1 %collective-permute-start.3 = (bf16[256,1664]{1,0:T(8,128)(2,1)}, bf16[256,1664]{1,0:T(8,128)(2,1)}, u32[]{:S(2)}, u32[]{:S(2)}) collective-permute-start(bf16[256,1664]{1,0:T(8,128)(2,1)} %bitcast.9.refs_4_), channel_id=1, source_target_pairs={{0,1},{1,0},{2,3},{3,2},{4,5},{5,4},{6,7},{7,6},{8,9},{9,8},{10,11... | collective-permute-start | bytes 2555912 | tf_op jit(solution)/shard_map/ppermute | solution.py:633
  139.5 43.3 %collective-permute-start.4 = (bf16[256,1664]{1,0:T(8,128)(2,1)}, bf16[256,1664]{1,0:T(8,128)(2,1)}, u32[]{:S(2)}, u32[]{:S(2)}) collective-permute-start(bf16[256,1664]{1,0:T(8,128)(2,1)} %bitcast.9.refs_4_), channel_id=1, source_target_pairs={{0,2},{1,3},{2,0},{3,1},{4,6},{5,7},{6,4},{7,5},{8,10},{9,11},{10,... | collective-permute-start | bytes 2555912 | tf_op jit(solution)/shard_map/ppermute | solution.py:633
  140.1 42.7 %collective-permute-start.5 = (bf16[256,1664]{1,0:T(8,128)(2,1)}, bf16[256,1664]{1,0:T(8,128)(2,1)}, u32[]{:S(2)}, u32[]{:S(2)}) collective-permute-start(bf16[256,1664]{1,0:T(8,128)(2,1)} %bitcast.9.refs_4_), channel_id=1, source_target_pairs={{0,3},{1,2},{2,1},{3,0},{4,7},{5,6},{6,5},{7,4},{8,11},{9,10},{10,... | collective-permute-start | bytes 2555912 | tf_op jit(solution)/shard_map/ppermute | solution.py:633
  143.3 270.0 %reduce-scatter.5.cloned.1.call-start = ((), (), s32[]{:S(2)}) async-start(), calls=%async_computation.6 | async-start | bytes 2359296 | tf_op jit(solution)/shard_map/reduce_scatter | solution.py:739
  176.2 76.3 %collective-permute-start = (bf16[128,1536]{1,0:T(8,128)(2,1)}, bf16[128,1536]{1,0:T(8,128)(2,1)}, u32[]{:S(2)}, u32[]{:S(2)}) collective-permute-start(bf16[128,1536]{1,0:T(8,128)(2,1)} %get-tuple-element.80.refs_0_.h2_ref), channel_id=1, source_target_pairs={{0,1},{1,0},{2,3},{3,2},{4,5},{5,4},{6,7},{7,6},{8,9},{9,8},{10,11... | collective-permute-start | bytes 1179656 | tf_op jit(solution)/shard_map/ppermute | solution.py:633
  177.7 74.8 %collective-permute-start.1 = (bf16[128,1536]{1,0:T(8,128)(2,1)}, bf16[128,1536]{1,0:T(8,128)(2,1)}, u32[]{:S(2)}, u32[]{:S(2)}) collective-permute-start(bf16[128,1536]{1,0:T(8,128)(2,1)} %get-tuple-element.80.refs_0_.h2_ref), channel_id=1, source_target_pairs={{0,2},{1,3},{2,0},{3,1},{4,6},{5,7},{6,4},{7,5},{8,10},{9,11},{10,... | collective-permute-start | bytes 1179656 | tf_op jit(solution)/shard_map/ppermute | solution.py:633
  179.2 73.4 %collective-permute-start.2 = (bf16[128,1536]{1,0:T(8,128)(2,1)}, bf16[128,1536]{1,0:T(8,128)(2,1)}, u32[]{:S(2)}, u32[]{:S(2)}) collective-permute-start(bf16[128,1536]{1,0:T(8,128)(2,1)} %get-tuple-element.80.refs_0_.h2_ref), channel_id=1, source_target_pairs={{0,3},{1,2},{2,1},{3,0},{4,7},{5,6},{6,5},{7,4},{8,11},{9,10},{10,... | collective-permute-start | bytes 1179656 | tf_op jit(solution)/shard_map/ppermute | solution.py:633
  274.3 21.0 %collective-permute-start.16 = (bf16[128,1664]{1,0:T(8,128)(2,1)}, bf16[128,1664]{1,0:T(8,128)(2,1)S(1)}, u32[]{:S(2)}, u32[]{:S(2)}) collective-permute-start(bf16[128,1664]{1,0:T(8,128)(2,1)} %get-tuple-element.93), channel_id=1, source_target_pairs={{0,2},{1,3},{2,0},{3,1},{4,6},{5,7},{6,4},{7,5},{8,10},{9,11},{10,... | collective-permute-start | bytes 1277960 | tf_op jit(solution)/shard_map/ppermute | solution.py:633
  275.8 19.6 %collective-permute-start.17 = (bf16[128,1664]{1,0:T(8,128)(2,1)}, bf16[128,1664]{1,0:T(8,128)(2,1)S(1)}, u32[]{:S(2)}, u32[]{:S(2)}) collective-permute-start(bf16[128,1664]{1,0:T(8,128)(2,1)} %get-tuple-element.94), channel_id=1, source_target_pairs={{0,3},{1,2},{2,1},{3,0},{4,7},{5,6},{6,5},{7,4},{8,11},{9,10},{10,... | collective-permute-start | bytes 1277960 | tf_op jit(solution)/shard_map/ppermute | solution.py:633
  315.0 130.2 %reduce-scatter.7.cloned.1.call-start = ((), (), s32[]{:S(2)}) async-start(), calls=%async_computation.7 | async-start | bytes 2359296 | tf_op jit(solution)/shard_map/reduce_scatter | solution.py:739
  331.3 18.6 %collective-permute-start.10 = (bf16[128,1536]{1,0:T(8,128)(2,1)S(1)}, bf16[128,1536]{1,0:T(8,128)(2,1)S(1)}, u32[]{:S(2)}, u32[]{:S(2)}) collective-permute-start(bf16[128,1536]{1,0:T(8,128)(2,1)S(1)} %get-tuple-element.86.refs_0_.h2_ref), channel_id=1, source_target_pairs={{0,2},{1,3},{2,0},{3,1},{4,6},{5,7},{6,4},{7,5},{8,10},{9,11},{10,... | collective-permute-start | bytes 1179656 | tf_op jit(solution)/shard_map/ppermute | solution.py:633
  372.1 18.0 %collective-permute-start.19 = (bf16[128,1664]{1,0:T(8,128)(2,1)}, bf16[128,1664]{1,0:T(8,128)(2,1)S(1)}, u32[]{:S(2)}, u32[]{:S(2)}) collective-permute-start(bf16[128,1664]{1,0:T(8,128)(2,1)} %get-tuple-element.98), channel_id=1, source_target_pairs={{0,2},{1,3},{2,0},{3,1},{4,6},{5,7},{6,4},{7,5},{8,10},{9,11},{10,... | collective-permute-start | bytes 1277960 | tf_op jit(solution)/shard_map/ppermute | solution.py:633
  411.5 169.8 %all-reduce.3.cloned.1.call-start = ((), (), s32[]{:S(2)}) async-start(), calls=%async_computation.10 | async-start | bytes 196608 | tf_op jit(solution)/shard_map/psum | solution.py:764
  461.8 222.3 %reduce-scatter.11.cloned.1.call-start = ((), (), s32[]{:S(2)}) async-start(), calls=%async_computation.9 | async-start | bytes 10616832 | tf_op jit(solution)/shard_map/reduce_scatter | solution.py:731
  486.3 357.5 %reduce-scatter.9.cloned.1.call-start = ((), (), s32[]{:S(2)}) async-start(), calls=%async_computation.8 | async-start | bytes 12976128 | tf_op jit(solution)/shard_map/reduce_scatter | solution.py:756
  505.2 20.6 %collective-permute-start.13 = (bf16[128,1536]{1,0:T(8,128)(2,1)S(1)}, bf16[128,1536]{1,0:T(8,128)(2,1)S(1)}, u32[]{:S(2)}, u32[]{:S(2)}) collective-permute-start(bf16[128,1536]{1,0:T(8,128)(2,1)S(1)} %copy-done.94), channel_id=1, source_target_pairs={{0,2},{1,3},{2,0},{3,1},{4,6},{5,7},{6,4},{7,5},{8,10},{9,11},{10,... | collective-permute-start | bytes 1179656 | tf_op jit(solution)/shard_map/ppermute | solution.py:633
  505.9 20.0 %collective-permute-start.12 = (bf16[128,1536]{1,0:T(8,128)(2,1)S(1)}, bf16[128,1536]{1,0:T(8,128)(2,1)S(1)}, u32[]{:S(2)}, u32[]{:S(2)}) collective-permute-start(bf16[128,1536]{1,0:T(8,128)(2,1)S(1)} %copy-done.93), channel_id=1, source_target_pairs={{0,1},{1,0},{2,3},{3,2},{4,5},{5,4},{6,7},{7,6},{8,9},{9,8},{10,11... | collective-permute-start | bytes 1179656 | tf_op jit(solution)/shard_map/ppermute | solution.py:633
  506.7 26.4 %collective-permute-start.8 = (bf16[128,1536]{1,0:T(8,128)(2,1)}, bf16[128,1536]{1,0:T(8,128)(2,1)S(1)}, u32[]{:S(2)}, u32[]{:S(2)}) collective-permute-start(bf16[128,1536]{1,0:T(8,128)(2,1)} %get-tuple-element.84), channel_id=1, source_target_pairs={{0,3},{1,2},{2,1},{3,0},{4,7},{5,6},{6,5},{7,4},{8,11},{9,10},{10,... | collective-permute-start | bytes 1179656 | tf_op jit(solution)/shard_map/ppermute | solution.py:633
  508.7 28.9 %collective-permute-start.7 = (bf16[128,1536]{1,0:T(8,128)(2,1)}, bf16[128,1536]{1,0:T(8,128)(2,1)S(1)}, u32[]{:S(2)}, u32[]{:S(2)}) collective-permute-start(bf16[128,1536]{1,0:T(8,128)(2,1)} %get-tuple-element.83), channel_id=1, source_target_pairs={{0,2},{1,3},{2,0},{3,1},{4,6},{5,7},{6,4},{7,5},{8,10},{9,11},{10,... | collective-permute-start | bytes 1179656 | tf_op jit(solution)/shard_map/ppermute | solution.py:633
  516.2 21.5 %collective-permute-start.6 = (bf16[128,1536]{1,0:T(8,128)(2,1)S(1)}, bf16[128,1536]{1,0:T(8,128)(2,1)S(1)}, u32[]{:S(2)}, u32[]{:S(2)}) collective-permute-start(bf16[128,1536]{1,0:T(8,128)(2,1)S(1)} %copy-done.92), channel_id=1, source_target_pairs={{0,1},{1,0},{2,3},{3,2},{4,5},{5,4},{6,7},{7,6},{8,9},{9,8},{10,11... | collective-permute-start | bytes 1179656 | tf_op jit(solution)/shard_map/ppermute | solution.py:633
  (104 other events, 1708.5 us)
Sparse Core Ops, SparseCore 0:
  11.5 98.7 all-gather.6
  132.6 27.3 all-gather.10
  162.2 90.2 all-gather.8
  254.0 27.5 all-gather.12
  315.2 33.2 reduce-scatter.4
  411.7 33.4 reduce-scatter.6
  461.9 119.3 all-reduce.2
  583.6 100.3 reduce-scatter.10
  690.1 153.7 reduce-scatter.8

commit v2 on v1

--- a/solution.py
+++ b/solution.py
@@ -116,84 +116,111 @@
         ref[:, pl.ds(pl.multiple_of(base + LANES * t, LANES), LANES)] = tiles[t].astype(ref.dtype)
 
 
-def project_kernel(order_ref, x_ref, gain_ref, w_ref, h_ref, q_ref, kv_ref, held, sems):
-    row_groups = x_ref.shape[-1] // BR
-    groups = held.shape[0]
+def project_kernel(
+    pieces, chips, members, slots, all_groups, order_ref, me_ref, x_ref, gain_ref, *refs
+):
+    piece_refs = refs[: len(pieces)]
+    h_ref, q_ref, kv_ref, win_ref, wout_ref, held, sems, out_sems = refs[len(pieces) :]
+    groups = held.shape[1] // BC
     q_groups = q_ref.shape[-1] // BC
-    all_groups = w_ref.shape[0] // row_groups
-    micros = x_ref.shape[0]
-    rows = x_ref.shape[1]
-
-    @pl.loop(0, groups)
-    def _(b):
-        for a in range(row_groups):
-            pltpu.make_async_copy(
-                w_ref.at[order_ref[a * all_groups + b]], held.at[b, pl.ds(a * BR, BR)], sems.at[b]
-            ).start()
+    micros, rows = x_ref.shape[:2]
+    ctx, shard = me_ref[0], me_ref[1]
+    chip, core = lax.div(ctx, 2), lax.rem(ctx, 2)
+
+    for ref, (other_core, offset, first, cut) in zip(piece_refs, pieces):
+
+        @pl.loop(0, ref.shape[0])
+        def _(i):
+            source = lax.rem(chip - (first + lax.div(i, slots)) + chips, chips) * 2
+            source = source + jnp.bitwise_xor(core, other_core)
+            source = source * members + jnp.bitwise_xor(shard, offset)
+            number = order_ref[source * slots + lax.rem(i, slots)]
+            a, b = lax.div(number, all_groups), lax.rem(number, all_groups)
+            down = pl.ds(pl.multiple_of(a * BR + cut, 32), ref.shape[1])
+
+            @pl.when(b < groups)
+            def _():
+                across = pl.ds(pl.multiple_of(b * BC, BC), BC)
+                pltpu.make_async_copy(ref.at[i], held.at[down, across], sems.at[b]).start()
+
+            @pl.when(b >= groups)
+            def _():
+                across = pl.ds(pl.multiple_of((b - groups) * BC, BC), BC)
+                pltpu.make_async_copy(ref.at[i], wout_ref.at[down, across], out_sems.at[0]).start()
 
     for m in range(micros):
         h_ref[pl.ds(m * rows, rows), :] = unit_rows(x_ref[m], gain_ref[0:1])[0].astype(low_type)
 
+    def make(b):
+        across = pl.ds(pl.multiple_of(b * BC, BC), BC)
+        wait_bytes(held.at[:, across], sems.at[b])
+        pltpu.make_async_copy(held.at[:, across], win_ref.at[:, across], out_sems.at[1]).start()
+        return dot(h_ref[...], held[:, across]).astype(low_type)
+
     @pl.loop(0, q_groups)
     def _(b):
-        wait_bytes(held.at[b], sems.at[b])
-        made = dot(h_ref[...], held[b]).astype(low_type)
+        made = make(b)
         for m in range(micros):
             q_ref[m, :, pl.ds(pl.multiple_of(b * BC, BC), BC)] = made[m * rows : (m + 1) * rows]
 
     @pl.loop(q_groups, groups)
     def _(b):
-        wait_bytes(held.at[b], sems.at[b])
-        made = dot(h_ref[...], held[b]).astype(low_type)
+        made = make(b)
         for m in range(micros):
             kv_ref[m, :, pl.ds(pl.multiple_of((b - q_groups) * BC, BC), BC)] = made[
                 m * rows : (m + 1) * rows
             ]
 
-
-def project(order, x, gains, w):
+    wait_bytes(wout_ref, out_sems.at[0])
+    wait_bytes(win_ref, out_sems.at[1])
+
+
+def project(pieces, arrays, chips, members, slots, order, me, x, gains):
     micros, rows, width = x.shape
-    groups = (HEADS + 2 * KVH) * HD // BC
+    in_width = (HEADS + 2 * KVH) * HD
+    out_width = HEADS * HD
     return call(
-        project_kernel,
+        functools.partial(
+            project_kernel, pieces, chips, members, slots, (in_width + out_width) // BC
+        ),
         (
             shaped((micros * rows, width), low_type),
             shaped((micros, rows, HEADS * HD), low_type),
             shaped((micros, rows, 2 * KVH * HD), low_type),
+            shaped((width, in_width), low_type),
+            shaped((width, out_width), low_type),
         ),
-        [in_smem, in_vmem, in_vmem, in_any],
-        (in_vmem, in_vmem, in_vmem),
-        [pltpu.VMEM((groups, width, BC), low_type), pltpu.SemaphoreType.DMA((groups,))],
-        2 * micros * rows * width * groups * BC,
-        groups * width * BC * 2,
+        [in_smem, in_smem, in_vmem, in_vmem] + [in_any] * len(arrays),
+        (in_vmem, in_vmem, in_vmem, in_any, in_any),
+        [
+            pltpu.VMEM((width, in_width), low_type),
+            pltpu.SemaphoreType.DMA((in_width // BC,)),
+            pltpu.SemaphoreType.DMA((2,)),
+        ],
+        2 * micros * rows * width * in_width,
+        2 * width * in_width * 2,
         24,
-    )(order, x, gains, w)
-
-
-def start_matrix(order_ref, w_ref, held, sem, first_group, all_groups):
-    row_groups = held.shape[0] // BR
-    groups = held.shape[1] // BC
-
-    @pl.loop(0, row_groups)
-    def _(a):
-        for b in range(groups):
-            pltpu.make_async_copy(
-                w_ref.at[order_ref[a * all_groups + first_group + b]],
-                held.at[pl.ds(pl.multiple_of(a * BR, 64), BR), pl.ds(b * BC, BC)],
-                sem,
-            ).start()
-
-
-def attend_kernel(
-    all_groups, order_ref, q_ref, kv_ref, rpos_ref, kpos_ref, x_ref, gain_ref, w_ref,
-    ob_ref, log_ref, x2_ref, h2_ref, bias, held, sem,
-):
+    )(order, me, x, gains, *arrays)
+
+
+def load_keys(parts, held, sem):
+    start = 0
+    for part in parts:
+        count = part.shape[0]
+        pltpu.make_async_copy(part, held.at[pl.ds(start, count)], sem).start()
+        start += count
+
+
+def attend_kernel(count, q_ref, rpos_ref, kpos_ref, x_ref, gain_ref, w_ref, *refs):
+    parts = refs[:count]
+    ob_ref, log_ref, x2_ref, h2_ref, bias, kv_ref, held, sems = refs[count:]
     rows = q_ref.shape[0]
-    in_groups = (HEADS + 2 * KVH) * HD // BC
-    start_matrix(order_ref, w_ref, held, sem, in_groups, all_groups)
+    load_keys(parts, kv_ref, sems.at[0])
+    pltpu.make_async_copy(w_ref, held, sems.at[1]).start()
     bias[...] = jnp.where(kpos_ref[...] <= rpos_ref[...], 0.0, masked_score)
     log_ref[...] = jnp.zeros_like(log_ref)
     length = kv_ref.shape[0]
+    wait_bytes(kv_ref, sems.at[0])
 
     @pl.loop(0, KVH // 2)
     def _(pair):
@@ -214,36 +241,37 @@
             )
         unstack_heads(ob_ref, pair, mixed[0], mixed[1])
 
-    wait_bytes(held, sem)
+    wait_bytes(held, sems.at[1])
     for n in range(held.shape[0] // BC):
         cut = slice(n * BC, (n + 1) * BC)
         x2_ref[:, cut] = x_ref[:, cut] + dot(ob_ref[...], held[cut, :], NT)
     h2_ref[...] = unit_rows(x2_ref[...], gain_ref[1:2])[0].astype(low_type)
 
 
-def attend(order, q, kv, rows_pos, key_pos, x, gains, w):
+def attend(q, kv_parts, rows_pos, key_pos, x, gains, w):
     rows, width = q.shape
-    length = kv.shape[0]
+    length = key_pos.shape[1]
     model = x.shape[1]
     return call(
-        functools.partial(attend_kernel, w.shape[0] * BR // model),
+        functools.partial(attend_kernel, len(kv_parts)),
         (
             shaped((rows, width), low_type),
             shaped((3 * rows, LANES), jnp.float32),
             shaped((rows, model), jnp.float32),
             shaped((rows, model), low_type),
         ),
-        [in_smem] + [in_vmem] * 6 + [in_any],
+        [in_vmem] * 5 + [in_any] * (1 + len(kv_parts)),
         (in_vmem,) * 4,
         [
             pltpu.VMEM((rows, length), jnp.float32),
+            pltpu.VMEM((length, kv_parts[0].shape[1]), low_type),
             pltpu.VMEM((model, width), low_type),
-            pltpu.SemaphoreType.DMA,
+            pltpu.SemaphoreType.DMA((2,)),
         ],
         16 * rows * length * width,
         8 * MIB,
         40,
-    )(order, q, kv, rows_pos, key_pos, x, gains, w)
+    )(q, rows_pos, key_pos, x, gains, w, *kv_parts)
 
 
 def router_parts(h2, router, experts):
@@ -283,7 +311,7 @@
 
     wait_bytes(xs_ref, load_sem.at[0])
     wait_bytes(cs, load_sem.at[1])
-    me = me_ref[0]
+    me = me_ref[1]
     probs = router_parts(xs_ref[...], router_ref[...], sources)
     hits = cs[:, width:].astype(jnp.float32)
     mine = lane_ids(hits.shape) == me
@@ -415,21 +443,114 @@
     )(order, *flat)
 
 
+def xor_plan(members, offset):
+    if members != 4:
+        return list(range(1, members)), [0]
+    first = 1 if offset % 2 else 2
+    return [first, 3], [0, 3 - first]
+
+
+def slots_kernel(
+    counts, chips, members, slots, all_groups, in_groups, order_ref, me_ref, *refs
+):
+    lists = []
+    for count in counts:
+        lists.append(refs[:count])
+        refs = refs[count:]
+    outs = refs[: 2 * chips]
+    lefts, turned, rights, sems = refs[2 * chips :]
+    ctx, shard = me_ref[0], me_ref[1]
+    chip, core = lax.div(ctx, 2), lax.rem(ctx, 2)
+    h_width = lefts.shape[2]
+    q_width = lists[2][0].shape[1]
+    kv_width = lists[3][0].shape[1]
+    total = rights.shape[0]
+    targets = (
+        (lefts.at[0], 0, h_width, 0),
+        (lefts.at[1], 0, h_width, 1),
+        (rights, 0, q_width, 2),
+        (rights, q_width, kv_width, 2),
+        (rights, q_width + kv_width, q_width, 2),
+    )
+    for group, (target, lane, lanes, sem) in zip(lists, targets):
+        start = 0
+        for ref in group:
+            pltpu.make_async_copy(
+                ref, target.at[pl.ds(start, ref.shape[0]), pl.ds(lane, lanes)], sems.at[sem]
+            ).start()
+            start += ref.shape[0]
+    for side in range(2):
+        wait_bytes(lefts.at[side], sems.at[side])
+        for r in range(0, total, LANES):
+            turned[side, :, r : r + LANES] = lefts[side, r : r + LANES, :].T
+    wait_bytes(rights, sems.at[2])
+    for offset in range(chips):
+        there = lax.rem(chip - offset + chips, chips) * 2 + core
+        for out, hops in zip(outs[2 * offset : 2 * offset + 2], xor_plan(members, offset)):
+            for place, hop in enumerate(hops):
+                base = (there * members + jnp.bitwise_xor(shard, hop)) * slots
+
+                @pl.loop(0, slots)
+                def _(i):
+                    number = order_ref[base + i]
+                    a, b = lax.div(number, all_groups), lax.rem(number, all_groups)
+                    side = (b >= in_groups).astype(jnp.int32)
+                    out[place * slots + i] = dot(
+                        turned[side, pl.ds(pl.multiple_of(a * BR, 64), BR), :],
+                        rights[:, pl.ds(pl.multiple_of(b * BC, BC), BC)],
+                    ).astype(low_type)
+
+
+def slot_blocks(chips, members, slots, order, me, h1, da, dq, dkv, ob):
+    lists = (h1, da, dq, dkv, ob)
+    total = sum(part.shape[0] for part in h1)
+    width = h1[0].shape[1]
+    in_width = dq[0].shape[1] + dkv[0].shape[1]
+    all_width = in_width + ob[0].shape[1]
+    outs = []
+    for offset in range(chips):
+        for hops in xor_plan(members, offset):
+            outs.append(shaped((len(hops) * slots, BR, BC), low_type))
+    made = call(
+        functools.partial(
+            slots_kernel,
+            tuple(len(group) for group in lists),
+            chips,
+            members,
+            slots,
+            all_width // BC,
+            in_width // BC,
+        ),
+        tuple(outs),
+        [in_smem, in_smem] + [in_any] * sum(len(group) for group in lists),
+        (in_vmem,) * len(outs),
+        [
+            pltpu.VMEM((2, total, width), low_type),
+            pltpu.VMEM((2, width, total), low_type),
+            pltpu.VMEM((total, all_width), low_type),
+            pltpu.SemaphoreType.DMA((3,)),
+        ],
+        2 * total * chips * members * slots * BR * BC,
+        16 * MIB,
+        40,
+    )(order, me, *[part for group in lists for part in group])
+    return [(made[2 * offset], made[2 * offset + 1]) for offset in range(chips)]
+
+
 def merge_kernel(
-    all_groups, sources, order_ref, me_ref, x2_ref, cot_ref, h2_ref, gain_ref, router_ref, w_ref, *refs
+    sources, me_ref, x2_ref, cot_ref, h2_ref, gain_ref, router_ref, w_ref, *refs
 ):
     back_refs = refs[:sources]
     dx_ref, da_ref, do_ref, stat_ref, held, sem = refs[sources:]
     rows, width = x2_ref.shape
-    in_groups = (HEADS + 2 * KVH) * HD // BC
-    start_matrix(order_ref, w_ref, held, sem, in_groups, all_groups)
+    pltpu.make_async_copy(w_ref, held, sem).start()
     lanes = lane_ids((rows, LANES))
     prob_grad = jnp.zeros((rows, LANES), jnp.float32)
     gathered = jnp.zeros((rows, width), jnp.float32)
     for j in range(sources):
         tail = back_refs[j][:, width:].astype(jnp.float32)
         told = jnp.sum(tail, axis=-1, keepdims=True)
-        expert = jnp.bitwise_xor(me_ref[0], j)
+        expert = jnp.bitwise_xor(me_ref[1], j)
         prob_grad = prob_grad + jnp.where(lanes == expert, told, 0.0)
         gathered = gathered + back_refs[j][:, :width].astype(jnp.float32)
     h2 = h2_ref[...]
@@ -454,33 +575,35 @@
         do_ref[:, cut] = dot(da_ref[...], held[:, cut]).astype(low_type)
 
 
-def merge(order, me, x2, cot, h2, gains, router, w, backs):
+def merge(me, x2, cot, h2, gains, router, w, backs):
     rows, width = x2.shape
     sources = len(backs)
     experts_up = -(-sources // 8) * 8
     return call(
-        functools.partial(merge_kernel, w.shape[0] * BR // width, sources),
+        functools.partial(merge_kernel, sources),
         (
             shaped((rows, width), jnp.float32),
             shaped((rows, width), low_type),
             shaped((rows, HEADS * HD), low_type),
             shaped((experts_up + 8, width), jnp.float32),
         ),
-        [in_smem, in_smem] + [in_vmem] * 5 + [in_any] + [in_vmem] * sources,
+        [in_smem] + [in_vmem] * 5 + [in_any] + [in_vmem] * sources,
         (in_vmem,) * 4,
         [pltpu.VMEM((width, HEADS * HD), low_type), pltpu.SemaphoreType.DMA],
         2 * rows * width * HEADS * HD,
         10 * MIB,
         40,
-    )(order, me, x2, cot, h2, gains, router, w, *backs)
-
-
-def attend_back_kernel(
-    q_ref, kv_ref, rpos_ref, kpos_ref, ob_ref, log_ref, do_ref, dq_ref, dkv_ref, bias
-):
+    )(me, x2, cot, h2, gains, router, w, *backs)
+
+
+def attend_back_kernel(count, q_ref, rpos_ref, kpos_ref, ob_ref, log_ref, do_ref, *refs):
+    parts = refs[:count]
+    dq_ref, own_ref, other_ref, bias, kv_ref, sem = refs[count:]
     rows = q_ref.shape[0]
+    load_keys(parts, kv_ref, sem)
     length = kv_ref.shape[0]
     bias[...] = jnp.where(kpos_ref[...] <= rpos_ref[...], 0.0, masked_score)
+    wait_bytes(kv_ref, sem)
 
     @pl.loop(0, KVH // 2)
     def _(pair):
@@ -513,33 +636,40 @@
             value_grad = value_term if part == 0 else value_grad + value_term
             query_grads.append(dot(score_grad, keys) * HD**-0.5)
         unstack_heads(dq_ref, pair, query_grads[0], query_grads[1])
-        dkv_ref[:, pl.ds(lane, LANES)] = key_grad.astype(low_type)
-        dkv_ref[:, pl.ds(value_lane, LANES)] = value_grad.astype(low_type)
-
-
-def attend_back(q, kv, rows_pos, key_pos, ob, log_total, do):
+        half = length // 2
+        for ref, cut in ((own_ref, slice(0, half)), (other_ref, slice(half, length))):
+            ref[:, pl.ds(lane, LANES)] = key_grad[cut].astype(low_type)
+            ref[:, pl.ds(value_lane, LANES)] = value_grad[cut].astype(low_type)
+
+
+def attend_back(q, kv_parts, rows_pos, key_pos, ob, log_total, do):
     rows, width = q.shape
-    length = kv.shape[0]
+    length = key_pos.shape[1]
+    kv_width = kv_parts[0].shape[1]
     return call(
-        attend_back_kernel,
-        (shaped((rows, width), low_type), shaped(kv.shape, low_type)),
-        [in_vmem] * 7,
-        (in_vmem,) * 2,
-        [pltpu.VMEM((rows, length), jnp.float32)],
+        functools.partial(attend_back_kernel, len(kv_parts)),
+        (shaped((rows, width), low_type),) + (shaped((length // 2, kv_width), low_type),) * 2,
+        [in_vmem] * 6 + [in_any] * len(kv_parts),
+        (in_vmem,) * 3,
+        [
+            pltpu.VMEM((rows, length), jnp.float32),
+            pltpu.VMEM((length, kv_width), low_type),
+            pltpu.SemaphoreType.DMA,
+        ],
         40 * rows * length * width,
         8 * MIB,
         48,
-    )(q, kv, rows_pos, key_pos, ob, log_total, do)
-
-
-def input_kernel(all_groups, order_ref, x_ref, gain_ref, w_ref, *refs):
+    )(q, rows_pos, key_pos, ob, log_total, do, *kv_parts)
+
+
+def input_kernel(x_ref, gain_ref, w_ref, *refs):
     micros = x_ref.shape[0]
     rows = x_ref.shape[1]
     dx_refs = refs[:micros]
     dq_refs = refs[micros : 2 * micros]
     dkv_refs = refs[2 * micros : 3 * micros]
     out_ref, stat_ref, grad, held, sem = refs[3 * micros :]
-    start_matrix(order_ref, w_ref, held, sem, 0, all_groups)
+    pltpu.make_async_copy(w_ref, held, sem).start()
     q_width = dq_refs[0].shape[-1]
     wait_bytes(held, sem)
     for n in range(held.shape[0] // BC):
@@ -558,13 +688,13 @@
     stat_ref[...] = jnp.broadcast_to(total, stat_ref.shape)
 
 
-def input_back(order, x, gains, w, dxs, dqs, dkvs):
+def input_back(x, gains, w, dxs, dqs, dkvs):
     micros, rows, width = x.shape
     in_width = (HEADS + 2 * KVH) * HD
     return call(
-        functools.partial(input_kernel, w.shape[0] * BR // width),
+        input_kernel,
         (shaped(x.shape, jnp.float32), shaped((8, width), jnp.float32)),
-        [in_smem, in_vmem, in_vmem, in_any] + [in_vmem] * (3 * micros),
+        [in_vmem, in_vmem, in_any] + [in_vmem] * (3 * micros),
         (in_vmem,) * 2,
         [
             pltpu.VMEM(x.shape, jnp.float32),
@@ -574,7 +704,7 @@
         2 * micros * rows * width * in_width,
         14 * MIB,
         40,
-    )(order, x, gains, w, *dxs, *dqs, *dkvs)
+    )(x, gains, w, *dxs, *dqs, *dkvs)
 
 
 def rotate_kernel(
@@ -631,6 +761,94 @@
         return array
     count = lax.axis_size("shard")
     return lax.ppermute(array, "shard", [(i, i ^ offset) for i in range(count)])
+
+
+def to_ctx(array, offset):
+    count = lax.axis_size("ctx")
+    return lax.ppermute(array, "ctx", [(i, i ^ offset) for i in range(count)])
+
+
+def to_next_chip(array):
+    count = lax.axis_size("ctx")
+    return lax.ppermute(array, "ctx", [(i, (i + 2) % count) for i in range(count)])
+
+
+def chip_ring(array, chips):
+    parts = [array]
+    for _ in range(chips - 1):
+        parts.append(to_next_chip(parts[-1]))
+    return parts
+
+
+def wide(array):
+    return array.astype(jnp.float32)
+
+
+def ring_sum(parts, chips):
+    total = None
+    for offset in list(range(1, chips)) + [0]:
+        total = parts[offset] if total is None else wide(to_next_chip(total)) + parts[offset]
+        if offset != 0:
+            total = total.astype(low_type)
+    return total
+
+
+def gather_weights(blocks, chips, members):
+    parts = chip_ring(blocks, chips)
+    groups = [(0, parts[0])]
+    if chips > 1:
+        groups.append((1, jnp.concatenate(parts[1:], axis=0)))
+    pieces, arrays = [], []
+
+    def add(array, offset, first, cut):
+        pieces.append((0, offset, first, cut))
+        arrays.append(array)
+
+    for first, group in groups:
+        add(group, 0, first, 0)
+        if members == 4:
+            by_one, by_two = to_partner(group, 1), to_partner(group, 2)
+            add(by_one, 1, first, 0)
+            add(by_two, 2, first, 0)
+            half = BR // 2
+            add(to_partner(by_one[:, :half], 2), 3, first, 0)
+            add(to_partner(by_two[:, half:], 1), 3, first, half)
+        else:
+            for offset in range(1, members):
+                add(to_partner(group, offset), offset, first, 0)
+    swapped = [to_ctx(array, 1) for array in arrays]
+    return pieces + [(1,) + piece[1:] for piece in pieces], arrays + swapped
+
+
+def sum_slots(made, chips, members, slots):
+    sums = []
+    for offset in range(chips):
+        sent, kept = made[offset]
+        hops, keeps = xor_plan(members, offset)
+        total = wide(kept[:slots])
+        if members == 4:
+            first, second = hops[0], keeps[1]
+            got = to_partner(sent, first)
+            total = total + wide(got[:slots])
+            relay = (wide(kept[slots:]) + wide(got[slots:])).astype(low_type)
+            total = total + wide(to_partner(relay, second))
+        else:
+            for place, hop in enumerate(hops):
+                total = total + wide(to_partner(sent[place * slots : (place + 1) * slots], hop))
+        sums.append(total)
+    return ring_sum(sums, chips)
+
+
+def sum_all(array):
+    step = 1
+    while step < lax.axis_size("ctx"):
+        array = array + to_ctx(array, step)
+        step *= 2
+    step = 1
+    while step < lax.axis_size("shard"):
+        array = array + to_partner(array, step)
+        step *= 2
+    return array
 
 
 def shards(
@@ -659,28 +877,27 @@
 ):
     ctx_count = lax.axis_size("ctx")
     shard_count = lax.axis_size("shard")
+    chips = ctx_count // 2
     micros, rows, width = tokens.shape
+    slots = dense_weight.shape[0]
     span = rows // 2
-    length = rows * ctx_count
-    dense_groups = (2 * HEADS + 2 * KVH) * HD // BC
-    in_groups = (HEADS + 2 * KVH) * HD // BC
     row_groups = width // BR
     ff_groups = FF // BC
-    dense_blocks = row_groups * dense_groups
     expert_blocks = 3 * row_groups * ff_groups
 
-    dense_inverse = inverse_order(dense_order)
     expert_inverse = inverse_order(expert_order)
+    ctx = lax.axis_index("ctx").astype(jnp.int32)
+    me = jnp.stack([ctx, lax.axis_index("shard").astype(jnp.int32)])
     row_ids = jnp.arange(rows, dtype=jnp.int32)
-    all_pos = (assign[:, row_ids // span] * span + row_ids % span).reshape(length)
-    rows_pos = lax.dynamic_slice_in_dim(all_pos, lax.axis_index("ctx") * rows, rows)
-    rows_pos = rows_pos.reshape(rows, 1)
-    key_pos = all_pos.reshape(1, length)
-    me = lax.axis_index("shard").astype(jnp.int32).reshape(1)
+    all_pos = assign[:, row_ids // span] * span + row_ids % span
+    ring_ids = (ctx // 2 - jnp.arange(chips, dtype=jnp.int32)) % chips * 2
+    key_ids = jnp.concatenate([ring_ids + ctx % 2, ring_ids + (1 - ctx % 2)])
+    key_pos = all_pos[key_ids].reshape(1, rows * ctx_count)
+    rows_pos = all_pos[ctx].reshape(rows, 1)
     router_pad = jnp.pad(router.astype(low_type), ((0, 0), (0, LANES - shard_count)))
 
-    dense_all = lax.all_gather(dense_weight.astype(low_type), ("ctx", "shard"), axis=0, tiled=True)
     expert_all = lax.all_gather(expert_weight[0].astype(low_type), "ctx", axis=0, tiled=True)
+    pieces, arrays = gather_weights(dense_weight.astype(low_type), chips, shard_count)
 
     lanes = jnp.arange(LANES, dtype=jnp.int32)
     hits = jnp.sum((routes[..., None] == lanes).astype(low_type), axis=2)
@@ -688,25 +905,30 @@
     cot_rows = cot_rows.reshape(micros * rows, width + LANES)
     cot_parts = [to_partner(cot_rows, j) for j in range(shard_count)]
 
-    h1, q, kv = project(dense_inverse, tokens, norm_gains, dense_all)
-    kv_all = [lax.all_gather(kv[m], "ctx", axis=0, tiled=True) for m in range(micros)]
-    obs, logs, x2s, h2s = [], [], [], []
+    h1, q, kv, w_in, w_out = project(
+        pieces, arrays, chips, shard_count, slots, dense_order, me, tokens, norm_gains
+    )
+    h1_other = to_ctx(h1, 1)
+    kvs, obs, logs, x2s, h2s = [], [], [], [], []
     for m in range(micros):
+        parts = chip_ring(kv[m], chips)
+        parts = parts + [to_ctx(part, 1) for part in parts]
         ob, log_total, x2, h2 = attend(
-            dense_inverse, q[m], kv_all[m], rows_pos, key_pos, tokens[m], norm_gains, dense_all
+            q[m], parts, rows_pos, key_pos, tokens[m], norm_gains, w_out
         )
+        kvs.append(parts)
         obs.append(ob)
         logs.append(log_total)
         x2s.append(x2)
         h2s.append(h2)
 
-    outputs, backs = [], []
+    backs, outs = [], []
     zs, dgs, dus, dys, xs = [], [], [], [], []
     for m in range(micros):
         h_parts = [to_partner(h2s[m], j) for j in range(shard_count)]
         made = run_expert(m, expert_inverse, me, router_pad, h_parts, cot_parts, expert_all)
         back = made[:shard_count]
-        out = made[shard_count : 2 * shard_count]
+        outs.append(made[shard_count : 2 * shard_count])
         z, dg, du, dy, x = made[2 * shard_count :]
         zs.append(z)
         dgs.append(dg)
@@ -714,15 +936,9 @@
         dys.append(dy)
         xs.append(x)
         backs.append([to_partner(back[j], j) for j in range(shard_count)])
-        arrived = [to_partner(out[j], j) for j in range(shard_count)]
-        total = x2s[m]
-        for part in arrived:
-            total = total + part.astype(jnp.float32)
-        outputs.append(total)
-
-    expert_slots = inverse_slots = expert_inverse
+
     expert_term = outer_blocks(
-        expert_slots,
+        expert_inverse,
         lambda k: (k * row_groups * ff_groups, ff_groups),
         [xs, xs, dys],
         [dgs, dus, zs],
@@ -733,37 +949,54 @@
     dxs, das, dqs, dkvs, stats = [], [], [], [], []
     for m in range(micros):
         dx, da, do, stat = merge(
-            dense_inverse, me, x2s[m], cotangent[m], h2s[m], norm_gains, router_pad, dense_all, backs[m]
+            me, x2s[m], cotangent[m], h2s[m], norm_gains, router_pad, w_out, backs[m]
         )
-        dq, dkv_part = attend_back(q[m], kv_all[m], rows_pos, key_pos, obs[m], logs[m], do)
-        dkv = lax.psum_scatter(dkv_part, "ctx", scatter_dimension=0, tiled=True)
+        dq, dkv_own, dkv_other = attend_back(
+            q[m], kvs[m], rows_pos, key_pos, obs[m], logs[m], do
+        )
+        got = to_ctx(dkv_other, 1)
+        dkv = ring_sum(
+            [
+                wide(dkv_own[o * rows : (o + 1) * rows]) + wide(got[o * rows : (o + 1) * rows])
+                for o in range(chips)
+            ],
+            chips,
+        ).astype(low_type)
         dxs.append(dx)
         das.append(da)
         dqs.append(dq)
         dkvs.append(dkv)
         stats.append(stat)
 
-    h1s = [h1[m * rows : (m + 1) * rows] for m in range(micros)]
-    q_groups = HEADS * HD // BC
-    starts = (0, q_groups, in_groups)
-    dense_term = outer_blocks(
-        dense_inverse,
-        lambda k: (starts[k], dense_groups),
-        [h1s, h1s, das],
-        [dqs, dkvs, obs],
-        dense_blocks,
-    )
-    dense_sum = lax.psum_scatter(dense_term, ("ctx", "shard"), scatter_dimension=0, tiled=True)
-    input_grad, gain_stat = input_back(
-        dense_inverse, tokens, norm_gains, dense_all, dxs, dqs, dkvs
-    )
+    def both_cores(parts):
+        return parts + [to_ctx(part, 1) for part in parts]
+
+    made = slot_blocks(
+        chips,
+        shard_count,
+        slots,
+        dense_order,
+        me,
+        [h1, h1_other],
+        both_cores(das),
+        both_cores(dqs),
+        both_cores(dkvs),
+        both_cores(obs),
+    )
+    dense_sum = sum_slots(made, chips, shard_count, slots)
+    input_grad, gain_stat = input_back(tokens, norm_gains, w_in, dxs, dqs, dkvs)
     experts_up = stats[0].shape[0] - 8
-    stat_rows = jnp.concatenate(
-        [sum(stats)[: experts_up + 1], gain_stat[: 7]], axis=0
-    )
-    stat_rows = lax.psum(stat_rows, ("ctx", "shard"))
+    stat_rows = jnp.concatenate([sum(stats)[: experts_up + 1], gain_stat[:7]], axis=0)
+    stat_rows = sum_all(stat_rows)
     router_grad = stat_rows[:shard_count].T
     gains_grad = jnp.stack([stat_rows[experts_up + 1], stat_rows[experts_up]])
+
+    outputs = []
+    for m in range(micros):
+        total = x2s[m]
+        for j in range(shard_count):
+            total = total + wide(to_partner(outs[m][j], j))
+        outputs.append(total)
 
     expert_grad, expert_new, expert_moment_new, expert_second_new = rotate(
         expert_weight[0], expert_sum, expert_moment[0], expert_second[0], expert_left[0], expert_right[0]

time: 870 us -> 596 us (0.69)
  waiting for transfers between devices: 575 us -> 260 us
  starting transfers between devices: 26.4 us -> 85.7 us
  local copies, waits for them, and re-layouts: 66.7 us -> 51.9 us
    reduce_scatter x3 -> x0, waiting for transfers between devices: 173 us -> none  [the longest x1 141 us: shards(): lax.psum_scatter(dense_term, ('ctx', 'shard'), scatter_dimension=0, tiled...]
    ppermute x0 -> x50, waiting for transfers between devices: none -> 151 us  [the longest x18 142 us: to_next_chip(): lax.ppermute(array, 'ctx', [(i, (i + 2) % count) for i in range(count)])]
    all_gather x3 -> x0, waiting for transfers between devices: 115 us -> none  [the longest x1 100 us: shards(): lax.all_gather(dense_weight.astype(low_type), ('ctx', 'shard'), axis=0, t...]
    reduce_scatter x1, waiting for transfers between devices: 99.7 us -> 0.01 us  [shards(): lax.psum_scatter(expert_term, 'ctx', scatter_dimension=0, tiled=True)]
    all_gather x1, waiting for transfers between devices: 69.7 us -> 0.01 us  [shards(): lax.all_gather(expert_weight[0].astype(low_type), 'ctx', axis=0, tiled=True)]
    psum x1 -> x0, waiting for transfers between devices: 42.2 us -> none  [shards(): stat_rows = lax.psum(stat_rows, ('ctx', 'shard'))]
    ppermute x0 -> x50, starting transfers between devices: none -> 39.4 us  [the longest x18 33.4 us: to_next_chip(): lax.ppermute(array, 'ctx', [(i, (i + 2) % count) for i in range(count)])]
    ppermute x21 -> x39, waiting for transfers between devices: 76 us -> 109 us  [to_partner(): return lax.ppermute(array, 'shard', [(i, i ^ offset) for i in range(count)])]
  transfers between devices with their start and end apart: 30 -> 91, of which waited for: 17 -> 38; matrix products, arithmetic and copies ran while one was open for 2% -> 4% of each run, Pallas kernels for 15% -> 19%
where the time goes in v2:
time: 596 us; the launch traced here: 590 us
  waiting for transfers between devices  260 us (44%)
  Pallas kernels  160 us (27%)
  starting transfers between devices  85.7 us (14%)
  local copies, waits for them, and re-layouts  51.9 us (9%)
  other arithmetic  16.4 us (3%)
  between operations  15.8 us (3%)
    ppermute x18, waiting for transfers between devices, to_next_chip(): lax.ppermute(array, 'ctx', [(i, (i + 2) % count) for i in range(count)])  142 us
    ppermute x39, waiting for transfers between devices, to_partner(): return lax.ppermute(array, 'shard', [(i, i ^ offset) for i in range(count)])  109 us
    ppermute x39, starting transfers between devices, to_partner(): return lax.ppermute(array, 'shard', [(i, i ^ offset) for i in range(count)])  46.3 us
    pallas_call x2, Pallas kernels, run_expert(): call(functools.partial(expert_kernel, sources, micro), tuple([shaped((row...  40.6 us
    unnamed x240, local copies, waits for them, and re-layouts  40.2 us
    ppermute x18, starting transfers between devices, to_next_chip(): lax.ppermute(array, 'ctx', [(i, (i + 2) % count) for i in range(count)])  33.4 us
    pallas_call x2, Pallas kernels, attend_back(): call(functools.partial(attend_back_kernel, len(kv_parts)), (shaped((rows,...  24.2 us
    pallas_call x2, Pallas kernels, attend(): call(functools.partial(attend_kernel, len(kv_parts)), (shaped((rows, widt...  21.3 us
  transfers between devices with their start and end apart: 91, of which 38 were waited for; matrix products, arithmetic and copies ran while one was open for 4% of the time, Pallas kernels for 19%

profile of v2, /device:TPU:0, one launch (start us, length us, event | category | flops | bytes accessed | tf_op | source)
XLA Modules:
  0.0 589.7 jit_solution(2155750731074808473)
XLA Ops:
  14.0 11.5 %collective-permute-done.4 = bf16[4,192,256]{2,1,0:T(8,128)(2,1)S(1)} collective-permute-done((bf16[4,192,256]{2,1,0:T(8,128)(2,1)}, bf16[4,192,256]{2,1,0:T(8,128)(2,1)S(1)}, u32[]{:S(2)}, u32[]{:S(2)}) %collective-permute-start.4) | collective-permute-done | bytes 393248 | tf_op jit(solution)/shard_map/ppermute | solution.py:773
  27.9 19.1 %collective-permute-done.5 = bf16[4,192,256]{2,1,0:T(8,128)(2,1)S(1)} collective-permute-done((bf16[4,192,256]{2,1,0:T(8,128)(2,1)S(1)}, bf16[4,192,256]{2,1,0:T(8,128)(2,1)S(1)}, u32[]{:S(2)}, u32[]{:S(2)}) %collective-permute-start.5) | collective-permute-done | bytes 393248 | tf_op jit(solution)/shard_map/ppermute | solution.py:773
  47.1 8.9 %collective-permute-start.6 = (bf16[4,192,256]{2,1,0:T(8,128)(2,1)S(1)}, bf16[4,192,256]{2,1,0:T(8,128)(2,1)S(1)}, u32[]{:S(2)}, u32[]{:S(2)}) collective-permute-start(bf16[4,192,256]{2,1,0:T(8,128)(2,1)S(1)} %collective-permute-done.5), channel_id=1, source_target_pairs={{0,8},{4,12},{8,16},{12,20},{16,24},{20,28},{24,0},{28,4},{1,9},{5... | collective-permute-start | bytes 1179656 | tf_op jit(solution)/shard_map/ppermute | solution.py:773
  56.0 19.4 %collective-permute-done.6 = bf16[4,192,256]{2,1,0:T(8,128)(2,1)S(1)} collective-permute-done((bf16[4,192,256]{2,1,0:T(8,128)(2,1)S(1)}, bf16[4,192,256]{2,1,0:T(8,128)(2,1)S(1)}, u32[]{:S(2)}, u32[]{:S(2)}) %collective-permute-start.6) | collective-permute-done | bytes 393248 | tf_op jit(solution)/shard_map/ppermute | solution.py:773
  79.5 28.8 %collective-permute-done.refs_1_ = bf16[4,192,256]{2,1,0:T(8,128)(2,1)} collective-permute-done((bf16[4,192,256]{2,1,0:T(8,128)(2,1)}, bf16[4,192,256]{2,1,0:T(8,128)(2,1)}, u32[]{:S(2)}, u32[]{:S(2)}) %collective-permute-start) | collective-permute-done | bytes 393248 | tf_op jit(solution)/shard_map/ppermute | solution.py:763
  125.0 12.0 %collective-permute-done.9.refs_8_ = bf16[12,96,256]{2,1,0:T(8,128)(2,1)S(1)} collective-permute-done((bf16[12,96,256]{2,1,0:T(8,128)(2,1)S(1)}, bf16[12,96,256]{2,1,0:T(8,128)(2,1)S(1)}, u32[]{:S(2)}, u32[]{:S(2)}) %collective-permute-start.9) | collective-permute-done | bytes 589856 | tf_op jit(solution)/shard_map/ppermute | solution.py:763
  139.9 10.8 %shard_map.349 = (bf16[256,1536]{1,0:T(8,128)(2,1)S(1)}, bf16[2,128,1536]{2,1,0:T(8,128)(2,1)S(1)}, bf16[2,128,1024]{2,1,0:T(8,128)(2,1)S(1)}, bf16[1536,2560]{1,0:T(8,128)(2,1)S(1)}, bf16[1536,1536]{1,0:T(8,128)(2,1)S(1)}) custom-call(s32[128]{0:T(128)S(1)} %copy-done.52, s32[2]{0:T(128)S(1)} %pad_add_fusion.me_ref, f32[2,128,1536]{2,1,0:T(8,128)S(1)} %copy-done.5, ...), custom_call_target="tpu_custom_call" | custom-call | flops 2013265920 | bytes 15728640 | tf_op jit(solution)/shard_map/pallas_call | solution.py:182
  208.5 10.4 %shard_map.352 = (bf16[128,1536]{1,0:T(8,128)(2,1)S(1)}, f32[384,128]{1,0:T(8,128)S(1)}, f32[128,1536]{1,0:T(8,128)S(1)}, bf16[128,1536]{1,0:T(8,128)(2,1)S(1)}) custom-call(bf16[128,1536]{1,0:T(8,128)(2,1)S(1)} %get-tuple-element.173.q_ref, s32[128,1]{1,0:T(8,128)S(1)} %constant_dynamic-slice_fusion.rpos_ref, s32[1,1024]{1,0:T(1,128)S(1)} %bitcast.57, ...), custom_call_target="tpu_custom_call" | custom-call | flops 3221225472 | bytes 8388608 | tf_op jit(solution)/shard_map/pallas_call | solution.py:255
  224.0 10.9 %shard_map.350 = (bf16[128,1536]{1,0:T(8,128)(2,1)S(1)}, f32[384,128]{1,0:T(8,128)S(1)}, f32[128,1536]{1,0:T(8,128)S(1)}, bf16[128,1536]{1,0:T(8,128)(2,1)}) custom-call(bf16[128,1536]{1,0:T(8,128)(2,1)S(1)} %get-tuple-element.172.q_ref, s32[128,1]{1,0:T(8,128)S(1)} %constant_dynamic-slice_fusion.rpos_ref, s32[1,1024]{1,0:T(1,128)S(1)} %bitcast.58, ...), custom_call_target="tpu_custom_call" | custom-call | flops 3221225472 | bytes 8388608 | tf_op jit(solution)/shard_map/pallas_call | solution.py:255
  244.9 20.0 %shard_map.353 = (bf16[128,1664]{1,0:T(8,128)(2,1)}, bf16[128,1664]{1,0:T(8,128)(2,1)}, bf16[128,1664]{1,0:T(8,128)(2,1)}, bf16[128,1664]{1,0:T(8,128)(2,1)}, bf...) custom-call(s32[96]{0:T(128)} %select_reduce_fusion.order_ref, ...), custom_call_target="tpu_custom_call" | custom-call | flops 9663676416 | bytes 20971520 | tf_op jit(solution)/shard_map/pallas_call | solution.py:363
  265.0 20.6 %shard_map.351 = (bf16[128,1664]{1,0:T(8,128)(2,1)}, bf16[128,1664]{1,0:T(8,128)(2,1)}, bf16[128,1664]{1,0:T(8,128)(2,1)}, bf16[128,1664]{1,0:T(8,128)(2,1)}, bf...) custom-call(s32[96]{0:T(128)} %select_reduce_fusion.order_ref, ...), custom_call_target="tpu_custom_call" | custom-call | flops 9663676416 | bytes 20971520 | tf_op jit(solution)/shard_map/pallas_call | solution.py:363
  289.3 17.4 %shard_map.361 = bf16[96,192,256]{2,1,0:T(8,128)(2,1)} custom-call(s32[96]{0:T(128)S(1)} %copy-done.85, bf16[512,1536]{1,0:T(8,128)(2,1)} %get-tuple-element.143.refs_0_.refs_2_, bf16[512,1536]{1,0:T(8,128)(2,1)} %get-tuple-element.144.refs_1_.refs_3_, bf16[512,1536]{1,0:T(8,128)(2,1)} %get-tuple-element.143.refs_0_.refs_2_, ...), custom_call_target="tpu_custom_call" | custom-call | flops 9663676416 | bytes 25165824 | tf_op jit(solution)/shard_map/pallas_call | solution.py:434
  321.4 8.6 %collective-permute-done.51.refs_2_ = bf16[128,1664]{1,0:T(8,128)(2,1)S(1)} collective-permute-done((bf16[128,1664]{1,0:T(8,128)(2,1)}, bf16[128,1664]{1,0:T(8,128)(2,1)S(1)}, u32[]{:S(2)}, u32[]{:S(2)}) %collective-permute-start.51) | collective-permute-done | bytes 426016 | tf_op jit(solution)/shard_map/ppermute | solution.py:763
  338.8 12.6 %shard_map.356 = (bf16[128,1536]{1,0:T(8,128)(2,1)S(1)}, bf16[512,1024]{1,0:T(8,128)(2,1)S(1)}, bf16[512,1024]{1,0:T(8,128)(2,1)}) custom-call(bf16[128,1536]{1,0:T(8,128)(2,1)S(1)} %copy-done.39, s32[128,1]{1,0:T(8,128)S(1)} %copy-done.47, s32[1,1024]{1,0:T(1,128)S(1)} %bitcast.59, bf16[128,1536]{1,0:T(8,128)(2,1)S(1)} %copy-done.59, ...), custom_call_target="tpu_custom_call" | custom-call | flops 8053063680 | bytes 8388608 | tf_op jit(solution)/shard_map/pallas_call | solution.py:649
  363.2 11.6 %shard_map.357 = (bf16[128,1536]{1,0:T(8,128)(2,1)S(1)}, bf16[512,1024]{1,0:T(8,128)(2,1)S(1)}, bf16[512,1024]{1,0:T(8,128)(2,1)S(1)}) custom-call(bf16[128,1536]{1,0:T(8,128)(2,1)S(1)} %copy-done.37, s32[128,1]{1,0:T(8,128)S(1)} %copy-done.47, s32[1,1024]{1,0:T(1,128)S(1)} %bitcast.60, bf16[128,1536]{1,0:T(8,128)(2,1)S(1)} %copy-done.57, ...), custom_call_target="tpu_custom_call" | custom-call | flops 8053063680 | bytes 8388608 | tf_op jit(solution)/shard_map/pallas_call | solution.py:649
  379.0 14.1 %collective-permute-done.57 = bf16[128,1024]{1,0:T(8,128)(2,1)S(1)} collective-permute-done((bf16[128,1024]{1,0:T(8,128)(2,1)S(1)}, bf16[128,1024]{1,0:T(8,128)(2,1)S(1)}, u32[]{:S(2)}, u32[]{:S(2)}) %collective-permute-start.57) | collective-permute-done | bytes 262176 | tf_op jit(solution)/shard_map/ppermute | solution.py:773
  394.3 10.1 %collective-permute-done.61 = bf16[128,1024]{1,0:T(8,128)(2,1)S(1)} collective-permute-done((bf16[128,1024]{1,0:T(8,128)(2,1)S(1)}, bf16[128,1024]{1,0:T(8,128)(2,1)S(1)}, u32[]{:S(2)}, u32[]{:S(2)}) %collective-permute-start.61) | collective-permute-done | bytes 262176 | tf_op jit(solution)/shard_map/ppermute | solution.py:773
  405.2 10.4 %collective-permute-done.58 = bf16[128,1024]{1,0:T(8,128)(2,1)S(1)} collective-permute-done((bf16[128,1024]{1,0:T(8,128)(2,1)S(1)}, bf16[128,1024]{1,0:T(8,128)(2,1)S(1)}, u32[]{:S(2)}, u32[]{:S(2)}) %collective-permute-start.58) | collective-permute-done | bytes 262176 | tf_op jit(solution)/shard_map/ppermute | solution.py:773
  416.8 10.1 %collective-permute-done.62 = bf16[128,1024]{1,0:T(8,128)(2,1)S(1)} collective-permute-done((bf16[128,1024]{1,0:T(8,128)(2,1)S(1)}, bf16[128,1024]{1,0:T(8,128)(2,1)S(1)}, u32[]{:S(2)}, u32[]{:S(2)}) %collective-permute-start.62) | collective-permute-done | bytes 262176 | tf_op jit(solution)/shard_map/ppermute | solution.py:773
  462.2 17.3 %shard_map.359 = (bf16[8,192,256]{2,1,0:T(8,128)(2,1)S(1)}, bf16[8,192,256]{2,1,0:T(8,128)(2,1)S(1)}, bf16[8,192,256]{2,1,0:T(8,128)(2,1)S(1)}, bf16[8,192,256]{...) custom-call(s32[128]{0:T(128)S(1)} %copy-done.53, ...), custom_call_target="tpu_custom_call" | custom-call | flops 3221225472 | bytes 16777216 | tf_op jit(solution)/shard_map/pallas_call | solution.py:514
  492.0 18.2 %collective-permute-done.87 = f32[16,1536]{1,0:T(8,128)S(1)} collective-permute-done((f32[16,1536]{1,0:T(8,128)S(1)}, f32[16,1536]{1,0:T(8,128)S(1)}, u32[]{:S(2)}, u32[]{:S(2)}) %collective-permute-start.87) | collective-permute-done | bytes 98336 | tf_op jit(solution)/shard_map/ppermute | solution.py:763
  527.0 7.8 %collective-permute-done.79 = bf16[8,192,256]{2,1,0:T(8,128)(2,1)S(1)} collective-permute-done((bf16[8,192,256]{2,1,0:T(8,128)(2,1)S(1)}, bf16[8,192,256]{2,1,0:T(8,128)(2,1)S(1)}, u32[]{:S(2)}, u32[]{:S(2)}) %collective-permute-start.79) | collective-permute-done | bytes 786464 | tf_op jit(solution)/shard_map/ppermute | solution.py:763
  552.4 8.9 %collective-permute-done.81 = bf16[4,192,256]{2,1,0:T(8,128)(2,1)S(1)} collective-permute-done((bf16[4,192,256]{2,1,0:T(8,128)(2,1)S(1)}, bf16[4,192,256]{2,1,0:T(8,128)(2,1)S(1)}, u32[]{:S(2)}, u32[]{:S(2)}) %collective-permute-start.81) | collective-permute-done | bytes 393248 | tf_op jit(solution)/shard_map/ppermute | solution.py:773
  573.3 9.3 %shard_map.362 = (f32[12,192,256]{2,1,0:T(8,128)}, f32[12,192,256]{2,1,0:T(8,128)}, f32[12,192,256]{2,1,0:T(8,128)}, f32[12,192,256]{2,1,0:T(8,128)}) custom-call(f32[12,192,256]{2,1,0:T(8,128)S(1)} %bitcast.50, bf16[12,192,256]{2,1,0:T(8,128)(2,1)S(1)} %copy-done.19, f32[12,192,256]{2,1,0:T(8,128)S(1)} %bitcast.52, f32[12,192,256]{2,1,0:T(8,128)S(1)} %bitcast.53, ...), custom_call_target="tpu_custom_call" | custom-call | flops 1056964608 | bytes 25165824 | tf_op jit(solution)/shard_map/pallas_call | solution.py:734
  (475 shorter events, 245.4 us)
Async XLA Ops:
  7.2 237.7 %all-gather.2.cloned.1.call-start = ((), (), s32[]{:S(2)}) async-start(), calls=%async_computation.1 | async-start | bytes 10616832 | tf_op jit(solution)/shard_map/all_gather | solution.py:899
  10.2 555.0 %reduce-scatter.2.cloned.1.call-start = ((), (), s32[]{:S(2)}) async-start(), calls=%async_computation.2 | async-start | bytes 10616832 | tf_op jit(solution)/shard_map/reduce_scatter | solution.py:947
  47.1 28.3 %collective-permute-start.6 = (bf16[4,192,256]{2,1,0:T(8,128)(2,1)S(1)}, bf16[4,192,256]{2,1,0:T(8,128)(2,1)S(1)}, u32[]{:S(2)}, u32[]{:S(2)}) collective-permute-start(bf16[4,192,256]{2,1,0:T(8,128)(2,1)S(1)} %collective-permute-done.5), channel_id=1, source_target_pairs={{0,8},{4,12},{8,16},{12,20},{16,24},{20,28},{24,0},{28,4},{1,9},{5... | collective-permute-start | bytes 1179656 | tf_op jit(solution)/shard_map/ppermute | solution.py:773
  75.4 42.9 %collective-permute-start.7 = (bf16[12,192,256]{2,1,0:T(8,128)(2,1)S(1)}, bf16[12,192,256]{2,1,0:T(8,128)(2,1)S(1)}, u32[]{:S(2)}, u32[]{:S(2)}) collective-permute-start(bf16[12,192,256]{2,1,0:T(8,128)(2,1)S(1)} %constant_dynamic-update-slice_fusion.refs_5_), channel_id=1, source_target_pairs={{0,1},{1,0},{2,3},{3,2},{4,5},{5,4},{6,7},{7,6},{8,9},{9,8},{10,11... | collective-permute-start | bytes 3538952 | tf_op jit(solution)/shard_map/ppermute | solution.py:763
  76.8 42.1 %collective-permute-start.8 = (bf16[12,192,256]{2,1,0:T(8,128)(2,1)S(1)}, bf16[12,192,256]{2,1,0:T(8,128)(2,1)}, u32[]{:S(2)}, u32[]{:S(2)}) collective-permute-start(bf16[12,192,256]{2,1,0:T(8,128)(2,1)S(1)} %constant_dynamic-update-slice_fusion.refs_5_), channel_id=1, source_target_pairs={{0,2},{1,3},{2,0},{3,1},{4,6},{5,7},{6,4},{7,5},{8,10},{9,11},{10,... | collective-permute-start | bytes 3538952 | tf_op jit(solution)/shard_map/ppermute | solution.py:763
  78.3 30.0 %collective-permute-start = (bf16[4,192,256]{2,1,0:T(8,128)(2,1)}, bf16[4,192,256]{2,1,0:T(8,128)(2,1)}, u32[]{:S(2)}, u32[]{:S(2)}) collective-permute-start(bf16[4,192,256]{2,1,0:T(8,128)(2,1)} %convert_element_type.223.refs_0_), channel_id=1, source_target_pairs={{0,1},{1,0},{2,3},{3,2},{4,5},{5,4},{6,7},{7,6},{8,9},{9,8},{10,11... | collective-permute-start | bytes 1179656 | tf_op jit(solution)/shard_map/ppermute | solution.py:763
  78.8 32.7 %collective-permute-start.1 = (bf16[4,192,256]{2,1,0:T(8,128)(2,1)}, bf16[4,192,256]{2,1,0:T(8,128)(2,1)}, u32[]{:S(2)}, u32[]{:S(2)}) collective-permute-start(bf16[4,192,256]{2,1,0:T(8,128)(2,1)} %convert_element_type.223.refs_0_), channel_id=1, source_target_pairs={{0,2},{1,3},{2,0},{3,1},{4,6},{5,7},{6,4},{7,5},{8,10},{9,11},{10,... | collective-permute-start | bytes 1179656 | tf_op jit(solution)/shard_map/ppermute | solution.py:763
  139.3 43.2 %collective-permute-start.31 = (bf16[256,1664]{1,0:T(8,128)(2,1)}, bf16[256,1664]{1,0:T(8,128)(2,1)}, u32[]{:S(2)}, u32[]{:S(2)}) collective-permute-start(bf16[256,1664]{1,0:T(8,128)(2,1)} %bitcast.11.refs_4_), channel_id=1, source_target_pairs={{0,1},{1,0},{2,3},{3,2},{4,5},{5,4},{6,7},{7,6},{8,9},{9,8},{10,11... | collective-permute-start | bytes 2555912 | tf_op jit(solution)/shard_map/ppermute | solution.py:763
  186.9 49.5 %collective-permute-start.32 = (bf16[256,1664]{1,0:T(8,128)(2,1)}, bf16[256,1664]{1,0:T(8,128)(2,1)S(1)}, u32[]{:S(2)}, u32[]{:S(2)}) collective-permute-start(bf16[256,1664]{1,0:T(8,128)(2,1)} %bitcast.11.refs_4_), channel_id=1, source_target_pairs={{0,2},{1,3},{2,0},{3,1},{4,6},{5,7},{6,4},{7,5},{8,10},{9,11},{10,... | collective-permute-start | bytes 2555912 | tf_op jit(solution)/shard_map/ppermute | solution.py:763
  188.5 48.8 %collective-permute-start.33 = (bf16[256,1664]{1,0:T(8,128)(2,1)}, bf16[256,1664]{1,0:T(8,128)(2,1)S(1)}, u32[]{:S(2)}, u32[]{:S(2)}) collective-permute-start(bf16[256,1664]{1,0:T(8,128)(2,1)} %bitcast.11.refs_4_), channel_id=1, source_target_pairs={{0,3},{1,2},{2,1},{3,0},{4,7},{5,6},{6,5},{7,4},{8,11},{9,10},{10,... | collective-permute-start | bytes 2555912 | tf_op jit(solution)/shard_map/ppermute | solution.py:763
  236.4 28.6 %collective-permute-start.28 = (bf16[128,1536]{1,0:T(8,128)(2,1)}, bf16[128,1536]{1,0:T(8,128)(2,1)}, u32[]{:S(2)}, u32[]{:S(2)}) collective-permute-start(bf16[128,1536]{1,0:T(8,128)(2,1)} %get-tuple-element.93.refs_0_.h2_ref), channel_id=1, source_target_pairs={{0,1},{1,0},{2,3},{3,2},{4,5},{5,4},{6,7},{7,6},{8,9},{9,8},{10,11... | collective-permute-start | bytes 1179656 | tf_op jit(solution)/shard_map/ppermute | solution.py:763
  237.3 27.7 %collective-permute-start.29 = (bf16[128,1536]{1,0:T(8,128)(2,1)}, bf16[128,1536]{1,0:T(8,128)(2,1)}, u32[]{:S(2)}, u32[]{:S(2)}) collective-permute-start(bf16[128,1536]{1,0:T(8,128)(2,1)} %get-tuple-element.93.refs_0_.h2_ref), channel_id=1, source_target_pairs={{0,2},{1,3},{2,0},{3,1},{4,6},{5,7},{6,4},{7,5},{8,10},{9,11},{10,... | collective-permute-start | bytes 1179656 | tf_op jit(solution)/shard_map/ppermute | solution.py:763
  238.2 26.8 %collective-permute-start.30 = (bf16[128,1536]{1,0:T(8,128)(2,1)}, bf16[128,1536]{1,0:T(8,128)(2,1)}, u32[]{:S(2)}, u32[]{:S(2)}) collective-permute-start(bf16[128,1536]{1,0:T(8,128)(2,1)} %get-tuple-element.93.refs_0_.h2_ref), channel_id=1, source_target_pairs={{0,3},{1,2},{2,1},{3,0},{4,7},{5,6},{6,5},{7,4},{8,11},{9,10},{10,... | collective-permute-start | bytes 1179656 | tf_op jit(solution)/shard_map/ppermute | solution.py:763
  311.9 40.4 %collective-permute-start.53 = (bf16[128,1664]{1,0:T(8,128)(2,1)}, bf16[128,1664]{1,0:T(8,128)(2,1)}, u32[]{:S(2)}, u32[]{:S(2)}) collective-permute-start(bf16[128,1664]{1,0:T(8,128)(2,1)} %get-tuple-element.111), channel_id=1, source_target_pairs={{0,1},{1,0},{2,3},{3,2},{4,5},{5,4},{6,7},{7,6},{8,9},{9,8},{10,11... | collective-permute-start | bytes 1277960 | tf_op jit(solution)/shard_map/ppermute | solution.py:763
  313.2 39.2 %collective-permute-start.54 = (bf16[128,1664]{1,0:T(8,128)(2,1)}, bf16[128,1664]{1,0:T(8,128)(2,1)}, u32[]{:S(2)}, u32[]{:S(2)}) collective-permute-start(bf16[128,1664]{1,0:T(8,128)(2,1)} %get-tuple-element.112), channel_id=1, source_target_pairs={{0,2},{1,3},{2,0},{3,1},{4,6},{5,7},{6,4},{7,5},{8,10},{9,11},{10,... | collective-permute-start | bytes 1277960 | tf_op jit(solution)/shard_map/ppermute | solution.py:763
  319.8 32.6 %collective-permute-start.55 = (bf16[128,1664]{1,0:T(8,128)(2,1)}, bf16[128,1664]{1,0:T(8,128)(2,1)}, u32[]{:S(2)}, u32[]{:S(2)}) collective-permute-start(bf16[128,1664]{1,0:T(8,128)(2,1)} %get-tuple-element.113), channel_id=1, source_target_pairs={{0,3},{1,2},{2,1},{3,0},{4,7},{5,6},{6,5},{7,4},{8,11},{9,10},{10,... | collective-permute-start | bytes 1277960 | tf_op jit(solution)/shard_map/ppermute | solution.py:763
  404.6 46.0 %collective-permute-start.64 = (bf16[256,1536]{1,0:T(8,128)(2,1)S(1)}, bf16[256,1536]{1,0:T(8,128)(2,1)S(1)}, u32[]{:S(2)}, u32[]{:S(2)}) collective-permute-start(bf16[256,1536]{1,0:T(8,128)(2,1)S(1)} %copy-done.55), channel_id=1, source_target_pairs={{0,4},{4,0},{8,12},{12,8},{16,20},{20,16},{24,28},{28,24},{1,5},{5... | collective-permute-start | bytes 2359304 | tf_op jit(solution)/shard_map/ppermute | solution.py:768
  404.6 46.4 %collective-permute-start.71 = (bf16[128,1536]{1,0:T(8,128)(2,1)S(1)}, bf16[128,1536]{1,0:T(8,128)(2,1)S(1)}, u32[]{:S(2)}, u32[]{:S(2)}) collective-permute-start(bf16[128,1536]{1,0:T(8,128)(2,1)S(1)} %copy-done.60), channel_id=1, source_target_pairs={{0,4},{4,0},{8,12},{12,8},{16,20},{20,16},{24,28},{28,24},{1,5},{5... | collective-permute-start | bytes 1179656 | tf_op jit(solution)/shard_map/ppermute | solution.py:768
  405.1 46.0 %collective-permute-start.72 = (bf16[128,1536]{1,0:T(8,128)(2,1)S(1)}, bf16[128,1536]{1,0:T(8,128)(2,1)S(1)}, u32[]{:S(2)}, u32[]{:S(2)}) collective-permute-start(bf16[128,1536]{1,0:T(8,128)(2,1)S(1)} %copy-done.57), channel_id=1, source_target_pairs={{0,4},{4,0},{8,12},{12,8},{16,20},{20,16},{24,28},{28,24},{1,5},{5... | collective-permute-start | bytes 1179656 | tf_op jit(solution)/shard_map/ppermute | solution.py:768
  460.1 28.8 %collective-permute-start.36 = (bf16[128,1536]{1,0:T(8,128)(2,1)S(1)}, bf16[128,1536]{1,0:T(8,128)(2,1)S(1)}, u32[]{:S(2)}, u32[]{:S(2)}) collective-permute-start(bf16[128,1536]{1,0:T(8,128)(2,1)S(1)} %copy-done.110), channel_id=1, source_target_pairs={{0,3},{1,2},{2,1},{3,0},{4,7},{5,6},{6,5},{7,4},{8,11},{9,10},{10,... | collective-permute-start | bytes 1179656 | tf_op jit(solution)/shard_map/ppermute | solution.py:763
  461.6 29.6 %collective-permute-start.35 = (bf16[128,1536]{1,0:T(8,128)(2,1)S(1)}, bf16[128,1536]{1,0:T(8,128)(2,1)S(1)}, u32[]{:S(2)}, u32[]{:S(2)}) collective-permute-start(bf16[128,1536]{1,0:T(8,128)(2,1)S(1)} %copy-done.109), channel_id=1, source_target_pairs={{0,2},{1,3},{2,0},{3,1},{4,6},{5,7},{6,4},{7,5},{8,10},{9,11},{10,... | collective-permute-start | bytes 1179656 | tf_op jit(solution)/shard_map/ppermute | solution.py:763
  481.1 29.7 %collective-permute-start.73 = (bf16[8,192,256]{2,1,0:T(8,128)(2,1)S(1)}, bf16[8,192,256]{2,1,0:T(8,128)(2,1)S(1)}, u32[]{:S(2)}, u32[]{:S(2)}) collective-permute-start(bf16[8,192,256]{2,1,0:T(8,128)(2,1)S(1)} %get-tuple-element.132), channel_id=1, source_target_pairs={{0,1},{1,0},{2,3},{3,2},{4,5},{5,4},{6,7},{7,6},{8,9},{9,8},{10,11... | collective-permute-start | bytes 2359304 | tf_op jit(solution)/shard_map/ppermute | solution.py:763
  487.4 28.6 %collective-permute-start.76 = (bf16[8,192,256]{2,1,0:T(8,128)(2,1)S(1)}, bf16[8,192,256]{2,1,0:T(8,128)(2,1)S(1)}, u32[]{:S(2)}, u32[]{:S(2)}) collective-permute-start(bf16[8,192,256]{2,1,0:T(8,128)(2,1)S(1)} %get-tuple-element.134), channel_id=1, source_target_pairs={{0,2},{1,3},{2,0},{3,1},{4,6},{5,7},{6,4},{7,5},{8,10},{9,11},{10,... | collective-permute-start | bytes 2359304 | tf_op jit(solution)/shard_map/ppermute | solution.py:763
  513.7 28.8 %collective-permute-start.82 = (bf16[8,192,256]{2,1,0:T(8,128)(2,1)S(1)}, bf16[8,192,256]{2,1,0:T(8,128)(2,1)S(1)}, u32[]{:S(2)}, u32[]{:S(2)}) collective-permute-start(bf16[8,192,256]{2,1,0:T(8,128)(2,1)S(1)} %get-tuple-element.138), channel_id=1, source_target_pairs={{0,2},{1,3},{2,0},{3,1},{4,6},{5,7},{6,4},{7,5},{8,10},{9,11},{10,... | collective-permute-start | bytes 2359304 | tf_op jit(solution)/shard_map/ppermute | solution.py:763
  (186 other events, 2583.1 us)
Sparse Core Ops, SparseCore 0:
  10.3 110.3 all-gather.1
  306.8 124.2 reduce-scatter.1

commit v3 on v2

--- a/solution.py
+++ b/solution.py
@@ -24,6 +24,7 @@
 masked_score = -1e30
 low_type = jnp.bfloat16
 MIB = 1 << 20
+VMEM_LIMIT = 60 * MIB
 
 NN = (((1,), (0,)), ((), ()))
 NT = (((1,), (1,)), ((), ()))
@@ -38,14 +39,14 @@
     return lax.dot_general(left_side, right_side, dims, preferred_element_type=jnp.float32)
 
 
-def call(kernel, out_shapes, in_specs, out_specs, scratch, flops, moved, limit):
+def call(kernel, out_shapes, in_specs, out_specs, scratch, flops, moved):
     return pl.pallas_call(
         kernel,
         out_shape=out_shapes,
         in_specs=in_specs,
         out_specs=out_specs,
         scratch_shapes=scratch,
-        compiler_params=pltpu.CompilerParams(vmem_limit_bytes=limit * MIB),
+        compiler_params=pltpu.CompilerParams(vmem_limit_bytes=VMEM_LIMIT),
         cost_estimate=pl.CostEstimate(flops=flops, bytes_accessed=moved, transcendentals=0),
     )
 
@@ -199,7 +200,6 @@
         ],
         2 * micros * rows * width * in_width,
         2 * width * in_width * 2,
-        24,
     )(order, me, x, gains, *arrays)
 
 
@@ -270,7 +270,6 @@
         ],
         16 * rows * length * width,
         8 * MIB,
-        40,
     )(q, rows_pos, key_pos, x, gains, w, *kv_parts)
 
 
@@ -379,7 +378,6 @@
         ],
         12 * total * width * FF,
         20 * MIB,
-        56,
     )(order, me, router, *h_parts, *c_parts, w)
 
 
@@ -439,7 +437,6 @@
         [pltpu.VMEM((2, 2 * BR, widest), low_type), pltpu.SemaphoreType.DMA((2,))],
         2 * rows * blocks * BR * BC,
         blocks * BR * BC * 2 + sum(f.size * 2 for f in flat),
-        48,
     )(order, *flat)
 
 
@@ -532,7 +529,6 @@
         ],
         2 * total * chips * members * slots * BR * BC,
         16 * MIB,
-        40,
     )(order, me, *[part for group in lists for part in group])
     return [(made[2 * offset], made[2 * offset + 1]) for offset in range(chips)]
 
@@ -592,7 +588,6 @@
         [pltpu.VMEM((width, HEADS * HD), low_type), pltpu.SemaphoreType.DMA],
         2 * rows * width * HEADS * HD,
         10 * MIB,
-        40,
     )(me, x2, cot, h2, gains, router, w, *backs)
 
 
@@ -658,26 +653,64 @@
         ],
         40 * rows * length * width,
         8 * MIB,
-        48,
     )(q, rows_pos, key_pos, ob, log_total, do, *kv_parts)
 
 
-def input_kernel(x_ref, gain_ref, w_ref, *refs):
-    micros = x_ref.shape[0]
-    rows = x_ref.shape[1]
-    dx_refs = refs[:micros]
-    dq_refs = refs[micros : 2 * micros]
-    dkv_refs = refs[2 * micros : 3 * micros]
-    out_ref, stat_ref, grad, held, sem = refs[3 * micros :]
-    pltpu.make_async_copy(w_ref, held, sem).start()
-    q_width = dq_refs[0].shape[-1]
-    wait_bytes(held, sem)
+def query_back_kernel(w_ref, *refs):
+    micros = (len(refs) - 3) // 2
+    dq_refs, out_refs = refs[:micros], refs[micros : 2 * micros]
+    rows_ref, held, sem = refs[2 * micros :]
+    rows = dq_refs[0].shape[0]
+    copy = pltpu.make_async_copy(w_ref.at[:, pl.ds(0, held.shape[1])], held, sem)
+    copy.start()
+    for m in range(micros):
+        rows_ref[m * rows : (m + 1) * rows] = dq_refs[m][...]
+    copy.wait()
     for n in range(held.shape[0] // BC):
         cut = slice(n * BC, (n + 1) * BC)
+        made = dot(rows_ref[...], held[cut, :], NT)
         for m in range(micros):
-            grad[m, :, cut] = dot(dq_refs[m][...], held[cut, :q_width], NT) + dot(
-                dkv_refs[m][...], held[cut, q_width:], NT
-            )
+            out_refs[m][:, cut] = made[m * rows : (m + 1) * rows]
+
+
+def query_back(w, dqs):
+    micros = len(dqs)
+    rows, q_width = dqs[0].shape
+    width = w.shape[0]
+    return call(
+        query_back_kernel,
+        tuple([shaped((rows, width), jnp.float32)] * micros),
+        [in_any] + [in_vmem] * micros,
+        tuple([in_vmem] * micros),
+        [
+            pltpu.VMEM((micros * rows, q_width), low_type),
+            pltpu.VMEM((width, q_width), low_type),
+            pltpu.SemaphoreType.DMA,
+        ],
+        2 * micros * rows * width * q_width,
+        7 * MIB,
+    )(w, *dqs)
+
+
+def input_kernel(x_ref, gain_ref, w_ref, *refs):
+    micros, rows = x_ref.shape[:2]
+    dx_refs = refs[:micros]
+    part_refs = refs[micros : 2 * micros]
+    dkv_refs = refs[2 * micros : 3 * micros]
+    out_ref, stat_ref, rows_ref, grad, held, sem = refs[3 * micros :]
+    kv_width = held.shape[1]
+    copy = pltpu.make_async_copy(
+        w_ref.at[:, pl.ds(w_ref.shape[1] - kv_width, kv_width)], held, sem
+    )
+    copy.start()
+    for m in range(micros):
+        rows_ref[m * rows : (m + 1) * rows] = dkv_refs[m][...]
+    copy.wait()
+    for n in range(held.shape[0] // BC):
+        cut = slice(n * BC, (n + 1) * BC)
+        made = dot(rows_ref[...], held[cut, :], NT)
+        for m in range(micros):
+            grad[m, :, cut] = part_refs[m][:, cut] + made[m * rows : (m + 1) * rows]
     total = jnp.zeros((1, x_ref.shape[-1]), jnp.float32)
     for m in range(micros):
         x = x_ref[m]
@@ -688,23 +721,23 @@
     stat_ref[...] = jnp.broadcast_to(total, stat_ref.shape)
 
 
-def input_back(x, gains, w, dxs, dqs, dkvs):
+def input_back(x, gains, w, dxs, parts, dkvs):
     micros, rows, width = x.shape
-    in_width = (HEADS + 2 * KVH) * HD
+    kv_width = dkvs[0].shape[1]
     return call(
         input_kernel,
         (shaped(x.shape, jnp.float32), shaped((8, width), jnp.float32)),
         [in_vmem, in_vmem, in_any] + [in_vmem] * (3 * micros),
         (in_vmem,) * 2,
         [
+            pltpu.VMEM((micros * rows, kv_width), low_type),
             pltpu.VMEM(x.shape, jnp.float32),
-            pltpu.VMEM((width, in_width), low_type),
+            pltpu.VMEM((width, kv_width), low_type),
             pltpu.SemaphoreType.DMA,
         ],
-        2 * micros * rows * width * in_width,
+        2 * micros * rows * width * kv_width,
         14 * MIB,
-        40,
-    )(x, gains, w, *dxs, *dqs, *dkvs)
+    )(x, gains, w, *dxs, *parts, *dkvs)
 
 
 def rotate_kernel(
@@ -737,7 +770,7 @@
         out_shape=(shaped(weight.shape, jnp.float32),) * 4,
         in_specs=[block] * 4 + [spec(BR, BR), spec(BC, BC)],
         out_specs=(block,) * 4,
-        compiler_params=pltpu.CompilerParams(vmem_limit_bytes=24 * MIB),
+        compiler_params=pltpu.CompilerParams(vmem_limit_bytes=VMEM_LIMIT),
         cost_estimate=pl.CostEstimate(
             flops=4 * count * BR * BC * (BR + BC),
             bytes_accessed=count * 2 * MIB,
@@ -768,60 +801,62 @@
     return lax.ppermute(array, "ctx", [(i, i ^ offset) for i in range(count)])
 
 
-def to_next_chip(array):
+def to_chip(array, offset):
     count = lax.axis_size("ctx")
-    return lax.ppermute(array, "ctx", [(i, (i + 2) % count) for i in range(count)])
-
-
-def chip_ring(array, chips):
-    parts = [array]
-    for _ in range(chips - 1):
-        parts.append(to_next_chip(parts[-1]))
-    return parts
+    return lax.ppermute(array, "ctx", [(i, (i + 2 * offset) % count) for i in range(count)])
+
+
+def after(value, *others):
+    return lax.optimization_barrier((value, others))[0]
+
+
+def from_chips(array, chips):
+    return [array] + [to_chip(array, offset) for offset in range(1, chips)]
 
 
 def wide(array):
     return array.astype(jnp.float32)
 
 
-def ring_sum(parts, chips):
-    total = None
-    for offset in list(range(1, chips)) + [0]:
-        total = parts[offset] if total is None else wide(to_next_chip(total)) + parts[offset]
-        if offset != 0:
-            total = total.astype(low_type)
+def sum_to_chips(parts):
+    total = wide(parts[0])
+    for offset in range(1, len(parts)):
+        total = total + wide(to_chip(parts[offset], -offset))
     return total
 
 
 def gather_weights(blocks, chips, members):
-    parts = chip_ring(blocks, chips)
-    groups = [(0, parts[0])]
-    if chips > 1:
-        groups.append((1, jnp.concatenate(parts[1:], axis=0)))
+    parts = from_chips(blocks, chips)
     pieces, arrays = [], []
 
     def add(array, offset, first, cut):
         pieces.append((0, offset, first, cut))
         arrays.append(array)
-
-    for first, group in groups:
-        add(group, 0, first, 0)
+        pieces.append((1, offset, first, cut))
+        arrays.append(to_ctx(array, 1))
+        return array
+
+    add(blocks, 0, 0, 0)
+    for offset in range(1, members):
+        add(to_partner(blocks, offset), offset, 0, 0)
+    near = list(arrays)
+    if chips > 1:
+        far = after(jnp.concatenate(parts[1:], axis=0), *near)
+        add(far, 0, 1, 0)
         if members == 4:
-            by_one, by_two = to_partner(group, 1), to_partner(group, 2)
-            add(by_one, 1, first, 0)
-            add(by_two, 2, first, 0)
+            by_one = add(to_partner(far, 1), 1, 1, 0)
+            by_two = add(to_partner(far, 2), 2, 1, 0)
             half = BR // 2
-            add(to_partner(by_one[:, :half], 2), 3, first, 0)
-            add(to_partner(by_two[:, half:], 1), 3, first, half)
+            add(to_partner(by_one[:, :half], 2), 3, 1, 0)
+            add(to_partner(by_two[:, half:], 1), 3, 1, half)
         else:
             for offset in range(1, members):
-                add(to_partner(group, offset), offset, first, 0)
-    swapped = [to_ctx(array, 1) for array in arrays]
-    return pieces + [(1,) + piece[1:] for piece in pieces], arrays + swapped
+                add(to_partner(far, offset), offset, 1, 0)
+    return near + parts[1:], pieces, arrays
 
 
 def sum_slots(made, chips, members, slots):
-    sums = []
+    sums, first_got = [], []
     for offset in range(chips):
         sent, kept = made[offset]
         hops, keeps = xor_plan(members, offset)
@@ -834,9 +869,11 @@
             total = total + wide(to_partner(relay, second))
         else:
             for place, hop in enumerate(hops):
-                total = total + wide(to_partner(sent[place * slots : (place + 1) * slots], hop))
-        sums.append(total)
-    return ring_sum(sums, chips)
+                got = to_partner(sent[place * slots : (place + 1) * slots], hop)
+                total = total + wide(got)
+        sums.append(total if offset == 0 else total.astype(low_type))
+        first_got.append(got)
+    return sums, first_got
 
 
 def sum_all(array):
@@ -896,13 +933,15 @@
     rows_pos = all_pos[ctx].reshape(rows, 1)
     router_pad = jnp.pad(router.astype(low_type), ((0, 0), (0, LANES - shard_count)))
 
-    expert_all = lax.all_gather(expert_weight[0].astype(low_type), "ctx", axis=0, tiled=True)
-    pieces, arrays = gather_weights(dense_weight.astype(low_type), chips, shard_count)
+    far, pieces, arrays = gather_weights(dense_weight.astype(low_type), chips, shard_count)
+    expert_low = after(expert_weight[0].astype(low_type), *far)
+    expert_all = lax.all_gather(expert_low, "ctx", axis=0, tiled=True)
 
     lanes = jnp.arange(LANES, dtype=jnp.int32)
     hits = jnp.sum((routes[..., None] == lanes).astype(low_type), axis=2)
     cot_rows = jnp.concatenate([cotangent.astype(low_type), hits], axis=2)
     cot_rows = cot_rows.reshape(micros * rows, width + LANES)
+    cot_rows = after(cot_rows, *arrays[::2])
     cot_parts = [to_partner(cot_rows, j) for j in range(shard_count)]
 
     h1, q, kv, w_in, w_out = project(
@@ -910,24 +949,34 @@
     )
     h1_other = to_ctx(h1, 1)
     kvs, obs, logs, x2s, h2s = [], [], [], [], []
+    chip_kv = []
     for m in range(micros):
-        parts = chip_ring(kv[m], chips)
-        parts = parts + [to_ctx(part, 1) for part in parts]
+        own = kv[m] if m == 0 else after(kv[m], chip_kv[m - 1][1 % chips])
+        chip_kv.append(from_chips(own, chips))
+    for m in range(micros):
+        query = q[m] if m == 0 else after(q[m], obs[m - 1])
+        parts = chip_kv[m]
+        swapped = parts if m == 0 else after(parts, obs[m - 1])
+        kvs.append(parts + [to_ctx(part, 1) for part in swapped])
         ob, log_total, x2, h2 = attend(
-            q[m], parts, rows_pos, key_pos, tokens[m], norm_gains, w_out
+            query, kvs[m], rows_pos, key_pos, tokens[m], norm_gains, w_out
         )
-        kvs.append(parts)
         obs.append(ob)
         logs.append(log_total)
         x2s.append(x2)
         h2s.append(h2)
-
-    backs, outs = [], []
+    ob_others = [to_ctx(ob, 1) for ob in obs]
+
+    h_parts = []
+    for m in range(micros):
+        own = after(h2s[m], *(cot_parts if m == 0 else h_parts[m - 1]))
+        h_parts.append([own] + [to_partner(own, j) for j in range(1, shard_count)])
+    outs, sent = [], []
     zs, dgs, dus, dys, xs = [], [], [], [], []
     for m in range(micros):
-        h_parts = [to_partner(h2s[m], j) for j in range(shard_count)]
-        made = run_expert(m, expert_inverse, me, router_pad, h_parts, cot_parts, expert_all)
-        back = made[:shard_count]
+        here = after(me, h2s[-1], h1_other, *ob_others) if m == 0 else after(me, zs[-1])
+        made = run_expert(m, expert_inverse, here, router_pad, h_parts[m], cot_parts, expert_all)
+        sent.append(made[:shard_count])
         outs.append(made[shard_count : 2 * shard_count])
         z, dg, du, dy, x = made[2 * shard_count :]
         zs.append(z)
@@ -935,56 +984,71 @@
         dus.append(du)
         dys.append(dy)
         xs.append(x)
-        backs.append([to_partner(back[j], j) for j in range(shard_count)])
-
-    expert_term = outer_blocks(
-        expert_inverse,
-        lambda k: (k * row_groups * ff_groups, ff_groups),
-        [xs, xs, dys],
-        [dgs, dus, zs],
-        expert_blocks,
-    )
-    expert_sum = lax.psum_scatter(expert_term, "ctx", scatter_dimension=0, tiled=True)
-
-    dxs, das, dqs, dkvs, stats = [], [], [], [], []
+    backs = [[to_partner(sent[m][j], j) for j in range(shard_count)] for m in range(micros)]
+    arrived = []
     for m in range(micros):
+        own = [after(part, *(arrived[-1] if arrived else backs[-1])) for part in outs[m]]
+        arrived.append([to_partner(own[j], j) for j in range(shard_count)])
+
+    dxs, das, dqs, stats, own_grads, far_grads = [], [], [], [], [], []
+    for m in range(micros):
+        here = after(me, zs[-1] if m == 0 else dqs[-1])
         dx, da, do, stat = merge(
-            me, x2s[m], cotangent[m], h2s[m], norm_gains, router_pad, w_out, backs[m]
+            here, x2s[m], cotangent[m], h2s[m], norm_gains, router_pad, w_out, backs[m]
         )
         dq, dkv_own, dkv_other = attend_back(
             q[m], kvs[m], rows_pos, key_pos, obs[m], logs[m], do
         )
         got = to_ctx(dkv_other, 1)
-        dkv = ring_sum(
-            [
-                wide(dkv_own[o * rows : (o + 1) * rows]) + wide(got[o * rows : (o + 1) * rows])
-                for o in range(chips)
-            ],
-            chips,
-        ).astype(low_type)
+        parts = []
+        for o in range(chips):
+            cut = slice(o * rows, (o + 1) * rows)
+            part = wide(dkv_own[cut]) + wide(got[cut])
+            parts.append(part if o == 0 else part.astype(low_type))
+        own_grads.append(parts[0])
+        far_grads.append(parts[1:])
         dxs.append(dx)
         das.append(da)
         dqs.append(dq)
-        dkvs.append(dkv)
         stats.append(stat)
 
-    def both_cores(parts):
-        return parts + [to_ctx(part, 1) for part in parts]
-
+    dkvs = [
+        sum_to_chips([own_grads[m]] + far_grads[m]).astype(low_type) for m in range(micros)
+    ]
+
+    def other_core(parts):
+        return [to_ctx(part, 1) for part in parts]
+
+    da_others, dq_others = other_core(das), other_core(dqs)
+    expert_term = outer_blocks(
+        after(expert_inverse, dqs[-1], dkvs[0], arrived[0]),
+        lambda k: (k * row_groups * ff_groups, ff_groups),
+        [xs, xs, dys],
+        [dgs, dus, zs],
+        expert_blocks,
+    )
+    parts_back = query_back(after(w_in, expert_term), dqs)
+    expert_sum = lax.psum_scatter(
+        after(expert_term, dkvs[-1]), "ctx", scatter_dimension=0, tiled=True
+    )
+    here = after(me, arrived[-1], parts_back)
     made = slot_blocks(
         chips,
         shard_count,
         slots,
         dense_order,
-        me,
+        here,
         [h1, h1_other],
-        both_cores(das),
-        both_cores(dqs),
-        both_cores(dkvs),
-        both_cores(obs),
-    )
-    dense_sum = sum_slots(made, chips, shard_count, slots)
-    input_grad, gain_stat = input_back(tokens, norm_gains, w_in, dxs, dqs, dkvs)
+        das + da_others,
+        dqs + dq_others,
+        dkvs + other_core(dkvs),
+        obs + ob_others,
+    )
+    sums, got = sum_slots(made, chips, shard_count, slots)
+    dense_sum = sum_to_chips(sums)
+    input_grad, gain_stat = input_back(
+        after(tokens, *got[:2]), norm_gains, w_in, dxs, parts_back, dkvs
+    )
     experts_up = stats[0].shape[0] - 8
     stat_rows = jnp.concatenate([sum(stats)[: experts_up + 1], gain_stat[:7]], axis=0)
     stat_rows = sum_all(stat_rows)
@@ -995,14 +1059,14 @@
     for m in range(micros):
         total = x2s[m]
         for j in range(shard_count):
-            total = total + wide(to_partner(outs[m][j], j))
+            total = total + wide(arrived[m][j])
         outputs.append(total)
 
     expert_grad, expert_new, expert_moment_new, expert_second_new = rotate(
-        expert_weight[0], expert_sum, expert_moment[0], expert_second[0], expert_left[0], expert_right[0]
+        expert_weight[0], after(expert_sum, *sums), expert_moment[0], expert_second[0], expert_left[0], expert_right[0]
     )
     dense_grad, dense_new, dense_moment_new, dense_second_new = rotate(
-        dense_weight, dense_sum, dense_moment, dense_second, dense_left, dense_right
+        dense_weight, after(dense_sum, expert_new), dense_moment, dense_second, dense_left, dense_right
     )
     gains_new, gains_moment_new, gains_second_new = adam(
         norm_gains, gains_grad, gains_moment, gains_second, gain_rate

time: 596 us -> 660 us (1.11)
  Pallas kernels: 160 us -> 329 us
  waiting for transfers between devices: 260 us -> 170 us
  local copies, waits for them, and re-layouts: 51.9 us -> 18.9 us
  starting transfers between devices: 85.7 us -> 96 us
  other arithmetic: 16.4 us -> 24.5 us
    pallas_call x1, Pallas kernels: 10.8 us -> 147 us  [project(): call(functools.partial(project_kernel, pieces, chips, members, slots, (in...]
    ppermute x18, waiting for transfers between devices: 142 us -> 84.1 us  [to_chip(): lax.ppermute(array, 'ctx', [(i, (i + 2 * offset) % count) for i in range(...]
    unnamed x240 -> x144, local copies, waits for them, and re-layouts: 40.2 us -> 9.43 us
    ppermute x39 -> x38, waiting for transfers between devices: 109 us -> 78.7 us  [to_partner(): return lax.ppermute(array, 'shard', [(i, i ^ offset) for i in range(count)])]
    pallas_call x2, Pallas kernels: 13 us -> 21.3 us  [rotate(): pl.pallas_call(rotate_kernel, grid=(count,), out_shape=(shaped(weight.sha...]
    ppermute x18, starting transfers between devices: 33.4 us -> 41.2 us  [to_chip(): lax.ppermute(array, 'ctx', [(i, (i + 2 * offset) % count) for i in range(...]
    ppermute x39 -> x38, starting transfers between devices: 46.3 us -> 45.7 us  [to_partner(): return lax.ppermute(array, 'shard', [(i, i ^ offset) for i in range(count)])]
  transfers between devices with their start and end apart: 91 -> 89, of which waited for: 38 -> 26; matrix products, arithmetic and copies ran while one was open for 4% -> 5% of each run, Pallas kernels for 19% -> 47%
where the time goes in v3:
time: 660 us; the launch traced here: 655 us
  Pallas kernels  329 us (50%)
  waiting for transfers between devices  170 us (26%)
  starting transfers between devices  96 us (15%)
  other arithmetic  24.5 us (4%)
  local copies, waits for them, and re-layouts  18.9 us (3%)
  between operations  15.4 us (2%)
    pallas_call x1, Pallas kernels, project(): call(functools.partial(project_kernel, pieces, chips, members, slots, (in...  147 us
    ppermute x18, waiting for transfers between devices, to_chip(): lax.ppermute(array, 'ctx', [(i, (i + 2 * offset) % count) for i in range(...  84.1 us
    ppermute x38, waiting for transfers between devices, to_partner(): return lax.ppermute(array, 'shard', [(i, i ^ offset) for i in range(count)])  78.7 us
    ppermute x38, starting transfers between devices, to_partner(): return lax.ppermute(array, 'shard', [(i, i ^ offset) for i in range(count)])  45.7 us
    ppermute x18, starting transfers between devices, to_chip(): lax.ppermute(array, 'ctx', [(i, (i + 2 * offset) % count) for i in range(...  41.2 us
    pallas_call x2, Pallas kernels, run_expert(): call(functools.partial(expert_kernel, sources, micro), tuple([shaped((row...  40.7 us
    pallas_call x2, Pallas kernels, attend_back(): call(functools.partial(attend_back_kernel, len(kv_parts)), (shaped((rows,...  29.9 us
    pallas_call x2, Pallas kernels, attend(): call(functools.partial(attend_kernel, len(kv_parts)), (shaped((rows, widt...  25.6 us
  transfers between devices with their start and end apart: 89, of which 26 were waited for; matrix products, arithmetic and copies ran while one was open for 5% of the time, Pallas kernels for 47%

profile of v3, /device:TPU:0, one launch (start us, length us, event | category | flops | bytes accessed | tf_op | source)
XLA Modules:
  0.0 654.5 jit_solution(14830627026670222467)
XLA Ops:
  24.8 14.8 %collective-permute-done.8 = bf16[4,192,256]{2,1,0:T(8,128)(2,1)S(1)} collective-permute-done((bf16[4,192,256]{2,1,0:T(8,128)(2,1)S(1)}, bf16[4,192,256]{2,1,0:T(8,128)(2,1)S(1)}, u32[]{:S(2)}, u32[]{:S(2)}) %collective-permute-start.8) | collective-permute-done | bytes 393248 | tf_op jit(solution)/shard_map/ppermute | solution.py:806
  51.3 21.5 %collective-permute-done.11.refs_10_ = bf16[12,192,256]{2,1,0:T(8,128)(2,1)S(1)} collective-permute-done((bf16[12,192,256]{2,1,0:T(8,128)(2,1)}, bf16[12,192,256]{2,1,0:T(8,128)(2,1)S(1)}, u32[]{:S(2)}, u32[]{:S(2)}) %collective-permute-start.11) | collective-permute-done | bytes 1179680 | tf_op jit(solution)/shard_map/ppermute | solution.py:796
  78.8 7.9 %collective-permute-done.15.refs_14_ = bf16[12,96,256]{2,1,0:T(8,128)(2,1)S(1)} collective-permute-done((bf16[12,96,256]{2,1,0:T(8,128)(2,1)S(1)}, bf16[12,96,256]{2,1,0:T(8,128)(2,1)S(1)}, u32[]{:S(2)}, u32[]{:S(2)}) %collective-permute-start.15) | collective-permute-done | bytes 589856 | tf_op jit(solution)/shard_map/ppermute | solution.py:796
  92.6 147.0 %shard_map.349 = (bf16[256,1536]{1,0:T(8,128)(2,1)}, bf16[2,128,1536]{2,1,0:T(8,128)(2,1)}, bf16[2,128,1024]{2,1,0:T(8,128)(2,1)}, bf16[1536,2560]{1,0:T(8,128)(2,1)}, bf16[1536,1536]{1,0:T(8,128)(2,1)}) custom-call(s32[128]{0:T(128)} %order_ref.3, s32[2]{0:T(128)} %pad_add_fusion.me_ref, f32[2,128,1536]{2,1,0:T(8,128)} %x_ref.2, f32[2,1536]{1,0:T(2,128)} %gain_ref.11, ...), custom_call_target="tpu_custom_call" | custom-call | flops 2013265920 | bytes 15728640 | tf_op jit(solution)/shard_map/pallas_call | solution.py:183
  240.8 9.1 %collective-permute-start.19 = (bf16[128,1024]{1,0:T(8,128)(2,1)S(1)}, bf16[128,1024]{1,0:T(8,128)(2,1)S(1)}, u32[]{:S(2)}, u32[]{:S(2)}) collective-permute-start(bf16[128,1024]{1,0:T(8,128)(2,1)S(1)} %get-tuple-element.247.refs_0_), channel_id=1, source_target_pairs={{0,8},{4,12},{8,16},{12,20},{16,24},{20,28},{24,0},{28,4},{1,9},{5... | collective-permute-start | bytes 786440 | tf_op jit(solution)/shard_map/ppermute | solution.py:806
  259.8 11.0 %collective-permute-done.20.refs_2_ = bf16[128,1024]{1,0:T(8,128)(2,1)} collective-permute-done((bf16[128,1024]{1,0:T(8,128)(2,1)S(1)}, bf16[128,1024]{1,0:T(8,128)(2,1)}, u32[]{:S(2)}, u32[]{:S(2)}) %collective-permute-start.20) | collective-permute-done | bytes 262176 | tf_op jit(solution)/shard_map/ppermute | solution.py:806
  288.9 12.8 %shard_map.350 = (bf16[128,1536]{1,0:T(8,128)(2,1)}, f32[384,128]{1,0:T(8,128)}, f32[128,1536]{1,0:T(8,128)}, bf16[128,1536]{1,0:T(8,128)(2,1)}) custom-call(bf16[128,1536]{1,0:T(8,128)(2,1)} %get-tuple-element.244.q_ref, s32[128,1]{1,0:T(8,128)} %constant_dynamic-slice_fusion.rpos_ref, s32[1,1024]{1,0:T(1,128)} %bitcast.60, ...), custom_call_target="tpu_custom_call" | custom-call | flops 3221225472 | bytes 8388608 | tf_op jit(solution)/shard_map/pallas_call | solution.py:255
  302.5 9.7 %collective-permute-done.37.refs_6_ = bf16[256,1664]{1,0:T(8,128)(2,1)} collective-permute-done((bf16[256,1664]{1,0:T(8,128)(2,1)}, bf16[256,1664]{1,0:T(8,128)(2,1)}, u32[]{:S(2)}, u32[]{:S(2)}) %collective-permute-start.37) | collective-permute-done | bytes 852000 | tf_op jit(solution)/shard_map/ppermute | solution.py:796
  317.7 12.7 %shard_map.351 = (bf16[128,1536]{1,0:T(8,128)(2,1)}, f32[384,128]{1,0:T(8,128)}, f32[128,1536]{1,0:T(8,128)}, bf16[128,1536]{1,0:T(8,128)(2,1)}) custom-call(bf16[128,1536]{1,0:T(8,128)(2,1)} %get-tuple-element.127.q_ref, s32[128,1]{1,0:T(8,128)} %constant_dynamic-slice_fusion.rpos_ref, s32[1,1024]{1,0:T(1,128)} %bitcast.61, ...), custom_call_target="tpu_custom_call" | custom-call | flops 3221225472 | bytes 8388608 | tf_op jit(solution)/shard_map/pallas_call | solution.py:255
  337.8 20.7 %shard_map.352 = (bf16[128,1664]{1,0:T(8,128)(2,1)}, bf16[128,1664]{1,0:T(8,128)(2,1)}, bf16[128,1664]{1,0:T(8,128)(2,1)}, bf16[128,1664]{1,0:T(8,128)(2,1)}, bf...) custom-call(s32[96]{0:T(128)} %select_reduce_fusion.order_ref, ...), custom_call_target="tpu_custom_call" | custom-call | flops 9663676416 | bytes 20971520 | tf_op jit(solution)/shard_map/pallas_call | solution.py:362
  362.8 20.0 %shard_map.353 = (bf16[128,1664]{1,0:T(8,128)(2,1)}, bf16[128,1664]{1,0:T(8,128)(2,1)}, bf16[128,1664]{1,0:T(8,128)(2,1)}, bf16[128,1664]{1,0:T(8,128)(2,1)}, bf...) custom-call(s32[96]{0:T(128)} %select_reduce_fusion.order_ref, ...), custom_call_target="tpu_custom_call" | custom-call | flops 9663676416 | bytes 20971520 | tf_op jit(solution)/shard_map/pallas_call | solution.py:362
  393.3 15.0 %shard_map.355 = (bf16[128,1536]{1,0:T(8,128)(2,1)}, bf16[512,1024]{1,0:T(8,128)(2,1)}, bf16[512,1024]{1,0:T(8,128)(2,1)}) custom-call(bf16[128,1536]{1,0:T(8,128)(2,1)} %get-tuple-element.244.q_ref, s32[128,1]{1,0:T(8,128)} %constant_dynamic-slice_fusion.rpos_ref, s32[1,1024]{1,0:T(1,128)} %bitcast.62, ...), custom_call_target="tpu_custom_call" | custom-call | flops 8053063680 | bytes 8388608 | tf_op jit(solution)/shard_map/pallas_call | solution.py:644
  409.5 6.0 shard_map.356
  415.5 14.9 %shard_map.357 = (bf16[128,1536]{1,0:T(8,128)(2,1)}, bf16[512,1024]{1,0:T(8,128)(2,1)}, bf16[512,1024]{1,0:T(8,128)(2,1)}) custom-call(bf16[128,1536]{1,0:T(8,128)(2,1)} %get-tuple-element.127.q_ref, s32[128,1]{1,0:T(8,128)} %constant_dynamic-slice_fusion.rpos_ref, s32[1,1024]{1,0:T(1,128)} %bitcast.63, ...), custom_call_target="tpu_custom_call" | custom-call | flops 8053063680 | bytes 8388608 | tf_op jit(solution)/shard_map/pallas_call | solution.py:644
  447.4 15.6 %collective-permute-done.59 = bf16[128,1024]{1,0:T(8,128)(2,1)S(1)} collective-permute-done((bf16[128,1024]{1,0:T(8,128)(2,1)S(1)}, bf16[128,1024]{1,0:T(8,128)(2,1)S(1)}, u32[]{:S(2)}, u32[]{:S(2)}) %collective-permute-start.59) | collective-permute-done | bytes 262176 | tf_op jit(solution)/shard_map/ppermute | solution.py:806
  466.4 18.7 %shard_map.358 = bf16[96,192,256]{2,1,0:T(8,128)(2,1)} custom-call(s32[96]{0:T(128)} %select_reduce_fusion.order_ref, bf16[512,1536]{1,0:T(8,128)(2,1)} %get-tuple-element.182.refs_0_.refs_2_, bf16[512,1536]{1,0:T(8,128)(2,1)} %get-tuple-element.183.refs_1_.refs_3_, bf16[512,1536]{1,0:T(8,128)(2,1)} %get-tuple-element.182.refs_0_.refs_2_, ...), custom_call_target="tpu_custom_call" | custom-call | flops 9663676416 | bytes 25165824 | tf_op jit(solution)/shard_map/pallas_call | solution.py:432
  491.9 8.6 %collective-permute-done.51 = bf16[128,1536]{1,0:T(8,128)(2,1)S(1)} collective-permute-done((bf16[128,1536]{1,0:T(8,128)(2,1)}, bf16[128,1536]{1,0:T(8,128)(2,1)S(1)}, u32[]{:S(2)}, u32[]{:S(2)}) %collective-permute-start.51) | collective-permute-done | bytes 393248 | tf_op jit(solution)/shard_map/ppermute | solution.py:796
  501.1 7.5 %collective-permute-done.53 = bf16[128,1536]{1,0:T(8,128)(2,1)S(1)} collective-permute-done((bf16[128,1536]{1,0:T(8,128)(2,1)S(1)}, bf16[128,1536]{1,0:T(8,128)(2,1)S(1)}, u32[]{:S(2)}, u32[]{:S(2)}) %collective-permute-start.53) | collective-permute-done | bytes 393248 | tf_op jit(solution)/shard_map/ppermute | solution.py:796
  511.0 6.1 shard_map.359
  517.9 21.0 %shard_map.360 = (bf16[8,192,256]{2,1,0:T(8,128)(2,1)}, bf16[8,192,256]{2,1,0:T(8,128)(2,1)}, bf16[8,192,256]{2,1,0:T(8,128)(2,1)}, bf16[8,192,256]{2,1,0:T(8,12...) custom-call(s32[128]{0:T(128)} %order_ref.3, ...), custom_call_target="tpu_custom_call" | custom-call | flops 3221225472 | bytes 16777216 | tf_op jit(solution)/shard_map/pallas_call | solution.py:511
  545.8 13.8 %collective-permute-done.71 = bf16[8,192,256]{2,1,0:T(8,128)(2,1)S(1)} collective-permute-done((bf16[8,192,256]{2,1,0:T(8,128)(2,1)}, bf16[8,192,256]{2,1,0:T(8,128)(2,1)S(1)}, u32[]{:S(2)}, u32[]{:S(2)}) %collective-permute-start.71) | collective-permute-done | bytes 786464 | tf_op jit(solution)/shard_map/ppermute | solution.py:796
  561.3 7.2 %shard_map.361 = (f32[2,128,1536]{2,1,0:T(8,128)}, f32[8,1536]{1,0:T(8,128)}) custom-call(f32[2,128,1536]{2,1,0:T(8,128)} %x_ref.2, f32[2,1536]{1,0:T(2,128)} %gain_ref.11, bf16[1536,2560]{1,0:T(8,128)(2,1)} %get-tuple-element.190.w_ref, f32[128,1536]{1,0:T(8,128)} %get-tuple-element.201.refs_0_, f32[128,1536]{1,0:T(8,128)} %get-tuple-element.202.refs_1_, ...), custom_call_target="tpu_custom_call" | custom-call | flops 805306368 | bytes 14680064 | tf_op jit(solution)/shard_map/pallas_call | solution.py:727
  603.5 21.3 %collective-permute-done.78 = bf16[4,192,256]{2,1,0:T(8,128)(2,1)S(1)} collective-permute-done((bf16[4,192,256]{2,1,0:T(8,128)(2,1)S(1)}, bf16[4,192,256]{2,1,0:T(8,128)(2,1)S(1)}, u32[]{:S(2)}, u32[]{:S(2)}) %collective-permute-start.78) | collective-permute-done | bytes 393248 | tf_op jit(solution)/shard_map/ppermute | solution.py:806
  626.1 15.3 %shard_map.362 = (f32[12,192,256]{2,1,0:T(8,128)}, f32[12,192,256]{2,1,0:T(8,128)}, f32[12,192,256]{2,1,0:T(8,128)}, f32[12,192,256]{2,1,0:T(8,128)}) custom-call(f32[12,192,256]{2,1,0:T(8,128)} %bitcast.48, bf16[12,192,256]{2,1,0:T(8,128)(2,1)} %reduce-scatter.2.cloned.1.call-done.g_ref, f32[12,192,256]{2,1,0:T(8,128)} %bitcast.50, ...), custom_call_target="tpu_custom_call" | custom-call | flops 1056964608 | bytes 25165824 | tf_op jit(solution)/shard_map/pallas_call | solution.py:767
  (369 shorter events, 180.8 us)
Async XLA Ops:
  7.2 330.6 %all-gather.2.cloned.1.call-start = ((), (), s32[]{:S(2)}) async-start(), calls=%async_computation.1 | async-start | bytes 10616832 | tf_op jit(solution)/shard_map/all_gather | solution.py:938
  11.5 28.1 %collective-permute-start.8 = (bf16[4,192,256]{2,1,0:T(8,128)(2,1)S(1)}, bf16[4,192,256]{2,1,0:T(8,128)(2,1)S(1)}, u32[]{:S(2)}, u32[]{:S(2)}) collective-permute-start(bf16[4,192,256]{2,1,0:T(8,128)(2,1)S(1)} %convert_element_type.223.refs_0_), channel_id=1, source_target_pairs={{0,16},{4,20},{8,24},{12,28},{16,0},{20,4},{24,8},{28,12},{1,17},{... | collective-permute-start | bytes 1179656 | tf_op jit(solution)/shard_map/ppermute | solution.py:806
  14.1 25.5 %collective-permute-start.1 = (bf16[4,192,256]{2,1,0:T(8,128)(2,1)S(1)}, bf16[4,192,256]{2,1,0:T(8,128)(2,1)S(1)}, u32[]{:S(2)}, u32[]{:S(2)}) collective-permute-start(bf16[4,192,256]{2,1,0:T(8,128)(2,1)S(1)} %convert_element_type.223.refs_0_), channel_id=1, source_target_pairs={{0,1},{1,0},{2,3},{3,2},{4,5},{5,4},{6,7},{7,6},{8,9},{9,8},{10,11... | collective-permute-start | bytes 1179656 | tf_op jit(solution)/shard_map/ppermute | solution.py:796
  45.3 580.8 %reduce-scatter.2.cloned.1.call-start = ((), (), s32[]{:S(2)}) async-start(), calls=%async_computation.2 | async-start | bytes 10616832 | tf_op jit(solution)/shard_map/reduce_scatter | solution.py:1031
  46.5 26.4 %collective-permute-start.11 = (bf16[12,192,256]{2,1,0:T(8,128)(2,1)}, bf16[12,192,256]{2,1,0:T(8,128)(2,1)S(1)}, u32[]{:S(2)}, u32[]{:S(2)}) collective-permute-start(bf16[12,192,256]{2,1,0:T(8,128)(2,1)} %pad_maximum_fusion.1.refs_8_), channel_id=1, source_target_pairs={{0,1},{1,0},{2,3},{3,2},{4,5},{5,4},{6,7},{7,6},{8,9},{9,8},{10,11... | collective-permute-start | bytes 3538952 | tf_op jit(solution)/shard_map/ppermute | solution.py:796
  48.0 27.2 %collective-permute-start.13 = (bf16[12,192,256]{2,1,0:T(8,128)(2,1)}, bf16[12,192,256]{2,1,0:T(8,128)(2,1)}, u32[]{:S(2)}, u32[]{:S(2)}) collective-permute-start(bf16[12,192,256]{2,1,0:T(8,128)(2,1)} %pad_maximum_fusion.1.refs_8_), channel_id=1, source_target_pairs={{0,2},{1,3},{2,0},{3,1},{4,6},{5,7},{6,4},{7,5},{8,10},{9,11},{10,... | collective-permute-start | bytes 3538952 | tf_op jit(solution)/shard_map/ppermute | solution.py:796
  51.3 38.9 %collective-permute-start.10 = (bf16[12,192,256]{2,1,0:T(8,128)(2,1)}, bf16[12,192,256]{2,1,0:T(8,128)(2,1)S(1)}, u32[]{:S(2)}, u32[]{:S(2)}) collective-permute-start(bf16[12,192,256]{2,1,0:T(8,128)(2,1)} %pad_maximum_fusion.1.refs_8_), channel_id=1, source_target_pairs={{0,4},{4,0},{8,12},{12,8},{16,20},{20,16},{24,28},{28,24},{1,5},{5... | collective-permute-start | bytes 3538952 | tf_op jit(solution)/shard_map/ppermute | solution.py:801
  270.9 31.5 %collective-permute-start.36 = (bf16[256,1664]{1,0:T(8,128)(2,1)}, bf16[256,1664]{1,0:T(8,128)(2,1)}, u32[]{:S(2)}, u32[]{:S(2)}) collective-permute-start(bf16[256,1664]{1,0:T(8,128)(2,1)} %bitcast.53), channel_id=1, source_target_pairs={{0,1},{1,0},{2,3},{3,2},{4,5},{5,4},{6,7},{7,6},{8,9},{9,8},{10,11... | collective-permute-start | bytes 2555912 | tf_op jit(solution)/shard_map/ppermute | solution.py:796
  272.5 39.7 %collective-permute-start.37 = (bf16[256,1664]{1,0:T(8,128)(2,1)}, bf16[256,1664]{1,0:T(8,128)(2,1)}, u32[]{:S(2)}, u32[]{:S(2)}) collective-permute-start(bf16[256,1664]{1,0:T(8,128)(2,1)} %bitcast.54), channel_id=1, source_target_pairs={{0,2},{1,3},{2,0},{3,1},{4,6},{5,7},{6,4},{7,5},{8,10},{9,11},{10,... | collective-permute-start | bytes 2555912 | tf_op jit(solution)/shard_map/ppermute | solution.py:796
  274.3 39.0 %collective-permute-start.38 = (bf16[256,1664]{1,0:T(8,128)(2,1)}, bf16[256,1664]{1,0:T(8,128)(2,1)}, u32[]{:S(2)}, u32[]{:S(2)}) collective-permute-start(bf16[256,1664]{1,0:T(8,128)(2,1)} %bitcast.55), channel_id=1, source_target_pairs={{0,3},{1,2},{2,1},{3,0},{4,7},{5,6},{6,5},{7,4},{8,11},{9,10},{10,... | collective-permute-start | bytes 2555912 | tf_op jit(solution)/shard_map/ppermute | solution.py:796
  334.2 27.4 %collective-permute-start.42 = (bf16[128,1536]{1,0:T(8,128)(2,1)S(1)}, bf16[128,1536]{1,0:T(8,128)(2,1)S(1)}, u32[]{:S(2)}, u32[]{:S(2)}) collective-permute-start(bf16[128,1536]{1,0:T(8,128)(2,1)S(1)} %copy-done.34), channel_id=1, source_target_pairs={{0,1},{1,0},{2,3},{3,2},{4,5},{5,4},{6,7},{7,6},{8,9},{9,8},{10,11... | collective-permute-start | bytes 1179656 | tf_op jit(solution)/shard_map/ppermute | solution.py:796
  336.2 25.9 %collective-permute-start.43 = (bf16[128,1536]{1,0:T(8,128)(2,1)S(1)}, bf16[128,1536]{1,0:T(8,128)(2,1)S(1)}, u32[]{:S(2)}, u32[]{:S(2)}) collective-permute-start(bf16[128,1536]{1,0:T(8,128)(2,1)S(1)} %copy-done.34), channel_id=1, source_target_pairs={{0,2},{1,3},{2,0},{3,1},{4,6},{5,7},{6,4},{7,5},{8,10},{9,11},{10,... | collective-permute-start | bytes 1179656 | tf_op jit(solution)/shard_map/ppermute | solution.py:796
  358.5 27.4 %collective-permute-start.54 = (bf16[128,1664]{1,0:T(8,128)(2,1)}, bf16[128,1664]{1,0:T(8,128)(2,1)S(1)}, u32[]{:S(2)}, u32[]{:S(2)}) collective-permute-start(bf16[128,1664]{1,0:T(8,128)(2,1)} %get-tuple-element.171), channel_id=1, source_target_pairs={{0,1},{1,0},{2,3},{3,2},{4,5},{5,4},{6,7},{7,6},{8,9},{9,8},{10,11... | collective-permute-start | bytes 1277960 | tf_op jit(solution)/shard_map/ppermute | solution.py:796
  360.5 25.9 %collective-permute-start.55 = (bf16[128,1664]{1,0:T(8,128)(2,1)}, bf16[128,1664]{1,0:T(8,128)(2,1)S(1)}, u32[]{:S(2)}, u32[]{:S(2)}) collective-permute-start(bf16[128,1664]{1,0:T(8,128)(2,1)} %get-tuple-element.172), channel_id=1, source_target_pairs={{0,2},{1,3},{2,0},{3,1},{4,6},{5,7},{6,4},{7,5},{8,10},{9,11},{10,... | collective-permute-start | bytes 1277960 | tf_op jit(solution)/shard_map/ppermute | solution.py:796
  382.8 25.6 %collective-permute-start.45 = (bf16[128,1664]{1,0:T(8,128)(2,1)}, bf16[128,1664]{1,0:T(8,128)(2,1)S(1)}, u32[]{:S(2)}, u32[]{:S(2)}) collective-permute-start(bf16[128,1664]{1,0:T(8,128)(2,1)} %get-tuple-element.146), channel_id=1, source_target_pairs={{0,1},{1,0},{2,3},{3,2},{4,5},{5,4},{6,7},{7,6},{8,9},{9,8},{10,11... | collective-permute-start | bytes 1277960 | tf_op jit(solution)/shard_map/ppermute | solution.py:796
  437.6 25.3 %collective-permute-start.59 = (bf16[128,1024]{1,0:T(8,128)(2,1)S(1)}, bf16[128,1024]{1,0:T(8,128)(2,1)S(1)}, u32[]{:S(2)}, u32[]{:S(2)}) collective-permute-start(bf16[128,1024]{1,0:T(8,128)(2,1)S(1)} %get-tuple-element.239), channel_id=1, source_target_pairs={{0,16},{4,20},{8,24},{12,28},{16,0},{20,4},{24,8},{28,12},{1,17},{... | collective-permute-start | bytes 786440 | tf_op jit(solution)/shard_map/ppermute | solution.py:806
  440.8 25.6 %collective-permute-start.49 = (bf16[128,1536]{1,0:T(8,128)(2,1)S(1)}, bf16[128,1536]{1,0:T(8,128)(2,1)}, u32[]{:S(2)}, u32[]{:S(2)}) collective-permute-start(bf16[128,1536]{1,0:T(8,128)(2,1)S(1)} %copy-done.57), channel_id=1, source_target_pairs={{0,2},{1,3},{2,0},{3,1},{4,6},{5,7},{6,4},{7,5},{8,10},{9,11},{10,... | collective-permute-start | bytes 1179656 | tf_op jit(solution)/shard_map/ppermute | solution.py:796
  487.9 29.2 %collective-permute-start.63 = (bf16[128,1536]{1,0:T(8,128)(2,1)S(1)}, bf16[128,1536]{1,0:T(8,128)(2,1)}, u32[]{:S(2)}, u32[]{:S(2)}) collective-permute-start(bf16[128,1536]{1,0:T(8,128)(2,1)S(1)} %copy-done.32), channel_id=1, source_target_pairs={{0,4},{4,0},{8,12},{12,8},{16,20},{20,16},{24,28},{28,24},{1,5},{5... | collective-permute-start | bytes 1179656 | tf_op jit(solution)/shard_map/ppermute | solution.py:801
  491.9 25.3 %collective-permute-start.62 = (bf16[128,1536]{1,0:T(8,128)(2,1)}, bf16[128,1536]{1,0:T(8,128)(2,1)}, u32[]{:S(2)}, u32[]{:S(2)}) collective-permute-start(bf16[128,1536]{1,0:T(8,128)(2,1)} %get-tuple-element.195.refs_3_), channel_id=1, source_target_pairs={{0,4},{4,0},{8,12},{12,8},{16,20},{20,16},{24,28},{28,24},{1,5},{5... | collective-permute-start | bytes 1179656 | tf_op jit(solution)/shard_map/ppermute | solution.py:801
  544.5 31.8 %collective-permute-start.76 = (bf16[8,192,256]{2,1,0:T(8,128)(2,1)}, bf16[8,192,256]{2,1,0:T(8,128)(2,1)S(1)}, u32[]{:S(2)}, u32[]{:S(2)}) collective-permute-start(bf16[8,192,256]{2,1,0:T(8,128)(2,1)} %get-tuple-element.207), channel_id=1, source_target_pairs={{0,2},{1,3},{2,0},{3,1},{4,6},{5,7},{6,4},{7,5},{8,10},{9,11},{10,... | collective-permute-start | bytes 2359304 | tf_op jit(solution)/shard_map/ppermute | solution.py:796
  545.5 38.0 %collective-permute-start.79 = (bf16[8,192,256]{2,1,0:T(8,128)(2,1)}, bf16[8,192,256]{2,1,0:T(8,128)(2,1)}, u32[]{:S(2)}, u32[]{:S(2)}) collective-permute-start(bf16[8,192,256]{2,1,0:T(8,128)(2,1)} %get-tuple-element.209), channel_id=1, source_target_pairs={{0,1},{1,0},{2,3},{3,2},{4,5},{5,4},{6,7},{7,6},{8,9},{9,8},{10,11... | collective-permute-start | bytes 2359304 | tf_op jit(solution)/shard_map/ppermute | solution.py:796
  569.6 33.9 %collective-permute-start.73 = (bf16[4,192,256]{2,1,0:T(8,128)(2,1)S(1)}, bf16[4,192,256]{2,1,0:T(8,128)(2,1)S(1)}, u32[]{:S(2)}, u32[]{:S(2)}) collective-permute-start(bf16[4,192,256]{2,1,0:T(8,128)(2,1)S(1)} %add_convert_fusion.6), channel_id=1, source_target_pairs={{0,1},{1,0},{2,3},{3,2},{4,5},{5,4},{6,7},{7,6},{8,9},{9,8},{10,11... | collective-permute-start | bytes 1179656 | tf_op jit(solution)/shard_map/ppermute | solution.py:796
  594.4 30.5 %collective-permute-start.78 = (bf16[4,192,256]{2,1,0:T(8,128)(2,1)S(1)}, bf16[4,192,256]{2,1,0:T(8,128)(2,1)S(1)}, u32[]{:S(2)}, u32[]{:S(2)}) collective-permute-start(bf16[4,192,256]{2,1,0:T(8,128)(2,1)S(1)} %add_convert_fusion.2), channel_id=1, source_target_pairs={{0,16},{4,20},{8,24},{12,28},{16,0},{20,4},{24,8},{28,12},{1,17},{... | collective-permute-start | bytes 1179656 | tf_op jit(solution)/shard_map/ppermute | solution.py:806
  599.7 25.1 %collective-permute-start.81 = (bf16[4,192,256]{2,1,0:T(8,128)(2,1)S(1)}, bf16[4,192,256]{2,1,0:T(8,128)(2,1)S(1)}, u32[]{:S(2)}, u32[]{:S(2)}) collective-permute-start(bf16[4,192,256]{2,1,0:T(8,128)(2,1)S(1)} %add_convert_fusion), channel_id=1, source_target_pairs={{0,8},{4,12},{8,16},{12,20},{16,24},{20,28},{24,0},{28,4},{1,9},{5... | collective-permute-start | bytes 1179656 | tf_op jit(solution)/shard_map/ppermute | solution.py:806
  (137 other events, 1823.0 us)
Sparse Core Ops, SparseCore 0:
  45.4 96.5 all-gather.1
  486.9 102.5 reduce-scatter.1

commit v4 on v3

--- a/solution.py
+++ b/solution.py
@@ -24,7 +24,6 @@
 masked_score = -1e30
 low_type = jnp.bfloat16
 MIB = 1 << 20
-VMEM_LIMIT = 60 * MIB
 
 NN = (((1,), (0,)), ((), ()))
 NT = (((1,), (1,)), ((), ()))
@@ -39,14 +38,14 @@
     return lax.dot_general(left_side, right_side, dims, preferred_element_type=jnp.float32)
 
 
-def call(kernel, out_shapes, in_specs, out_specs, scratch, flops, moved):
+def call(kernel, out_shapes, in_specs, out_specs, scratch, flops, moved, limit):
     return pl.pallas_call(
         kernel,
         out_shape=out_shapes,
         in_specs=in_specs,
         out_specs=out_specs,
         scratch_shapes=scratch,
-        compiler_params=pltpu.CompilerParams(vmem_limit_bytes=VMEM_LIMIT),
+        compiler_params=pltpu.CompilerParams(vmem_limit_bytes=limit * MIB),
         cost_estimate=pl.CostEstimate(flops=flops, bytes_accessed=moved, transcendentals=0),
     )
 
@@ -118,13 +117,18 @@
 
 
 def project_kernel(
-    pieces, chips, members, slots, all_groups, order_ref, me_ref, x_ref, gain_ref, *refs
+    pieces, chips, members, slots, all_groups, micros, order_ref, me_ref, *refs
 ):
-    piece_refs = refs[: len(pieces)]
-    h_ref, q_ref, kv_ref, win_ref, wout_ref, held, sems, out_sems = refs[len(pieces) :]
+    x_refs = refs[:micros]
+    gain_ref = refs[micros]
+    piece_refs = refs[micros + 1 : micros + 1 + len(pieces)]
+    refs = refs[micros + 1 + len(pieces) :]
+    h_ref = refs[0]
+    kv_refs = refs[1 : 1 + micros]
+    win_ref, wout_ref, held, held_out, sems, out_sems = refs[1 + micros :]
     groups = held.shape[1] // BC
-    q_groups = q_ref.shape[-1] // BC
-    micros, rows = x_ref.shape[:2]
+    kv_groups = kv_refs[0].shape[-1] // BC
+    rows = x_refs[0].shape[0]
     ctx, shard = me_ref[0], me_ref[1]
     chip, core = lax.div(ctx, 2), lax.rem(ctx, 2)
 
@@ -147,60 +151,104 @@
             @pl.when(b >= groups)
             def _():
                 across = pl.ds(pl.multiple_of((b - groups) * BC, BC), BC)
-                pltpu.make_async_copy(ref.at[i], wout_ref.at[down, across], out_sems.at[0]).start()
+                pltpu.make_async_copy(ref.at[i], held_out.at[down, across], sems.at[groups]).start()
 
     for m in range(micros):
-        h_ref[pl.ds(m * rows, rows), :] = unit_rows(x_ref[m], gain_ref[0:1])[0].astype(low_type)
-
-    def make(b):
+        h_ref[m * rows : (m + 1) * rows, :] = unit_rows(x_refs[m][...], gain_ref[0:1])[0].astype(
+            low_type
+        )
+    q_groups = groups - kv_groups
+
+    @pl.loop(0, kv_groups)
+    def _(b):
+        across = pl.ds(pl.multiple_of((q_groups + b) * BC, BC), BC)
+        wait_bytes(held.at[:, across], sems.at[q_groups + b])
+        made = dot(h_ref[...], held[:, across]).astype(low_type)
+        for m in range(micros):
+            kv_refs[m][:, pl.ds(pl.multiple_of(b * BC, BC), BC)] = made[m * rows : (m + 1) * rows]
+
+    @pl.loop(0, q_groups)
+    def _(b):
         across = pl.ds(pl.multiple_of(b * BC, BC), BC)
         wait_bytes(held.at[:, across], sems.at[b])
-        pltpu.make_async_copy(held.at[:, across], win_ref.at[:, across], out_sems.at[1]).start()
-        return dot(h_ref[...], held[:, across]).astype(low_type)
-
-    @pl.loop(0, q_groups)
-    def _(b):
-        made = make(b)
-        for m in range(micros):
-            q_ref[m, :, pl.ds(pl.multiple_of(b * BC, BC), BC)] = made[m * rows : (m + 1) * rows]
-
-    @pl.loop(q_groups, groups)
-    def _(b):
-        made = make(b)
-        for m in range(micros):
-            kv_ref[m, :, pl.ds(pl.multiple_of((b - q_groups) * BC, BC), BC)] = made[
-                m * rows : (m + 1) * rows
-            ]
-
-    wait_bytes(wout_ref, out_sems.at[0])
-    wait_bytes(win_ref, out_sems.at[1])
-
-
-def project(pieces, arrays, chips, members, slots, order, me, x, gains):
-    micros, rows, width = x.shape
+
+    wait_bytes(held_out, sems.at[groups])
+    copies = [
+        pltpu.make_async_copy(held, win_ref, out_sems.at[0]),
+        pltpu.make_async_copy(held_out, wout_ref, out_sems.at[1]),
+    ]
+    for copy in copies:
+        copy.start()
+    for copy in copies:
+        copy.wait()
+
+
+def project(pieces, arrays, chips, members, slots, order, me, xs, gains):
+    micros = len(xs)
+    rows, width = xs[0].shape
     in_width = (HEADS + 2 * KVH) * HD
     out_width = HEADS * HD
-    return call(
+    kv_width = 2 * KVH * HD
+    made = call(
         functools.partial(
-            project_kernel, pieces, chips, members, slots, (in_width + out_width) // BC
+            project_kernel, pieces, chips, members, slots, (in_width + out_width) // BC, micros
         ),
-        (
-            shaped((micros * rows, width), low_type),
-            shaped((micros, rows, HEADS * HD), low_type),
-            shaped((micros, rows, 2 * KVH * HD), low_type),
-            shaped((width, in_width), low_type),
-            shaped((width, out_width), low_type),
+        tuple(
+            [shaped((micros * rows, width), low_type)]
+            + [shaped((rows, kv_width), low_type)] * micros
+            + [shaped((width, in_width), low_type), shaped((width, out_width), low_type)]
         ),
-        [in_smem, in_smem, in_vmem, in_vmem] + [in_any] * len(arrays),
-        (in_vmem, in_vmem, in_vmem, in_any, in_any),
+        [in_smem, in_smem] + [in_vmem] * (micros + 1) + [in_any] * len(arrays),
+        tuple([in_vmem] * (1 + micros) + [in_any, in_any]),
         [
             pltpu.VMEM((width, in_width), low_type),
-            pltpu.SemaphoreType.DMA((in_width // BC,)),
+            pltpu.VMEM((width, out_width), low_type),
+            pltpu.SemaphoreType.DMA((in_width // BC + 1,)),
             pltpu.SemaphoreType.DMA((2,)),
         ],
-        2 * micros * rows * width * in_width,
-        2 * width * in_width * 2,
-    )(order, me, x, gains, *arrays)
+        2 * micros * rows * width * kv_width,
+        4 * width * (in_width + out_width),
+        24,
+    )(order, me, *xs, gains, *arrays)
+    return made[0], made[1 : 1 + micros], made[1 + micros], made[2 + micros]
+
+
+def query_kernel(h_ref, w_ref, *refs):
+    q_refs = refs[:-2]
+    held, sems = refs[-2:]
+    groups = held.shape[1] // BC
+    rows = q_refs[0].shape[0]
+
+    def copy(b):
+        across = pl.ds(pl.multiple_of(b * BC, BC), BC)
+        return pltpu.make_async_copy(w_ref.at[:, across], held.at[:, across], sems.at[b])
+
+    @pl.loop(0, groups)
+    def _(b):
+        copy(b).start()
+
+    @pl.loop(0, groups)
+    def _(b):
+        copy(b).wait()
+        across = pl.ds(pl.multiple_of(b * BC, BC), BC)
+        made = dot(h_ref[...], held[:, across]).astype(low_type)
+        for m, ref in enumerate(q_refs):
+            ref[:, across] = made[m * rows : (m + 1) * rows]
+
+
+def make_queries(h, w, micros):
+    total, width = h.shape
+    q_width = HEADS * HD
+    return call(
+        query_kernel,
+        tuple([shaped((total // micros, q_width), low_type)] * micros),
+        [in_vmem, in_any],
+        tuple([in_vmem] * micros),
+        [pltpu.VMEM((width, q_width), low_type), pltpu.SemaphoreType.DMA((q_width // BC,))],
+        2 * total * width * q_width,
+        2 * width * q_width,
+        16,
+    )(h, w)
 
 
 def load_keys(parts, held, sem):
@@ -270,6 +318,7 @@
         ],
         16 * rows * length * width,
         8 * MIB,
+        32,
     )(q, rows_pos, key_pos, x, gains, w, *kv_parts)
 
 
@@ -286,9 +335,8 @@
     w_ref = refs[2 * sources]
     outs = refs[2 * sources + 1 :]
     back_refs = outs[:sources]
-    out_refs = outs[sources : 2 * sources]
-    z_ref, dg_ref, du_ref, dy_ref, xs_ref = outs[2 * sources : 2 * sources + 5]
-    cs, held, chance, load_sem, w_sems = outs[2 * sources + 5 :]
+    z_ref, dg_ref, du_ref, cs, xs_ref = outs[sources : sources + 5]
+    held, chance, load_sem, w_sems = outs[sources + 5 :]
     rows, width = h_parts[0].shape
     row_groups = width // BR
     col_groups = FF // BC
@@ -297,15 +345,15 @@
         pltpu.make_async_copy(
             c_parts[j].at[pl.ds(micro * rows, rows)], cs.at[pl.ds(j * rows, rows)], load_sem.at[1]
         ).start()
-    for k in (0, 1, 2):
+    for b in range(col_groups):
 
         @pl.loop(0, row_groups)
         def _(a):
-            for b in range(col_groups):
+            for k in range(3):
                 pltpu.make_async_copy(
                     w_ref.at[order_ref[(k * row_groups + a) * col_groups + b]],
                     held.at[k, pl.ds(pl.multiple_of(a * BR, 64), BR), pl.ds(b * BC, BC)],
-                    w_sems.at[k],
+                    w_sems.at[b],
                 ).start()
 
     wait_bytes(xs_ref, load_sem.at[0])
@@ -316,24 +364,22 @@
     mine = lane_ids(hits.shape) == me
     hit = jnp.sum(jnp.where(mine, hits, 0.0), axis=-1, keepdims=True)
     weight = jnp.sum(jnp.where(mine, probs, 0.0), axis=-1, keepdims=True) * hit
-    dy_ref[...] = (weight * cs[:, :width].astype(jnp.float32)).astype(low_type)
     chance[...] = jnp.zeros_like(chance)
-    for k in (0, 1, 2):
-        wait_bytes(held.at[k], w_sems.at[k])
 
     @pl.loop(0, col_groups)
     def _(b):
         cut = pl.ds(pl.multiple_of(b * BC, BC), BC)
+        wait_bytes(held.at[:, :, cut], w_sems.at[b])
         gate = dot(xs_ref[...], held[0, :, cut])
         up = dot(xs_ref[...], held[1, :, cut])
         down = dot(cs[:, :width], held[2, :, cut])
         sig = jax.nn.sigmoid(gate)
         act = gate * sig
         hidden = act * up
-        z_ref[:, cut] = hidden.astype(low_type)
         chance[...] += jnp.sum(down * hidden, axis=-1, keepdims=True)
+        z_ref[:, cut] = (hidden * weight).astype(low_type)
         down = down * weight
-        dg_ref[:, cut] = (down * up * sig * (1.0 + gate * (1.0 - sig))).astype(low_type)
+        dg_ref[:, cut] = (down * up * (sig + act * (1.0 - sig))).astype(low_type)
         du_ref[:, cut] = (down * act).astype(low_type)
 
     for n in range(width // BC):
@@ -348,11 +394,6 @@
     tail = jnp.where(lanes == 0, high_part, jnp.where(lanes == 1, low_part, jnp.zeros_like(low_part)))
     for j in range(sources):
         back_refs[j][:, width:] = tail[j * rows : (j + 1) * rows]
-    for n in range(width // BC):
-        cut = slice(n * BC, (n + 1) * BC)
-        made = dot(z_ref[...], held[2, cut, :], NT) * weight
-        for j in range(sources):
-            out_refs[j][:, cut] = made[j * rows : (j + 1) * rows].astype(low_type)
 
 
 def run_expert(micro, order, me, router, h_parts, c_parts, w):
@@ -363,26 +404,74 @@
         functools.partial(expert_kernel, sources, micro),
         tuple(
             [shaped((rows, width + LANES), low_type)] * sources
-            + [shaped((rows, width), low_type)] * sources
             + [shaped((total, FF), low_type)] * 3
-            + [shaped((total, width), low_type)] * 2
+            + [shaped((total, width + LANES), low_type), shaped((total, width), low_type)]
         ),
         [in_smem, in_smem, in_vmem] + [in_any] * (2 * sources + 1),
-        tuple([in_vmem] * (2 * sources + 5)),
+        tuple([in_vmem] * (sources + 5)),
         [
-            pltpu.VMEM((total, width + LANES), low_type),
             pltpu.VMEM((3, width, FF), low_type),
             pltpu.VMEM((total, 1), jnp.float32),
             pltpu.SemaphoreType.DMA((2,)),
-            pltpu.SemaphoreType.DMA((3,)),
+            pltpu.SemaphoreType.DMA((FF // BC,)),
         ],
-        12 * total * width * FF,
+        10 * total * width * FF,
         20 * MIB,
+        44,
     )(order, me, router, *h_parts, *c_parts, w)
 
 
-def outer_kernel(place, pairs, order_ref, *refs):
-    count = len(pairs)
+def produce_kernel(sources, order_ref, w_ref, *refs):
+    out_refs = refs[-3 - sources : -3]
+    z_refs = refs[: -3 - sources]
+    zs, held, sem = refs[-3:]
+    width = held.shape[0]
+    total = z_refs[0].shape[0]
+    rows = total // sources
+    row_groups, col_groups = width // BR, FF // BC
+
+    @pl.loop(0, row_groups)
+    def _(a):
+        for b in range(col_groups):
+            pltpu.make_async_copy(
+                w_ref.at[order_ref[(2 * row_groups + a) * col_groups + b]],
+                held.at[pl.ds(pl.multiple_of(a * BR, 64), BR), pl.ds(b * BC, BC)],
+                sem,
+            ).start()
+
+    for m, z_ref in enumerate(z_refs):
+        zs[m * total : (m + 1) * total] = z_ref[...]
+    wait_bytes(held, sem)
+    for n in range(width // BC):
+        cut = slice(n * BC, (n + 1) * BC)
+        made = dot(zs[...], held[cut, :], NT).astype(low_type)
+        for m in range(len(z_refs)):
+            for j in range(sources):
+                start = m * total + j * rows
+                out_refs[j][m * rows : (m + 1) * rows, cut] = made[start : start + rows]
+
+
+def produce(order, w, zs, sources, width):
+    micros = len(zs)
+    total = zs[0].shape[0]
+    return call(
+        functools.partial(produce_kernel, sources),
+        tuple([shaped((micros * total // sources, width), low_type)] * sources),
+        [in_smem, in_any] + [in_vmem] * micros,
+        tuple([in_vmem] * sources),
+        [
+            pltpu.VMEM((micros * total, FF), low_type),
+            pltpu.VMEM((width, FF), low_type),
+            pltpu.SemaphoreType.DMA,
+        ],
+        2 * micros * total * width * FF,
+        8 * MIB,
+        24,
+    )(order, w, *zs)
+
+
+def outer_kernel(place, widths, order_ref, *refs):
+    count = len(widths)
     micros = len(refs[:-3]) // (2 * count)
     lefts = refs[: count * micros]
     rights = refs[count * micros : 2 * count * micros]
@@ -390,7 +479,7 @@
     span = 2 * BR
     steps = []
     for k in range(count):
-        for p in range(lefts[k * micros].shape[-1] // span):
+        for p in range(widths[k] // span):
             steps.append((k, p))
 
     def wait_stage(slot, cols):
@@ -424,19 +513,19 @@
             wait_stage(slot, used[slot])
 
 
-def outer_blocks(order, place, lefts, rights, blocks):
-    pairs = [(l[0].shape[-1], r[0].shape[-1]) for l, r in zip(lefts, rights)]
-    widest = max(r for _, r in pairs)
+def outer_blocks(order, place, widths, lefts, rights, blocks):
+    widest = max(r[0].shape[-1] for r in rights)
     rows = sum(l.shape[0] for l in lefts[0])
     flat = [l for group in lefts for l in group] + [r for group in rights for r in group]
     return call(
-        functools.partial(outer_kernel, place, pairs),
+        functools.partial(outer_kernel, place, widths),
         shaped((blocks, BR, BC), low_type),
         [in_smem] + [in_vmem] * len(flat),
         in_any,
         [pltpu.VMEM((2, 2 * BR, widest), low_type), pltpu.SemaphoreType.DMA((2,))],
         2 * rows * blocks * BR * BC,
         blocks * BR * BC * 2 + sum(f.size * 2 for f in flat),
+        40,
     )(order, *flat)
 
 
@@ -529,6 +618,7 @@
         ],
         2 * total * chips * members * slots * BR * BC,
         16 * MIB,
+        28,
     )(order, me, *[part for group in lists for part in group])
     return [(made[2 * offset], made[2 * offset + 1]) for offset in range(chips)]
 
@@ -588,6 +678,7 @@
         [pltpu.VMEM((width, HEADS * HD), low_type), pltpu.SemaphoreType.DMA],
         2 * rows * width * HEADS * HD,
         10 * MIB,
+        24,
     )(me, x2, cot, h2, gains, router, w, *backs)
 
 
@@ -653,6 +744,7 @@
         ],
         40 * rows * length * width,
         8 * MIB,
+        40,
     )(q, rows_pos, key_pos, ob, log_total, do, *kv_parts)
 
 
@@ -689,6 +781,7 @@
         ],
         2 * micros * rows * width * q_width,
         7 * MIB,
+        16,
     )(w, *dqs)
 
 
@@ -737,6 +830,7 @@
         ],
         2 * micros * rows * width * kv_width,
         14 * MIB,
+        16,
     )(x, gains, w, *dxs, *parts, *dkvs)
 
 
@@ -759,6 +853,7 @@
 
 def rotate(weight, gradient, moment, second, left, right):
     count = weight.shape[0]
+    limit = 16
 
     def spec(rows, cols):
         return pl.BlockSpec((1, rows, cols), lambda i: (i, 0, 0))
@@ -770,7 +865,7 @@
         out_shape=(shaped(weight.shape, jnp.float32),) * 4,
         in_specs=[block] * 4 + [spec(BR, BR), spec(BC, BC)],
         out_specs=(block,) * 4,
-        compiler_params=pltpu.CompilerParams(vmem_limit_bytes=VMEM_LIMIT),
+        compiler_params=pltpu.CompilerParams(vmem_limit_bytes=limit * MIB),
         cost_estimate=pl.CostEstimate(
             flops=4 * count * BR * BC * (BR + BC),
             bytes_accessed=count * 2 * MIB,
@@ -944,9 +1039,18 @@
     cot_rows = after(cot_rows, *arrays[::2])
     cot_parts = [to_partner(cot_rows, j) for j in range(shard_count)]
 
-    h1, q, kv, w_in, w_out = project(
-        pieces, arrays, chips, shard_count, slots, dense_order, me, tokens, norm_gains
-    )
+    h1, kv, w_in, w_out = project(
+        pieces,
+        arrays,
+        chips,
+        shard_count,
+        slots,
+        dense_order,
+        me,
+        [tokens[m] for m in range(micros)],
+        norm_gains,
+    )
+    q = make_queries(h1, w_in, micros)
     h1_other = to_ctx(h1, 1)
     kvs, obs, logs, x2s, h2s = [], [], [], [], []
     chip_kv = []
@@ -954,7 +1058,7 @@
         own = kv[m] if m == 0 else after(kv[m], chip_kv[m - 1][1 % chips])
         chip_kv.append(from_chips(own, chips))
     for m in range(micros):
-        query = q[m] if m == 0 else after(q[m], obs[m - 1])
+        query = after(q[m], *(cot_parts if m == 0 else obs[m - 1 : m]))
         parts = chip_kv[m]
         swapped = parts if m == 0 else after(parts, obs[m - 1])
         kvs.append(parts + [to_ctx(part, 1) for part in swapped])
@@ -969,28 +1073,23 @@
 
     h_parts = []
     for m in range(micros):
-        own = after(h2s[m], *(cot_parts if m == 0 else h_parts[m - 1]))
+        own = h2s[m] if m == 0 else after(h2s[m], *h_parts[m - 1])
         h_parts.append([own] + [to_partner(own, j) for j in range(1, shard_count)])
-    outs, sent = [], []
-    zs, dgs, dus, dys, xs = [], [], [], [], []
+    sent = []
+    zs, dgs, dus, cs, xs = [], [], [], [], []
     for m in range(micros):
         here = after(me, h2s[-1], h1_other, *ob_others) if m == 0 else after(me, zs[-1])
         made = run_expert(m, expert_inverse, here, router_pad, h_parts[m], cot_parts, expert_all)
         sent.append(made[:shard_count])
-        outs.append(made[shard_count : 2 * shard_count])
-        z, dg, du, dy, x = made[2 * shard_count :]
+        z, dg, du, c, x = made[shard_count:]
         zs.append(z)
         dgs.append(dg)
         dus.append(du)
-        dys.append(dy)
+        cs.append(c)
         xs.append(x)
     backs = [[to_partner(sent[m][j], j) for j in range(shard_count)] for m in range(micros)]
-    arrived = []
-    for m in range(micros):
-        own = [after(part, *(arrived[-1] if arrived else backs[-1])) for part in outs[m]]
-        arrived.append([to_partner(own[j], j) for j in range(shard_count)])
-
-    dxs, das, dqs, stats, own_grads, far_grads = [], [], [], [], [], []
+
+    dxs, das, dqs, stats, own_grads, far_arrived = [], [], [], [], [], []
     for m in range(micros):
         here = after(me, zs[-1] if m == 0 else dqs[-1])
         dx, da, do, stat = merge(
@@ -1006,14 +1105,15 @@
             part = wide(dkv_own[cut]) + wide(got[cut])
             parts.append(part if o == 0 else part.astype(low_type))
         own_grads.append(parts[0])
-        far_grads.append(parts[1:])
+        far_arrived.append([to_chip(parts[o], -o) for o in range(1, chips)])
         dxs.append(dx)
         das.append(da)
         dqs.append(dq)
         stats.append(stat)
 
     dkvs = [
-        sum_to_chips([own_grads[m]] + far_grads[m]).astype(low_type) for m in range(micros)
+        sum([wide(part) for part in far_arrived[m]], own_grads[m]).astype(low_type)
+        for m in range(micros)
     ]
 
     def other_core(parts):
@@ -1021,9 +1121,10 @@
 
     da_others, dq_others = other_core(das), other_core(dqs)
     expert_term = outer_blocks(
-        after(expert_inverse, dqs[-1], dkvs[0], arrived[0]),
+        after(expert_inverse, dqs[-1]),
         lambda k: (k * row_groups * ff_groups, ff_groups),
-        [xs, xs, dys],
+        (width,) * 3,
+        [xs, xs, cs],
         [dgs, dus, zs],
         expert_blocks,
     )
@@ -1031,7 +1132,7 @@
     expert_sum = lax.psum_scatter(
         after(expert_term, dkvs[-1]), "ctx", scatter_dimension=0, tiled=True
     )
-    here = after(me, arrived[-1], parts_back)
+    here = after(me, parts_back)
     made = slot_blocks(
         chips,
         shard_count,
@@ -1055,11 +1156,14 @@
     router_grad = stat_rows[:shard_count].T
     gains_grad = jnp.stack([stat_rows[experts_up + 1], stat_rows[experts_up]])
 
+    made = produce(after(expert_inverse, *got[:2]), expert_all, zs, shard_count, width)
+    made = after(list(made), *sums)
+    arrived = [to_partner(made[j], j) for j in range(shard_count)]
     outputs = []
     for m in range(micros):
         total = x2s[m]
-        for j in range(shard_count):
-            total = total + wide(arrived[m][j])
+        for part in arrived:
+            total = total + wide(part[m * rows : (m + 1) * rows])
         outputs.append(total)
 
     expert_grad, expert_new, expert_moment_new, expert_second_new = rotate(

time: 660 us -> 594 us (0.900)
  the two profiles are of different devices: /device:TPU:0 before, /device:TPU:9 now
where the time goes in v4:
time: 594 us; the launch traced here: 587 us
  waiting for transfers between devices  219 us (37%)
  Pallas kernels  151 us (25%)
  starting transfers between devices  99.9 us (17%)
  local copies, waits for them, and re-layouts  79.5 us (13%)
  other arithmetic  21.5 us (4%)
  between operations  15.8 us (3%)
    ppermute x35, waiting for transfers between devices, to_partner(): return lax.ppermute(array, 'shard', [(i, i ^ offset) for i in range(count)])  122 us
    ppermute x18, waiting for transfers between devices, to_chip(): lax.ppermute(array, 'ctx', [(i, (i + 2 * offset) % count) for i in range(...  87.9 us
    unnamed x324, local copies, waits for them, and re-layouts  70.1 us
    ppermute x31, starting transfers between devices, to_ctx(): return lax.ppermute(array, 'ctx', [(i, i ^ offset) for i in range(count)])  48 us
    ppermute x35, starting transfers between devices, to_partner(): return lax.ppermute(array, 'shard', [(i, i ^ offset) for i in range(count)])  31.4 us
    pallas_call x2, Pallas kernels, run_expert(): call(functools.partial(expert_kernel, sources, micro), tuple([shaped((row...  28.3 us
    pallas_call x2, Pallas kernels, attend_back(): call(functools.partial(attend_back_kernel, len(kv_parts)), (shaped((rows,...  25.5 us
    pallas_call x2, Pallas kernels, attend(): call(functools.partial(attend_kernel, len(kv_parts)), (shaped((rows, widt...  22.2 us
  transfers between devices with their start and end apart: 86, of which 31 were waited for; matrix products, arithmetic and copies ran while one was open for 4% of the time, Pallas kernels for 21%

profile of v4, /device:TPU:9, one launch (start us, length us, event | category | flops | bytes accessed | tf_op | source)
XLA Modules:
  0.0 587.0 jit_solution(9459972253621703493)
XLA Ops:
  21.2 6.9 %collective-permute-done.3.refs_7_ = bf16[4,192,256]{2,1,0:T(8,128)(2,1)S(1)} collective-permute-done((bf16[4,192,256]{2,1,0:T(8,128)(2,1)S(1)}, bf16[4,192,256]{2,1,0:T(8,128)(2,1)S(1)}, u32[]{:S(2)}, u32[]{:S(2)}) %collective-permute-start.3) | collective-permute-done | bytes 393248 | tf_op jit(solution)/shard_map/ppermute | solution.py:891
  30.5 11.2 %collective-permute-start.6 = (bf16[4,192,256]{2,1,0:T(8,128)(2,1)S(1)}, bf16[4,192,256]{2,1,0:T(8,128)(2,1)S(1)}, u32[]{:S(2)}, u32[]{:S(2)}) collective-permute-start(bf16[4,192,256]{2,1,0:T(8,128)(2,1)S(1)} %collective-permute-done.5.refs_9_), channel_id=1, source_target_pairs={{0,4},{4,0},{8,12},{12,8},{16,20},{20,16},{24,28},{28,24},{1,5},{5... | collective-permute-start | bytes 1179656 | tf_op jit(solution)/shard_map/ppermute | solution.py:896
  55.0 23.6 %collective-permute-done.11.refs_13_ = bf16[12,192,256]{2,1,0:T(8,128)(2,1)} collective-permute-done((bf16[12,192,256]{2,1,0:T(8,128)(2,1)S(1)}, bf16[12,192,256]{2,1,0:T(8,128)(2,1)}, u32[]{:S(2)}, u32[]{:S(2)}) %collective-permute-start.11) | collective-permute-done | bytes 1179680 | tf_op jit(solution)/shard_map/ppermute | solution.py:891
  87.4 9.0 %collective-permute-done.15.refs_17_ = bf16[12,96,256]{2,1,0:T(8,128)(2,1)} collective-permute-done((bf16[12,96,256]{2,1,0:T(8,128)(2,1)S(1)}, bf16[12,96,256]{2,1,0:T(8,128)(2,1)}, u32[]{:S(2)}, u32[]{:S(2)}) %collective-permute-start.15) | collective-permute-done | bytes 589856 | tf_op jit(solution)/shard_map/ppermute | solution.py:891
  118.3 9.1 %shard_map.349 = (bf16[256,1536]{1,0:T(8,128)(2,1)}, bf16[128,1024]{1,0:T(8,128)(2,1)}, bf16[128,1024]{1,0:T(8,128)(2,1)S(1)}, bf16[1536,2560]{1,0:T(8,128)(2,1)S(1)}, bf16[1536,1536]{1,0:T(8,128)(2,1)S(1)}) custom-call(s32[128]{0:T(128)S(1)} %copy-done.65, s32[2]{0:T(128)S(1)} %pad_add_fusion.me_ref, f32[128,1536]{1,0:T(8,128)S(1)} %copy-done.17, ...), custom_call_target="tpu_custom_call" | custom-call | flops 805306368 | bytes 25165824 | tf_op jit(solution)/shard_map/pallas_call | solution.py:192
  137.1 5.5 collective-permute-done.20.refs_6_
  144.9 10.6 %collective-permute-start.26 = (bf16[128,1024]{1,0:T(8,128)(2,1)S(1)}, bf16[128,1024]{1,0:T(8,128)(2,1)S(1)}, u32[]{:S(2)}, u32[]{:S(2)}) collective-permute-start(bf16[128,1024]{1,0:T(8,128)(2,1)S(1)} %collective-permute-done.22.refs_1_), channel_id=1, source_target_pairs={{0,4},{4,0},{8,12},{12,8},{16,20},{20,16},{24,28},{28,24},{1,5},{5... | collective-permute-start | bytes 786440 | tf_op jit(solution)/shard_map/ppermute | solution.py:896
  179.1 10.9 %shard_map.351 = (bf16[128,1536]{1,0:T(8,128)(2,1)}, f32[384,128]{1,0:T(8,128)S(1)}, f32[128,1536]{1,0:T(8,128)S(1)}, bf16[128,1536]{1,0:T(8,128)(2,1)}) custom-call(bf16[128,1536]{1,0:T(8,128)(2,1)S(1)} %get-tuple-element.121.q_ref, s32[128,1]{1,0:T(8,128)S(1)} %constant_dynamic-slice_fusion.rpos_ref, s32[1,1024]{1,0:T(1,128)S(1)} %bitcast.51, ...), custom_call_target="tpu_custom_call" | custom-call | flops 3221225472 | bytes 8388608 | tf_op jit(solution)/shard_map/pallas_call | solution.py:303
  214.0 11.2 %shard_map.352 = (bf16[128,1536]{1,0:T(8,128)(2,1)S(1)}, f32[384,128]{1,0:T(8,128)S(1)}, f32[128,1536]{1,0:T(8,128)S(1)}, bf16[128,1536]{1,0:T(8,128)(2,1)}) custom-call(bf16[128,1536]{1,0:T(8,128)(2,1)S(1)} %copy-done.81, s32[128,1]{1,0:T(8,128)S(1)} %copy-done.60, s32[1,1024]{1,0:T(1,128)S(1)} %bitcast.52, f32[128,1536]{1,0:T(8,128)S(1)} %copy-done.16, ...), custom_call_target="tpu_custom_call" | custom-call | flops 3221225472 | bytes 8388608 | tf_op jit(solution)/shard_map/pallas_call | solution.py:303
  239.0 15.0 %shard_map.353 = (bf16[128,1664]{1,0:T(8,128)(2,1)S(1)}, bf16[128,1664]{1,0:T(8,128)(2,1)}, bf16[128,1664]{1,0:T(8,128)(2,1)}, bf16[128,1664]{1,0:T(8,128)(2,1)}...) custom-call(s32[96]{0:T(128)S(1)} %copy-done.120, ...), custom_call_target="tpu_custom_call" | custom-call | flops 8053063680 | bytes 20971520 | tf_op jit(solution)/shard_map/pallas_call | solution.py:403
  259.7 13.3 %shard_map.354 = (bf16[128,1664]{1,0:T(8,128)(2,1)S(1)}, bf16[128,1664]{1,0:T(8,128)(2,1)S(1)}, bf16[128,1664]{1,0:T(8,128)(2,1)S(1)}, bf16[128,1664]{1,0:T(8,12...) custom-call(s32[96]{0:T(128)S(1)} %copy-done.120, ...), custom_call_target="tpu_custom_call" | custom-call | flops 8053063680 | bytes 20971520 | tf_op jit(solution)/shard_map/pallas_call | solution.py:403
  283.6 12.6 %shard_map.356 = (bf16[128,1536]{1,0:T(8,128)(2,1)S(1)}, bf16[512,1024]{1,0:T(8,128)(2,1)S(1)}, bf16[512,1024]{1,0:T(8,128)(2,1)S(1)}) custom-call(bf16[128,1536]{1,0:T(8,128)(2,1)S(1)} %copy-done.84, s32[128,1]{1,0:T(8,128)S(1)} %copy-done.61, s32[1,1024]{1,0:T(1,128)S(1)} %bitcast.53, bf16[128,1536]{1,0:T(8,128)(2,1)} %get-tuple-element.126.ob_ref.refs_14_, ...), custom_call_target="tpu_custom_call" | custom-call | flops 8053063680 | bytes 8388608 | tf_op jit(solution)/shard_map/pallas_call | solution.py:735
  302.8 12.9 %shard_map.358 = (bf16[128,1536]{1,0:T(8,128)(2,1)S(1)}, bf16[512,1024]{1,0:T(8,128)(2,1)}, bf16[512,1024]{1,0:T(8,128)(2,1)S(1)}) custom-call(bf16[128,1536]{1,0:T(8,128)(2,1)S(1)} %copy-done.82, s32[128,1]{1,0:T(8,128)S(1)} %copy-done.61, s32[1,1024]{1,0:T(1,128)S(1)} %bitcast.54, bf16[128,1536]{1,0:T(8,128)(2,1)S(1)} %copy-done.76, ...), custom_call_target="tpu_custom_call" | custom-call | flops 8053063680 | bytes 8388608 | tf_op jit(solution)/shard_map/pallas_call | solution.py:735
  328.1 13.6 %shard_map.359 = bf16[96,192,256]{2,1,0:T(8,128)(2,1)} custom-call(s32[96]{0:T(128)S(1)} %copy-done.121, bf16[512,1536]{1,0:T(8,128)(2,1)S(1)} %copy-done.130, bf16[512,1536]{1,0:T(8,128)(2,1)S(1)} %copy-done.131, bf16[512,1536]{1,0:T(8,128)(2,1)S(1)} %copy-done.130, bf16[512,1536]{1,0:T(8,128)(2,1)S(1)} %copy-done.131, bf16[512,1664]{1,0:T(8,128)(2,1)S(1)} %copy-done.128, ...), custom_call_target="tpu_custom_call" | custom-call | flops 9663676416 | bytes 25427968 | tf_op jit(solution)/shard_map/pallas_call | solution.py:520
  341.7 5.9 collective-permute-done.61
  360.2 10.0 %collective-permute-done.58 = bf16[128,1024]{1,0:T(8,128)(2,1)S(1)} collective-permute-done((bf16[128,1024]{1,0:T(8,128)(2,1)S(1)}, bf16[128,1024]{1,0:T(8,128)(2,1)S(1)}, u32[]{:S(2)}, u32[]{:S(2)}) %collective-permute-start.58) | collective-permute-done | bytes 262176 | tf_op jit(solution)/shard_map/ppermute | solution.py:901
  371.7 23.9 %collective-permute-done.57 = bf16[128,1024]{1,0:T(8,128)(2,1)S(1)} collective-permute-done((bf16[128,1024]{1,0:T(8,128)(2,1)S(1)}, bf16[128,1024]{1,0:T(8,128)(2,1)S(1)}, u32[]{:S(2)}, u32[]{:S(2)}) %collective-permute-start.57) | collective-permute-done | bytes 262176 | tf_op jit(solution)/shard_map/ppermute | solution.py:901
  405.3 18.0 %shard_map.361 = (bf16[8,192,256]{2,1,0:T(8,128)(2,1)S(1)}, bf16[8,192,256]{2,1,0:T(8,128)(2,1)S(1)}, bf16[8,192,256]{2,1,0:T(8,128)(2,1)S(1)}, bf16[8,192,256]{...) custom-call(s32[128]{0:T(128)S(1)} %copy-done.66, ...), custom_call_target="tpu_custom_call" | custom-call | flops 3221225472 | bytes 16777216 | tf_op jit(solution)/shard_map/pallas_call | solution.py:600
  426.3 15.9 %collective-permute-done.65 = bf16[8,192,256]{2,1,0:T(8,128)(2,1)S(1)} collective-permute-done((bf16[8,192,256]{2,1,0:T(8,128)(2,1)S(1)}, bf16[8,192,256]{2,1,0:T(8,128)(2,1)S(1)}, u32[]{:S(2)}, u32[]{:S(2)}) %collective-permute-start.65) | collective-permute-done | bytes 786464 | tf_op jit(solution)/shard_map/ppermute | solution.py:891
  442.4 16.9 %collective-permute-done.71 = bf16[8,192,256]{2,1,0:T(8,128)(2,1)S(1)} collective-permute-done((bf16[8,192,256]{2,1,0:T(8,128)(2,1)S(1)}, bf16[8,192,256]{2,1,0:T(8,128)(2,1)S(1)}, u32[]{:S(2)}, u32[]{:S(2)}) %collective-permute-start.71) | collective-permute-done | bytes 786464 | tf_op jit(solution)/shard_map/ppermute | solution.py:891
  488.7 23.4 %collective-permute-done.77 = bf16[4,192,256]{2,1,0:T(8,128)(2,1)S(1)} collective-permute-done((bf16[4,192,256]{2,1,0:T(8,128)(2,1)S(1)}, bf16[4,192,256]{2,1,0:T(8,128)(2,1)S(1)}, u32[]{:S(2)}, u32[]{:S(2)}) %collective-permute-start.77) | collective-permute-done | bytes 393248 | tf_op jit(solution)/shard_map/ppermute | solution.py:901
  522.7 15.6 %collective-permute-done.75 = bf16[256,1536]{1,0:T(8,128)(2,1)S(1)} collective-permute-done((bf16[256,1536]{1,0:T(8,128)(2,1)S(1)}, bf16[256,1536]{1,0:T(8,128)(2,1)S(1)}, u32[]{:S(2)}, u32[]{:S(2)}) %collective-permute-start.75) | collective-permute-done | bytes 786464 | tf_op jit(solution)/shard_map/ppermute | solution.py:891
  538.3 17.7 %collective-permute-done.74 = bf16[256,1536]{1,0:T(8,128)(2,1)S(1)} collective-permute-done((bf16[256,1536]{1,0:T(8,128)(2,1)S(1)}, bf16[256,1536]{1,0:T(8,128)(2,1)S(1)}, u32[]{:S(2)}, u32[]{:S(2)}) %collective-permute-start.74) | collective-permute-done | bytes 786464 | tf_op jit(solution)/shard_map/ppermute | solution.py:891
  566.9 9.4 %shard_map.364 = (f32[12,192,256]{2,1,0:T(8,128)}, f32[12,192,256]{2,1,0:T(8,128)}, f32[12,192,256]{2,1,0:T(8,128)}, f32[12,192,256]{2,1,0:T(8,128)}) custom-call(f32[12,192,256]{2,1,0:T(8,128)S(1)} %bitcast.44, bf16[12,192,256]{2,1,0:T(8,128)(2,1)S(1)} %copy-done.24, f32[12,192,256]{2,1,0:T(8,128)S(1)} %bitcast.46, f32[12,192,256]{2,1,0:T(8,128)S(1)} %bitcast.47, ...), custom_call_target="tpu_custom_call" | custom-call | flops 1056964608 | bytes 25165824 | tf_op jit(solution)/shard_map/pallas_call | solution.py:862
  (545 shorter events, 249.2 us)
Async XLA Ops:
  7.2 227.0 %all-gather.2.cloned.1.call-start = ((), (), s32[]{:S(2)}) async-start(), calls=%async_computation.1 | async-start | bytes 10616832 | tf_op jit(solution)/shard_map/all_gather | solution.py:1033
  12.6 31.9 %collective-permute-start.8 = (bf16[4,192,256]{2,1,0:T(8,128)(2,1)S(1)}, bf16[4,192,256]{2,1,0:T(8,128)(2,1)S(1)}, u32[]{:S(2)}, u32[]{:S(2)}) collective-permute-start(bf16[4,192,256]{2,1,0:T(8,128)(2,1)S(1)} %convert_element_type.223.refs_3_), channel_id=1, source_target_pairs={{0,16},{4,20},{8,24},{12,28},{16,0},{20,4},{24,8},{28,12},{1,17},{... | collective-permute-start | bytes 1179656 | tf_op jit(solution)/shard_map/ppermute | solution.py:901
  19.9 29.3 %collective-permute-start.7 = (bf16[4,192,256]{2,1,0:T(8,128)(2,1)S(1)}, bf16[4,192,256]{2,1,0:T(8,128)(2,1)}, u32[]{:S(2)}, u32[]{:S(2)}) collective-permute-start(bf16[4,192,256]{2,1,0:T(8,128)(2,1)S(1)} %convert_element_type.223.refs_3_), channel_id=1, source_target_pairs={{0,8},{4,12},{8,16},{12,20},{16,24},{20,28},{24,0},{28,4},{1,9},{5... | collective-permute-start | bytes 1179656 | tf_op jit(solution)/shard_map/ppermute | solution.py:901
  50.2 507.5 %reduce-scatter.2.cloned.1.call-start = ((), (), s32[]{:S(2)}) async-start(), calls=%async_computation.2 | async-start | bytes 10616832 | tf_op jit(solution)/shard_map/reduce_scatter | solution.py:1132
  52.6 29.9 %collective-permute-start.13 = (bf16[12,192,256]{2,1,0:T(8,128)(2,1)S(1)}, bf16[12,192,256]{2,1,0:T(8,128)(2,1)}, u32[]{:S(2)}, u32[]{:S(2)}) collective-permute-start(bf16[12,192,256]{2,1,0:T(8,128)(2,1)S(1)} %pad_maximum_fusion.1.refs_11_), channel_id=1, source_target_pairs={{0,2},{1,3},{2,0},{3,1},{4,6},{5,7},{6,4},{7,5},{8,10},{9,11},{10,... | collective-permute-start | bytes 3538952 | tf_op jit(solution)/shard_map/ppermute | solution.py:891
  53.8 47.2 %collective-permute-start.10 = (bf16[12,192,256]{2,1,0:T(8,128)(2,1)S(1)}, bf16[12,192,256]{2,1,0:T(8,128)(2,1)S(1)}, u32[]{:S(2)}, u32[]{:S(2)}) collective-permute-start(bf16[12,192,256]{2,1,0:T(8,128)(2,1)S(1)} %pad_maximum_fusion.1.refs_11_), channel_id=1, source_target_pairs={{0,4},{4,0},{8,12},{12,8},{16,20},{20,16},{24,28},{28,24},{1,5},{5... | collective-permute-start | bytes 3538952 | tf_op jit(solution)/shard_map/ppermute | solution.py:896
  98.5 37.2 %collective-permute-start.19 = (bf16[256,1664]{1,0:T(8,128)(2,1)}, bf16[256,1664]{1,0:T(8,128)(2,1)}, u32[]{:S(2)}, u32[]{:S(2)}) collective-permute-start(bf16[256,1664]{1,0:T(8,128)(2,1)} %bitcast.4.refs_4_), channel_id=1, source_target_pairs={{0,1},{1,0},{2,3},{3,2},{4,5},{5,4},{6,7},{7,6},{8,9},{9,8},{10,11... | collective-permute-start | bytes 2555912 | tf_op jit(solution)/shard_map/ppermute | solution.py:891
  104.1 38.6 %collective-permute-start.20 = (bf16[256,1664]{1,0:T(8,128)(2,1)}, bf16[256,1664]{1,0:T(8,128)(2,1)S(1)}, u32[]{:S(2)}, u32[]{:S(2)}) collective-permute-start(bf16[256,1664]{1,0:T(8,128)(2,1)} %bitcast.4.refs_4_), channel_id=1, source_target_pairs={{0,2},{1,3},{2,0},{3,1},{4,6},{5,7},{6,4},{7,5},{8,10},{9,11},{10,... | collective-permute-start | bytes 2555912 | tf_op jit(solution)/shard_map/ppermute | solution.py:891
  106.1 65.2 %collective-permute-start.21 = (bf16[256,1664]{1,0:T(8,128)(2,1)}, bf16[256,1664]{1,0:T(8,128)(2,1)}, u32[]{:S(2)}, u32[]{:S(2)}) collective-permute-start(bf16[256,1664]{1,0:T(8,128)(2,1)} %bitcast.4.refs_4_), channel_id=1, source_target_pairs={{0,3},{1,2},{2,1},{3,0},{4,7},{5,6},{6,5},{7,4},{8,11},{9,10},{10,... | collective-permute-start | bytes 2555912 | tf_op jit(solution)/shard_map/ppermute | solution.py:891
  202.3 29.0 %collective-permute-start.36 = (bf16[256,1536]{1,0:T(8,128)(2,1)}, bf16[256,1536]{1,0:T(8,128)(2,1)S(1)}, u32[]{:S(2)}, u32[]{:S(2)}) collective-permute-start(bf16[256,1536]{1,0:T(8,128)(2,1)} %get-tuple-element.117.h_ref.refs_0_), channel_id=1, source_target_pairs={{0,4},{4,0},{8,12},{12,8},{16,20},{20,16},{24,28},{28,24},{1,5},{5... | collective-permute-start | bytes 2359304 | tf_op jit(solution)/shard_map/ppermute | solution.py:896
  203.7 29.0 %collective-permute-start.37 = (bf16[128,1536]{1,0:T(8,128)(2,1)}, bf16[128,1536]{1,0:T(8,128)(2,1)S(1)}, u32[]{:S(2)}, u32[]{:S(2)}) collective-permute-start(bf16[128,1536]{1,0:T(8,128)(2,1)} %get-tuple-element.126.ob_ref.refs_14_), channel_id=1, source_target_pairs={{0,4},{4,0},{8,12},{12,8},{16,20},{20,16},{24,28},{28,24},{1,5},{5... | collective-permute-start | bytes 1179656 | tf_op jit(solution)/shard_map/ppermute | solution.py:896
  229.2 29.9 %collective-permute-start.42 = (bf16[128,1536]{1,0:T(8,128)(2,1)}, bf16[128,1536]{1,0:T(8,128)(2,1)}, u32[]{:S(2)}, u32[]{:S(2)}) collective-permute-start(bf16[128,1536]{1,0:T(8,128)(2,1)} %get-tuple-element.143.refs_0_.h2_ref), channel_id=1, source_target_pairs={{0,1},{1,0},{2,3},{3,2},{4,5},{5,4},{6,7},{7,6},{8,9},{9,8},{10,11... | collective-permute-start | bytes 1179656 | tf_op jit(solution)/shard_map/ppermute | solution.py:891
  230.5 29.2 %collective-permute-start.43 = (bf16[128,1536]{1,0:T(8,128)(2,1)}, bf16[128,1536]{1,0:T(8,128)(2,1)}, u32[]{:S(2)}, u32[]{:S(2)}) collective-permute-start(bf16[128,1536]{1,0:T(8,128)(2,1)} %get-tuple-element.143.refs_0_.h2_ref), channel_id=1, source_target_pairs={{0,2},{1,3},{2,0},{3,1},{4,6},{5,7},{6,4},{7,5},{8,10},{9,11},{10,... | collective-permute-start | bytes 1179656 | tf_op jit(solution)/shard_map/ppermute | solution.py:891
  356.6 39.0 %collective-permute-start.57 = (bf16[128,1024]{1,0:T(8,128)(2,1)S(1)}, bf16[128,1024]{1,0:T(8,128)(2,1)S(1)}, u32[]{:S(2)}, u32[]{:S(2)}) collective-permute-start(bf16[128,1024]{1,0:T(8,128)(2,1)S(1)} %get-tuple-element.231), channel_id=1, source_target_pairs={{0,16},{4,20},{8,24},{12,28},{16,0},{20,4},{24,8},{28,12},{1,17},{... | collective-permute-start | bytes 786440 | tf_op jit(solution)/shard_map/ppermute | solution.py:901
  357.2 40.4 %collective-permute-start.56 = (bf16[128,1024]{1,0:T(8,128)(2,1)S(1)}, bf16[128,1024]{1,0:T(8,128)(2,1)S(1)}, u32[]{:S(2)}, u32[]{:S(2)}) collective-permute-start(bf16[128,1024]{1,0:T(8,128)(2,1)S(1)} %get-tuple-element.229), channel_id=1, source_target_pairs={{0,24},{4,28},{8,0},{12,4},{16,8},{20,12},{24,16},{28,20},{1,25},{... | collective-permute-start | bytes 786440 | tf_op jit(solution)/shard_map/ppermute | solution.py:901
  358.9 41.0 %collective-permute-start.51 = (bf16[128,1536]{1,0:T(8,128)(2,1)S(1)}, bf16[128,1536]{1,0:T(8,128)(2,1)S(1)}, u32[]{:S(2)}, u32[]{:S(2)}) collective-permute-start(bf16[128,1536]{1,0:T(8,128)(2,1)S(1)} %copy-done.86), channel_id=1, source_target_pairs={{0,4},{4,0},{8,12},{12,8},{16,20},{20,16},{24,28},{28,24},{1,5},{5... | collective-permute-start | bytes 1179656 | tf_op jit(solution)/shard_map/ppermute | solution.py:896
  360.2 45.0 %collective-permute-start.53 = (bf16[128,1536]{1,0:T(8,128)(2,1)S(1)}, bf16[128,1536]{1,0:T(8,128)(2,1)S(1)}, u32[]{:S(2)}, u32[]{:S(2)}) collective-permute-start(bf16[128,1536]{1,0:T(8,128)(2,1)S(1)} %copy-done.37), channel_id=1, source_target_pairs={{0,4},{4,0},{8,12},{12,8},{16,20},{20,16},{24,28},{28,24},{1,5},{5... | collective-permute-start | bytes 1179656 | tf_op jit(solution)/shard_map/ppermute | solution.py:896
  370.2 35.0 %collective-permute-start.54 = (bf16[128,1536]{1,0:T(8,128)(2,1)S(1)}, bf16[128,1536]{1,0:T(8,128)(2,1)S(1)}, u32[]{:S(2)}, u32[]{:S(2)}) collective-permute-start(bf16[128,1536]{1,0:T(8,128)(2,1)S(1)} %copy-done.39), channel_id=1, source_target_pairs={{0,4},{4,0},{8,12},{12,8},{16,20},{20,16},{24,28},{28,24},{1,5},{5... | collective-permute-start | bytes 1179656 | tf_op jit(solution)/shard_map/ppermute | solution.py:896
  424.6 34.6 %collective-permute-start.71 = (bf16[8,192,256]{2,1,0:T(8,128)(2,1)S(1)}, bf16[8,192,256]{2,1,0:T(8,128)(2,1)S(1)}, u32[]{:S(2)}, u32[]{:S(2)}) collective-permute-start(bf16[8,192,256]{2,1,0:T(8,128)(2,1)S(1)} %get-tuple-element.191), channel_id=1, source_target_pairs={{0,1},{1,0},{2,3},{3,2},{4,5},{5,4},{6,7},{7,6},{8,9},{9,8},{10,11... | collective-permute-start | bytes 2359304 | tf_op jit(solution)/shard_map/ppermute | solution.py:891
  425.4 35.1 %collective-permute-start.69 = (bf16[8,192,256]{2,1,0:T(8,128)(2,1)S(1)}, bf16[8,192,256]{2,1,0:T(8,128)(2,1)S(1)}, u32[]{:S(2)}, u32[]{:S(2)}) collective-permute-start(bf16[8,192,256]{2,1,0:T(8,128)(2,1)S(1)} %get-tuple-element.189), channel_id=1, source_target_pairs={{0,2},{1,3},{2,0},{3,1},{4,6},{5,7},{6,4},{7,5},{8,10},{9,11},{10,... | collective-permute-start | bytes 2359304 | tf_op jit(solution)/shard_map/ppermute | solution.py:891
  479.9 32.1 %collective-permute-start.77 = (bf16[4,192,256]{2,1,0:T(8,128)(2,1)S(1)}, bf16[4,192,256]{2,1,0:T(8,128)(2,1)S(1)}, u32[]{:S(2)}, u32[]{:S(2)}) collective-permute-start(bf16[4,192,256]{2,1,0:T(8,128)(2,1)S(1)} %add_convert_fusion.2), channel_id=1, source_target_pairs={{0,16},{4,20},{8,24},{12,28},{16,0},{20,4},{24,8},{28,12},{1,17},{... | collective-permute-start | bytes 1179656 | tf_op jit(solution)/shard_map/ppermute | solution.py:901
  483.8 33.8 %collective-permute-start.76 = (bf16[4,192,256]{2,1,0:T(8,128)(2,1)S(1)}, bf16[4,192,256]{2,1,0:T(8,128)(2,1)S(1)}, u32[]{:S(2)}, u32[]{:S(2)}) collective-permute-start(bf16[4,192,256]{2,1,0:T(8,128)(2,1)S(1)} %add_convert_fusion.4), channel_id=1, source_target_pairs={{0,24},{4,28},{8,0},{12,4},{16,8},{20,12},{24,16},{28,20},{1,25},{... | collective-permute-start | bytes 1179656 | tf_op jit(solution)/shard_map/ppermute | solution.py:901
  519.9 36.0 %collective-permute-start.74 = (bf16[256,1536]{1,0:T(8,128)(2,1)S(1)}, bf16[256,1536]{1,0:T(8,128)(2,1)S(1)}, u32[]{:S(2)}, u32[]{:S(2)}) collective-permute-start(bf16[256,1536]{1,0:T(8,128)(2,1)S(1)} %get-tuple-element.194), channel_id=1, source_target_pairs={{0,2},{1,3},{2,0},{3,1},{4,6},{5,7},{6,4},{7,5},{8,10},{9,11},{10,... | collective-permute-start | bytes 2359304 | tf_op jit(solution)/shard_map/ppermute | solution.py:891
  520.5 35.4 %collective-permute-start.73 = (bf16[256,1536]{1,0:T(8,128)(2,1)S(1)}, bf16[256,1536]{1,0:T(8,128)(2,1)S(1)}, u32[]{:S(2)}, u32[]{:S(2)}) collective-permute-start(bf16[256,1536]{1,0:T(8,128)(2,1)S(1)} %get-tuple-element.193), channel_id=1, source_target_pairs={{0,1},{1,0},{2,3},{3,2},{4,5},{5,4},{6,7},{7,6},{8,9},{9,8},{10,11... | collective-permute-start | bytes 2359304 | tf_op jit(solution)/shard_map/ppermute | solution.py:891
  (224 other events, 2648.7 us)
Sparse Core Ops, SparseCore 0:
  49.4 89.7 all-gather.1
  352.2 118.4 reduce-scatter.1

commit v5 on v4

--- a/solution.py
+++ b/solution.py
@@ -24,6 +24,7 @@
 masked_score = -1e30
 low_type = jnp.bfloat16
 MIB = 1 << 20
+VMEM_LIMIT = 60 * MIB
 
 NN = (((1,), (0,)), ((), ()))
 NT = (((1,), (1,)), ((), ()))
@@ -38,14 +39,14 @@
     return lax.dot_general(left_side, right_side, dims, preferred_element_type=jnp.float32)
 
 
-def call(kernel, out_shapes, in_specs, out_specs, scratch, flops, moved, limit):
+def call(kernel, out_shapes, in_specs, out_specs, scratch, flops, moved):
     return pl.pallas_call(
         kernel,
         out_shape=out_shapes,
         in_specs=in_specs,
         out_specs=out_specs,
         scratch_shapes=scratch,
-        compiler_params=pltpu.CompilerParams(vmem_limit_bytes=limit * MIB),
+        compiler_params=pltpu.CompilerParams(vmem_limit_bytes=VMEM_LIMIT),
         cost_estimate=pl.CostEstimate(flops=flops, bytes_accessed=moved, transcendentals=0),
     )
 
@@ -208,7 +209,6 @@
         ],
         2 * micros * rows * width * kv_width,
         4 * width * (in_width + out_width),
-        24,
     )(order, me, *xs, gains, *arrays)
     return made[0], made[1 : 1 + micros], made[1 + micros], made[2 + micros]
 
@@ -247,7 +247,6 @@
         [pltpu.VMEM((width, q_width), low_type), pltpu.SemaphoreType.DMA((q_width // BC,))],
         2 * total * width * q_width,
         2 * width * q_width,
-        16,
     )(h, w)
 
 
@@ -318,7 +317,6 @@
         ],
         16 * rows * length * width,
         8 * MIB,
-        32,
     )(q, rows_pos, key_pos, x, gains, w, *kv_parts)
 
 
@@ -417,7 +415,6 @@
         ],
         10 * total * width * FF,
         20 * MIB,
-        44,
     )(order, me, router, *h_parts, *c_parts, w)
 
 
@@ -466,11 +463,10 @@
         ],
         2 * micros * total * width * FF,
         8 * MIB,
-        24,
     )(order, w, *zs)
 
 
-def outer_kernel(place, widths, order_ref, *refs):
+def outer_kernel(place, widths, side, order_ref, *refs):
     count = len(widths)
     micros = len(refs[:-3]) // (2 * count)
     lefts = refs[: count * micros]
@@ -491,20 +487,25 @@
         cols = rights[k * micros].shape[-1]
         if used[slot] is not None:
             wait_stage(slot, used[slot])
-        used[slot] = cols
+        used[slot] = cols // 2
         cut = slice(p * span, (p + 1) * span)
-        for c in range(0, cols, 512):
-            part = slice(c, c + 512)
-            made = sum(
-                dot(lefts[k * micros + m][:, cut], rights[k * micros + m][:, part], TN)
-                for m in range(micros)
+        made = 0.0
+        for m in range(micros):
+            left = lefts[k * micros + m][:, cut]
+            right = jnp.concatenate(
+                [
+                    rights[k * micros + m][:, start : start + LANES]
+                    for start in range(side * LANES, cols, BC)
+                ],
+                axis=1,
             )
-            stage[slot, :, part] = made.astype(low_type)
+            made = made + dot(left, right, TN)
+        stage[slot, :, : cols // 2] = made.astype(low_type)
         first, row_step = place(k)
         for half in range(2):
             for b in range(cols // BC):
                 pltpu.make_async_copy(
-                    stage.at[slot, pl.ds(half * BR, BR), pl.ds(b * BC, BC)],
+                    stage.at[slot, pl.ds(half * BR, BR), pl.ds(b * LANES, LANES)],
                     out_ref.at[order_ref[first + (2 * p + half) * row_step + b]],
                     sems.at[slot],
                 ).start()
@@ -513,19 +514,18 @@
             wait_stage(slot, used[slot])
 
 
-def outer_blocks(order, place, widths, lefts, rights, blocks):
+def outer_blocks(order, place, widths, side, lefts, rights, blocks):
     widest = max(r[0].shape[-1] for r in rights)
     rows = sum(l.shape[0] for l in lefts[0])
     flat = [l for group in lefts for l in group] + [r for group in rights for r in group]
     return call(
-        functools.partial(outer_kernel, place, widths),
-        shaped((blocks, BR, BC), low_type),
+        functools.partial(outer_kernel, place, widths, side),
+        shaped((blocks, BR, LANES), low_type),
         [in_smem] + [in_vmem] * len(flat),
         in_any,
-        [pltpu.VMEM((2, 2 * BR, widest), low_type), pltpu.SemaphoreType.DMA((2,))],
-        2 * rows * blocks * BR * BC,
-        blocks * BR * BC * 2 + sum(f.size * 2 for f in flat),
-        40,
+        [pltpu.VMEM((2, 2 * BR, widest // 2), low_type), pltpu.SemaphoreType.DMA((2,))],
+        rows * blocks * BR * BC,
+        blocks * BR * BC + sum(f.size * 2 for f in flat),
     )(order, *flat)
 
 
@@ -618,7 +618,6 @@
         ],
         2 * total * chips * members * slots * BR * BC,
         16 * MIB,
-        28,
     )(order, me, *[part for group in lists for part in group])
     return [(made[2 * offset], made[2 * offset + 1]) for offset in range(chips)]
 
@@ -678,7 +677,6 @@
         [pltpu.VMEM((width, HEADS * HD), low_type), pltpu.SemaphoreType.DMA],
         2 * rows * width * HEADS * HD,
         10 * MIB,
-        24,
     )(me, x2, cot, h2, gains, router, w, *backs)
 
 
@@ -744,7 +742,6 @@
         ],
         40 * rows * length * width,
         8 * MIB,
-        40,
     )(q, rows_pos, key_pos, ob, log_total, do, *kv_parts)
 
 
@@ -781,7 +778,6 @@
         ],
         2 * micros * rows * width * q_width,
         7 * MIB,
-        16,
     )(w, *dqs)
 
 
@@ -830,14 +826,13 @@
         ],
         2 * micros * rows * width * kv_width,
         14 * MIB,
-        16,
     )(x, gains, w, *dxs, *parts, *dkvs)
 
 
-def rotate_kernel(
-    b_ref, g_ref, m_ref, s_ref, l_ref, r_ref, grad_ref, new_ref, moment_ref, second_ref
-):
-    gradient = g_ref[0].astype(jnp.float32)
+def rotate_kernel(b_ref, m_ref, s_ref, l_ref, r_ref, *refs):
+    grad_ref, new_ref, moment_ref, second_ref = refs[-4:]
+    parts = [ref[0].astype(jnp.float32) for ref in refs[:-4]]
+    gradient = parts[0] if len(parts) == 1 else jnp.concatenate(parts, axis=1)
     grad_ref[0] = gradient
     left = l_ref[0].astype(low_type)
     right = r_ref[0].astype(low_type)
@@ -851,9 +846,8 @@
     new_ref[0] = b_ref[0] - rate * turned
 
 
-def rotate(weight, gradient, moment, second, left, right):
+def rotate(weight, gradients, moment, second, left, right):
     count = weight.shape[0]
-    limit = 16
 
     def spec(rows, cols):
         return pl.BlockSpec((1, rows, cols), lambda i: (i, 0, 0))
@@ -863,15 +857,17 @@
         rotate_kernel,
         grid=(count,),
         out_shape=(shaped(weight.shape, jnp.float32),) * 4,
-        in_specs=[block] * 4 + [spec(BR, BR), spec(BC, BC)],
+        in_specs=[block] * 3
+        + [spec(BR, BR), spec(BC, BC)]
+        + [spec(BR, part.shape[2]) for part in gradients],
         out_specs=(block,) * 4,
-        compiler_params=pltpu.CompilerParams(vmem_limit_bytes=limit * MIB),
+        compiler_params=pltpu.CompilerParams(vmem_limit_bytes=VMEM_LIMIT),
         cost_estimate=pl.CostEstimate(
             flops=4 * count * BR * BC * (BR + BC),
             bytes_accessed=count * 2 * MIB,
             transcendentals=0,
         ),
-    )(weight, gradient, moment, second, left, right)
+    )(weight, moment, second, left, right, *gradients)
 
 
 def adam(weight, gradient, moment, second, step_rate):
@@ -923,31 +919,44 @@
 def gather_weights(blocks, chips, members):
     parts = from_chips(blocks, chips)
     pieces, arrays = [], []
+    gate = []
 
     def add(array, offset, first, cut):
         pieces.append((0, offset, first, cut))
         arrays.append(array)
         pieces.append((1, offset, first, cut))
-        arrays.append(to_ctx(array, 1))
+        arrays.append(to_ctx(after(array, *gate), 1))
         return array
 
+    def spread(group, first):
+        add(group, 0, first, 0)
+        if members == 4 and first > 0:
+            by_one, by_two = to_partner(group, 1), to_partner(group, 2)
+            add(by_one, 1, first, 0)
+            add(by_two, 2, first, 0)
+            half = BR // 2
+            add(to_partner(by_one[:, :half], 2), 3, first, 0)
+            add(to_partner(by_two[:, half:], 1), 3, first, half)
+            return [by_one, by_two]
+        got = [to_partner(group, offset) for offset in range(1, members)]
+        for offset in range(1, members):
+            add(got[offset - 1], offset, first, 0)
+        return got
+
+    got = [to_partner(blocks, offset) for offset in range(1, members)]
+    gate.append(got[0])
     add(blocks, 0, 0, 0)
     for offset in range(1, members):
-        add(to_partner(blocks, offset), offset, 0, 0)
-    near = list(arrays)
+        add(got[offset - 1], offset, 0, 0)
+    last = list(got)
     if chips > 1:
-        far = after(jnp.concatenate(parts[1:], axis=0), *near)
-        add(far, 0, 1, 0)
-        if members == 4:
-            by_one = add(to_partner(far, 1), 1, 1, 0)
-            by_two = add(to_partner(far, 2), 2, 1, 0)
-            half = BR // 2
-            add(to_partner(by_one[:, :half], 2), 3, 1, 0)
-            add(to_partner(by_two[:, half:], 1), 3, 1, half)
-        else:
-            for offset in range(1, members):
-                add(to_partner(far, offset), offset, 1, 0)
-    return near + parts[1:], pieces, arrays
+        last = spread(after(parts[1], *last), 1)
+        gate[:] = last
+        got = last
+    if chips > 2:
+        group = after(jnp.concatenate(parts[2:], axis=0), *last)
+        spread(group, 2)
+    return got + parts[1:], pieces, arrays
 
 
 def sum_slots(made, chips, members, slots):
@@ -1039,6 +1048,9 @@
     cot_rows = after(cot_rows, *arrays[::2])
     cot_parts = [to_partner(cot_rows, j) for j in range(shard_count)]
 
+    here, expert_inverse, router_pad, key_pos, rows_pos = lax.optimization_barrier(
+        (me, expert_inverse, router_pad, key_pos, rows_pos)
+    )
     h1, kv, w_in, w_out = project(
         pieces,
         arrays,
@@ -1046,7 +1058,7 @@
         shard_count,
         slots,
         dense_order,
-        me,
+        here,
         [tokens[m] for m in range(micros)],
         norm_gains,
     )
@@ -1060,7 +1072,7 @@
     for m in range(micros):
         query = after(q[m], *(cot_parts if m == 0 else obs[m - 1 : m]))
         parts = chip_kv[m]
-        swapped = parts if m == 0 else after(parts, obs[m - 1])
+        swapped = after(parts, q[0] if m == 0 else obs[m - 1])
         kvs.append(parts + [to_ctx(part, 1) for part in swapped])
         ob, log_total, x2, h2 = attend(
             query, kvs[m], rows_pos, key_pos, tokens[m], norm_gains, w_out
@@ -1089,7 +1101,7 @@
         xs.append(x)
     backs = [[to_partner(sent[m][j], j) for j in range(shard_count)] for m in range(micros)]
 
-    dxs, das, dqs, stats, own_grads, far_arrived = [], [], [], [], [], []
+    dxs, das, dqs, stats, own_grads = [], [], [], [], []
     for m in range(micros):
         here = after(me, zs[-1] if m == 0 else dqs[-1])
         dx, da, do, stat = merge(
@@ -1104,35 +1116,43 @@
             cut = slice(o * rows, (o + 1) * rows)
             part = wide(dkv_own[cut]) + wide(got[cut])
             parts.append(part if o == 0 else part.astype(low_type))
-        own_grads.append(parts[0])
-        far_arrived.append([to_chip(parts[o], -o) for o in range(1, chips)])
+        own_grads.append(parts)
         dxs.append(dx)
         das.append(da)
         dqs.append(dq)
         stats.append(stat)
 
-    dkvs = [
-        sum([wide(part) for part in far_arrived[m]], own_grads[m]).astype(low_type)
-        for m in range(micros)
+    far_sums = [
+        to_chip(jnp.concatenate([parts[o] for parts in own_grads], axis=0), -o)
+        for o in range(1, chips)
     ]
+    dkvs = []
+    for m in range(micros):
+        total = own_grads[m][0]
+        for part in far_sums:
+            total = total + wide(part[m * rows : (m + 1) * rows])
+        dkvs.append(total.astype(low_type))
 
     def other_core(parts):
         return [to_ctx(part, 1) for part in parts]
 
     da_others, dq_others = other_core(das), other_core(dqs)
-    expert_term = outer_blocks(
-        after(expert_inverse, dqs[-1]),
-        lambda k: (k * row_groups * ff_groups, ff_groups),
-        (width,) * 3,
-        [xs, xs, cs],
-        [dgs, dus, zs],
-        expert_blocks,
-    )
-    parts_back = query_back(after(w_in, expert_term), dqs)
-    expert_sum = lax.psum_scatter(
-        after(expert_term, dkvs[-1]), "ctx", scatter_dimension=0, tiled=True
-    )
-    here = after(me, parts_back)
+    expert_sums = []
+    for side in range(2):
+        term = outer_blocks(
+            expert_inverse if side == 0 else after(expert_inverse, *backs[-1]),
+            lambda k: (k * row_groups * ff_groups, ff_groups),
+            (width,) * 3,
+            side,
+            [xs, xs, cs],
+            [dgs, dus, zs],
+            expert_blocks,
+        )
+        expert_sums.append(lax.psum_scatter(term, "ctx", scatter_dimension=0, tiled=True))
+    parts_back = query_back(w_in, dqs)
+    made = produce(after(expert_inverse, dqs[0]), expert_all, zs, shard_count, width)
+    arrived = [to_partner(made[j], j) for j in range(shard_count)]
+    here = after(me, parts_back, *arrived)
     made = slot_blocks(
         chips,
         shard_count,
@@ -1146,7 +1166,6 @@
         obs + ob_others,
     )
     sums, got = sum_slots(made, chips, shard_count, slots)
-    dense_sum = sum_to_chips(sums)
     input_grad, gain_stat = input_back(
         after(tokens, *got[:2]), norm_gains, w_in, dxs, parts_back, dkvs
     )
@@ -1156,9 +1175,6 @@
     router_grad = stat_rows[:shard_count].T
     gains_grad = jnp.stack([stat_rows[experts_up + 1], stat_rows[experts_up]])
 
-    made = produce(after(expert_inverse, *got[:2]), expert_all, zs, shard_count, width)
-    made = after(list(made), *sums)
-    arrived = [to_partner(made[j], j) for j in range(shard_count)]
     outputs = []
     for m in range(micros):
         total = x2s[m]
@@ -1167,10 +1183,13 @@
         outputs.append(total)
 
     expert_grad, expert_new, expert_moment_new, expert_second_new = rotate(
-        expert_weight[0], after(expert_sum, *sums), expert_moment[0], expert_second[0], expert_left[0], expert_right[0]
-    )
+        expert_weight[0], after(expert_sums, *sums), expert_moment[0], expert_second[0], expert_left[0], expert_right[0]
+    )
+    last = [sums[0]] + [to_chip(sums[o], -o) for o in range(1, chips)]
+    last = after(last, expert_new)
+    dense_sum = sum([wide(part) for part in last[1:]], last[0])
     dense_grad, dense_new, dense_moment_new, dense_second_new = rotate(
-        dense_weight, after(dense_sum, expert_new), dense_moment, dense_second, dense_left, dense_right
+        dense_weight, [dense_sum], dense_moment, dense_second, dense_left, dense_right
     )
     gains_new, gains_moment_new, gains_second_new = adam(
         norm_gains, gains_grad, gains_moment, gains_second, gain_rate

time: 594 us -> 555 us (0.934)
  the two profiles are of different devices: /device:TPU:9 before, /device:TPU:0 now
where the time goes in v5:
time: 555 us; the launch traced here: 549 us
  Pallas kernels  212 us (38%)
  waiting for transfers between devices  157 us (28%)
  starting transfers between devices  116 us (21%)
  other arithmetic  29.8 us (5%)
  local copies, waits for them, and re-layouts  18.1 us (3%)
  between operations  15 us (3%)
    ppermute x15, waiting for transfers between devices, to_chip(): lax.ppermute(array, 'ctx', [(i, (i + 2 * offset) % count) for i in range(...  78.8 us
    ppermute x39, waiting for transfers between devices, to_partner(): return lax.ppermute(array, 'shard', [(i, i ^ offset) for i in range(count)])  66.5 us
    ppermute x39, starting transfers between devices, to_partner(): return lax.ppermute(array, 'shard', [(i, i ^ offset) for i in range(count)])  47.1 us
    ppermute x15, starting transfers between devices, to_chip(): lax.ppermute(array, 'ctx', [(i, (i + 2 * offset) % count) for i in range(...  44.8 us
    pallas_call x2, Pallas kernels, run_expert(): call(functools.partial(expert_kernel, sources, micro), tuple([shaped((row...  32.2 us
    pallas_call x2, Pallas kernels, attend_back(): call(functools.partial(attend_back_kernel, len(kv_parts)), (shaped((rows,...  29.9 us
    pallas_call x2, Pallas kernels, outer_blocks(): call(functools.partial(outer_kernel, place, widths, side), shaped((blocks...  29.6 us
    pallas_call x2, Pallas kernels, attend(): call(functools.partial(attend_kernel, len(kv_parts)), (shaped((rows, widt...  25.5 us
  transfers between devices with their start and end apart: 93, of which 29 were waited for; matrix products, arithmetic and copies ran while one was open for 7% of the time, Pallas kernels for 32%

profile of v5, /device:TPU:0, one launch (start us, length us, event | category | flops | bytes accessed | tf_op | source)
XLA Modules:
  0.0 548.8 jit_solution(14615874785399668884)
XLA Ops:
  35.4 15.2 %collective-permute-done.17 = bf16[4,192,256]{2,1,0:T(8,128)(2,1)S(1)} collective-permute-done((bf16[4,192,256]{2,1,0:T(8,128)(2,1)S(1)}, bf16[4,192,256]{2,1,0:T(8,128)(2,1)S(1)}, u32[]{:S(2)}, u32[]{:S(2)}) %collective-permute-start.17) | collective-permute-done | bytes 393248 | tf_op jit(solution)/shard_map/ppermute | solution.py:897
  61.2 11.4 %collective-permute-done.20.refs_23_ = bf16[8,192,256]{2,1,0:T(8,128)(2,1)} collective-permute-done((bf16[8,192,256]{2,1,0:T(8,128)(2,1)}, bf16[8,192,256]{2,1,0:T(8,128)(2,1)}, u32[]{:S(2)}, u32[]{:S(2)}) %collective-permute-start.20) | collective-permute-done | bytes 786464 | tf_op jit(solution)/shard_map/ppermute | solution.py:887
  83.2 7.0 %collective-permute-done.24.refs_27_ = bf16[8,96,256]{2,1,0:T(8,128)(2,1)} collective-permute-done((bf16[8,96,256]{2,1,0:T(8,128)(2,1)S(1)}, bf16[8,96,256]{2,1,0:T(8,128)(2,1)}, u32[]{:S(2)}, u32[]{:S(2)}) %collective-permute-start.24) | collective-permute-done | bytes 393248 | tf_op jit(solution)/shard_map/ppermute | solution.py:887
  104.7 13.9 %shard_map.349 = (bf16[256,1536]{1,0:T(8,128)(2,1)}, bf16[128,1024]{1,0:T(8,128)(2,1)}, bf16[128,1024]{1,0:T(8,128)(2,1)}, bf16[1536,2560]{1,0:T(8,128)(2,1)}, bf16[1536,1536]{1,0:T(8,128)(2,1)}) custom-call(s32[128]{0:T(128)} %order_ref.3, s32[2]{0:T(128)} %pad_add_fusion.me_ref, f32[128,1536]{1,0:T(8,128)} %get-tuple-element.279.refs_0_.x_ref, ...), custom_call_target="tpu_custom_call" | custom-call | flops 805306368 | bytes 25165824 | tf_op jit(solution)/shard_map/pallas_call | solution.py:193
  120.8 14.6 %collective-permute-done.31.refs_1_ = bf16[128,1024]{1,0:T(8,128)(2,1)S(1)} collective-permute-done((bf16[128,1024]{1,0:T(8,128)(2,1)}, bf16[128,1024]{1,0:T(8,128)(2,1)S(1)}, u32[]{:S(2)}, u32[]{:S(2)}) %collective-permute-start.31) | collective-permute-done | bytes 262176 | tf_op jit(solution)/shard_map/ppermute | solution.py:897
  145.2 7.5 %collective-permute-done.32.refs_2_ = bf16[128,1024]{1,0:T(8,128)(2,1)S(1)} collective-permute-done((bf16[128,1024]{1,0:T(8,128)(2,1)}, bf16[128,1024]{1,0:T(8,128)(2,1)S(1)}, u32[]{:S(2)}, u32[]{:S(2)}) %collective-permute-start.32) | collective-permute-done | bytes 262176 | tf_op jit(solution)/shard_map/ppermute | solution.py:897
  153.8 9.7 %collective-permute-start.38 = (bf16[128,1024]{1,0:T(8,128)(2,1)S(1)}, bf16[128,1024]{1,0:T(8,128)(2,1)}, u32[]{:S(2)}, u32[]{:S(2)}) collective-permute-start(bf16[128,1024]{1,0:T(8,128)(2,1)S(1)} %copy-done.57), channel_id=1, source_target_pairs={{0,8},{4,12},{8,16},{12,20},{16,24},{20,28},{24,0},{28,4},{1,9},{5... | collective-permute-start | bytes 786440 | tf_op jit(solution)/shard_map/ppermute | solution.py:897
  168.2 12.8 %shard_map.351 = (bf16[128,1536]{1,0:T(8,128)(2,1)}, f32[384,128]{1,0:T(8,128)}, f32[128,1536]{1,0:T(8,128)}, bf16[128,1536]{1,0:T(8,128)(2,1)}) custom-call(bf16[128,1536]{1,0:T(8,128)(2,1)} %get-tuple-element.159.q_ref, s32[128,1]{1,0:T(8,128)} %constant_dynamic-slice_fusion.rpos_ref, s32[1,1024]{1,0:T(1,128)} %bitcast.52, ...), custom_call_target="tpu_custom_call" | custom-call | flops 3221225472 | bytes 8388608 | tf_op jit(solution)/shard_map/pallas_call | solution.py:302
  188.1 12.7 %shard_map.352 = (bf16[128,1536]{1,0:T(8,128)(2,1)}, f32[384,128]{1,0:T(8,128)}, f32[128,1536]{1,0:T(8,128)}, bf16[128,1536]{1,0:T(8,128)(2,1)}) custom-call(bf16[128,1536]{1,0:T(8,128)(2,1)} %get-tuple-element.173.q_ref, s32[128,1]{1,0:T(8,128)} %constant_dynamic-slice_fusion.rpos_ref, s32[1,1024]{1,0:T(1,128)} %bitcast.53, ...), custom_call_target="tpu_custom_call" | custom-call | flops 3221225472 | bytes 8388608 | tf_op jit(solution)/shard_map/pallas_call | solution.py:302
  208.5 16.0 %shard_map.353 = (bf16[128,1664]{1,0:T(8,128)(2,1)}, bf16[128,1664]{1,0:T(8,128)(2,1)}, bf16[128,1664]{1,0:T(8,128)(2,1)}, bf16[128,1664]{1,0:T(8,128)(2,1)}, bf...) custom-call(s32[96]{0:T(128)} %select_reduce_fusion.order_ref, ...), custom_call_target="tpu_custom_call" | custom-call | flops 8053063680 | bytes 20971520 | tf_op jit(solution)/shard_map/pallas_call | solution.py:401
  225.9 16.2 %shard_map.354 = (bf16[128,1664]{1,0:T(8,128)(2,1)}, bf16[128,1664]{1,0:T(8,128)(2,1)}, bf16[128,1664]{1,0:T(8,128)(2,1)}, bf16[128,1664]{1,0:T(8,128)(2,1)}, bf...) custom-call(s32[96]{0:T(128)} %select_reduce_fusion.order_ref, ...), custom_call_target="tpu_custom_call" | custom-call | flops 8053063680 | bytes 20971520 | tf_op jit(solution)/shard_map/pallas_call | solution.py:401
  242.1 14.6 %shard_map.363 = bf16[96,192,128]{2,1,0:T(8,128)(2,1)} custom-call(s32[96]{0:T(128)} %select_reduce_fusion.order_ref, bf16[512,1536]{1,0:T(8,128)(2,1)} %get-tuple-element.232.refs_0_.refs_2_, bf16[512,1536]{1,0:T(8,128)(2,1)} %get-tuple-element.233.refs_1_.refs_3_, bf16[512,1536]{1,0:T(8,128)(2,1)} %get-tuple-element.232.refs_0_.refs_2_, ...), custom_call_target="tpu_custom_call" | custom-call | flops 4831838208 | bytes 20709376 | tf_op jit(solution)/shard_map/pallas_call | solution.py:521
  271.7 8.2 %collective-permute-done.55.refs_2_ = bf16[128,1664]{1,0:T(8,128)(2,1)S(1)} collective-permute-done((bf16[128,1664]{1,0:T(8,128)(2,1)}, bf16[128,1664]{1,0:T(8,128)(2,1)S(1)}, u32[]{:S(2)}, u32[]{:S(2)}) %collective-permute-start.55) | collective-permute-done | bytes 426016 | tf_op jit(solution)/shard_map/ppermute | solution.py:887
  286.9 15.2 %shard_map.356 = (bf16[128,1536]{1,0:T(8,128)(2,1)}, bf16[512,1024]{1,0:T(8,128)(2,1)}, bf16[512,1024]{1,0:T(8,128)(2,1)}) custom-call(bf16[128,1536]{1,0:T(8,128)(2,1)} %get-tuple-element.159.q_ref, s32[128,1]{1,0:T(8,128)} %constant_dynamic-slice_fusion.rpos_ref, s32[1,1024]{1,0:T(1,128)} %bitcast.54, ...), custom_call_target="tpu_custom_call" | custom-call | flops 8053063680 | bytes 8388608 | tf_op jit(solution)/shard_map/pallas_call | solution.py:733
  302.2 15.0 %shard_map.364 = bf16[96,192,128]{2,1,0:T(8,128)(2,1)} custom-call(s32[96]{0:T(128)} %select_reduce_fusion.order_ref, bf16[512,1536]{1,0:T(8,128)(2,1)} %get-tuple-element.232.refs_0_.refs_2_, bf16[512,1536]{1,0:T(8,128)(2,1)} %get-tuple-element.233.refs_1_.refs_3_, bf16[512,1536]{1,0:T(8,128)(2,1)} %get-tuple-element.232.refs_0_.refs_2_, ...), custom_call_target="tpu_custom_call" | custom-call | flops 4831838208 | bytes 20709376 | tf_op jit(solution)/shard_map/pallas_call | solution.py:521
  323.2 14.8 %shard_map.359 = (bf16[128,1536]{1,0:T(8,128)(2,1)}, bf16[512,1024]{1,0:T(8,128)(2,1)}, bf16[512,1024]{1,0:T(8,128)(2,1)}) custom-call(bf16[128,1536]{1,0:T(8,128)(2,1)} %get-tuple-element.173.q_ref, s32[128,1]{1,0:T(8,128)} %constant_dynamic-slice_fusion.rpos_ref, s32[1,1024]{1,0:T(1,128)} %bitcast.55, ...), custom_call_target="tpu_custom_call" | custom-call | flops 8053063680 | bytes 8388608 | tf_op jit(solution)/shard_map/pallas_call | solution.py:733
  353.4 8.7 %shard_map.357 = (bf16[256,1536]{1,0:T(8,128)(2,1)}, bf16[256,1536]{1,0:T(8,128)(2,1)}, bf16[256,1536]{1,0:T(8,128)(2,1)}, bf16[256,1536]{1,0:T(8,128)(2,1)}) custom-call(s32[96]{0:T(128)} %select_reduce_fusion.order_ref, bf16[96,192,256]{2,1,0:T(8,128)(2,1)} %all-gather.2.cloned.1.call-done.refs_8_.w_ref, ...), custom_call_target="tpu_custom_call" | custom-call | flops 3221225472 | bytes 8388608 | tf_op jit(solution)/shard_map/pallas_call | solution.py:454
  364.8 11.0 %collective-permute-done.71 = bf16[256,1024]{1,0:T(8,128)(2,1)} collective-permute-done((bf16[256,1024]{1,0:T(8,128)(2,1)}, bf16[256,1024]{1,0:T(8,128)(2,1)}, u32[]{:S(2)}, u32[]{:S(2)}) %collective-permute-start.71) | collective-permute-done | bytes 524320 | tf_op jit(solution)/shard_map/ppermute | solution.py:897
  377.0 27.1 %collective-permute-done.70 = bf16[256,1024]{1,0:T(8,128)(2,1)} collective-permute-done((bf16[256,1024]{1,0:T(8,128)(2,1)S(1)}, bf16[256,1024]{1,0:T(8,128)(2,1)}, u32[]{:S(2)}, u32[]{:S(2)}) %collective-permute-start.70) | collective-permute-done | bytes 524320 | tf_op jit(solution)/shard_map/ppermute | solution.py:897
  415.0 20.8 %shard_map.361 = (bf16[8,192,256]{2,1,0:T(8,128)(2,1)}, bf16[8,192,256]{2,1,0:T(8,128)(2,1)}, bf16[8,192,256]{2,1,0:T(8,128)(2,1)}, bf16[8,192,256]{2,1,0:T(8,12...) custom-call(s32[128]{0:T(128)} %order_ref.3, ...), custom_call_target="tpu_custom_call" | custom-call | flops 3221225472 | bytes 16777216 | tf_op jit(solution)/shard_map/pallas_call | solution.py:600
  443.4 13.1 %collective-permute-done.74 = bf16[8,192,256]{2,1,0:T(8,128)(2,1)S(1)} collective-permute-done((bf16[8,192,256]{2,1,0:T(8,128)(2,1)}, bf16[8,192,256]{2,1,0:T(8,128)(2,1)S(1)}, u32[]{:S(2)}, u32[]{:S(2)}) %collective-permute-start.74) | collective-permute-done | bytes 786464 | tf_op jit(solution)/shard_map/ppermute | solution.py:887
  460.3 7.1 %shard_map.362 = (f32[2,128,1536]{2,1,0:T(8,128)}, f32[8,1536]{1,0:T(8,128)}) custom-call(f32[2,128,1536]{2,1,0:T(8,128)} %x_ref, f32[2,1536]{1,0:T(2,128)} %gain_ref.9, bf16[1536,2560]{1,0:T(8,128)(2,1)} %get-tuple-element.156.w_ref, f32[128,1536]{1,0:T(8,128)} %get-tuple-element.223.refs_0_, f32[128,1536]{1,0:T(8,128)} %get-tuple-element.224.refs_1_, ...), custom_call_target="tpu_custom_call" | custom-call | flops 805306368 | bytes 14680064 | tf_op jit(solution)/shard_map/pallas_call | solution.py:816
  470.5 16.7 %collective-permute-start.86 = (f32[16,1536]{1,0:T(8,128)S(1)}, f32[16,1536]{1,0:T(8,128)S(1)}, u32[]{:S(2)}, u32[]{:S(2)}) collective-permute-start(f32[16,1536]{1,0:T(8,128)S(1)} %fusion.11), channel_id=1, source_target_pairs={{0,8},{4,12},{8,0},{12,4},{16,24},{20,28},{24,16},{28,20},{1,9},{5... | collective-permute-start | bytes 294920 | tf_op jit(solution)/shard_map/ppermute | solution.py:892
  515.9 15.1 %shard_map.365 = (f32[12,192,256]{2,1,0:T(8,128)}, f32[12,192,256]{2,1,0:T(8,128)}, f32[12,192,256]{2,1,0:T(8,128)}, f32[12,192,256]{2,1,0:T(8,128)}) custom-call(f32[12,192,256]{2,1,0:T(8,128)} %bitcast.40, f32[12,192,256]{2,1,0:T(8,128)} %bitcast.42, f32[12,192,256]{2,1,0:T(8,128)} %bitcast.43, f32[12,192,192]{2,1,0:T(8,128)} %bitcast.44, ...), custom_call_target="tpu_custom_call" | custom-call | flops 1056964608 | bytes 25165824 | tf_op jit(solution)/shard_map/pallas_call | solution.py:856
  (383 shorter events, 209.7 us)
Async XLA Ops:
  7.2 201.2 %all-gather.2.cloned.1.call-start = ((), (), s32[]{:S(2)}) async-start(), calls=%async_computation.2 | async-start | bytes 10616832 | tf_op jit(solution)/shard_map/all_gather | solution.py:1042
  21.4 29.2 %collective-permute-start.17 = (bf16[4,192,256]{2,1,0:T(8,128)(2,1)S(1)}, bf16[4,192,256]{2,1,0:T(8,128)(2,1)S(1)}, u32[]{:S(2)}, u32[]{:S(2)}) collective-permute-start(bf16[4,192,256]{2,1,0:T(8,128)(2,1)S(1)} %convert_element_type.224.refs_3_), channel_id=1, source_target_pairs={{0,16},{4,20},{8,24},{12,28},{16,0},{20,4},{24,8},{28,12},{1,17},{... | collective-permute-start | bytes 1179656 | tf_op jit(solution)/shard_map/ppermute | solution.py:897
  50.6 465.2 %reduce-scatter.3.cloned.1.call-start = ((), (), s32[]{:S(2)}) async-start(), calls=%async_computation.3 | async-start | bytes 5308416 | tf_op jit(solution)/shard_map/reduce_scatter | solution.py:1151
  93.8 59.5 %collective-permute-start.28 = (bf16[256,1664]{1,0:T(8,128)(2,1)}, bf16[256,1664]{1,0:T(8,128)(2,1)}, u32[]{:S(2)}, u32[]{:S(2)}) collective-permute-start(bf16[256,1664]{1,0:T(8,128)(2,1)} %bitcast.45), channel_id=1, source_target_pairs={{0,1},{1,0},{2,3},{3,2},{4,5},{5,4},{6,7},{7,6},{8,9},{9,8},{10,11... | collective-permute-start | bytes 2555912 | tf_op jit(solution)/shard_map/ppermute | solution.py:887
  94.3 59.2 %collective-permute-start.29 = (bf16[256,1664]{1,0:T(8,128)(2,1)}, bf16[256,1664]{1,0:T(8,128)(2,1)}, u32[]{:S(2)}, u32[]{:S(2)}) collective-permute-start(bf16[256,1664]{1,0:T(8,128)(2,1)} %bitcast.46), channel_id=1, source_target_pairs={{0,2},{1,3},{2,0},{3,1},{4,6},{5,7},{6,4},{7,5},{8,10},{9,11},{10,... | collective-permute-start | bytes 2555912 | tf_op jit(solution)/shard_map/ppermute | solution.py:887
  102.5 51.3 %collective-permute-start.30 = (bf16[256,1664]{1,0:T(8,128)(2,1)}, bf16[256,1664]{1,0:T(8,128)(2,1)}, u32[]{:S(2)}, u32[]{:S(2)}) collective-permute-start(bf16[256,1664]{1,0:T(8,128)(2,1)} %bitcast.47), channel_id=1, source_target_pairs={{0,3},{1,2},{2,1},{3,0},{4,7},{5,6},{6,5},{7,4},{8,11},{9,10},{10,... | collective-permute-start | bytes 2555912 | tf_op jit(solution)/shard_map/ppermute | solution.py:887
  118.7 34.0 %collective-permute-start.32 = (bf16[128,1024]{1,0:T(8,128)(2,1)}, bf16[128,1024]{1,0:T(8,128)(2,1)S(1)}, u32[]{:S(2)}, u32[]{:S(2)}) collective-permute-start(bf16[128,1024]{1,0:T(8,128)(2,1)} %get-tuple-element.164.refs_0_), channel_id=1, source_target_pairs={{0,16},{4,20},{8,24},{12,28},{16,0},{20,4},{24,8},{28,12},{1,17},{... | collective-permute-start | bytes 786440 | tf_op jit(solution)/shard_map/ppermute | solution.py:897
  153.8 27.2 %collective-permute-start.38 = (bf16[128,1024]{1,0:T(8,128)(2,1)S(1)}, bf16[128,1024]{1,0:T(8,128)(2,1)}, u32[]{:S(2)}, u32[]{:S(2)}) collective-permute-start(bf16[128,1024]{1,0:T(8,128)(2,1)S(1)} %copy-done.57), channel_id=1, source_target_pairs={{0,8},{4,12},{8,16},{12,20},{16,24},{20,28},{24,0},{28,4},{1,9},{5... | collective-permute-start | bytes 786440 | tf_op jit(solution)/shard_map/ppermute | solution.py:897
  256.7 259.1 %reduce-scatter.5.cloned.1.call-start = ((), (), s32[]{:S(2)}) async-start(), calls=%async_computation.4 | async-start | bytes 5308416 | tf_op jit(solution)/shard_map/reduce_scatter | solution.py:1151
  261.6 40.5 %collective-permute-start.60 = (bf16[128,1664]{1,0:T(8,128)(2,1)}, bf16[128,1664]{1,0:T(8,128)(2,1)S(1)}, u32[]{:S(2)}, u32[]{:S(2)}) collective-permute-start(bf16[128,1664]{1,0:T(8,128)(2,1)} %get-tuple-element.206), channel_id=1, source_target_pairs={{0,1},{1,0},{2,3},{3,2},{4,5},{5,4},{6,7},{7,6},{8,9},{9,8},{10,11... | collective-permute-start | bytes 1277960 | tf_op jit(solution)/shard_map/ppermute | solution.py:887
  262.5 39.6 %collective-permute-start.61 = (bf16[128,1664]{1,0:T(8,128)(2,1)S(1)}, bf16[128,1664]{1,0:T(8,128)(2,1)S(1)}, u32[]{:S(2)}, u32[]{:S(2)}) collective-permute-start(bf16[128,1664]{1,0:T(8,128)(2,1)S(1)} %copy-done.51), channel_id=1, source_target_pairs={{0,2},{1,3},{2,0},{3,1},{4,6},{5,7},{6,4},{7,5},{8,10},{9,11},{10,... | collective-permute-start | bytes 1277960 | tf_op jit(solution)/shard_map/ppermute | solution.py:887
  269.8 32.3 %collective-permute-start.62 = (bf16[128,1664]{1,0:T(8,128)(2,1)S(1)}, bf16[128,1664]{1,0:T(8,128)(2,1)S(1)}, u32[]{:S(2)}, u32[]{:S(2)}) collective-permute-start(bf16[128,1664]{1,0:T(8,128)(2,1)S(1)} %copy-done.50), channel_id=1, source_target_pairs={{0,3},{1,2},{2,1},{3,0},{4,7},{5,6},{6,5},{7,4},{8,11},{9,10},{10,... | collective-permute-start | bytes 1277960 | tf_op jit(solution)/shard_map/ppermute | solution.py:887
  343.7 32.1 %collective-permute-start.71 = (bf16[256,1024]{1,0:T(8,128)(2,1)}, bf16[256,1024]{1,0:T(8,128)(2,1)}, u32[]{:S(2)}, u32[]{:S(2)}) collective-permute-start(bf16[256,1024]{1,0:T(8,128)(2,1)} %pad_maximum_fusion.5), channel_id=1, source_target_pairs={{0,8},{4,12},{8,16},{12,20},{16,24},{20,28},{24,0},{28,4},{1,9},{5... | collective-permute-start | bytes 1572872 | tf_op jit(solution)/shard_map/ppermute | solution.py:897
  350.2 53.9 %collective-permute-start.70 = (bf16[256,1024]{1,0:T(8,128)(2,1)S(1)}, bf16[256,1024]{1,0:T(8,128)(2,1)}, u32[]{:S(2)}, u32[]{:S(2)}) collective-permute-start(bf16[256,1024]{1,0:T(8,128)(2,1)S(1)} %pad_maximum_fusion.4), channel_id=1, source_target_pairs={{0,16},{4,20},{8,24},{12,28},{16,0},{20,4},{24,8},{28,12},{1,17},{... | collective-permute-start | bytes 1572872 | tf_op jit(solution)/shard_map/ppermute | solution.py:897
  353.0 51.2 %collective-permute-start.69 = (bf16[256,1024]{1,0:T(8,128)(2,1)}, bf16[256,1024]{1,0:T(8,128)(2,1)}, u32[]{:S(2)}, u32[]{:S(2)}) collective-permute-start(bf16[256,1024]{1,0:T(8,128)(2,1)} %pad_maximum_fusion.3), channel_id=1, source_target_pairs={{0,24},{4,28},{8,0},{12,4},{16,8},{20,12},{24,16},{28,20},{1,25},{... | collective-permute-start | bytes 1572872 | tf_op jit(solution)/shard_map/ppermute | solution.py:897
  362.1 44.6 %collective-permute-start.59 = (bf16[256,1536]{1,0:T(8,128)(2,1)}, bf16[256,1536]{1,0:T(8,128)(2,1)}, u32[]{:S(2)}, u32[]{:S(2)}) collective-permute-start(bf16[256,1536]{1,0:T(8,128)(2,1)} %get-tuple-element.201), channel_id=1, source_target_pairs={{0,3},{1,2},{2,1},{3,0},{4,7},{5,6},{6,5},{7,4},{8,11},{9,10},{10,... | collective-permute-start | bytes 2359304 | tf_op jit(solution)/shard_map/ppermute | solution.py:887
  363.9 43.1 %collective-permute-start.58 = (bf16[256,1536]{1,0:T(8,128)(2,1)}, bf16[256,1536]{1,0:T(8,128)(2,1)}, u32[]{:S(2)}, u32[]{:S(2)}) collective-permute-start(bf16[256,1536]{1,0:T(8,128)(2,1)} %get-tuple-element.200), channel_id=1, source_target_pairs={{0,2},{1,3},{2,0},{3,1},{4,6},{5,7},{6,4},{7,5},{8,10},{9,11},{10,... | collective-permute-start | bytes 2359304 | tf_op jit(solution)/shard_map/ppermute | solution.py:887
  375.8 31.4 %collective-permute-start.57 = (bf16[256,1536]{1,0:T(8,128)(2,1)}, bf16[256,1536]{1,0:T(8,128)(2,1)S(1)}, u32[]{:S(2)}, u32[]{:S(2)}) collective-permute-start(bf16[256,1536]{1,0:T(8,128)(2,1)} %get-tuple-element.199), channel_id=1, source_target_pairs={{0,1},{1,0},{2,3},{3,2},{4,5},{5,4},{6,7},{7,6},{8,9},{9,8},{10,11... | collective-permute-start | bytes 2359304 | tf_op jit(solution)/shard_map/ppermute | solution.py:887
  442.2 45.0 %collective-permute-start.79 = (bf16[8,192,256]{2,1,0:T(8,128)(2,1)}, bf16[8,192,256]{2,1,0:T(8,128)(2,1)S(1)}, u32[]{:S(2)}, u32[]{:S(2)}) collective-permute-start(bf16[8,192,256]{2,1,0:T(8,128)(2,1)} %get-tuple-element.229), channel_id=1, source_target_pairs={{0,2},{1,3},{2,0},{3,1},{4,6},{5,7},{6,4},{7,5},{8,10},{9,11},{10,... | collective-permute-start | bytes 2359304 | tf_op jit(solution)/shard_map/ppermute | solution.py:887
  442.8 48.3 %collective-permute-start.82 = (bf16[8,192,256]{2,1,0:T(8,128)(2,1)}, bf16[8,192,256]{2,1,0:T(8,128)(2,1)S(1)}, u32[]{:S(2)}, u32[]{:S(2)}) collective-permute-start(bf16[8,192,256]{2,1,0:T(8,128)(2,1)} %get-tuple-element.231), channel_id=1, source_target_pairs={{0,1},{1,0},{2,3},{3,2},{4,5},{5,4},{6,7},{7,6},{8,9},{9,8},{10,11... | collective-permute-start | bytes 2359304 | tf_op jit(solution)/shard_map/ppermute | solution.py:887
  458.8 51.7 %collective-permute-start.76 = (bf16[4,192,256]{2,1,0:T(8,128)(2,1)}, bf16[4,192,256]{2,1,0:T(8,128)(2,1)}, u32[]{:S(2)}, u32[]{:S(2)}) collective-permute-start(bf16[4,192,256]{2,1,0:T(8,128)(2,1)} %add_convert_fusion.6), channel_id=1, source_target_pairs={{0,1},{1,0},{2,3},{3,2},{4,5},{5,4},{6,7},{7,6},{8,9},{9,8},{10,11... | collective-permute-start | bytes 1179656 | tf_op jit(solution)/shard_map/ppermute | solution.py:887
  468.5 29.9 %collective-permute-start.77 = (bf16[4,192,256]{2,1,0:T(8,128)(2,1)S(1)}, bf16[4,192,256]{2,1,0:T(8,128)(2,1)S(1)}, u32[]{:S(2)}, u32[]{:S(2)}) collective-permute-start(bf16[4,192,256]{2,1,0:T(8,128)(2,1)S(1)} %add_convert_fusion.5), channel_id=1, source_target_pairs={{0,2},{1,3},{2,0},{3,1},{4,6},{5,7},{6,4},{7,5},{8,10},{9,11},{10,... | collective-permute-start | bytes 1179656 | tf_op jit(solution)/shard_map/ppermute | solution.py:887
  499.3 31.7 %collective-permute-start.78 = (bf16[4,192,256]{2,1,0:T(8,128)(2,1)}, bf16[4,192,256]{2,1,0:T(8,128)(2,1)}, u32[]{:S(2)}, u32[]{:S(2)}) collective-permute-start(bf16[4,192,256]{2,1,0:T(8,128)(2,1)} %add_convert_fusion.4), channel_id=1, source_target_pairs={{0,24},{4,28},{8,0},{12,4},{16,8},{20,12},{24,16},{28,20},{1,25},{... | collective-permute-start | bytes 1179656 | tf_op jit(solution)/shard_map/ppermute | solution.py:897
  501.4 32.5 %collective-permute-start.81 = (bf16[4,192,256]{2,1,0:T(8,128)(2,1)}, bf16[4,192,256]{2,1,0:T(8,128)(2,1)S(1)}, u32[]{:S(2)}, u32[]{:S(2)}) collective-permute-start(bf16[4,192,256]{2,1,0:T(8,128)(2,1)} %add_convert_fusion.2), channel_id=1, source_target_pairs={{0,16},{4,20},{8,24},{12,28},{16,0},{20,4},{24,8},{28,12},{1,17},{... | collective-permute-start | bytes 1179656 | tf_op jit(solution)/shard_map/ppermute | solution.py:897
  (141 other events, 1779.9 us)
Sparse Core Ops, SparseCore 0:
  50.8 110.7 all-gather.1
  256.8 59.6 reduce-scatter.2
  318.8 88.2 reduce-scatter.4

commit v6 on v5

--- a/solution.py
+++ b/solution.py
@@ -466,66 +466,60 @@
     )(order, w, *zs)
 
 
-def outer_kernel(place, widths, side, order_ref, *refs):
-    count = len(widths)
-    micros = len(refs[:-3]) // (2 * count)
-    lefts = refs[: count * micros]
-    rights = refs[count * micros : 2 * count * micros]
-    out_ref, stage, sems = refs[-3:]
+def outer_kernel(groups, col_groups, order_ref, *refs):
+    micros = len(refs[:-4]) // (len(groups) + 2)
+    lefts = [refs[i * micros : (i + 1) * micros] for i in range(2)]
+    rights = [refs[(2 + i) * micros : (3 + i) * micros] for i in range(len(groups))]
+    out_ref, turned, stage, sems = refs[-4:]
+    rows = rights[0][0].shape[0]
+    width = turned.shape[1]
     span = 2 * BR
-    steps = []
-    for k in range(count):
-        for p in range(widths[k] // span):
-            steps.append((k, p))
-
-    def wait_stage(slot, cols):
-        wait_bytes(stage.at[slot, :, pl.ds(0, cols)], sems.at[slot])
-
-    used = [None, None]
+    for side in range(2):
+        for m in range(micros):
+            for r in range(0, rows, LANES):
+                part = lefts[side][m][r : r + LANES, :width]
+                turned[side, :, m * rows + r : m * rows + r + LANES] = part.T
+    row_groups = width // BR
+    steps = [(k, p) for k in range(len(groups)) for p in range(width // span)]
     for n, (k, p) in enumerate(steps):
         slot = n % 2
-        cols = rights[k * micros].shape[-1]
-        if used[slot] is not None:
-            wait_stage(slot, used[slot])
-        used[slot] = cols // 2
+        if n >= 2:
+            wait_bytes(stage.at[slot], sems.at[slot])
         cut = slice(p * span, (p + 1) * span)
         made = 0.0
         for m in range(micros):
-            left = lefts[k * micros + m][:, cut]
-            right = jnp.concatenate(
-                [
-                    rights[k * micros + m][:, start : start + LANES]
-                    for start in range(side * LANES, cols, BC)
-                ],
-                axis=1,
-            )
-            made = made + dot(left, right, TN)
-        stage[slot, :, : cols // 2] = made.astype(low_type)
-        first, row_step = place(k)
+            left = turned[groups[k], cut, m * rows : (m + 1) * rows]
+            made = made + dot(left, rights[k][m][...])
+        stage[slot] = made.astype(low_type)
         for half in range(2):
-            for b in range(cols // BC):
+            for b in range(col_groups):
+                number = (k * row_groups + 2 * p + half) * col_groups + b
                 pltpu.make_async_copy(
-                    stage.at[slot, pl.ds(half * BR, BR), pl.ds(b * LANES, LANES)],
-                    out_ref.at[order_ref[first + (2 * p + half) * row_step + b]],
+                    stage.at[slot, pl.ds(half * BR, BR), pl.ds(b * BC, BC)],
+                    out_ref.at[order_ref[number]],
                     sems.at[slot],
                 ).start()
     for slot in range(2):
-        if used[slot] is not None:
-            wait_stage(slot, used[slot])
-
-
-def outer_blocks(order, place, widths, side, lefts, rights, blocks):
-    widest = max(r[0].shape[-1] for r in rights)
-    rows = sum(l.shape[0] for l in lefts[0])
-    flat = [l for group in lefts for l in group] + [r for group in rights for r in group]
+        wait_bytes(stage.at[slot], sems.at[slot])
+
+
+def outer_blocks(order, width, groups, lefts, rights):
+    flat = [part for group in lefts + rights for part in group]
+    rows = sum(part.shape[0] for part in rights[0])
+    cols = rights[0][0].shape[1]
+    blocks = len(groups) * width * cols // (BR * BC)
     return call(
-        functools.partial(outer_kernel, place, widths, side),
-        shaped((blocks, BR, LANES), low_type),
+        functools.partial(outer_kernel, groups, cols // BC),
+        shaped((blocks, BR, BC), low_type),
         [in_smem] + [in_vmem] * len(flat),
         in_any,
-        [pltpu.VMEM((2, 2 * BR, widest // 2), low_type), pltpu.SemaphoreType.DMA((2,))],
-        rows * blocks * BR * BC,
-        blocks * BR * BC + sum(f.size * 2 for f in flat),
+        [
+            pltpu.VMEM((2, width, rows), low_type),
+            pltpu.VMEM((2, 2 * BR, cols), low_type),
+            pltpu.SemaphoreType.DMA((2,)),
+        ],
+        2 * rows * blocks * BR * BC,
+        blocks * BR * BC * 2 + sum(f.size * 2 for f in flat),
     )(order, *flat)
 
 
@@ -959,7 +953,7 @@
     return got + parts[1:], pieces, arrays
 
 
-def sum_slots(made, chips, members, slots):
+def sum_slots(made, ready, chips, members, slots):
     sums, first_got = [], []
     for offset in range(chips):
         sent, kept = made[offset]
@@ -967,7 +961,7 @@
         total = wide(kept[:slots])
         if members == 4:
             first, second = hops[0], keeps[1]
-            got = to_partner(sent, first)
+            got = after(to_partner(sent, first), ready)
             total = total + wide(got[:slots])
             relay = (wide(kept[slots:]) + wide(got[slots:])).astype(low_type)
             total = total + wide(to_partner(relay, second))
@@ -1046,7 +1040,7 @@
     cot_rows = jnp.concatenate([cotangent.astype(low_type), hits], axis=2)
     cot_rows = cot_rows.reshape(micros * rows, width + LANES)
     cot_rows = after(cot_rows, *arrays[::2])
-    cot_parts = [to_partner(cot_rows, j) for j in range(shard_count)]
+    cot_parts = [to_partner(cot_rows, j) for j in range(min(3, shard_count))]
 
     here, expert_inverse, router_pad, key_pos, rows_pos = lax.optimization_barrier(
         (me, expert_inverse, router_pad, key_pos, rows_pos)
@@ -1069,8 +1063,10 @@
     for m in range(micros):
         own = kv[m] if m == 0 else after(kv[m], chip_kv[m - 1][1 % chips])
         chip_kv.append(from_chips(own, chips))
+    late_rows = after(cot_rows, *chip_kv[0])
+    cot_parts = cot_parts + [to_partner(late_rows, j) for j in range(3, shard_count)]
     for m in range(micros):
-        query = after(q[m], *(cot_parts if m == 0 else obs[m - 1 : m]))
+        query = after(q[m], *(cot_parts[:3] if m == 0 else obs[m - 1 : m]))
         parts = chip_kv[m]
         swapped = after(parts, q[0] if m == 0 else obs[m - 1])
         kvs.append(parts + [to_ctx(part, 1) for part in swapped])
@@ -1137,20 +1133,12 @@
         return [to_ctx(part, 1) for part in parts]
 
     da_others, dq_others = other_core(das), other_core(dqs)
-    expert_sums = []
-    for side in range(2):
-        term = outer_blocks(
-            expert_inverse if side == 0 else after(expert_inverse, *backs[-1]),
-            lambda k: (k * row_groups * ff_groups, ff_groups),
-            (width,) * 3,
-            side,
-            [xs, xs, cs],
-            [dgs, dus, zs],
-            expert_blocks,
-        )
-        expert_sums.append(lax.psum_scatter(term, "ctx", scatter_dimension=0, tiled=True))
+    expert_term = outer_blocks(
+        after(expert_inverse, *backs[0]), width, (0, 0, 1), [xs, cs], [dgs, dus, zs]
+    )
+    expert_sum = lax.psum_scatter(expert_term, "ctx", scatter_dimension=0, tiled=True)
     parts_back = query_back(w_in, dqs)
-    made = produce(after(expert_inverse, dqs[0]), expert_all, zs, shard_count, width)
+    made = produce(after(expert_inverse, own_grads[-1][1 % chips]), expert_all, zs, shard_count, width)
     arrived = [to_partner(made[j], j) for j in range(shard_count)]
     here = after(me, parts_back, *arrived)
     made = slot_blocks(
@@ -1165,13 +1153,13 @@
         dkvs + other_core(dkvs),
         obs + ob_others,
     )
-    sums, got = sum_slots(made, chips, shard_count, slots)
     input_grad, gain_stat = input_back(
-        after(tokens, *got[:2]), norm_gains, w_in, dxs, parts_back, dkvs
-    )
+        after(tokens, made[0][0]), norm_gains, w_in, dxs, parts_back, dkvs
+    )
+    sums, got = sum_slots(made, input_grad, chips, shard_count, slots)
     experts_up = stats[0].shape[0] - 8
     stat_rows = jnp.concatenate([sum(stats)[: experts_up + 1], gain_stat[:7]], axis=0)
-    stat_rows = sum_all(stat_rows)
+    stat_rows = sum_all(after(stat_rows, *sums))
     router_grad = stat_rows[:shard_count].T
     gains_grad = jnp.stack([stat_rows[experts_up + 1], stat_rows[experts_up]])
 
@@ -1183,7 +1171,7 @@
         outputs.append(total)
 
     expert_grad, expert_new, expert_moment_new, expert_second_new = rotate(
-        expert_weight[0], after(expert_sums, *sums), expert_moment[0], expert_second[0], expert_left[0], expert_right[0]
+        expert_weight[0], [after(expert_sum, *sums)], expert_moment[0], expert_second[0], expert_left[0], expert_right[0]
     )
     last = [sums[0]] + [to_chip(sums[o], -o) for o in range(1, chips)]
     last = after(last, expert_new)

time: 555 us -> 586 us (1.056)
  waiting for transfers between devices: 157 us -> 211 us
  Pallas kernels: 212 us -> 200 us
  other arithmetic: 29.8 us -> 21.6 us
  starting transfers between devices: 116 us -> 109 us
    ppermute x39, waiting for transfers between devices: 66.5 us -> 92.6 us  [to_partner(): return lax.ppermute(array, 'shard', [(i, i ^ offset) for i in range(count)])]
    ppermute x15, waiting for transfers between devices: 78.8 us -> 104 us  [to_chip(): lax.ppermute(array, 'ctx', [(i, (i + 2 * offset) % count) for i in range(...]
    pallas_call x2 -> x1, Pallas kernels: 29.6 us -> 17.9 us  [outer_blocks(): call(functools.partial(outer_kernel, groups, cols // BC), shaped((blocks,...]
    ppermute x15, starting transfers between devices: 44.8 us -> 36.8 us  [to_chip(): lax.ppermute(array, 'ctx', [(i, (i + 2 * offset) % count) for i in range(...]
    unnamed x144 -> x164, local copies, waits for them, and re-layouts: 6.66 us -> 13.2 us
  transfers between devices with their start and end apart: 93 -> 92, of which waited for: 29 -> 29; matrix products, arithmetic and copies ran while one was open for 7% -> 5% of each run, Pallas kernels for 32% -> 30%
where the time goes in v6:
time: 586 us; the launch traced here: 580 us
  waiting for transfers between devices  211 us (36%)
  Pallas kernels  200 us (34%)
  starting transfers between devices  109 us (19%)
  local copies, waits for them, and re-layouts  21.9 us (4%)
  other arithmetic  21.6 us (4%)
  between operations  15.7 us (3%)
    ppermute x15, waiting for transfers between devices, to_chip(): lax.ppermute(array, 'ctx', [(i, (i + 2 * offset) % count) for i in range(...  104 us
    ppermute x39, waiting for transfers between devices, to_partner(): return lax.ppermute(array, 'shard', [(i, i ^ offset) for i in range(count)])  92.6 us
    ppermute x39, starting transfers between devices, to_partner(): return lax.ppermute(array, 'shard', [(i, i ^ offset) for i in range(count)])  49.8 us
    ppermute x15, starting transfers between devices, to_chip(): lax.ppermute(array, 'ctx', [(i, (i + 2 * offset) % count) for i in range(...  36.8 us
    pallas_call x2, Pallas kernels, run_expert(): call(functools.partial(expert_kernel, sources, micro), tuple([shaped((row...  32.2 us
    pallas_call x2, Pallas kernels, attend_back(): call(functools.partial(attend_back_kernel, len(kv_parts)), (shaped((rows,...  29.9 us
    pallas_call x2, Pallas kernels, attend(): call(functools.partial(attend_kernel, len(kv_parts)), (shaped((rows, widt...  25.5 us
    ppermute x36, starting transfers between devices, to_ctx(): return lax.ppermute(array, 'ctx', [(i, i ^ offset) for i in range(count)])  22.6 us
  transfers between devices with their start and end apart: 92, of which 29 were waited for; matrix products, arithmetic and copies ran while one was open for 5% of the time, Pallas kernels for 30%

profile of v6, /device:TPU:0, one launch (start us, length us, event | category | flops | bytes accessed | tf_op | source)
XLA Modules:
  0.0 579.7 jit_solution(10395553654751641244)
XLA Ops:
  36.8 13.8 %collective-permute-done.17 = bf16[4,192,256]{2,1,0:T(8,128)(2,1)S(1)} collective-permute-done((bf16[4,192,256]{2,1,0:T(8,128)(2,1)S(1)}, bf16[4,192,256]{2,1,0:T(8,128)(2,1)S(1)}, u32[]{:S(2)}, u32[]{:S(2)}) %collective-permute-start.17) | collective-permute-done | bytes 393248 | tf_op jit(solution)/shard_map/ppermute | solution.py:891
  59.0 13.2 %collective-permute-done.20.refs_23_ = bf16[8,192,256]{2,1,0:T(8,128)(2,1)S(1)} collective-permute-done((bf16[8,192,256]{2,1,0:T(8,128)(2,1)}, bf16[8,192,256]{2,1,0:T(8,128)(2,1)S(1)}, u32[]{:S(2)}, u32[]{:S(2)}) %collective-permute-start.20) | collective-permute-done | bytes 786464 | tf_op jit(solution)/shard_map/ppermute | solution.py:881
  102.7 13.2 %shard_map.349 = (bf16[256,1536]{1,0:T(8,128)(2,1)}, bf16[128,1024]{1,0:T(8,128)(2,1)}, bf16[128,1024]{1,0:T(8,128)(2,1)}, bf16[1536,2560]{1,0:T(8,128)(2,1)}, bf16[1536,1536]{1,0:T(8,128)(2,1)}) custom-call(s32[128]{0:T(128)} %order_ref.3, s32[2]{0:T(128)} %pad_add_fusion.me_ref, f32[128,1536]{1,0:T(8,128)} %get-tuple-element.289.refs_0_.x_ref, ...), custom_call_target="tpu_custom_call" | custom-call | flops 805306368 | bytes 25165824 | tf_op jit(solution)/shard_map/pallas_call | solution.py:193
  132.7 19.6 %collective-permute-done.31.refs_2_ = bf16[128,1024]{1,0:T(8,128)(2,1)S(1)} collective-permute-done((bf16[128,1024]{1,0:T(8,128)(2,1)}, bf16[128,1024]{1,0:T(8,128)(2,1)S(1)}, u32[]{:S(2)}, u32[]{:S(2)}) %collective-permute-start.31) | collective-permute-done | bytes 262176 | tf_op jit(solution)/shard_map/ppermute | solution.py:891
  153.4 10.0 %collective-permute-start.37 = (bf16[128,1024]{1,0:T(8,128)(2,1)S(1)}, bf16[128,1024]{1,0:T(8,128)(2,1)}, u32[]{:S(2)}, u32[]{:S(2)}) collective-permute-start(bf16[128,1024]{1,0:T(8,128)(2,1)S(1)} %copy-done.65), channel_id=1, source_target_pairs={{0,8},{4,12},{8,16},{12,20},{16,24},{20,28},{24,0},{28,4},{1,9},{5... | collective-permute-start | bytes 786440 | tf_op jit(solution)/shard_map/ppermute | solution.py:891
  168.2 12.8 %shard_map.351 = (bf16[128,1536]{1,0:T(8,128)(2,1)}, f32[384,128]{1,0:T(8,128)}, f32[128,1536]{1,0:T(8,128)}, bf16[128,1536]{1,0:T(8,128)(2,1)}) custom-call(bf16[128,1536]{1,0:T(8,128)(2,1)} %get-tuple-element.164.q_ref, s32[128,1]{1,0:T(8,128)} %constant_dynamic-slice_fusion.rpos_ref, s32[1,1024]{1,0:T(1,128)} %bitcast.51, ...), custom_call_target="tpu_custom_call" | custom-call | flops 3221225472 | bytes 8388608 | tf_op jit(solution)/shard_map/pallas_call | solution.py:302
  189.4 12.7 %shard_map.352 = (bf16[128,1536]{1,0:T(8,128)(2,1)}, f32[384,128]{1,0:T(8,128)}, f32[128,1536]{1,0:T(8,128)}, bf16[128,1536]{1,0:T(8,128)(2,1)}) custom-call(bf16[128,1536]{1,0:T(8,128)(2,1)} %get-tuple-element.177.q_ref, s32[128,1]{1,0:T(8,128)} %constant_dynamic-slice_fusion.rpos_ref, s32[1,1024]{1,0:T(1,128)} %bitcast.52, ...), custom_call_target="tpu_custom_call" | custom-call | flops 3221225472 | bytes 8388608 | tf_op jit(solution)/shard_map/pallas_call | solution.py:302
  202.2 11.8 %collective-permute-done.47.refs_1_ = bf16[128,1536]{1,0:T(8,128)(2,1)} collective-permute-done((bf16[128,1536]{1,0:T(8,128)(2,1)}, bf16[128,1536]{1,0:T(8,128)(2,1)}, u32[]{:S(2)}, u32[]{:S(2)}) %collective-permute-start.47) | collective-permute-done | bytes 393248 | tf_op jit(solution)/shard_map/ppermute | solution.py:881
  225.5 16.0 %shard_map.353 = (bf16[128,1664]{1,0:T(8,128)(2,1)}, bf16[128,1664]{1,0:T(8,128)(2,1)}, bf16[128,1664]{1,0:T(8,128)(2,1)}, bf16[128,1664]{1,0:T(8,128)(2,1)}, bf...) custom-call(s32[96]{0:T(128)} %select_reduce_fusion.order_ref, ...), custom_call_target="tpu_custom_call" | custom-call | flops 8053063680 | bytes 20971520 | tf_op jit(solution)/shard_map/pallas_call | solution.py:401
  245.8 16.2 %shard_map.354 = (bf16[128,1664]{1,0:T(8,128)(2,1)}, bf16[128,1664]{1,0:T(8,128)(2,1)}, bf16[128,1664]{1,0:T(8,128)(2,1)}, bf16[128,1664]{1,0:T(8,128)(2,1)}, bf...) custom-call(s32[96]{0:T(128)} %select_reduce_fusion.order_ref, ...), custom_call_target="tpu_custom_call" | custom-call | flops 8053063680 | bytes 20971520 | tf_op jit(solution)/shard_map/pallas_call | solution.py:401
  262.4 17.9 %shard_map.363 = bf16[96,192,256]{2,1,0:T(8,128)(2,1)} custom-call(s32[96]{0:T(128)} %select_reduce_fusion.order_ref, bf16[512,1536]{1,0:T(8,128)(2,1)} %get-tuple-element.243.refs_0_, bf16[512,1536]{1,0:T(8,128)(2,1)} %get-tuple-element.244.refs_1_, bf16[512,1664]{1,0:T(8,128)(2,1)} %get-tuple-element.245.refs_2_, ...), custom_call_target="tpu_custom_call" | custom-call | flops 9663676416 | bytes 22282240 | tf_op jit(solution)/shard_map/pallas_call | solution.py:511
  291.4 15.0 %shard_map.356 = (bf16[128,1536]{1,0:T(8,128)(2,1)}, bf16[512,1024]{1,0:T(8,128)(2,1)}, bf16[512,1024]{1,0:T(8,128)(2,1)}) custom-call(bf16[128,1536]{1,0:T(8,128)(2,1)} %get-tuple-element.164.q_ref, s32[128,1]{1,0:T(8,128)} %constant_dynamic-slice_fusion.rpos_ref, s32[1,1024]{1,0:T(1,128)} %bitcast.53, ...), custom_call_target="tpu_custom_call" | custom-call | flops 8053063680 | bytes 8388608 | tf_op jit(solution)/shard_map/pallas_call | solution.py:727
  313.6 14.9 %shard_map.358 = (bf16[128,1536]{1,0:T(8,128)(2,1)}, bf16[512,1024]{1,0:T(8,128)(2,1)}, bf16[512,1024]{1,0:T(8,128)(2,1)}) custom-call(bf16[128,1536]{1,0:T(8,128)(2,1)} %get-tuple-element.177.q_ref, s32[128,1]{1,0:T(8,128)} %constant_dynamic-slice_fusion.rpos_ref, s32[1,1024]{1,0:T(1,128)} %bitcast.54, ...), custom_call_target="tpu_custom_call" | custom-call | flops 8053063680 | bytes 8388608 | tf_op jit(solution)/shard_map/pallas_call | solution.py:727
  341.7 8.6 %shard_map.359 = (bf16[256,1536]{1,0:T(8,128)(2,1)}, bf16[256,1536]{1,0:T(8,128)(2,1)}, bf16[256,1536]{1,0:T(8,128)(2,1)}, bf16[256,1536]{1,0:T(8,128)(2,1)}) custom-call(s32[96]{0:T(128)} %select_reduce_fusion.order_ref, bf16[96,192,256]{2,1,0:T(8,128)(2,1)} %all-gather.2.cloned.1.call-done.refs_8_.w_ref, ...), custom_call_target="tpu_custom_call" | custom-call | flops 3221225472 | bytes 8388608 | tf_op jit(solution)/shard_map/pallas_call | solution.py:454
  357.1 10.5 %collective-permute-done.71 = bf16[256,1024]{1,0:T(8,128)(2,1)} collective-permute-done((bf16[256,1024]{1,0:T(8,128)(2,1)}, bf16[256,1024]{1,0:T(8,128)(2,1)}, u32[]{:S(2)}, u32[]{:S(2)}) %collective-permute-start.71) | collective-permute-done | bytes 524320 | tf_op jit(solution)/shard_map/ppermute | solution.py:891
  369.1 32.6 %collective-permute-done.70 = bf16[256,1024]{1,0:T(8,128)(2,1)S(1)} collective-permute-done((bf16[256,1024]{1,0:T(8,128)(2,1)S(1)}, bf16[256,1024]{1,0:T(8,128)(2,1)S(1)}, u32[]{:S(2)}, u32[]{:S(2)}) %collective-permute-start.70) | collective-permute-done | bytes 524320 | tf_op jit(solution)/shard_map/ppermute | solution.py:891
  401.7 7.3 %collective-permute-done.69 = bf16[256,1024]{1,0:T(8,128)(2,1)S(1)} collective-permute-done((bf16[256,1024]{1,0:T(8,128)(2,1)S(1)}, bf16[256,1024]{1,0:T(8,128)(2,1)S(1)}, u32[]{:S(2)}, u32[]{:S(2)}) %collective-permute-start.69) | collective-permute-done | bytes 524320 | tf_op jit(solution)/shard_map/ppermute | solution.py:891
  421.5 20.7 %shard_map.361 = (bf16[8,192,256]{2,1,0:T(8,128)(2,1)}, bf16[8,192,256]{2,1,0:T(8,128)(2,1)}, bf16[8,192,256]{2,1,0:T(8,128)(2,1)}, bf16[8,192,256]{2,1,0:T(8,12...) custom-call(s32[128]{0:T(128)} %order_ref.3, ...), custom_call_target="tpu_custom_call" | custom-call | flops 3221225472 | bytes 16777216 | tf_op jit(solution)/shard_map/pallas_call | solution.py:594
  454.4 8.5 %collective-permute-done.74 = bf16[8,192,256]{2,1,0:T(8,128)(2,1)} collective-permute-done((bf16[8,192,256]{2,1,0:T(8,128)(2,1)}, bf16[8,192,256]{2,1,0:T(8,128)(2,1)}, u32[]{:S(2)}, u32[]{:S(2)}) %collective-permute-start.74) | collective-permute-done | bytes 786464 | tf_op jit(solution)/shard_map/ppermute | solution.py:881
  467.1 12.6 %collective-permute-done.79 = bf16[8,192,256]{2,1,0:T(8,128)(2,1)S(1)} collective-permute-done((bf16[8,192,256]{2,1,0:T(8,128)(2,1)}, bf16[8,192,256]{2,1,0:T(8,128)(2,1)S(1)}, u32[]{:S(2)}, u32[]{:S(2)}) %collective-permute-start.79) | collective-permute-done | bytes 786464 | tf_op jit(solution)/shard_map/ppermute | solution.py:881
  489.0 8.1 %collective-permute-done.80 = bf16[4,192,256]{2,1,0:T(8,128)(2,1)S(1)} collective-permute-done((bf16[4,192,256]{2,1,0:T(8,128)(2,1)S(1)}, bf16[4,192,256]{2,1,0:T(8,128)(2,1)S(1)}, u32[]{:S(2)}, u32[]{:S(2)}) %collective-permute-start.80) | collective-permute-done | bytes 393248 | tf_op jit(solution)/shard_map/ppermute | solution.py:881
  500.2 15.2 %collective-permute-start.86 = (f32[16,1536]{1,0:T(8,128)S(1)}, f32[16,1536]{1,0:T(8,128)S(1)}, u32[]{:S(2)}, u32[]{:S(2)}) collective-permute-start(f32[16,1536]{1,0:T(8,128)S(1)} %add.332), channel_id=1, source_target_pairs={{0,8},{4,12},{8,0},{12,4},{16,24},{20,28},{24,16},{28,20},{1,9},{5... | collective-permute-start | bytes 294920 | tf_op jit(solution)/shard_map/ppermute | solution.py:886
  536.7 15.1 %shard_map.364 = (f32[12,192,256]{2,1,0:T(8,128)}, f32[12,192,256]{2,1,0:T(8,128)}, f32[12,192,256]{2,1,0:T(8,128)}, f32[12,192,256]{2,1,0:T(8,128)}) custom-call(f32[12,192,256]{2,1,0:T(8,128)} %bitcast.40, f32[12,192,256]{2,1,0:T(8,128)} %bitcast.42, f32[12,192,256]{2,1,0:T(8,128)} %bitcast.43, f32[12,192,192]{2,1,0:T(8,128)} %bitcast.44, ...), custom_call_target="tpu_custom_call" | custom-call | flops 1056964608 | bytes 25165824 | tf_op jit(solution)/shard_map/pallas_call | solution.py:850
  551.8 13.7 %collective-permute-done.81 = bf16[4,192,256]{2,1,0:T(8,128)(2,1)S(1)} collective-permute-done((bf16[4,192,256]{2,1,0:T(8,128)(2,1)S(1)}, bf16[4,192,256]{2,1,0:T(8,128)(2,1)S(1)}, u32[]{:S(2)}, u32[]{:S(2)}) %collective-permute-start.81) | collective-permute-done | bytes 393248 | tf_op jit(solution)/shard_map/ppermute | solution.py:891
  (399 shorter events, 224.4 us)
Async XLA Ops:
  7.2 218.3 %all-gather.2.cloned.1.call-start = ((), (), s32[]{:S(2)}) async-start(), calls=%async_computation.1 | async-start | bytes 10616832 | tf_op jit(solution)/shard_map/all_gather | solution.py:1036
  21.5 29.1 %collective-permute-start.17 = (bf16[4,192,256]{2,1,0:T(8,128)(2,1)S(1)}, bf16[4,192,256]{2,1,0:T(8,128)(2,1)S(1)}, u32[]{:S(2)}, u32[]{:S(2)}) collective-permute-start(bf16[4,192,256]{2,1,0:T(8,128)(2,1)S(1)} %convert_element_type.224.refs_3_), channel_id=1, source_target_pairs={{0,16},{4,20},{8,24},{12,28},{16,0},{20,4},{24,8},{28,12},{1,17},{... | collective-permute-start | bytes 1179656 | tf_op jit(solution)/shard_map/ppermute | solution.py:891
  50.6 486.1 %reduce-scatter.2.cloned.1.call-start = ((), (), s32[]{:S(2)}) async-start(), calls=%async_computation.2 | async-start | bytes 10616832 | tf_op jit(solution)/shard_map/reduce_scatter | solution.py:1139
  94.8 58.1 %collective-permute-start.28 = (bf16[256,1664]{1,0:T(8,128)(2,1)S(1)}, bf16[256,1664]{1,0:T(8,128)(2,1)}, u32[]{:S(2)}, u32[]{:S(2)}) collective-permute-start(bf16[256,1664]{1,0:T(8,128)(2,1)S(1)} %bitcast.45), channel_id=1, source_target_pairs={{0,1},{1,0},{2,3},{3,2},{4,5},{5,4},{6,7},{7,6},{8,9},{9,8},{10,11... | collective-permute-start | bytes 2555912 | tf_op jit(solution)/shard_map/ppermute | solution.py:881
  97.2 56.2 %collective-permute-start.29 = (bf16[256,1664]{1,0:T(8,128)(2,1)S(1)}, bf16[256,1664]{1,0:T(8,128)(2,1)}, u32[]{:S(2)}, u32[]{:S(2)}) collective-permute-start(bf16[256,1664]{1,0:T(8,128)(2,1)S(1)} %bitcast.46), channel_id=1, source_target_pairs={{0,2},{1,3},{2,0},{3,1},{4,6},{5,7},{6,4},{7,5},{8,10},{9,11},{10,... | collective-permute-start | bytes 2555912 | tf_op jit(solution)/shard_map/ppermute | solution.py:881
  116.0 36.3 %collective-permute-start.31 = (bf16[128,1024]{1,0:T(8,128)(2,1)}, bf16[128,1024]{1,0:T(8,128)(2,1)S(1)}, u32[]{:S(2)}, u32[]{:S(2)}) collective-permute-start(bf16[128,1024]{1,0:T(8,128)(2,1)} %get-tuple-element.169.refs_0_), channel_id=1, source_target_pairs={{0,16},{4,20},{8,24},{12,28},{16,0},{20,4},{24,8},{28,12},{1,17},{... | collective-permute-start | bytes 786440 | tf_op jit(solution)/shard_map/ppermute | solution.py:891
  118.8 33.5 %collective-permute-start.32 = (bf16[128,1024]{1,0:T(8,128)(2,1)}, bf16[128,1024]{1,0:T(8,128)(2,1)S(1)}, u32[]{:S(2)}, u32[]{:S(2)}) collective-permute-start(bf16[128,1024]{1,0:T(8,128)(2,1)} %get-tuple-element.169.refs_0_), channel_id=1, source_target_pairs={{0,24},{4,28},{8,0},{12,4},{16,8},{20,12},{24,16},{28,20},{1,25},{... | collective-permute-start | bytes 786440 | tf_op jit(solution)/shard_map/ppermute | solution.py:891
  153.4 27.6 %collective-permute-start.37 = (bf16[128,1024]{1,0:T(8,128)(2,1)S(1)}, bf16[128,1024]{1,0:T(8,128)(2,1)}, u32[]{:S(2)}, u32[]{:S(2)}) collective-permute-start(bf16[128,1024]{1,0:T(8,128)(2,1)S(1)} %copy-done.65), channel_id=1, source_target_pairs={{0,8},{4,12},{8,16},{12,20},{16,24},{20,28},{24,0},{28,4},{1,9},{5... | collective-permute-start | bytes 786440 | tf_op jit(solution)/shard_map/ppermute | solution.py:891
  182.4 43.1 %collective-permute-start.50 = (bf16[256,1664]{1,0:T(8,128)(2,1)S(1)}, bf16[256,1664]{1,0:T(8,128)(2,1)}, u32[]{:S(2)}, u32[]{:S(2)}) collective-permute-start(bf16[256,1664]{1,0:T(8,128)(2,1)S(1)} %bitcast.47), channel_id=1, source_target_pairs={{0,3},{1,2},{2,1},{3,0},{4,7},{5,6},{6,5},{7,4},{8,11},{9,10},{10,... | collective-permute-start | bytes 2555912 | tf_op jit(solution)/shard_map/ppermute | solution.py:881
  185.0 37.9 %collective-permute-start.44 = (bf16[256,1536]{1,0:T(8,128)(2,1)S(1)}, bf16[256,1536]{1,0:T(8,128)(2,1)}, u32[]{:S(2)}, u32[]{:S(2)}) collective-permute-start(bf16[256,1536]{1,0:T(8,128)(2,1)S(1)} %copy-done.16), channel_id=1, source_target_pairs={{0,4},{4,0},{8,12},{12,8},{16,20},{20,16},{24,28},{28,24},{1,5},{5... | collective-permute-start | bytes 2359304 | tf_op jit(solution)/shard_map/ppermute | solution.py:886
  185.1 28.8 %collective-permute-start.47 = (bf16[128,1536]{1,0:T(8,128)(2,1)}, bf16[128,1536]{1,0:T(8,128)(2,1)}, u32[]{:S(2)}, u32[]{:S(2)}) collective-permute-start(bf16[128,1536]{1,0:T(8,128)(2,1)} %get-tuple-element.190.refs_0_.h2_ref), channel_id=1, source_target_pairs={{0,1},{1,0},{2,3},{3,2},{4,5},{5,4},{6,7},{7,6},{8,9},{9,8},{10,11... | collective-permute-start | bytes 1179656 | tf_op jit(solution)/shard_map/ppermute | solution.py:881
  185.7 28.2 %collective-permute-start.48 = (bf16[128,1536]{1,0:T(8,128)(2,1)}, bf16[128,1536]{1,0:T(8,128)(2,1)}, u32[]{:S(2)}, u32[]{:S(2)}) collective-permute-start(bf16[128,1536]{1,0:T(8,128)(2,1)} %get-tuple-element.190.refs_0_.h2_ref), channel_id=1, source_target_pairs={{0,2},{1,3},{2,0},{3,1},{4,6},{5,7},{6,4},{7,5},{8,10},{9,11},{10,... | collective-permute-start | bytes 1179656 | tf_op jit(solution)/shard_map/ppermute | solution.py:881
  187.4 33.8 %collective-permute-start.49 = (bf16[128,1536]{1,0:T(8,128)(2,1)}, bf16[128,1536]{1,0:T(8,128)(2,1)}, u32[]{:S(2)}, u32[]{:S(2)}) collective-permute-start(bf16[128,1536]{1,0:T(8,128)(2,1)} %get-tuple-element.190.refs_0_.h2_ref), channel_id=1, source_target_pairs={{0,3},{1,2},{2,1},{3,0},{4,7},{5,6},{6,5},{7,4},{8,11},{9,10},{10,... | collective-permute-start | bytes 1179656 | tf_op jit(solution)/shard_map/ppermute | solution.py:881
  335.5 32.1 %collective-permute-start.71 = (bf16[256,1024]{1,0:T(8,128)(2,1)}, bf16[256,1024]{1,0:T(8,128)(2,1)}, u32[]{:S(2)}, u32[]{:S(2)}) collective-permute-start(bf16[256,1024]{1,0:T(8,128)(2,1)} %pad_maximum_fusion.5), channel_id=1, source_target_pairs={{0,8},{4,12},{8,16},{12,20},{16,24},{20,28},{24,0},{28,4},{1,9},{5... | collective-permute-start | bytes 1572872 | tf_op jit(solution)/shard_map/ppermute | solution.py:891
  350.3 58.7 %collective-permute-start.63 = (bf16[256,1536]{1,0:T(8,128)(2,1)}, bf16[256,1536]{1,0:T(8,128)(2,1)S(1)}, u32[]{:S(2)}, u32[]{:S(2)}) collective-permute-start(bf16[256,1536]{1,0:T(8,128)(2,1)} %get-tuple-element.217), channel_id=1, source_target_pairs={{0,3},{1,2},{2,1},{3,0},{4,7},{5,6},{6,5},{7,4},{8,11},{9,10},{10,... | collective-permute-start | bytes 2359304 | tf_op jit(solution)/shard_map/ppermute | solution.py:881
  353.8 47.9 %collective-permute-start.70 = (bf16[256,1024]{1,0:T(8,128)(2,1)S(1)}, bf16[256,1024]{1,0:T(8,128)(2,1)S(1)}, u32[]{:S(2)}, u32[]{:S(2)}) collective-permute-start(bf16[256,1024]{1,0:T(8,128)(2,1)S(1)} %pad_maximum_fusion.4), channel_id=1, source_target_pairs={{0,16},{4,20},{8,24},{12,28},{16,0},{20,4},{24,8},{28,12},{1,17},{... | collective-permute-start | bytes 1572872 | tf_op jit(solution)/shard_map/ppermute | solution.py:891
  356.0 53.0 %collective-permute-start.69 = (bf16[256,1024]{1,0:T(8,128)(2,1)S(1)}, bf16[256,1024]{1,0:T(8,128)(2,1)S(1)}, u32[]{:S(2)}, u32[]{:S(2)}) collective-permute-start(bf16[256,1024]{1,0:T(8,128)(2,1)S(1)} %pad_maximum_fusion.3), channel_id=1, source_target_pairs={{0,24},{4,28},{8,0},{12,4},{16,8},{20,12},{24,16},{28,20},{1,25},{... | collective-permute-start | bytes 1572872 | tf_op jit(solution)/shard_map/ppermute | solution.py:891
  356.6 55.4 %collective-permute-start.62 = (bf16[256,1536]{1,0:T(8,128)(2,1)S(1)}, bf16[256,1536]{1,0:T(8,128)(2,1)S(1)}, u32[]{:S(2)}, u32[]{:S(2)}) collective-permute-start(bf16[256,1536]{1,0:T(8,128)(2,1)S(1)} %copy-done.57), channel_id=1, source_target_pairs={{0,2},{1,3},{2,0},{3,1},{4,6},{5,7},{6,4},{7,5},{8,10},{9,11},{10,... | collective-permute-start | bytes 2359304 | tf_op jit(solution)/shard_map/ppermute | solution.py:881
  367.6 44.5 %collective-permute-start.61 = (bf16[256,1536]{1,0:T(8,128)(2,1)S(1)}, bf16[256,1536]{1,0:T(8,128)(2,1)S(1)}, u32[]{:S(2)}, u32[]{:S(2)}) collective-permute-start(bf16[256,1536]{1,0:T(8,128)(2,1)S(1)} %copy-done.56), channel_id=1, source_target_pairs={{0,1},{1,0},{2,3},{3,2},{4,5},{5,4},{6,7},{7,6},{8,9},{9,8},{10,11... | collective-permute-start | bytes 2359304 | tf_op jit(solution)/shard_map/ppermute | solution.py:881
  445.1 34.6 %collective-permute-start.79 = (bf16[8,192,256]{2,1,0:T(8,128)(2,1)}, bf16[8,192,256]{2,1,0:T(8,128)(2,1)S(1)}, u32[]{:S(2)}, u32[]{:S(2)}) collective-permute-start(bf16[8,192,256]{2,1,0:T(8,128)(2,1)} %get-tuple-element.237), channel_id=1, source_target_pairs={{0,2},{1,3},{2,0},{3,1},{4,6},{5,7},{6,4},{7,5},{8,10},{9,11},{10,... | collective-permute-start | bytes 2359304 | tf_op jit(solution)/shard_map/ppermute | solution.py:881
  445.7 35.5 %collective-permute-start.82 = (bf16[8,192,256]{2,1,0:T(8,128)(2,1)}, bf16[8,192,256]{2,1,0:T(8,128)(2,1)S(1)}, u32[]{:S(2)}, u32[]{:S(2)}) collective-permute-start(bf16[8,192,256]{2,1,0:T(8,128)(2,1)} %get-tuple-element.240), channel_id=1, source_target_pairs={{0,1},{1,0},{2,3},{3,2},{4,5},{5,4},{6,7},{7,6},{8,9},{9,8},{10,11... | collective-permute-start | bytes 2359304 | tf_op jit(solution)/shard_map/ppermute | solution.py:881
  464.1 33.4 %collective-permute-start.75 = (bf16[4,192,256]{2,1,0:T(8,128)(2,1)S(1)}, bf16[4,192,256]{2,1,0:T(8,128)(2,1)S(1)}, u32[]{:S(2)}, u32[]{:S(2)}) collective-permute-start(bf16[4,192,256]{2,1,0:T(8,128)(2,1)S(1)} %add_convert_fusion.6), channel_id=1, source_target_pairs={{0,1},{1,0},{2,3},{3,2},{4,5},{5,4},{6,7},{7,6},{8,9},{9,8},{10,11... | collective-permute-start | bytes 1179656 | tf_op jit(solution)/shard_map/ppermute | solution.py:881
  533.9 31.6 %collective-permute-start.81 = (bf16[4,192,256]{2,1,0:T(8,128)(2,1)S(1)}, bf16[4,192,256]{2,1,0:T(8,128)(2,1)S(1)}, u32[]{:S(2)}, u32[]{:S(2)}) collective-permute-start(bf16[4,192,256]{2,1,0:T(8,128)(2,1)S(1)} %add_convert_fusion.2), channel_id=1, source_target_pairs={{0,16},{4,20},{8,24},{12,28},{16,0},{20,4},{24,8},{28,12},{1,17},{... | collective-permute-start | bytes 1179656 | tf_op jit(solution)/shard_map/ppermute | solution.py:891
  534.2 31.2 %collective-permute-start.84 = (bf16[4,192,256]{2,1,0:T(8,128)(2,1)S(1)}, bf16[4,192,256]{2,1,0:T(8,128)(2,1)S(1)}, u32[]{:S(2)}, u32[]{:S(2)}) collective-permute-start(bf16[4,192,256]{2,1,0:T(8,128)(2,1)S(1)} %add_convert_fusion), channel_id=1, source_target_pairs={{0,8},{4,12},{8,16},{12,20},{16,24},{20,28},{24,0},{28,4},{1,9},{5... | collective-permute-start | bytes 1179656 | tf_op jit(solution)/shard_map/ppermute | solution.py:891
  (150 other events, 1956.5 us)
Sparse Core Ops, SparseCore 0:
  50.8 111.7 all-gather.1
  280.5 138.3 reduce-scatter.1

commit v7 on v6

--- a/solution.py
+++ b/solution.py
@@ -160,15 +160,7 @@
         )
     q_groups = groups - kv_groups
 
-    @pl.loop(0, kv_groups)
-    def _(b):
-        across = pl.ds(pl.multiple_of((q_groups + b) * BC, BC), BC)
-        wait_bytes(held.at[:, across], sems.at[q_groups + b])
-        made = dot(h_ref[...], held[:, across]).astype(low_type)
-        for m in range(micros):
-            kv_refs[m][:, pl.ds(pl.multiple_of(b * BC, BC), BC)] = made[m * rows : (m + 1) * rows]
-
-    @pl.loop(0, q_groups)
+    @pl.loop(0, groups)
     def _(b):
         across = pl.ds(pl.multiple_of(b * BC, BC), BC)
         wait_bytes(held.at[:, across], sems.at[b])
@@ -180,6 +172,14 @@
     ]
     for copy in copies:
         copy.start()
+
+    @pl.loop(0, kv_groups)
+    def _(b):
+        across = pl.ds(pl.multiple_of((q_groups + b) * BC, BC), BC)
+        made = dot(h_ref[...], held[:, across]).astype(low_type)
+        for m in range(micros):
+            kv_refs[m][:, pl.ds(pl.multiple_of(b * BC, BC), BC)] = made[m * rows : (m + 1) * rows]
+
     for copy in copies:
         copy.wait()
 
@@ -467,10 +467,10 @@
 
 
 def outer_kernel(groups, col_groups, order_ref, *refs):
-    micros = len(refs[:-4]) // (len(groups) + 2)
+    micros = len(refs[:-5]) // (len(groups) + 2)
     lefts = [refs[i * micros : (i + 1) * micros] for i in range(2)]
     rights = [refs[(2 + i) * micros : (3 + i) * micros] for i in range(len(groups))]
-    out_ref, turned, stage, sems = refs[-4:]
+    out_refs, (turned, stage, sems) = refs[-5:-3], refs[-3:]
     rows = rights[0][0].shape[0]
     width = turned.shape[1]
     span = 2 * BR
@@ -494,11 +494,15 @@
         for half in range(2):
             for b in range(col_groups):
                 number = (k * row_groups + 2 * p + half) * col_groups + b
-                pltpu.make_async_copy(
-                    stage.at[slot, pl.ds(half * BR, BR), pl.ds(b * BC, BC)],
-                    out_ref.at[order_ref[number]],
-                    sems.at[slot],
-                ).start()
+                place = order_ref[number]
+                for side in range(2):
+                    pltpu.make_async_copy(
+                        stage.at[
+                            slot, pl.ds(half * BR, BR), pl.ds(b * BC + side * LANES, LANES)
+                        ],
+                        out_refs[side].at[place],
+                        sems.at[slot],
+                    ).start()
     for slot in range(2):
         wait_bytes(stage.at[slot], sems.at[slot])
 
@@ -510,9 +514,9 @@
     blocks = len(groups) * width * cols // (BR * BC)
     return call(
         functools.partial(outer_kernel, groups, cols // BC),
-        shaped((blocks, BR, BC), low_type),
+        (shaped((blocks, BR, LANES), low_type),) * 2,
         [in_smem] + [in_vmem] * len(flat),
-        in_any,
+        (in_any,) * 2,
         [
             pltpu.VMEM((2, width, rows), low_type),
             pltpu.VMEM((2, 2 * BR, cols), low_type),
@@ -530,90 +534,103 @@
     return [first, 3], [0, 3 - first]
 
 
-def slots_kernel(
-    counts, chips, members, slots, all_groups, in_groups, order_ref, me_ref, *refs
-):
+def pieces_kernel(members, counts, cols, turned_first, me_ref, *refs):
+    row_groups = 8
     lists = []
-    for count in counts:
-        lists.append(refs[:count])
-        refs = refs[count:]
-    outs = refs[: 2 * chips]
-    lefts, turned, rights, sems = refs[2 * chips :]
+    for left_count, right_count in counts:
+        lists.append((refs[:left_count], refs[left_count : left_count + right_count]))
+        refs = refs[left_count + right_count :]
+    outs, refs = refs[:4], refs[4:]
+    extra = refs[0] if not turned_first else None
+    turned, rights, stage, sems = refs[0 if turned_first else 1 :]
     ctx, shard = me_ref[0], me_ref[1]
-    chip, core = lax.div(ctx, 2), lax.rem(ctx, 2)
-    h_width = lefts.shape[2]
-    q_width = lists[2][0].shape[1]
-    kv_width = lists[3][0].shape[1]
-    total = rights.shape[0]
-    targets = (
-        (lefts.at[0], 0, h_width, 0),
-        (lefts.at[1], 0, h_width, 1),
-        (rights, 0, q_width, 2),
-        (rights, q_width, kv_width, 2),
-        (rights, q_width + kv_width, q_width, 2),
-    )
-    for group, (target, lane, lanes, sem) in zip(lists, targets):
+    core = lax.rem(ctx, 2)
+    total = turned.shape[2]
+    row_groups = turned.shape[1] // BR
+    base = 0
+    for g, (_, parts) in enumerate(lists):
         start = 0
-        for ref in group:
-            pltpu.make_async_copy(
-                ref, target.at[pl.ds(start, ref.shape[0]), pl.ds(lane, lanes)], sems.at[sem]
-            ).start()
-            start += ref.shape[0]
-    for side in range(2):
-        wait_bytes(lefts.at[side], sems.at[side])
-        for r in range(0, total, LANES):
-            turned[side, :, r : r + LANES] = lefts[side, r : r + LANES, :].T
-    wait_bytes(rights, sems.at[2])
-    for offset in range(chips):
-        there = lax.rem(chip - offset + chips, chips) * 2 + core
-        for out, hops in zip(outs[2 * offset : 2 * offset + 2], xor_plan(members, offset)):
-            for place, hop in enumerate(hops):
-                base = (there * members + jnp.bitwise_xor(shard, hop)) * slots
-
-                @pl.loop(0, slots)
-                def _(i):
-                    number = order_ref[base + i]
-                    a, b = lax.div(number, all_groups), lax.rem(number, all_groups)
-                    side = (b >= in_groups).astype(jnp.int32)
-                    out[place * slots + i] = dot(
-                        turned[side, pl.ds(pl.multiple_of(a * BR, 64), BR), :],
-                        rights[:, pl.ds(pl.multiple_of(b * BC, BC), BC)],
-                    ).astype(low_type)
-
-
-def slot_blocks(chips, members, slots, order, me, h1, da, dq, dkv, ob):
-    lists = (h1, da, dq, dkv, ob)
-    total = sum(part.shape[0] for part in h1)
-    width = h1[0].shape[1]
-    in_width = dq[0].shape[1] + dkv[0].shape[1]
-    all_width = in_width + ob[0].shape[1]
+        for part in parts:
+            count = part.shape[0]
+            for b in range(cols[g]):
+                lane = pl.multiple_of(b * BC + core * LANES, LANES)
+                pltpu.make_async_copy(
+                    part.at[:, pl.ds(lane, LANES)],
+                    rights.at[pl.ds(start, count), pl.ds((base + b) * LANES, LANES)],
+                    sems.at[g],
+                ).start()
+            start += count
+        base += cols[g]
+    for g, (parts, _) in enumerate(lists):
+        if g == 0 and turned_first:
+            turned[0] = parts[0][...]
+            continue
+        start = 0
+        for part in parts:
+            for r in range(0, part.shape[0], LANES):
+                turned[g, :, start : start + LANES] = part[r : r + LANES, :].T
+                start += LANES
+    if extra is not None:
+        extra[...] = turned[0]
+    all_cols = sum(cols)
+    half_blocks = row_groups // 2 * all_cols
+    span = BR // members
+    base = 0
+    for g in range(len(lists)):
+        wide_cols = cols[g] * LANES
+        wait_bytes(rights.at[:, pl.ds(base * LANES, wide_cols)], sems.at[g])
+        for a in range(row_groups):
+            made = dot(
+                turned[g, a * BR : (a + 1) * BR, :],
+                rights[:, base * LANES : base * LANES + wide_cols],
+            )
+            stage[a % 2, :, :wide_cols] = made.astype(stage.dtype)
+            half = a // (row_groups // 2)
+            first = (a % (row_groups // 2)) * all_cols + base
+            for out, hops in zip(outs[2 * half : 2 * half + 2], xor_plan(members, 1 - half)):
+                for place, hop in enumerate(hops):
+                    down = pl.multiple_of(jnp.bitwise_xor(shard, hop) * span, 16 if span % 16 == 0 else 8)
+                    for b in range(cols[g]):
+                        out[place * half_blocks + first + b] = stage[
+                            a % 2, pl.ds(down, span), b * LANES : (b + 1) * LANES
+                        ].astype(low_type)
+        base += cols[g]
+
+
+def gradient_pieces(members, me, groups, cols, turned_first):
+    counts = tuple((len(left), len(right)) for left, right in groups)
+    flat = [part for left, right in groups for part in left + right]
+    total = sum(part.shape[0] for part in groups[0][1])
+    width = groups[0][0][0].shape[0 if turned_first else 1]
+    row_groups = width // BR
+    half_blocks = row_groups // 2 * sum(cols)
+    span = BR // members
+    stage_type = jnp.float32 if span % 16 else low_type
     outs = []
-    for offset in range(chips):
-        for hops in xor_plan(members, offset):
-            outs.append(shaped((len(hops) * slots, BR, BC), low_type))
-    made = call(
-        functools.partial(
-            slots_kernel,
-            tuple(len(group) for group in lists),
-            chips,
-            members,
-            slots,
-            all_width // BC,
-            in_width // BC,
-        ),
+    for half in range(2):
+        for hops in xor_plan(members, 1 - half):
+            outs.append(shaped((len(hops) * half_blocks, span, LANES), low_type))
+    out_specs = [in_vmem] * 4
+    if not turned_first:
+        outs.append(shaped((width, total), low_type))
+        out_specs.append(in_vmem)
+    in_specs = [in_smem]
+    for left, right in groups:
+        in_specs += [in_vmem] * len(left) + [in_any] * len(right)
+    return call(
+        functools.partial(pieces_kernel, members, counts, tuple(cols), turned_first),
         tuple(outs),
-        [in_smem, in_smem] + [in_any] * sum(len(group) for group in lists),
-        (in_vmem,) * len(outs),
+        in_specs,
+        tuple(out_specs),
         [
-            pltpu.VMEM((2, total, width), low_type),
-            pltpu.VMEM((2, width, total), low_type),
-            pltpu.VMEM((total, all_width), low_type),
-            pltpu.SemaphoreType.DMA((3,)),
+            pltpu.VMEM((len(groups), width, total), low_type),
+            pltpu.VMEM((total, sum(cols) * LANES), low_type),
+            pltpu.VMEM((2, BR, max(cols) * LANES), stage_type),
+            pltpu.SemaphoreType.DMA((len(groups),)),
         ],
-        2 * total * chips * members * slots * BR * BC,
+        2 * total * width * sum(cols) * LANES,
         16 * MIB,
-    )(order, me, *[part for group in lists for part in group])
-    return [(made[2 * offset], made[2 * offset + 1]) for offset in range(chips)]
+    )(me, *flat)
 
 
 def merge_kernel(
@@ -874,6 +891,17 @@
     )
 
 
+def piece_places(row_groups, q_groups, kv_groups):
+    all_groups = 2 * q_groups + kv_groups
+    out_groups = list(range(q_groups)) + list(range(q_groups + kv_groups, all_groups))
+    numbers = [a * all_groups + b for a in range(row_groups) for b in out_groups]
+    numbers += [a * all_groups + q_groups + b for a in range(row_groups) for b in range(kv_groups)]
+    places = [0] * len(numbers)
+    for place, number in enumerate(numbers):
+        places[number] = place
+    return places
+
+
 def to_partner(array, offset):
     if offset == 0:
         return array
@@ -911,7 +939,9 @@
 
 
 def gather_weights(blocks, chips, members):
-    parts = from_chips(blocks, chips)
+    parts = [blocks]
+    for _ in range(chips - 1):
+        parts.append(to_chip(parts[-1], 1))
     pieces, arrays = [], []
     gate = []
 
@@ -953,37 +983,43 @@
     return got + parts[1:], pieces, arrays
 
 
-def sum_slots(made, ready, chips, members, slots):
-    sums, first_got = [], []
-    for offset in range(chips):
-        sent, kept = made[offset]
-        hops, keeps = xor_plan(members, offset)
-        total = wide(kept[:slots])
+def add_wide(parts):
+    total = wide(parts[0])
+    for part in parts[1:]:
+        total = total + wide(part)
+    return total
+
+
+def sum_members(made, ready, members):
+    sums, seen = [], []
+    for half in range(2):
+        sent, kept = made[2 * half : 2 * half + 2]
+        hops, keeps = xor_plan(members, 1 - half)
+        count = kept.shape[0] // len(keeps)
+        total = wide(kept[:count])
         if members == 4:
-            first, second = hops[0], keeps[1]
-            got = after(to_partner(sent, first), ready)
-            total = total + wide(got[:slots])
-            relay = (wide(kept[slots:]) + wide(got[slots:])).astype(low_type)
-            total = total + wide(to_partner(relay, second))
+            got = to_partner(sent, hops[0])
+            got = got if ready is None else after(got, ready)
+            total = total + wide(got[:count])
+            relay = (wide(kept[count:]) + wide(got[count:])).astype(low_type)
+            second = to_partner(relay, keeps[1])
+            seen.append(second)
+            total = total + wide(second)
         else:
             for place, hop in enumerate(hops):
-                got = to_partner(sent[place * slots : (place + 1) * slots], hop)
-                total = total + wide(got)
-        sums.append(total if offset == 0 else total.astype(low_type))
-        first_got.append(got)
-    return sums, first_got
-
-
-def sum_all(array):
-    step = 1
-    while step < lax.axis_size("ctx"):
-        array = array + to_ctx(array, step)
-        step *= 2
-    step = 1
-    while step < lax.axis_size("shard"):
-        array = array + to_partner(array, step)
-        step *= 2
-    return array
+                total = total + wide(to_partner(sent[place * count : (place + 1) * count], hop))
+        sums.append(total.astype(low_type).reshape(count, -1))
+    return jnp.concatenate(sums, axis=0), seen
+
+
+def sum_chips(rows, chip, chips):
+    count = rows.shape[1] // chips
+
+    def piece(offset):
+        start = lax.rem(chip - offset + chips, chips) * count
+        return lax.dynamic_slice_in_dim(rows, start, count, axis=1)
+
+    return [piece(0)] + [to_chip(piece(offset), -offset) for offset in range(1, chips)]
 
 
 def shards(
@@ -1017,8 +1053,8 @@
     slots = dense_weight.shape[0]
     span = rows // 2
     row_groups = width // BR
-    ff_groups = FF // BC
-    expert_blocks = 3 * row_groups * ff_groups
+    q_groups = HEADS * HD // BC
+    kv_groups = 2 * KVH * HD // BC
 
     expert_inverse = inverse_order(expert_order)
     ctx = lax.axis_index("ctx").astype(jnp.int32)
@@ -1040,7 +1076,7 @@
     cot_rows = jnp.concatenate([cotangent.astype(low_type), hits], axis=2)
     cot_rows = cot_rows.reshape(micros * rows, width + LANES)
     cot_rows = after(cot_rows, *arrays[::2])
-    cot_parts = [to_partner(cot_rows, j) for j in range(min(3, shard_count))]
+    cot_parts = [to_partner(cot_rows, j) for j in range(shard_count)]
 
     here, expert_inverse, router_pad, key_pos, rows_pos = lax.optimization_barrier(
         (me, expert_inverse, router_pad, key_pos, rows_pos)
@@ -1063,10 +1099,8 @@
     for m in range(micros):
         own = kv[m] if m == 0 else after(kv[m], chip_kv[m - 1][1 % chips])
         chip_kv.append(from_chips(own, chips))
-    late_rows = after(cot_rows, *chip_kv[0])
-    cot_parts = cot_parts + [to_partner(late_rows, j) for j in range(3, shard_count)]
     for m in range(micros):
-        query = after(q[m], *(cot_parts[:3] if m == 0 else obs[m - 1 : m]))
+        query = after(q[m], *(cot_parts if m == 0 else obs[m - 1 : m]))
         parts = chip_kv[m]
         swapped = after(parts, q[0] if m == 0 else obs[m - 1])
         kvs.append(parts + [to_ctx(part, 1) for part in swapped])
@@ -1097,12 +1131,20 @@
         xs.append(x)
     backs = [[to_partner(sent[m][j], j) for j in range(shard_count)] for m in range(micros)]
 
-    dxs, das, dqs, stats, own_grads = [], [], [], [], []
+    expert_terms = outer_blocks(
+        after(expert_inverse, *backs[0]), width, (0, 0, 1), [xs, cs], [dgs, dus, zs]
+    )
+    dxs, das, dqs, stats, own_grads, far_grads = [], [], [], [], [], []
+    outs = None
     for m in range(micros):
-        here = after(me, zs[-1] if m == 0 else dqs[-1])
+        here = after(me, expert_terms, backs[-1]) if m == 0 else after(me, dqs[-1])
         dx, da, do, stat = merge(
             here, x2s[m], cotangent[m], h2s[m], norm_gains, router_pad, w_out, backs[m]
         )
+        if m == micros - 1:
+            ready = own_grads[-1][1 % chips] if m else da
+            outs = produce(after(expert_inverse, da, ready), expert_all, zs, shard_count, width)
+            do = after(do, outs[0], *(far_grads[-1][:1] + far_grads[-1][-1:] if m else []))
         dq, dkv_own, dkv_other = attend_back(
             q[m], kvs[m], rows_pos, key_pos, obs[m], logs[m], do
         )
@@ -1113,72 +1155,91 @@
             part = wide(dkv_own[cut]) + wide(got[cut])
             parts.append(part if o == 0 else part.astype(low_type))
         own_grads.append(parts)
+        far_grads.append([to_chip(part, -o) for o, part in enumerate(parts[1:], 1)])
         dxs.append(dx)
         das.append(da)
         dqs.append(dq)
         stats.append(stat)
 
-    far_sums = [
-        to_chip(jnp.concatenate([parts[o] for parts in own_grads], axis=0), -o)
-        for o in range(1, chips)
-    ]
-    dkvs = []
-    for m in range(micros):
-        total = own_grads[m][0]
-        for part in far_sums:
-            total = total + wide(part[m * rows : (m + 1) * rows])
-        dkvs.append(total.astype(low_type))
+    dkvs = [add_wide([own_grads[m][0]] + far_grads[m]).astype(low_type) for m in range(micros)]
 
     def other_core(parts):
         return [to_ctx(part, 1) for part in parts]
 
     da_others, dq_others = other_core(das), other_core(dqs)
-    expert_term = outer_blocks(
-        after(expert_inverse, *backs[0]), width, (0, 0, 1), [xs, cs], [dgs, dus, zs]
-    )
-    expert_sum = lax.psum_scatter(expert_term, "ctx", scatter_dimension=0, tiled=True)
-    parts_back = query_back(w_in, dqs)
-    made = produce(after(expert_inverse, own_grads[-1][1 % chips]), expert_all, zs, shard_count, width)
-    arrived = [to_partner(made[j], j) for j in range(shard_count)]
-    here = after(me, parts_back, *arrived)
-    made = slot_blocks(
-        chips,
+    first_term = after(expert_terms[0], *backs[-1])
+    expert_sums = [lax.psum_scatter(first_term, "ctx", scatter_dimension=0, tiled=True)]
+    late_term = after(expert_terms[1], *dkvs)
+    expert_sums.append(lax.psum_scatter(late_term, "ctx", scatter_dimension=0, tiled=True))
+    early = gradient_pieces(
         shard_count,
-        slots,
-        dense_order,
-        here,
-        [h1, h1_other],
-        das + da_others,
-        dqs + dq_others,
-        dkvs + other_core(dkvs),
-        obs + ob_others,
+        after(me, own_grads[-1][1 % chips]),
+        [([h1, h1_other], dqs + dq_others), (das + da_others, obs + ob_others)],
+        [q_groups, q_groups],
+        False,
+    )
+    h1_turned = early[4]
+    early_rows, early_seen = sum_members(early[:4], None, shard_count)
+    parts_back = query_back(after(w_in, early[0]), dqs)
+    dkv_others = other_core(after(dkvs, parts_back))
+    late = gradient_pieces(
+        shard_count,
+        after(me, *early_seen),
+        [([h1_turned], dkvs + dkv_others)],
+        [kv_groups],
+        True,
     )
     input_grad, gain_stat = input_back(
-        after(tokens, made[0][0]), norm_gains, w_in, dxs, parts_back, dkvs
-    )
-    sums, got = sum_slots(made, input_grad, chips, shard_count, slots)
+        after(tokens, late[0]), norm_gains, w_in, dxs, parts_back, dkvs
+    )
+    late_rows, late_seen = sum_members(late[:4], input_grad, shard_count)
+    arrived = [to_partner(part, j) for j, part in enumerate(after(list(outs), *late_seen))]
+    chip = ctx // 2
+    early_sum = add_wide(sum_chips(early_rows, chip, chips)).astype(low_type)
+    late_sum = add_wide(sum_chips(late_rows, chip, chips)).astype(low_type)
+    all_sums = jnp.concatenate([early_sum, late_sum], axis=0)
+    places = jnp.asarray(piece_places(row_groups, q_groups, kv_groups), jnp.int32)[dense_order]
+    chosen = (places[:, None] == jnp.arange(all_sums.shape[0])[None, :]).astype(low_type)
+    ordered = jnp.dot(chosen, all_sums, preferred_element_type=jnp.float32).astype(low_type)
+    devices = ctx_count * shard_count
+    piece_width = ordered.shape[1]
     experts_up = stats[0].shape[0] - 8
-    stat_rows = jnp.concatenate([sum(stats)[: experts_up + 1], gain_stat[:7]], axis=0)
-    stat_rows = sum_all(after(stat_rows, *sums))
+    stat_rows = add_wide(stats)
+    stat_rows = jnp.concatenate(
+        [stat_rows[:shard_count], gain_stat[:1], stat_rows[experts_up : experts_up + 1]], axis=0
+    )
+    stat_parts = stat_rows.astype(low_type).reshape(-1, piece_width)
+    extra = stat_parts.shape[0]
+    ordered = jnp.concatenate(
+        [
+            ordered.reshape(devices, slots, piece_width),
+            jnp.broadcast_to(stat_parts, (devices, extra, piece_width)),
+        ],
+        axis=1,
+    ).reshape(devices * (slots + extra), piece_width)
+    ordered = lax.all_to_all(ordered, ("ctx", "shard"), split_axis=0, concat_axis=0, tiled=True)
+    ordered = ordered.reshape(devices, slots + extra, piece_width)
+    stat_rows = jnp.sum(wide(ordered[:, slots:]), axis=0).reshape(shard_count + 2, width)
+    ordered = ordered[:, :slots].reshape(
+        chips, 2, shard_count, slots, BR // (shard_count * chips), LANES
+    )
+    dense_sum = ordered.transpose(3, 2, 0, 4, 1, 5).reshape(slots, BR, BC)
     router_grad = stat_rows[:shard_count].T
-    gains_grad = jnp.stack([stat_rows[experts_up + 1], stat_rows[experts_up]])
-
+    gains_grad = stat_rows[shard_count:]
+
+    expert_grad, expert_new, expert_moment_new, expert_second_new = rotate(
+        expert_weight[0], expert_sums, expert_moment[0], expert_second[0], expert_left[0], expert_right[0]
+    )
+    dense_grad, dense_new, dense_moment_new, dense_second_new = rotate(
+        dense_weight, [dense_sum], dense_moment, dense_second, dense_left, dense_right
+    )
     outputs = []
     for m in range(micros):
         total = x2s[m]
-        for part in arrived:
+        for part in after(arrived, dense_new, expert_new):
             total = total + wide(part[m * rows : (m + 1) * rows])
         outputs.append(total)
 
-    expert_grad, expert_new, expert_moment_new, expert_second_new = rotate(
-        expert_weight[0], [after(expert_sum, *sums)], expert_moment[0], expert_second[0], expert_left[0], expert_right[0]
-    )
-    last = [sums[0]] + [to_chip(sums[o], -o) for o in range(1, chips)]
-    last = after(last, expert_new)
-    dense_sum = sum([wide(part) for part in last[1:]], last[0])
-    dense_grad, dense_new, dense_moment_new, dense_second_new = rotate(
-        dense_weight, [dense_sum], dense_moment, dense_second, dense_left, dense_right
-    )
     gains_new, gains_moment_new, gains_second_new = adam(
         norm_gains, gains_grad, gains_moment, gains_second, gain_rate
     )

time: 586 us -> 563 us (0.961)
  starting transfers between devices: 109 us -> 96.1 us
  waiting for transfers between devices: 211 us -> 201 us
  Pallas kernels: 200 us -> 191 us
  other arithmetic: 21.6 us -> 28.7 us
    ppermute x39 -> x37, waiting for transfers between devices: 92.6 us -> 50.4 us  [to_partner(): return lax.ppermute(array, 'shard', [(i, i ^ offset) for i in range(count)])]
    all_to_all x0 -> x1, waiting for transfers between devices: none -> 34 us  [shards(): lax.all_to_all(ordered, ('ctx', 'shard'), split_axis=0, concat_axis=0, ti...]
    ppermute x36 -> x33, starting transfers between devices: 22.6 us -> 6.3 us  [to_ctx(): return lax.ppermute(array, 'ctx', [(i, i ^ offset) for i in range(count)])]
    ppermute x36 -> x33, waiting for transfers between devices: 15 us -> 3.6 us  [to_ctx(): return lax.ppermute(array, 'ctx', [(i, i ^ offset) for i in range(count)])]
    ppermute x15 -> x21, waiting for transfers between devices: 104 us -> 113 us  [to_chip(): lax.ppermute(array, 'ctx', [(i, (i + 2 * offset) % count) for i in range(...]
    ppermute x39 -> x37, starting transfers between devices: 49.8 us -> 41.9 us  [to_partner(): return lax.ppermute(array, 'shard', [(i, i ^ offset) for i in range(count)])]
    pallas_call x2 -> x3, Pallas kernels: 38.6 us -> 30.9 us  [the longest x1 17.9 us: outer_blocks(): call(functools.partial(outer_kernel, groups, cols // BC), (shaped((blocks...]
    convert_element_type x8 -> x12, other arithmetic: 4.23 us -> 11.9 us  [the longest x4 5.16 us: sum_members(): relay = (wide(kept[count:]) + wide(got[count:])).astype(low_type)]
  transfers between devices with their start and end apart: 92 -> 95, of which waited for: 29 -> 35; matrix products, arithmetic and copies ran while one was open for 5% -> 7% of each run, Pallas kernels for 30% -> 34%
where the time goes in v7:
time: 563 us; the launch traced here: 556 us
  waiting for transfers between devices  201 us (36%)
  Pallas kernels  191 us (34%)
  starting transfers between devices  96.1 us (17%)
  other arithmetic  28.7 us (5%)
  local copies, waits for them, and re-layouts  22.9 us (4%)
  between operations  15.4 us (3%)
    ppermute x21, waiting for transfers between devices, to_chip(): lax.ppermute(array, 'ctx', [(i, (i + 2 * offset) % count) for i in range(...  113 us
    ppermute x37, waiting for transfers between devices, to_partner(): return lax.ppermute(array, 'shard', [(i, i ^ offset) for i in range(count)])  50.4 us
    ppermute x21, starting transfers between devices, to_chip(): lax.ppermute(array, 'ctx', [(i, (i + 2 * offset) % count) for i in range(...  42.4 us
    ppermute x37, starting transfers between devices, to_partner(): return lax.ppermute(array, 'shard', [(i, i ^ offset) for i in range(count)])  41.9 us
    all_to_all x1, waiting for transfers between devices, shards(): lax.all_to_all(ordered, ('ctx', 'shard'), split_axis=0, concat_axis=0, ti...  34 us
    pallas_call x2, Pallas kernels, run_expert(): call(functools.partial(expert_kernel, sources, micro), tuple([shaped((row...  32.6 us
    pallas_call x2, Pallas kernels, attend_back(): call(functools.partial(attend_back_kernel, len(kv_parts)), (shaped((rows,...  29.6 us
    pallas_call x2, Pallas kernels, attend(): call(functools.partial(attend_kernel, len(kv_parts)), (shaped((rows, widt...  25.6 us
  transfers between devices with their start and end apart: 95, of which 35 were waited for; matrix products, arithmetic and copies ran while one was open for 7% of the time, Pallas kernels for 34%

profile of v7, /device:TPU:0, one launch (start us, length us, event | category | flops | bytes accessed | tf_op | source)
XLA Modules:
  0.0 555.7 jit_solution(1679876000616460441)
XLA Ops:
  15.0 7.8 %collective-permute-done.7.refs_11_ = bf16[4,192,256]{2,1,0:T(8,128)(2,1)} collective-permute-done((bf16[4,192,256]{2,1,0:T(8,128)(2,1)S(1)}, bf16[4,192,256]{2,1,0:T(8,128)(2,1)}, u32[]{:S(2)}, u32[]{:S(2)}) %collective-permute-start.7) | collective-permute-done | bytes 393248 | tf_op jit(solution)/shard_map/ppermute | solution.py:919
  23.7 8.2 %collective-permute-done.3.refs_7_ = bf16[4,192,256]{2,1,0:T(8,128)(2,1)} collective-permute-done((bf16[4,192,256]{2,1,0:T(8,128)(2,1)S(1)}, bf16[4,192,256]{2,1,0:T(8,128)(2,1)}, u32[]{:S(2)}, u32[]{:S(2)}) %collective-permute-start.3) | collective-permute-done | bytes 393248 | tf_op jit(solution)/shard_map/ppermute | solution.py:909
  55.6 12.6 %collective-permute-done.20.refs_23_ = bf16[8,192,256]{2,1,0:T(8,128)(2,1)} collective-permute-done((bf16[8,192,256]{2,1,0:T(8,128)(2,1)}, bf16[8,192,256]{2,1,0:T(8,128)(2,1)}, u32[]{:S(2)}, u32[]{:S(2)}) %collective-permute-start.20) | collective-permute-done | bytes 786464 | tf_op jit(solution)/shard_map/ppermute | solution.py:909
  96.4 12.1 %shard_map.358 = (bf16[256,1536]{1,0:T(8,128)(2,1)}, bf16[128,1024]{1,0:T(8,128)(2,1)}, bf16[128,1024]{1,0:T(8,128)(2,1)}, bf16[1536,2560]{1,0:T(8,128)(2,1)}, bf16[1536,1536]{1,0:T(8,128)(2,1)}) custom-call(s32[128]{0:T(128)} %order_ref.1, s32[2]{0:T(128)} %pad_add_fusion.me_ref, f32[128,1536]{1,0:T(8,128)} %get-tuple-element.305.refs_0_.x_ref, ...), custom_call_target="tpu_custom_call" | custom-call | flops 805306368 | bytes 25165824 | tf_op jit(solution)/shard_map/pallas_call | solution.py:193
  108.8 16.5 %collective-permute-done.31.refs_1_ = bf16[128,1024]{1,0:T(8,128)(2,1)S(1)} collective-permute-done((bf16[128,1024]{1,0:T(8,128)(2,1)}, bf16[128,1024]{1,0:T(8,128)(2,1)S(1)}, u32[]{:S(2)}, u32[]{:S(2)}) %collective-permute-start.31) | collective-permute-done | bytes 262176 | tf_op jit(solution)/shard_map/ppermute | solution.py:919
  134.3 8.5 %collective-permute-done.32.refs_2_ = bf16[128,1024]{1,0:T(8,128)(2,1)S(1)} collective-permute-done((bf16[128,1024]{1,0:T(8,128)(2,1)}, bf16[128,1024]{1,0:T(8,128)(2,1)S(1)}, u32[]{:S(2)}, u32[]{:S(2)}) %collective-permute-start.32) | collective-permute-done | bytes 262176 | tf_op jit(solution)/shard_map/ppermute | solution.py:919
  144.3 13.0 %collective-permute-start.38 = (bf16[128,1024]{1,0:T(8,128)(2,1)S(1)}, bf16[128,1024]{1,0:T(8,128)(2,1)S(1)}, u32[]{:S(2)}, u32[]{:S(2)}) collective-permute-start(bf16[128,1024]{1,0:T(8,128)(2,1)S(1)} %copy-done.51), channel_id=1, source_target_pairs={{0,8},{4,12},{8,16},{12,20},{16,24},{20,28},{24,0},{28,4},{1,9},{5... | collective-permute-start | bytes 786440 | tf_op jit(solution)/shard_map/ppermute | solution.py:919
  161.8 12.8 %shard_map.360 = (bf16[128,1536]{1,0:T(8,128)(2,1)}, f32[384,128]{1,0:T(8,128)}, f32[128,1536]{1,0:T(8,128)}, bf16[128,1536]{1,0:T(8,128)(2,1)}) custom-call(bf16[128,1536]{1,0:T(8,128)(2,1)} %get-tuple-element.173.q_ref, s32[128,1]{1,0:T(8,128)} %constant_dynamic-slice_fusion.6.rpos_ref, s32[1,1024]{1,0:T(1,128)} %bitcast.69, ...), custom_call_target="tpu_custom_call" | custom-call | flops 3221225472 | bytes 8388608 | tf_op jit(solution)/shard_map/pallas_call | solution.py:302
  181.2 12.8 %shard_map.361 = (bf16[128,1536]{1,0:T(8,128)(2,1)}, f32[384,128]{1,0:T(8,128)}, f32[128,1536]{1,0:T(8,128)}, bf16[128,1536]{1,0:T(8,128)(2,1)}) custom-call(bf16[128,1536]{1,0:T(8,128)(2,1)} %get-tuple-element.187.q_ref, s32[128,1]{1,0:T(8,128)} %constant_dynamic-slice_fusion.6.rpos_ref, s32[1,1024]{1,0:T(1,128)} %bitcast.70, ...), custom_call_target="tpu_custom_call" | custom-call | flops 3221225472 | bytes 8388608 | tf_op jit(solution)/shard_map/pallas_call | solution.py:302
  201.2 16.2 %shard_map.362 = (bf16[128,1664]{1,0:T(8,128)(2,1)}, bf16[128,1664]{1,0:T(8,128)(2,1)}, bf16[128,1664]{1,0:T(8,128)(2,1)}, bf16[128,1664]{1,0:T(8,128)(2,1)}, bf...) custom-call(s32[96]{0:T(128)} %select_reduce_fusion.order_ref, ...), custom_call_target="tpu_custom_call" | custom-call | flops 8053063680 | bytes 20971520 | tf_op jit(solution)/shard_map/pallas_call | solution.py:401
  221.8 16.4 %shard_map.363 = (bf16[128,1664]{1,0:T(8,128)(2,1)}, bf16[128,1664]{1,0:T(8,128)(2,1)}, bf16[128,1664]{1,0:T(8,128)(2,1)}, bf16[128,1664]{1,0:T(8,128)(2,1)}, bf...) custom-call(s32[96]{0:T(128)} %select_reduce_fusion.order_ref, ...), custom_call_target="tpu_custom_call" | custom-call | flops 8053063680 | bytes 20971520 | tf_op jit(solution)/shard_map/pallas_call | solution.py:401
  241.8 17.9 %shard_map.364 = (bf16[96,192,128]{2,1,0:T(8,128)(2,1)}, bf16[96,192,128]{2,1,0:T(8,128)(2,1)}) custom-call(s32[96]{0:T(128)} %select_reduce_fusion.order_ref, bf16[512,1536]{1,0:T(8,128)(2,1)} %get-tuple-element.205.refs_0_, bf16[512,1536]{1,0:T(8,128)(2,1)} %get-tuple-element.209.refs_1_, bf16[512,1664]{1,0:T(8,128)(2,1)} %get-tuple-element.210.refs_2_, ...), custom_call_target="tpu_custom_call" | custom-call | flops 9663676416 | bytes 22282240 | tf_op jit(solution)/shard_map/pallas_call | solution.py:515
  268.1 14.8 %shard_map.366 = (bf16[128,1536]{1,0:T(8,128)(2,1)}, bf16[512,1024]{1,0:T(8,128)(2,1)}, bf16[512,1024]{1,0:T(8,128)(2,1)}) custom-call(bf16[128,1536]{1,0:T(8,128)(2,1)} %get-tuple-element.173.q_ref, s32[128,1]{1,0:T(8,128)} %constant_dynamic-slice_fusion.6.rpos_ref, s32[1,1024]{1,0:T(1,128)} %bitcast.71, ...), custom_call_target="tpu_custom_call" | custom-call | flops 8053063680 | bytes 8388608 | tf_op jit(solution)/shard_map/pallas_call | solution.py:744
  289.5 8.6 %collective-permute-start.61 = (bf16[128,1024]{1,0:T(8,128)(2,1)S(1)}, bf16[128,1024]{1,0:T(8,128)(2,1)S(1)}, u32[]{:S(2)}, u32[]{:S(2)}) collective-permute-start(bf16[128,1024]{1,0:T(8,128)(2,1)S(1)} %get-tuple-element.301), channel_id=1, source_target_pairs={{0,24},{4,28},{8,0},{12,4},{16,8},{20,12},{24,16},{28,20},{1,25},{... | collective-permute-start | bytes 786440 | tf_op jit(solution)/shard_map/ppermute | solution.py:919
  298.3 8.6 %shard_map.368 = (bf16[256,1536]{1,0:T(8,128)(2,1)}, bf16[256,1536]{1,0:T(8,128)(2,1)}, bf16[256,1536]{1,0:T(8,128)(2,1)}, bf16[256,1536]{1,0:T(8,128)(2,1)}) custom-call(s32[96]{0:T(128)} %select_reduce_fusion.order_ref, bf16[96,192,256]{2,1,0:T(8,128)(2,1)} %all-gather.2.cloned.1.call-done.refs_8_.w_ref, ...), custom_call_target="tpu_custom_call" | custom-call | flops 3221225472 | bytes 8388608 | tf_op jit(solution)/shard_map/pallas_call | solution.py:454
  310.4 11.7 %collective-permute-done.62 = bf16[128,1024]{1,0:T(8,128)(2,1)S(1)} collective-permute-done((bf16[128,1024]{1,0:T(8,128)(2,1)S(1)}, bf16[128,1024]{1,0:T(8,128)(2,1)S(1)}, u32[]{:S(2)}, u32[]{:S(2)}) %collective-permute-start.62) | collective-permute-done | bytes 262176 | tf_op jit(solution)/shard_map/ppermute | solution.py:919
  322.1 14.8 %shard_map.369 = (bf16[128,1536]{1,0:T(8,128)(2,1)}, bf16[512,1024]{1,0:T(8,128)(2,1)}, bf16[512,1024]{1,0:T(8,128)(2,1)}) custom-call(bf16[128,1536]{1,0:T(8,128)(2,1)} %get-tuple-element.187.q_ref, s32[128,1]{1,0:T(8,128)} %constant_dynamic-slice_fusion.6.rpos_ref, s32[1,1024]{1,0:T(1,128)} %bitcast.72, ...), custom_call_target="tpu_custom_call" | custom-call | flops 8053063680 | bytes 8388608 | tf_op jit(solution)/shard_map/pallas_call | solution.py:744
  344.0 8.5 %shard_map.370 = (bf16[96,48,128]{2,1,0:T(8,128)(2,1)}, bf16[96,48,128]{2,1,0:T(8,128)(2,1)}, bf16[96,48,128]{2,1,0:T(8,128)(2,1)}, bf16[96,48,128]{2,1,0:T(8,128)(2,1)}, bf16[1536,512]{1,0:T(8,128)(2,1)}) custom-call(s32[2]{0:T(128)} %pad_add_fusion.me_ref, bf16[256,1536]{1,0:T(8,128)(2,1)} %get-tuple-element.169.h_ref.refs_0_, ...), custom_call_target="tpu_custom_call" | custom-call | flops 2415919104 | bytes 16777216 | tf_op jit(solution)/shard_map/pallas_call | solution.py:620
  356.1 13.1 %collective-permute-done.72 = bf16[128,1024]{1,0:T(8,128)(2,1)} collective-permute-done((bf16[128,1024]{1,0:T(8,128)(2,1)S(1)}, bf16[128,1024]{1,0:T(8,128)(2,1)}, u32[]{:S(2)}, u32[]{:S(2)}) %collective-permute-start.72) | collective-permute-done | bytes 262176 | tf_op jit(solution)/shard_map/ppermute | solution.py:919
  437.8 15.6 %collective-permute-done.86 = bf16[96,1536]{1,0:T(8,128)(2,1)S(1)} collective-permute-done((bf16[96,1536]{1,0:T(8,128)(2,1)S(1)}, bf16[96,1536]{1,0:T(8,128)(2,1)S(1)}, u32[]{:S(2)}, u32[]{:S(2)}) %collective-permute-start.86) | collective-permute-done | bytes 294944 | tf_op jit(solution)/shard_map/ppermute | solution.py:919
  457.0 9.9 %collective-permute-done.90 = bf16[32,1536]{1,0:T(8,128)(2,1)S(1)} collective-permute-done((bf16[32,1536]{1,0:T(8,128)(2,1)S(1)}, bf16[32,1536]{1,0:T(8,128)(2,1)S(1)}, u32[]{:S(2)}, u32[]{:S(2)}) %collective-permute-start.90) | collective-permute-done | bytes 98336 | tf_op jit(solution)/shard_map/ppermute | solution.py:919
  466.9 9.1 %collective-permute-done.89 = bf16[32,1536]{1,0:T(8,128)(2,1)S(1)} collective-permute-done((bf16[32,1536]{1,0:T(8,128)(2,1)S(1)}, bf16[32,1536]{1,0:T(8,128)(2,1)S(1)}, u32[]{:S(2)}, u32[]{:S(2)}) %collective-permute-start.89) | collective-permute-done | bytes 98336 | tf_op jit(solution)/shard_map/ppermute | solution.py:919
  487.2 34.0 %all-to-all-done = bf16[32,10,1536]{2,1,0:T(8,128)(2,1)S(1)} async-done(((bf16[32,10,1536]{2,1,0:T(8,128)(2,1)}), bf16[32,10,1536]{2,1,0:T(8,128)(2,1)S(1)}, u32[]{:S(2)}, u32[]{:S(2)}) %all-to-all-start) | async-done | bytes 983072 | tf_op jit(solution)/shard_map/all_to_all | solution.py:1220
  530.5 15.2 %shard_map.375 = (f32[12,192,256]{2,1,0:T(8,128)}, f32[12,192,256]{2,1,0:T(8,128)}, f32[12,192,256]{2,1,0:T(8,128)}, f32[12,192,256]{2,1,0:T(8,128)}) custom-call(f32[12,192,256]{2,1,0:T(8,128)} %bitcast.54, f32[12,192,256]{2,1,0:T(8,128)} %bitcast.58, f32[12,192,256]{2,1,0:T(8,128)} %bitcast.59, f32[12,192,192]{2,1,0:T(8,128)} %bitcast.60, ...), custom_call_target="tpu_custom_call" | custom-call | flops 1056964608 | bytes 25165824 | tf_op jit(solution)/shard_map/pallas_call | solution.py:867
  (393 shorter events, 221.8 us)
Async XLA Ops:
  7.2 194.0 %all-gather.2.cloned.1.call-start = ((), (), s32[]{:S(2)}) async-start(), calls=%async_computation.3 | async-start | bytes 10616832 | tf_op jit(solution)/shard_map/all_gather | solution.py:1072
  46.3 484.2 %reduce-scatter.3.cloned.1.call-start = ((), (), s32[]{:S(2)}) async-start(), calls=%async_computation.4 | async-start | bytes 5308416 | tf_op jit(solution)/shard_map/reduce_scatter | solution.py:1171
  87.8 55.9 %collective-permute-start.28 = (bf16[256,1664]{1,0:T(8,128)(2,1)}, bf16[256,1664]{1,0:T(8,128)(2,1)}, u32[]{:S(2)}, u32[]{:S(2)}) collective-permute-start(bf16[256,1664]{1,0:T(8,128)(2,1)} %bitcast.62), channel_id=1, source_target_pairs={{0,1},{1,0},{2,3},{3,2},{4,5},{5,4},{6,7},{7,6},{8,9},{9,8},{10,11... | collective-permute-start | bytes 2555912 | tf_op jit(solution)/shard_map/ppermute | solution.py:909
  88.5 55.4 %collective-permute-start.29 = (bf16[256,1664]{1,0:T(8,128)(2,1)}, bf16[256,1664]{1,0:T(8,128)(2,1)}, u32[]{:S(2)}, u32[]{:S(2)}) collective-permute-start(bf16[256,1664]{1,0:T(8,128)(2,1)} %bitcast.63), channel_id=1, source_target_pairs={{0,2},{1,3},{2,0},{3,1},{4,6},{5,7},{6,4},{7,5},{8,10},{9,11},{10,... | collective-permute-start | bytes 2555912 | tf_op jit(solution)/shard_map/ppermute | solution.py:909
  93.7 50.6 %collective-permute-start.30 = (bf16[256,1664]{1,0:T(8,128)(2,1)S(1)}, bf16[256,1664]{1,0:T(8,128)(2,1)}, u32[]{:S(2)}, u32[]{:S(2)}) collective-permute-start(bf16[256,1664]{1,0:T(8,128)(2,1)S(1)} %bitcast.66), channel_id=1, source_target_pairs={{0,3},{1,2},{2,1},{3,0},{4,7},{5,6},{6,5},{7,4},{8,11},{9,10},{10,... | collective-permute-start | bytes 2555912 | tf_op jit(solution)/shard_map/ppermute | solution.py:909
  108.6 34.2 %collective-permute-start.32 = (bf16[128,1024]{1,0:T(8,128)(2,1)}, bf16[128,1024]{1,0:T(8,128)(2,1)S(1)}, u32[]{:S(2)}, u32[]{:S(2)}) collective-permute-start(bf16[128,1024]{1,0:T(8,128)(2,1)} %get-tuple-element.178.refs_0_), channel_id=1, source_target_pairs={{0,16},{4,20},{8,24},{12,28},{16,0},{20,4},{24,8},{28,12},{1,17},{... | collective-permute-start | bytes 786440 | tf_op jit(solution)/shard_map/ppermute | solution.py:919
  144.3 30.3 %collective-permute-start.38 = (bf16[128,1024]{1,0:T(8,128)(2,1)S(1)}, bf16[128,1024]{1,0:T(8,128)(2,1)S(1)}, u32[]{:S(2)}, u32[]{:S(2)}) collective-permute-start(bf16[128,1024]{1,0:T(8,128)(2,1)S(1)} %copy-done.51), channel_id=1, source_target_pairs={{0,8},{4,12},{8,16},{12,20},{16,24},{20,28},{24,0},{28,4},{1,9},{5... | collective-permute-start | bytes 786440 | tf_op jit(solution)/shard_map/ppermute | solution.py:919
  175.7 24.2 %collective-permute-start.45 = (bf16[256,1536]{1,0:T(8,128)(2,1)S(1)}, bf16[256,1536]{1,0:T(8,128)(2,1)}, u32[]{:S(2)}, u32[]{:S(2)}) collective-permute-start(bf16[256,1536]{1,0:T(8,128)(2,1)S(1)} %copy-done.18), channel_id=1, source_target_pairs={{0,4},{4,0},{8,12},{12,8},{16,20},{20,16},{24,28},{28,24},{1,5},{5... | collective-permute-start | bytes 2359304 | tf_op jit(solution)/shard_map/ppermute | solution.py:914
  177.3 23.9 %collective-permute-start.46 = (bf16[128,1536]{1,0:T(8,128)(2,1)}, bf16[128,1536]{1,0:T(8,128)(2,1)S(1)}, u32[]{:S(2)}, u32[]{:S(2)}) collective-permute-start(bf16[128,1536]{1,0:T(8,128)(2,1)} %get-tuple-element.184.ob_ref.refs_10_), channel_id=1, source_target_pairs={{0,4},{4,0},{8,12},{12,8},{16,20},{20,16},{24,28},{28,24},{1,5},{5... | collective-permute-start | bytes 1179656 | tf_op jit(solution)/shard_map/ppermute | solution.py:914
  217.5 23.0 %collective-permute-start.51 = (bf16[128,1664]{1,0:T(8,128)(2,1)}, bf16[128,1664]{1,0:T(8,128)(2,1)S(1)}, u32[]{:S(2)}, u32[]{:S(2)}) collective-permute-start(bf16[128,1664]{1,0:T(8,128)(2,1)} %get-tuple-element.201), channel_id=1, source_target_pairs={{0,1},{1,0},{2,3},{3,2},{4,5},{5,4},{6,7},{7,6},{8,9},{9,8},{10,11... | collective-permute-start | bytes 1277960 | tf_op jit(solution)/shard_map/ppermute | solution.py:909
  218.6 23.2 %collective-permute-start.52 = (bf16[128,1664]{1,0:T(8,128)(2,1)}, bf16[128,1664]{1,0:T(8,128)(2,1)S(1)}, u32[]{:S(2)}, u32[]{:S(2)}) collective-permute-start(bf16[128,1664]{1,0:T(8,128)(2,1)} %get-tuple-element.202), channel_id=1, source_target_pairs={{0,2},{1,3},{2,0},{3,1},{4,6},{5,7},{6,4},{7,5},{8,10},{9,11},{10,... | collective-permute-start | bytes 1277960 | tf_op jit(solution)/shard_map/ppermute | solution.py:909
  260.7 269.9 %reduce-scatter.5.cloned.1.call-start = ((), (), s32[]{:S(2)}) async-start(), calls=%async_computation.5 | async-start | bytes 5308416 | tf_op jit(solution)/shard_map/reduce_scatter | solution.py:1173
  298.1 24.0 %collective-permute-start.62 = (bf16[128,1024]{1,0:T(8,128)(2,1)S(1)}, bf16[128,1024]{1,0:T(8,128)(2,1)S(1)}, u32[]{:S(2)}, u32[]{:S(2)}) collective-permute-start(bf16[128,1024]{1,0:T(8,128)(2,1)S(1)} %get-tuple-element.300), channel_id=1, source_target_pairs={{0,8},{4,12},{8,16},{12,20},{16,24},{20,28},{24,0},{28,4},{1,9},{5... | collective-permute-start | bytes 786440 | tf_op jit(solution)/shard_map/ppermute | solution.py:919
  352.5 28.4 %collective-permute-start.68 = (bf16[96,48,128]{2,1,0:T(8,128)(2,1)}, bf16[96,48,128]{2,1,0:T(8,128)(2,1)}, u32[]{:S(2)}, u32[]{:S(2)}) collective-permute-start(bf16[96,48,128]{2,1,0:T(8,128)(2,1)} %get-tuple-element.245), channel_id=1, source_target_pairs={{0,1},{1,0},{2,3},{3,2},{4,5},{5,4},{6,7},{7,6},{8,9},{9,8},{10,11... | collective-permute-start | bytes 3538952 | tf_op jit(solution)/shard_map/ppermute | solution.py:909
  353.4 30.6 %collective-permute-start.70 = (bf16[96,48,128]{2,1,0:T(8,128)(2,1)}, bf16[96,48,128]{2,1,0:T(8,128)(2,1)}, u32[]{:S(2)}, u32[]{:S(2)}) collective-permute-start(bf16[96,48,128]{2,1,0:T(8,128)(2,1)} %get-tuple-element.247), channel_id=1, source_target_pairs={{0,2},{1,3},{2,0},{3,1},{4,6},{5,7},{6,4},{7,5},{8,10},{9,11},{10,... | collective-permute-start | bytes 3538952 | tf_op jit(solution)/shard_map/ppermute | solution.py:909
  421.8 31.6 %collective-permute-start.86 = (bf16[96,1536]{1,0:T(8,128)(2,1)S(1)}, bf16[96,1536]{1,0:T(8,128)(2,1)S(1)}, u32[]{:S(2)}, u32[]{:S(2)}) collective-permute-start(bf16[96,1536]{1,0:T(8,128)(2,1)S(1)} %get-tuple-element.308), channel_id=1, source_target_pairs={{0,16},{4,20},{8,24},{12,28},{16,0},{20,4},{24,8},{28,12},{1,17},{... | collective-permute-start | bytes 884744 | tf_op jit(solution)/shard_map/ppermute | solution.py:919
  421.8 35.1 %collective-permute-start.85 = (bf16[96,1536]{1,0:T(8,128)(2,1)S(1)}, bf16[96,1536]{1,0:T(8,128)(2,1)S(1)}, u32[]{:S(2)}, u32[]{:S(2)}) collective-permute-start(bf16[96,1536]{1,0:T(8,128)(2,1)S(1)} %get-tuple-element.306), channel_id=1, source_target_pairs={{0,24},{4,28},{8,0},{12,4},{16,8},{20,12},{24,16},{28,20},{1,25},{... | collective-permute-start | bytes 884744 | tf_op jit(solution)/shard_map/ppermute | solution.py:919
  432.3 34.6 %collective-permute-start.90 = (bf16[32,1536]{1,0:T(8,128)(2,1)S(1)}, bf16[32,1536]{1,0:T(8,128)(2,1)S(1)}, u32[]{:S(2)}, u32[]{:S(2)}) collective-permute-start(bf16[32,1536]{1,0:T(8,128)(2,1)S(1)} %get-tuple-element.310), channel_id=1, source_target_pairs={{0,8},{4,12},{8,16},{12,20},{16,24},{20,28},{24,0},{28,4},{1,9},{5... | collective-permute-start | bytes 294920 | tf_op jit(solution)/shard_map/ppermute | solution.py:919
  432.4 43.6 %collective-permute-start.89 = (bf16[32,1536]{1,0:T(8,128)(2,1)S(1)}, bf16[32,1536]{1,0:T(8,128)(2,1)S(1)}, u32[]{:S(2)}, u32[]{:S(2)}) collective-permute-start(bf16[32,1536]{1,0:T(8,128)(2,1)S(1)} %get-tuple-element.311), channel_id=1, source_target_pairs={{0,16},{4,20},{8,24},{12,28},{16,0},{20,4},{24,8},{28,12},{1,17},{... | collective-permute-start | bytes 294920 | tf_op jit(solution)/shard_map/ppermute | solution.py:919
  437.4 38.6 %collective-permute-start.88 = (bf16[32,1536]{1,0:T(8,128)(2,1)S(1)}, bf16[32,1536]{1,0:T(8,128)(2,1)S(1)}, u32[]{:S(2)}, u32[]{:S(2)}) collective-permute-start(bf16[32,1536]{1,0:T(8,128)(2,1)S(1)} %get-tuple-element.309), channel_id=1, source_target_pairs={{0,24},{4,28},{8,0},{12,4},{16,8},{20,12},{24,16},{28,20},{1,25},{... | collective-permute-start | bytes 294920 | tf_op jit(solution)/shard_map/ppermute | solution.py:919
  478.2 42.9 %all-to-all-start = ((bf16[32,10,1536]{2,1,0:T(8,128)(2,1)}), bf16[32,10,1536]{2,1,0:T(8,128)(2,1)S(1)}, u32[]{:S(2)}, u32[]{:S(2)}) async-start(bf16[32,10,1536]{2,1,0:T(8,128)(2,1)} %pad_maximum_fusion), calls=%async_computation | async-start | bytes 3145728 | tf_op jit(solution)/shard_map/all_to_all | solution.py:1220
  483.6 62.2 %collective-permute-start.82 = (bf16[256,1536]{1,0:T(8,128)(2,1)}, bf16[256,1536]{1,0:T(8,128)(2,1)S(1)}, u32[]{:S(2)}, u32[]{:S(2)}) collective-permute-start(bf16[256,1536]{1,0:T(8,128)(2,1)} %get-tuple-element.266), channel_id=1, source_target_pairs={{0,1},{1,0},{2,3},{3,2},{4,5},{5,4},{6,7},{7,6},{8,9},{9,8},{10,11... | collective-permute-start | bytes 2359304 | tf_op jit(solution)/shard_map/ppermute | solution.py:909
  485.4 60.4 %collective-permute-start.83 = (bf16[256,1536]{1,0:T(8,128)(2,1)}, bf16[256,1536]{1,0:T(8,128)(2,1)S(1)}, u32[]{:S(2)}, u32[]{:S(2)}) collective-permute-start(bf16[256,1536]{1,0:T(8,128)(2,1)} %get-tuple-element.267), channel_id=1, source_target_pairs={{0,2},{1,3},{2,0},{3,1},{4,6},{5,7},{6,4},{7,5},{8,10},{9,11},{10,... | collective-permute-start | bytes 2359304 | tf_op jit(solution)/shard_map/ppermute | solution.py:909
  486.9 58.9 %collective-permute-start.84 = (bf16[256,1536]{1,0:T(8,128)(2,1)}, bf16[256,1536]{1,0:T(8,128)(2,1)}, u32[]{:S(2)}, u32[]{:S(2)}) collective-permute-start(bf16[256,1536]{1,0:T(8,128)(2,1)} %get-tuple-element.268), channel_id=1, source_target_pairs={{0,3},{1,2},{2,1},{3,0},{4,7},{5,6},{6,5},{7,4},{8,11},{9,10},{10,... | collective-permute-start | bytes 2359304 | tf_op jit(solution)/shard_map/ppermute | solution.py:909
  (139 other events, 1682.7 us)
Sparse Core Ops, SparseCore 0:
  46.4 110.7 all-gather.1
  259.9 71.3 reduce-scatter.2
  395.3 80.4 reduce-scatter.4

commit v8 on v7

--- a/solution.py
+++ b/solution.py
@@ -14,6 +14,7 @@
 BR = 192
 BC = 256
 LANES = 128
+UPPER = 128
 
 norm_eps = 1e-06
 beta_one = 0.9
@@ -125,10 +126,9 @@
     piece_refs = refs[micros + 1 : micros + 1 + len(pieces)]
     refs = refs[micros + 1 + len(pieces) :]
     h_ref = refs[0]
-    kv_refs = refs[1 : 1 + micros]
-    win_ref, wout_ref, held, held_out, sems, out_sems = refs[1 + micros :]
+    kv_ref, win_ref, wout_ref, held, held_out, sems, out_sems = refs[1:]
     groups = held.shape[1] // BC
-    kv_groups = kv_refs[0].shape[-1] // BC
+    kv_groups = kv_ref.shape[-1] // BC
     rows = x_refs[0].shape[0]
     ctx, shard = me_ref[0], me_ref[1]
     chip, core = lax.div(ctx, 2), lax.rem(ctx, 2)
@@ -177,8 +177,7 @@
     def _(b):
         across = pl.ds(pl.multiple_of((q_groups + b) * BC, BC), BC)
         made = dot(h_ref[...], held[:, across]).astype(low_type)
-        for m in range(micros):
-            kv_refs[m][:, pl.ds(pl.multiple_of(b * BC, BC), BC)] = made[m * rows : (m + 1) * rows]
+        kv_ref[:, pl.ds(pl.multiple_of(b * BC, BC), BC)] = made
 
     for copy in copies:
         copy.wait()
@@ -190,17 +189,17 @@
     in_width = (HEADS + 2 * KVH) * HD
     out_width = HEADS * HD
     kv_width = 2 * KVH * HD
-    made = call(
+    return call(
         functools.partial(
             project_kernel, pieces, chips, members, slots, (in_width + out_width) // BC, micros
         ),
         tuple(
             [shaped((micros * rows, width), low_type)]
-            + [shaped((rows, kv_width), low_type)] * micros
+            + [shaped((micros * rows, kv_width), low_type)]
             + [shaped((width, in_width), low_type), shaped((width, out_width), low_type)]
         ),
         [in_smem, in_smem] + [in_vmem] * (micros + 1) + [in_any] * len(arrays),
-        tuple([in_vmem] * (1 + micros) + [in_any, in_any]),
+        (in_vmem, in_vmem, in_any, in_any),
         [
             pltpu.VMEM((width, in_width), low_type),
             pltpu.VMEM((width, out_width), low_type),
@@ -210,7 +209,6 @@
         2 * micros * rows * width * kv_width,
         4 * width * (in_width + out_width),
     )(order, me, *xs, gains, *arrays)
-    return made[0], made[1 : 1 + micros], made[1 + micros], made[2 + micros]
 
 
 def query_kernel(h_ref, w_ref, *refs):
@@ -250,19 +248,25 @@
     )(h, w)
 
 
-def load_keys(parts, held, sem):
-    start = 0
-    for part in parts:
-        count = part.shape[0]
-        pltpu.make_async_copy(part, held.at[pl.ds(start, count)], sem).start()
-        start += count
-
-
-def attend_kernel(count, q_ref, rpos_ref, kpos_ref, x_ref, gain_ref, w_ref, *refs):
-    parts = refs[:count]
-    ob_ref, log_ref, x2_ref, h2_ref, bias, kv_ref, held, sems = refs[count:]
+def load_keys(kv_ref, micro, rows, held, sem):
+    count = held.shape[0] // rows
+    span = kv_ref.shape[0] // count
+
+    @pl.loop(0, count)
+    def _(i):
+        pltpu.make_async_copy(
+            kv_ref.at[pl.ds(pl.multiple_of(i * span + micro * rows, 16), rows)],
+            held.at[pl.ds(pl.multiple_of(i * rows, 16), rows)],
+            sem,
+        ).start()
+
+
+def attend_kernel(
+    micro, q_ref, rpos_ref, kpos_ref, x_ref, gain_ref, w_ref, all_ref,
+    ob_ref, log_ref, x2_ref, h2_ref, bias, kv_ref, held, sems,
+):
     rows = q_ref.shape[0]
-    load_keys(parts, kv_ref, sems.at[0])
+    load_keys(all_ref, micro, rows, kv_ref, sems.at[0])
     pltpu.make_async_copy(w_ref, held, sems.at[1]).start()
     bias[...] = jnp.where(kpos_ref[...] <= rpos_ref[...], 0.0, masked_score)
     log_ref[...] = jnp.zeros_like(log_ref)
@@ -295,29 +299,29 @@
     h2_ref[...] = unit_rows(x2_ref[...], gain_ref[1:2])[0].astype(low_type)
 
 
-def attend(q, kv_parts, rows_pos, key_pos, x, gains, w):
+def attend(micro, q, kv, rows_pos, key_pos, x, gains, w):
     rows, width = q.shape
     length = key_pos.shape[1]
     model = x.shape[1]
     return call(
-        functools.partial(attend_kernel, len(kv_parts)),
+        functools.partial(attend_kernel, micro),
         (
             shaped((rows, width), low_type),
             shaped((3 * rows, LANES), jnp.float32),
             shaped((rows, model), jnp.float32),
             shaped((rows, model), low_type),
         ),
-        [in_vmem] * 5 + [in_any] * (1 + len(kv_parts)),
+        [in_vmem] * 5 + [in_any] * 2,
         (in_vmem,) * 4,
         [
             pltpu.VMEM((rows, length), jnp.float32),
-            pltpu.VMEM((length, kv_parts[0].shape[1]), low_type),
+            pltpu.VMEM((length, kv.shape[1]), low_type),
             pltpu.VMEM((model, width), low_type),
             pltpu.SemaphoreType.DMA((2,)),
         ],
         16 * rows * length * width,
         8 * MIB,
-    )(q, rows_pos, key_pos, x, gains, w, *kv_parts)
+    )(q, rows_pos, key_pos, x, gains, w, kv)
 
 
 def router_parts(h2, router, experts):
@@ -330,8 +334,8 @@
 def expert_kernel(sources, micro, order_ref, me_ref, router_ref, *refs):
     h_parts = refs[:sources]
     c_parts = refs[sources : 2 * sources]
-    w_ref = refs[2 * sources]
-    outs = refs[2 * sources + 1 :]
+    w_refs = refs[2 * sources : 2 * sources + 2]
+    outs = refs[2 * sources + 2 :]
     back_refs = outs[:sources]
     z_ref, dg_ref, du_ref, cs, xs_ref = outs[sources : sources + 5]
     held, chance, load_sem, w_sems = outs[sources + 5 :]
@@ -348,11 +352,12 @@
         @pl.loop(0, row_groups)
         def _(a):
             for k in range(3):
-                pltpu.make_async_copy(
-                    w_ref.at[order_ref[(k * row_groups + a) * col_groups + b]],
-                    held.at[k, pl.ds(pl.multiple_of(a * BR, 64), BR), pl.ds(b * BC, BC)],
-                    w_sems.at[b],
-                ).start()
+                slot = order_ref[(k * row_groups + a) * col_groups + b]
+                for start, ref in zip((0, UPPER), w_refs):
+                    down = pl.ds(pl.multiple_of(a * BR + start, 64), ref.shape[1])
+                    pltpu.make_async_copy(
+                        ref.at[slot], held.at[k, down, pl.ds(b * BC, BC)], w_sems.at[b]
+                    ).start()
 
     wait_bytes(xs_ref, load_sem.at[0])
     wait_bytes(cs, load_sem.at[1])
@@ -394,7 +399,7 @@
         back_refs[j][:, width:] = tail[j * rows : (j + 1) * rows]
 
 
-def run_expert(micro, order, me, router, h_parts, c_parts, w):
+def run_expert(micro, order, me, router, h_parts, c_parts, ws):
     sources = len(h_parts)
     rows, width = h_parts[0].shape
     total = sources * rows
@@ -405,7 +410,7 @@
             + [shaped((total, FF), low_type)] * 3
             + [shaped((total, width + LANES), low_type), shaped((total, width), low_type)]
         ),
-        [in_smem, in_smem, in_vmem] + [in_any] * (2 * sources + 1),
+        [in_smem, in_smem, in_vmem] + [in_any] * (2 * sources + 2),
         tuple([in_vmem] * (sources + 5)),
         [
             pltpu.VMEM((3, width, FF), low_type),
@@ -415,10 +420,10 @@
         ],
         10 * total * width * FF,
         20 * MIB,
-    )(order, me, router, *h_parts, *c_parts, w)
-
-
-def produce_kernel(sources, order_ref, w_ref, *refs):
+    )(order, me, router, *h_parts, *c_parts, *ws)
+
+
+def produce_kernel(sources, order_ref, upper_ref, lower_ref, *refs):
     out_refs = refs[-3 - sources : -3]
     z_refs = refs[: -3 - sources]
     zs, held, sem = refs[-3:]
@@ -430,11 +435,12 @@
     @pl.loop(0, row_groups)
     def _(a):
         for b in range(col_groups):
-            pltpu.make_async_copy(
-                w_ref.at[order_ref[(2 * row_groups + a) * col_groups + b]],
-                held.at[pl.ds(pl.multiple_of(a * BR, 64), BR), pl.ds(b * BC, BC)],
-                sem,
-            ).start()
+            slot = order_ref[(2 * row_groups + a) * col_groups + b]
+            for start, ref in zip((0, UPPER), (upper_ref, lower_ref)):
+                down = pl.ds(pl.multiple_of(a * BR + start, 64), ref.shape[1])
+                pltpu.make_async_copy(
+                    ref.at[slot], held.at[down, pl.ds(b * BC, BC)], sem
+                ).start()
 
     for m, z_ref in enumerate(z_refs):
         zs[m * total : (m + 1) * total] = z_ref[...]
@@ -448,13 +454,13 @@
                 out_refs[j][m * rows : (m + 1) * rows, cut] = made[start : start + rows]
 
 
-def produce(order, w, zs, sources, width):
+def produce(order, ws, zs, sources, width):
     micros = len(zs)
     total = zs[0].shape[0]
     return call(
         functools.partial(produce_kernel, sources),
         tuple([shaped((micros * total // sources, width), low_type)] * sources),
-        [in_smem, in_any] + [in_vmem] * micros,
+        [in_smem, in_any, in_any] + [in_vmem] * micros,
         tuple([in_vmem] * sources),
         [
             pltpu.VMEM((micros * total, FF), low_type),
@@ -463,7 +469,7 @@
         ],
         2 * micros * total * width * FF,
         8 * MIB,
-    )(order, w, *zs)
+    )(order, *ws, *zs)
 
 
 def outer_kernel(groups, col_groups, order_ref, *refs):
@@ -691,14 +697,15 @@
     )(me, x2, cot, h2, gains, router, w, *backs)
 
 
-def attend_back_kernel(count, q_ref, rpos_ref, kpos_ref, ob_ref, log_ref, do_ref, *refs):
-    parts = refs[:count]
-    dq_ref, own_ref, other_ref, bias, kv_ref, sem = refs[count:]
+def attend_back_kernel(
+    micro, q_ref, rpos_ref, kpos_ref, ob_ref, log_ref, do_ref, all_ref, *refs
+):
+    dq_ref, out_ref, bias, kv_ref, grad_ref, sems = refs[-6:]
     rows = q_ref.shape[0]
-    load_keys(parts, kv_ref, sem)
+    load_keys(all_ref, micro, rows, kv_ref, sems.at[0])
     length = kv_ref.shape[0]
     bias[...] = jnp.where(kpos_ref[...] <= rpos_ref[...], 0.0, masked_score)
-    wait_bytes(kv_ref, sem)
+    wait_bytes(kv_ref, sems.at[0])
 
     @pl.loop(0, KVH // 2)
     def _(pair):
@@ -731,29 +738,50 @@
             value_grad = value_term if part == 0 else value_grad + value_term
             query_grads.append(dot(score_grad, keys) * HD**-0.5)
         unstack_heads(dq_ref, pair, query_grads[0], query_grads[1])
-        half = length // 2
-        for ref, cut in ((own_ref, slice(0, half)), (other_ref, slice(half, length))):
-            ref[:, pl.ds(lane, LANES)] = key_grad[cut].astype(low_type)
-            ref[:, pl.ds(value_lane, LANES)] = value_grad[cut].astype(low_type)
-
-
-def attend_back(q, kv_parts, rows_pos, key_pos, ob, log_total, do):
+        grad_ref[:, pl.ds(lane, LANES)] = key_grad.astype(low_type)
+        grad_ref[:, pl.ds(value_lane, LANES)] = value_grad.astype(low_type)
+
+    count = length // rows
+    span = out_ref.shape[0] // count
+
+    @pl.loop(0, count)
+    def _(i):
+        pltpu.make_async_copy(
+            grad_ref.at[pl.ds(pl.multiple_of(i * rows, 16), rows)],
+            out_ref.at[pl.ds(pl.multiple_of(i * span + micro * rows, 16), rows)],
+            sems.at[1],
+        ).start()
+
+    wait_bytes(grad_ref, sems.at[1])
+
+
+def attend_back(micro, q, kv, rows_pos, key_pos, ob, log_total, do, shared):
     rows, width = q.shape
     length = key_pos.shape[1]
-    kv_width = kv_parts[0].shape[1]
-    return call(
-        functools.partial(attend_back_kernel, len(kv_parts)),
-        (shaped((rows, width), low_type),) + (shaped((length // 2, kv_width), low_type),) * 2,
-        [in_vmem] * 6 + [in_any] * len(kv_parts),
-        (in_vmem,) * 3,
-        [
+    operands = [q, rows_pos, key_pos, ob, log_total, do, kv]
+    in_specs = [in_vmem] * 6 + [in_any]
+    aliases = {}
+    if shared is not None:
+        aliases = {len(operands): 1}
+        operands.append(shared)
+        in_specs.append(in_any)
+    return pl.pallas_call(
+        functools.partial(attend_back_kernel, micro),
+        out_shape=(shaped((rows, width), low_type), shaped(kv.shape, low_type)),
+        in_specs=in_specs,
+        out_specs=(in_vmem, in_any),
+        scratch_shapes=[
             pltpu.VMEM((rows, length), jnp.float32),
-            pltpu.VMEM((length, kv_width), low_type),
-            pltpu.SemaphoreType.DMA,
+            pltpu.VMEM((length, kv.shape[1]), low_type),
+            pltpu.VMEM((length, kv.shape[1]), low_type),
+            pltpu.SemaphoreType.DMA((2,)),
         ],
-        40 * rows * length * width,
-        8 * MIB,
-    )(q, rows_pos, key_pos, ob, log_total, do, *kv_parts)
+        input_output_aliases=aliases,
+        compiler_params=pltpu.CompilerParams(vmem_limit_bytes=VMEM_LIMIT),
+        cost_estimate=pl.CostEstimate(
+            flops=40 * rows * length * width, bytes_accessed=8 * MIB, transcendentals=0
+        ),
+    )(*operands)
 
 
 def query_back_kernel(w_ref, *refs):
@@ -796,19 +824,16 @@
     micros, rows = x_ref.shape[:2]
     dx_refs = refs[:micros]
     part_refs = refs[micros : 2 * micros]
-    dkv_refs = refs[2 * micros : 3 * micros]
-    out_ref, stat_ref, rows_ref, grad, held, sem = refs[3 * micros :]
+    dkv_ref, out_ref, stat_ref, grad, held, sem = refs[2 * micros :]
     kv_width = held.shape[1]
     copy = pltpu.make_async_copy(
         w_ref.at[:, pl.ds(w_ref.shape[1] - kv_width, kv_width)], held, sem
     )
     copy.start()
-    for m in range(micros):
-        rows_ref[m * rows : (m + 1) * rows] = dkv_refs[m][...]
     copy.wait()
     for n in range(held.shape[0] // BC):
         cut = slice(n * BC, (n + 1) * BC)
-        made = dot(rows_ref[...], held[cut, :], NT)
+        made = dot(dkv_ref[...], held[cut, :], NT)
         for m in range(micros):
             grad[m, :, cut] = part_refs[m][:, cut] + made[m * rows : (m + 1) * rows]
     total = jnp.zeros((1, x_ref.shape[-1]), jnp.float32)
@@ -821,23 +846,22 @@
     stat_ref[...] = jnp.broadcast_to(total, stat_ref.shape)
 
 
-def input_back(x, gains, w, dxs, parts, dkvs):
+def input_back(x, gains, w, dxs, parts, dkv):
     micros, rows, width = x.shape
-    kv_width = dkvs[0].shape[1]
+    kv_width = dkv.shape[1]
     return call(
         input_kernel,
         (shaped(x.shape, jnp.float32), shaped((8, width), jnp.float32)),
-        [in_vmem, in_vmem, in_any] + [in_vmem] * (3 * micros),
+        [in_vmem, in_vmem, in_any] + [in_vmem] * (2 * micros + 1),
         (in_vmem,) * 2,
         [
-            pltpu.VMEM((micros * rows, kv_width), low_type),
             pltpu.VMEM(x.shape, jnp.float32),
             pltpu.VMEM((width, kv_width), low_type),
             pltpu.SemaphoreType.DMA,
         ],
         2 * micros * rows * width * kv_width,
         14 * MIB,
-    )(x, gains, w, *dxs, *parts, *dkvs)
+    )(x, gains, w, *dxs, *parts, dkv)
 
 
 def rotate_kernel(b_ref, m_ref, s_ref, l_ref, r_ref, *refs):
@@ -1061,15 +1085,13 @@
     me = jnp.stack([ctx, lax.axis_index("shard").astype(jnp.int32)])
     row_ids = jnp.arange(rows, dtype=jnp.int32)
     all_pos = assign[:, row_ids // span] * span + row_ids % span
-    ring_ids = (ctx // 2 - jnp.arange(chips, dtype=jnp.int32)) % chips * 2
-    key_ids = jnp.concatenate([ring_ids + ctx % 2, ring_ids + (1 - ctx % 2)])
-    key_pos = all_pos[key_ids].reshape(1, rows * ctx_count)
+    key_pos = all_pos.reshape(1, rows * ctx_count)
     rows_pos = all_pos[ctx].reshape(rows, 1)
     router_pad = jnp.pad(router.astype(low_type), ((0, 0), (0, LANES - shard_count)))
 
     far, pieces, arrays = gather_weights(dense_weight.astype(low_type), chips, shard_count)
     expert_low = after(expert_weight[0].astype(low_type), *far)
-    expert_all = lax.all_gather(expert_low, "ctx", axis=0, tiled=True)
+    expert_all = [lax.all_gather(expert_low[:, :UPPER], "ctx", axis=0, tiled=True)]
 
     lanes = jnp.arange(LANES, dtype=jnp.int32)
     hits = jnp.sum((routes[..., None] == lanes).astype(low_type), axis=2)
@@ -1094,18 +1116,14 @@
     )
     q = make_queries(h1, w_in, micros)
     h1_other = to_ctx(h1, 1)
-    kvs, obs, logs, x2s, h2s = [], [], [], [], []
-    chip_kv = []
-    for m in range(micros):
-        own = kv[m] if m == 0 else after(kv[m], chip_kv[m - 1][1 % chips])
-        chip_kv.append(from_chips(own, chips))
+    obs, logs, x2s, h2s = [], [], [], []
+    kv_all = lax.all_gather(after(kv, expert_all[0]), "ctx", axis=0, tiled=True)
+    lower = after(expert_low[:, UPPER:], kv_all, q, cot_parts)
+    expert_all.append(lax.all_gather(lower, "ctx", axis=0, tiled=True))
     for m in range(micros):
         query = after(q[m], *(cot_parts if m == 0 else obs[m - 1 : m]))
-        parts = chip_kv[m]
-        swapped = after(parts, q[0] if m == 0 else obs[m - 1])
-        kvs.append(parts + [to_ctx(part, 1) for part in swapped])
         ob, log_total, x2, h2 = attend(
-            query, kvs[m], rows_pos, key_pos, tokens[m], norm_gains, w_out
+            m, query, kv_all, rows_pos, key_pos, tokens[m], norm_gains, w_out
         )
         obs.append(ob)
         logs.append(log_total)
@@ -1134,68 +1152,58 @@
     expert_terms = outer_blocks(
         after(expert_inverse, *backs[0]), width, (0, 0, 1), [xs, cs], [dgs, dus, zs]
     )
-    dxs, das, dqs, stats, own_grads, far_grads = [], [], [], [], [], []
-    outs = None
+    dxs, das, dqs, stats = [], [], [], []
+    dkv_terms = None
     for m in range(micros):
         here = after(me, expert_terms, backs[-1]) if m == 0 else after(me, dqs[-1])
         dx, da, do, stat = merge(
             here, x2s[m], cotangent[m], h2s[m], norm_gains, router_pad, w_out, backs[m]
         )
-        if m == micros - 1:
-            ready = own_grads[-1][1 % chips] if m else da
-            outs = produce(after(expert_inverse, da, ready), expert_all, zs, shard_count, width)
-            do = after(do, outs[0], *(far_grads[-1][:1] + far_grads[-1][-1:] if m else []))
-        dq, dkv_own, dkv_other = attend_back(
-            q[m], kvs[m], rows_pos, key_pos, obs[m], logs[m], do
+        dq, dkv_terms = attend_back(
+            m, q[m], kv_all, rows_pos, key_pos, obs[m], logs[m], do, dkv_terms
         )
-        got = to_ctx(dkv_other, 1)
-        parts = []
-        for o in range(chips):
-            cut = slice(o * rows, (o + 1) * rows)
-            part = wide(dkv_own[cut]) + wide(got[cut])
-            parts.append(part if o == 0 else part.astype(low_type))
-        own_grads.append(parts)
-        far_grads.append([to_chip(part, -o) for o, part in enumerate(parts[1:], 1)])
         dxs.append(dx)
         das.append(da)
         dqs.append(dq)
         stats.append(stat)
 
-    dkvs = [add_wide([own_grads[m][0]] + far_grads[m]).astype(low_type) for m in range(micros)]
-
     def other_core(parts):
         return [to_ctx(part, 1) for part in parts]
 
     da_others, dq_others = other_core(das), other_core(dqs)
     first_term = after(expert_terms[0], *backs[-1])
     expert_sums = [lax.psum_scatter(first_term, "ctx", scatter_dimension=0, tiled=True)]
-    late_term = after(expert_terms[1], *dkvs)
-    expert_sums.append(lax.psum_scatter(late_term, "ctx", scatter_dimension=0, tiled=True))
+    dkv = lax.psum_scatter(
+        after(dkv_terms, expert_sums[0]), "ctx", scatter_dimension=0, tiled=True
+    )
     early = gradient_pieces(
         shard_count,
-        after(me, own_grads[-1][1 % chips]),
+        after(me, dkv_terms),
         [([h1, h1_other], dqs + dq_others), (das + da_others, obs + ob_others)],
         [q_groups, q_groups],
         False,
     )
     h1_turned = early[4]
-    early_rows, early_seen = sum_members(early[:4], None, shard_count)
+    outs = produce(after(expert_inverse, early[0]), expert_all, zs, shard_count, width)
     parts_back = query_back(after(w_in, early[0]), dqs)
-    dkv_others = other_core(after(dkvs, parts_back))
+    early_rows, early_seen = sum_members(early[:4], (outs, parts_back), shard_count)
+    chip = ctx // 2
+    early_parts = sum_chips(early_rows, chip, chips)
     late = gradient_pieces(
         shard_count,
         after(me, *early_seen),
-        [([h1_turned], dkvs + dkv_others)],
+        [([h1_turned], [dkv, to_ctx(dkv, 1)])],
         [kv_groups],
         True,
     )
     input_grad, gain_stat = input_back(
-        after(tokens, late[0]), norm_gains, w_in, dxs, parts_back, dkvs
-    )
-    late_rows, late_seen = sum_members(late[:4], input_grad, shard_count)
+        after(tokens, late[0]), norm_gains, w_in, dxs, parts_back, dkv
+    )
+    late_rows, late_seen = sum_members(late[:4], (input_grad, early_parts), shard_count)
+    late_term = after(expert_terms[1], *late_seen)
+    expert_sums.append(lax.psum_scatter(late_term, "ctx", scatter_dimension=0, tiled=True))
     arrived = [to_partner(part, j) for j, part in enumerate(after(list(outs), *late_seen))]
-    chip = ctx // 2
-    early_sum = add_wide(sum_chips(early_rows, chip, chips)).astype(low_type)
+    early_sum = add_wide(early_parts).astype(low_type)
     late_sum = add_wide(sum_chips(late_rows, chip, chips)).astype(low_type)
     all_sums = jnp.concatenate([early_sum, late_sum], axis=0)
     places = jnp.asarray(piece_places(row_groups, q_groups, kv_groups), jnp.int32)[dense_order]
@@ -1216,7 +1224,7 @@
             jnp.broadcast_to(stat_parts, (devices, extra, piece_width)),
         ],
         axis=1,
-    ).reshape(devices * (slots + extra), piece_width)
+    ).reshape(devices * 2, (slots + extra) * piece_width // 2)
     ordered = lax.all_to_all(ordered, ("ctx", "shard"), split_axis=0, concat_axis=0, tiled=True)
     ordered = ordered.reshape(devices, slots + extra, piece_width)
     stat_rows = jnp.sum(wide(ordered[:, slots:]), axis=0).reshape(shard_count + 2, width)

time: 563 us -> 526 us (0.934)
  starting transfers between devices: 96.1 us -> 74 us
  waiting for transfers between devices: 201 us -> 190 us
  other arithmetic: 28.7 us -> 19.3 us
    ppermute x21 -> x9, waiting for transfers between devices: 113 us -> 33.6 us  [to_chip(): lax.ppermute(array, 'ctx', [(i, (i + 2 * offset) % count) for i in range(...]
    ppermute x37, waiting for transfers between devices: 50.4 us -> 102 us  [to_partner(): return lax.ppermute(array, 'shard', [(i, i ^ offset) for i in range(count)])]
    ppermute x21 -> x9, starting transfers between devices: 42.4 us -> 17.4 us  [to_chip(): lax.ppermute(array, 'ctx', [(i, (i + 2 * offset) % count) for i in range(...]
    reduce_scatter x1, waiting for transfers between devices: 0.01 us -> 8.34 us  [shards(): lax.psum_scatter(first_term, 'ctx', scatter_dimension=0, tiled=True)]
  transfers between devices with their start and end apart: 95 -> 75, of which waited for: 35 -> 35; matrix products, arithmetic and copies ran while one was open for 7% -> 6% of each run, Pallas kernels for 34% -> 37%
where the time goes in v8:
time: 526 us; the launch traced here: 518 us
  Pallas kernels  193 us (37%)
  waiting for transfers between devices  190 us (36%)
  starting transfers between devices  74 us (14%)
  local copies, waits for them, and re-layouts  26 us (5%)
  other arithmetic  19.3 us (4%)
  between operations  15.4 us (3%)
    ppermute x37, waiting for transfers between devices, to_partner(): return lax.ppermute(array, 'shard', [(i, i ^ offset) for i in range(count)])  102 us
    ppermute x37, starting transfers between devices, to_partner(): return lax.ppermute(array, 'shard', [(i, i ^ offset) for i in range(count)])  44.7 us
    all_to_all x1, waiting for transfers between devices, shards(): lax.all_to_all(ordered, ('ctx', 'shard'), split_axis=0, concat_axis=0, ti...  37.9 us
    ppermute x9, waiting for transfers between devices, to_chip(): lax.ppermute(array, 'ctx', [(i, (i + 2 * offset) % count) for i in range(...  33.6 us
    pallas_call x2, Pallas kernels, run_expert(): call(functools.partial(expert_kernel, sources, micro), tuple([shaped((row...  32.2 us
    pallas_call x2, Pallas kernels, attend_back(): pl.pallas_call(functools.partial(attend_back_kernel, micro), out_shape=(s...  31 us
    pallas_call x2, Pallas kernels, attend(): call(functools.partial(attend_kernel, micro), (shaped((rows, width), low_...  25.6 us
    pallas_call x2, Pallas kernels, rotate(): pl.pallas_call(rotate_kernel, grid=(count,), out_shape=(shaped(weight.sha...  21.1 us
  transfers between devices with their start and end apart: 75, of which 35 were waited for; matrix products, arithmetic and copies ran while one was open for 6% of the time, Pallas kernels for 37%

profile of v8, /device:TPU:0, one launch (start us, length us, event | category | flops | bytes accessed | tf_op | source)
XLA Modules:
  0.0 518.2 jit_solution(13643009630363470038)
XLA Ops:
  15.0 7.7 %collective-permute-done.7.refs_11_ = bf16[4,192,256]{2,1,0:T(8,128)(2,1)S(1)} collective-permute-done((bf16[4,192,256]{2,1,0:T(8,128)(2,1)S(1)}, bf16[4,192,256]{2,1,0:T(8,128)(2,1)S(1)}, u32[]{:S(2)}, u32[]{:S(2)}) %collective-permute-start.7) | collective-permute-done | bytes 393248 | tf_op jit(solution)/shard_map/ppermute | solution.py:943
  23.6 8.2 %collective-permute-done.3.refs_7_ = bf16[4,192,256]{2,1,0:T(8,128)(2,1)S(1)} collective-permute-done((bf16[4,192,256]{2,1,0:T(8,128)(2,1)S(1)}, bf16[4,192,256]{2,1,0:T(8,128)(2,1)S(1)}, u32[]{:S(2)}, u32[]{:S(2)}) %collective-permute-start.3) | collective-permute-done | bytes 393248 | tf_op jit(solution)/shard_map/ppermute | solution.py:933
  50.2 13.8 %collective-permute-done.20.refs_23_ = bf16[8,192,256]{2,1,0:T(8,128)(2,1)S(1)} collective-permute-done((bf16[8,192,256]{2,1,0:T(8,128)(2,1)S(1)}, bf16[8,192,256]{2,1,0:T(8,128)(2,1)S(1)}, u32[]{:S(2)}, u32[]{:S(2)}) %collective-permute-start.20) | collective-permute-done | bytes 786464 | tf_op jit(solution)/shard_map/ppermute | solution.py:933
  78.9 7.7 %collective-permute-done.15.refs_19_ = bf16[4,96,256]{2,1,0:T(8,128)(2,1)S(1)} collective-permute-done((bf16[4,96,256]{2,1,0:T(8,128)(2,1)S(1)}, bf16[4,96,256]{2,1,0:T(8,128)(2,1)S(1)}, u32[]{:S(2)}, u32[]{:S(2)}) %collective-permute-start.15) | collective-permute-done | bytes 196640 | tf_op jit(solution)/shard_map/ppermute | solution.py:933
  99.1 12.2 %shard_map.358 = (bf16[256,1536]{1,0:T(8,128)(2,1)}, bf16[256,1024]{1,0:T(8,128)(2,1)}, bf16[1536,2560]{1,0:T(8,128)(2,1)}, bf16[1536,1536]{1,0:T(8,128)(2,1)}) custom-call(s32[128]{0:T(128)} %order_ref.1, s32[2]{0:T(128)} %pad_add_fusion.me_ref, f32[128,1536]{1,0:T(8,128)} %get-tuple-element.281.refs_0_.x_ref, ...), custom_call_target="tpu_custom_call" | custom-call | flops 805306368 | bytes 25165824 | tf_op jit(solution)/shard_map/pallas_call | solution.py:192
  123.1 11.0 %collective-permute-done.28.refs_5_ = bf16[256,1664]{1,0:T(8,128)(2,1)} collective-permute-done((bf16[256,1664]{1,0:T(8,128)(2,1)S(1)}, bf16[256,1664]{1,0:T(8,128)(2,1)}, u32[]{:S(2)}, u32[]{:S(2)}) %collective-permute-start.28) | collective-permute-done | bytes 852000 | tf_op jit(solution)/shard_map/ppermute | solution.py:933
  134.9 18.0 %collective-permute-done.30.refs_7_ = bf16[256,1664]{1,0:T(8,128)(2,1)} collective-permute-done((bf16[256,1664]{1,0:T(8,128)(2,1)S(1)}, bf16[256,1664]{1,0:T(8,128)(2,1)}, u32[]{:S(2)}, u32[]{:S(2)}) %collective-permute-start.30) | collective-permute-done | bytes 852000 | tf_op jit(solution)/shard_map/ppermute | solution.py:933
  158.1 12.8 %shard_map.360 = (bf16[128,1536]{1,0:T(8,128)(2,1)}, f32[384,128]{1,0:T(8,128)}, f32[128,1536]{1,0:T(8,128)}, bf16[128,1536]{1,0:T(8,128)(2,1)}) custom-call(bf16[128,1536]{1,0:T(8,128)(2,1)} %get-tuple-element.163.q_ref, s32[128,1]{1,0:T(8,128)} %constant_dynamic-slice_fusion.7.rpos_ref, s32[1,1024]{1,0:T(1,128)} %bitcast.63, ...), custom_call_target="tpu_custom_call" | custom-call | flops 3221225472 | bytes 8388608 | tf_op jit(solution)/shard_map/pallas_call | solution.py:306
  174.5 12.8 %shard_map.361 = (bf16[128,1536]{1,0:T(8,128)(2,1)}, f32[384,128]{1,0:T(8,128)}, f32[128,1536]{1,0:T(8,128)}, bf16[128,1536]{1,0:T(8,128)(2,1)}) custom-call(bf16[128,1536]{1,0:T(8,128)(2,1)} %get-tuple-element.174.q_ref, s32[128,1]{1,0:T(8,128)} %constant_dynamic-slice_fusion.7.rpos_ref, s32[1,1024]{1,0:T(1,128)} %bitcast.64, ...), custom_call_target="tpu_custom_call" | custom-call | flops 3221225472 | bytes 8388608 | tf_op jit(solution)/shard_map/pallas_call | solution.py:306
  197.2 16.0 %shard_map.362 = (bf16[128,1664]{1,0:T(8,128)(2,1)}, bf16[128,1664]{1,0:T(8,128)(2,1)}, bf16[128,1664]{1,0:T(8,128)(2,1)}, bf16[128,1664]{1,0:T(8,128)(2,1)}, bf...) custom-call(s32[96]{0:T(128)} %select_reduce_fusion.order_ref, ...), custom_call_target="tpu_custom_call" | custom-call | flops 8053063680 | bytes 20971520 | tf_op jit(solution)/shard_map/pallas_call | solution.py:406
  217.5 16.2 %shard_map.363 = (bf16[128,1664]{1,0:T(8,128)(2,1)}, bf16[128,1664]{1,0:T(8,128)(2,1)}, bf16[128,1664]{1,0:T(8,128)(2,1)}, bf16[128,1664]{1,0:T(8,128)(2,1)}, bf...) custom-call(s32[96]{0:T(128)} %select_reduce_fusion.order_ref, ...), custom_call_target="tpu_custom_call" | custom-call | flops 8053063680 | bytes 20971520 | tf_op jit(solution)/shard_map/pallas_call | solution.py:406
  237.3 17.9 %shard_map.364 = (bf16[96,192,128]{2,1,0:T(8,128)(2,1)}, bf16[96,192,128]{2,1,0:T(8,128)(2,1)}) custom-call(s32[96]{0:T(128)} %select_reduce_fusion.order_ref, bf16[512,1536]{1,0:T(8,128)(2,1)} %get-tuple-element.188.refs_0_, bf16[512,1536]{1,0:T(8,128)(2,1)} %get-tuple-element.192.refs_1_, bf16[512,1664]{1,0:T(8,128)(2,1)} %get-tuple-element.193.refs_2_, ...), custom_call_target="tpu_custom_call" | custom-call | flops 9663676416 | bytes 22282240 | tf_op jit(solution)/shard_map/pallas_call | solution.py:521
  263.9 15.5 %shard_map.366 = (bf16[128,1536]{1,0:T(8,128)(2,1)}, bf16[2048,1024]{1,0:T(8,128)(2,1)}) custom-call(bf16[128,1536]{1,0:T(8,128)(2,1)} %get-tuple-element.163.q_ref, s32[128,1]{1,0:T(8,128)} %constant_dynamic-slice_fusion.7.rpos_ref, s32[1,1024]{1,0:T(1,128)} %bitcast.65, bf16[128,1536]{1,0:T(8,128)(2,1)} %get-tuple-element.173.ob_ref.refs_10_, ...), custom_call_target="tpu_custom_call" | custom-call | flops 8053063680 | bytes 8388608 | tf_op jit(solution)/shard_map/pallas_call | solution.py:768
  285.5 15.5 %shard_map.368 = (bf16[128,1536]{1,0:T(8,128)(2,1)}, bf16[2048,1024]{1,0:T(8,128)(2,1)}) custom-call(bf16[128,1536]{1,0:T(8,128)(2,1)} %get-tuple-element.174.q_ref, s32[128,1]{1,0:T(8,128)} %constant_dynamic-slice_fusion.7.rpos_ref, s32[1,1024]{1,0:T(1,128)} %bitcast.66, ...), custom_call_target="tpu_custom_call", output_to_operand_aliasing={{1}: (7, {})} | custom-call | flops 8053063680 | bytes 8388608 | tf_op jit(solution)/shard_map/pallas_call | solution.py:768
  301.0 8.3 %reduce-scatter.4.cloned.1.call-done.refs_0_ = bf16[12,192,128]{2,1,0:T(8,128)(2,1)} async-done(((bf16[96,192,128]{2,1,0:T(8,128)(2,1)}), bf16[12,192,128]{2,1,0:T(8,128)(2,1)}) %reduce-scatter.4.cloned.1.call-update) | async-done | bytes 589840 | tf_op jit(solution)/shard_map/reduce_scatter | solution.py:1175
  314.7 8.8 %shard_map.369 = (bf16[96,48,128]{2,1,0:T(8,128)(2,1)}, bf16[96,48,128]{2,1,0:T(8,128)(2,1)}, bf16[96,48,128]{2,1,0:T(8,128)(2,1)}, bf16[96,48,128]{2,1,0:T(8,128)(2,1)}, bf16[1536,512]{1,0:T(8,128)(2,1)}) custom-call(s32[2]{0:T(128)} %pad_add_fusion.me_ref, bf16[256,1536]{1,0:T(8,128)(2,1)} %get-tuple-element.159.h_ref.refs_0_, ...), custom_call_target="tpu_custom_call" | custom-call | flops 2415919104 | bytes 16777216 | tf_op jit(solution)/shard_map/pallas_call | solution.py:626
  332.5 8.6 %shard_map.370 = (bf16[256,1536]{1,0:T(8,128)(2,1)}, bf16[256,1536]{1,0:T(8,128)(2,1)}, bf16[256,1536]{1,0:T(8,128)(2,1)}, bf16[256,1536]{1,0:T(8,128)(2,1)}) custom-call(s32[96]{0:T(128)} %select_reduce_fusion.order_ref, bf16[96,128,256]{2,1,0:T(8,128)(2,1)} %all-gather.4.cloned.1.call-done.refs_8_.upper_ref, ...), custom_call_target="tpu_custom_call" | custom-call | flops 3221225472 | bytes 8388608 | tf_op jit(solution)/shard_map/pallas_call | solution.py:460
  341.2 10.7 %collective-permute-done.50 = bf16[96,48,128]{2,1,0:T(8,128)(2,1)} collective-permute-done((bf16[96,48,128]{2,1,0:T(8,128)(2,1)}, bf16[96,48,128]{2,1,0:T(8,128)(2,1)}, u32[]{:S(2)}, u32[]{:S(2)}) %collective-permute-start.50) | collective-permute-done | bytes 1179680 | tf_op jit(solution)/shard_map/ppermute | solution.py:933
  357.8 10.9 %collective-permute-done.51 = bf16[48,48,128]{2,1,0:T(8,128)(2,1)} collective-permute-done((bf16[48,48,128]{2,1,0:T(8,128)(2,1)}, bf16[48,48,128]{2,1,0:T(8,128)(2,1)}, u32[]{:S(2)}, u32[]{:S(2)}) %collective-permute-start.51) | collective-permute-done | bytes 589856 | tf_op jit(solution)/shard_map/ppermute | solution.py:933
  384.4 11.7 %collective-permute-done.57 = bf16[96,1536]{1,0:T(8,128)(2,1)S(1)} collective-permute-done((bf16[96,1536]{1,0:T(8,128)(2,1)S(1)}, bf16[96,1536]{1,0:T(8,128)(2,1)S(1)}, u32[]{:S(2)}, u32[]{:S(2)}) %collective-permute-start.57) | collective-permute-done | bytes 294944 | tf_op jit(solution)/shard_map/ppermute | solution.py:943
  397.3 7.1 %shard_map.373 = (f32[2,128,1536]{2,1,0:T(8,128)}, f32[8,1536]{1,0:T(8,128)}) custom-call(f32[2,128,1536]{2,1,0:T(8,128)} %x_ref, f32[2,1536]{1,0:T(2,128)} %gain_ref.9, bf16[1536,2560]{1,0:T(8,128)(2,1)} %get-tuple-element.225.w_ref, f32[128,1536]{1,0:T(8,128)} %get-tuple-element.239.refs_0_, f32[128,1536]{1,0:T(8,128)} %get-tuple-element.240.refs_1_, ...), custom_call_target="tpu_custom_call" | custom-call | flops 805306368 | bytes 14680064 | tf_op jit(solution)/shard_map/pallas_call | solution.py:852
  413.8 7.1 %collective-permute-start.67 = (bf16[32,1536]{1,0:T(8,128)(2,1)S(1)}, bf16[32,1536]{1,0:T(8,128)(2,1)S(1)}, u32[]{:S(2)}, u32[]{:S(2)}) collective-permute-start(bf16[32,1536]{1,0:T(8,128)(2,1)S(1)} %get-tuple-element.286), channel_id=1, source_target_pairs={{0,8},{4,12},{8,16},{12,20},{16,24},{20,28},{24,0},{28,4},{1,9},{5... | collective-permute-start | bytes 294920 | tf_op jit(solution)/shard_map/ppermute | solution.py:943
  444.6 37.9 %all-to-all-done = bf16[32,2,7680]{2,1,0:T(2,128)(2,1)S(1)} async-done(((bf16[32,2,7680]{2,1,0:T(2,128)(2,1)}), bf16[32,2,7680]{2,1,0:T(2,128)(2,1)S(1)}, u32[]{:S(2)}, u32[]{:S(2)}) %all-to-all-start) | async-done | bytes 983072 | tf_op jit(solution)/shard_map/all_to_all | solution.py:1228
  492.6 15.2 %shard_map.375 = (f32[12,192,256]{2,1,0:T(8,128)}, f32[12,192,256]{2,1,0:T(8,128)}, f32[12,192,256]{2,1,0:T(8,128)}, f32[12,192,256]{2,1,0:T(8,128)}) custom-call(f32[12,192,256]{2,1,0:T(8,128)} %bitcast.48, f32[12,192,256]{2,1,0:T(8,128)} %bitcast.52, f32[12,192,256]{2,1,0:T(8,128)} %bitcast.53, f32[12,192,192]{2,1,0:T(8,128)} %bitcast.54, ...), custom_call_target="tpu_custom_call" | custom-call | flops 1056964608 | bytes 25165824 | tf_op jit(solution)/shard_map/pallas_call | solution.py:891
  (339 shorter events, 191.4 us)
Async XLA Ops:
  7.2 104.1 %all-gather.4.cloned.1.call-start = ((), (), s32[]{:S(2)}) async-start(), calls=%async_computation.4 | async-start | bytes 7077888 | tf_op jit(solution)/shard_map/all_gather | solution.py:1094
  46.9 110.6 %all-gather.6.cloned.1.call-start = ((), (), s32[]{:S(2)}) async-start(), calls=%async_computation.5 | async-start | bytes 4718592 | tf_op jit(solution)/shard_map/all_gather | solution.py:1120
  111.4 85.8 %all-gather.8.cloned.1.call-start = ((), (), s32[]{:S(2)}) async-start(), calls=%async_computation.6 | async-start | bytes 3538944 | tf_op jit(solution)/shard_map/all_gather | solution.py:1122
  114.2 38.7 %collective-permute-start.30 = (bf16[256,1664]{1,0:T(8,128)(2,1)S(1)}, bf16[256,1664]{1,0:T(8,128)(2,1)}, u32[]{:S(2)}, u32[]{:S(2)}) collective-permute-start(bf16[256,1664]{1,0:T(8,128)(2,1)S(1)} %bitcast.58), channel_id=1, source_target_pairs={{0,3},{1,2},{2,1},{3,0},{4,7},{5,6},{6,5},{7,4},{8,11},{9,10},{10,... | collective-permute-start | bytes 2555912 | tf_op jit(solution)/shard_map/ppermute | solution.py:933
  157.6 151.7 %reduce-scatter.4.cloned.1.call-start = ((), (), s32[]{:S(2)}) async-start(), calls=%async_computation.7 | async-start | bytes 5308416 | tf_op jit(solution)/shard_map/reduce_scatter | solution.py:1175
  157.8 37.0 %collective-permute-start.31 = (bf16[256,1536]{1,0:T(8,128)(2,1)S(1)}, bf16[256,1536]{1,0:T(8,128)(2,1)S(1)}, u32[]{:S(2)}, u32[]{:S(2)}) collective-permute-start(bf16[256,1536]{1,0:T(8,128)(2,1)S(1)} %copy-done.19), channel_id=1, source_target_pairs={{0,4},{4,0},{8,12},{12,8},{16,20},{20,16},{24,28},{28,24},{1,5},{5... | collective-permute-start | bytes 2359304 | tf_op jit(solution)/shard_map/ppermute | solution.py:938
  172.6 23.8 %collective-permute-start.32 = (bf16[128,1536]{1,0:T(8,128)(2,1)}, bf16[128,1536]{1,0:T(8,128)(2,1)}, u32[]{:S(2)}, u32[]{:S(2)}) collective-permute-start(bf16[128,1536]{1,0:T(8,128)(2,1)} %get-tuple-element.173.ob_ref.refs_10_), channel_id=1, source_target_pairs={{0,4},{4,0},{8,12},{12,8},{16,20},{20,16},{24,28},{28,24},{1,5},{5... | collective-permute-start | bytes 1179656 | tf_op jit(solution)/shard_map/ppermute | solution.py:938
  192.9 23.3 %collective-permute-start.40 = (bf16[128,1536]{1,0:T(8,128)(2,1)}, bf16[128,1536]{1,0:T(8,128)(2,1)}, u32[]{:S(2)}, u32[]{:S(2)}) collective-permute-start(bf16[128,1536]{1,0:T(8,128)(2,1)} %get-tuple-element.191.refs_0_.h2_ref), channel_id=1, source_target_pairs={{0,1},{1,0},{2,3},{3,2},{4,5},{5,4},{6,7},{7,6},{8,9},{9,8},{10,11... | collective-permute-start | bytes 1179656 | tf_op jit(solution)/shard_map/ppermute | solution.py:933
  193.6 23.2 %collective-permute-start.41 = (bf16[128,1536]{1,0:T(8,128)(2,1)}, bf16[128,1536]{1,0:T(8,128)(2,1)}, u32[]{:S(2)}, u32[]{:S(2)}) collective-permute-start(bf16[128,1536]{1,0:T(8,128)(2,1)} %get-tuple-element.191.refs_0_.h2_ref), channel_id=1, source_target_pairs={{0,2},{1,3},{2,0},{3,1},{4,6},{5,7},{6,4},{7,5},{8,10},{9,11},{10,... | collective-permute-start | bytes 1179656 | tf_op jit(solution)/shard_map/ppermute | solution.py:933
  194.8 22.0 %collective-permute-start.42 = (bf16[128,1536]{1,0:T(8,128)(2,1)}, bf16[128,1536]{1,0:T(8,128)(2,1)S(1)}, u32[]{:S(2)}, u32[]{:S(2)}) collective-permute-start(bf16[128,1536]{1,0:T(8,128)(2,1)} %get-tuple-element.191.refs_0_.h2_ref), channel_id=1, source_target_pairs={{0,3},{1,2},{2,1},{3,0},{4,7},{5,6},{6,5},{7,4},{8,11},{9,10},{10,... | collective-permute-start | bytes 1179656 | tf_op jit(solution)/shard_map/ppermute | solution.py:933
  213.2 23.6 %collective-permute-start.37 = (bf16[128,1664]{1,0:T(8,128)(2,1)}, bf16[128,1664]{1,0:T(8,128)(2,1)S(1)}, u32[]{:S(2)}, u32[]{:S(2)}) collective-permute-start(bf16[128,1664]{1,0:T(8,128)(2,1)} %get-tuple-element.184), channel_id=1, source_target_pairs={{0,1},{1,0},{2,3},{3,2},{4,5},{5,4},{6,7},{7,6},{8,9},{9,8},{10,11... | collective-permute-start | bytes 1277960 | tf_op jit(solution)/shard_map/ppermute | solution.py:933
  214.7 22.5 %collective-permute-start.38 = (bf16[128,1664]{1,0:T(8,128)(2,1)}, bf16[128,1664]{1,0:T(8,128)(2,1)S(1)}, u32[]{:S(2)}, u32[]{:S(2)}) collective-permute-start(bf16[128,1664]{1,0:T(8,128)(2,1)} %get-tuple-element.185), channel_id=1, source_target_pairs={{0,2},{1,3},{2,0},{3,1},{4,6},{5,7},{6,4},{7,5},{8,10},{9,11},{10,... | collective-permute-start | bytes 1277960 | tf_op jit(solution)/shard_map/ppermute | solution.py:933
  256.0 116.3 %reduce-scatter.6.cloned.1.call-start = ((), (), s32[]{:S(2)}) async-start(), calls=%async_computation.8 | async-start | bytes 4718592 | tf_op jit(solution)/shard_map/reduce_scatter | solution.py:1176
  309.3 183.3 %reduce-scatter.8.cloned.1.call-start = ((), (), s32[]{:S(2)}) async-start(), calls=%async_computation.9 | async-start | bytes 5308416 | tf_op jit(solution)/shard_map/reduce_scatter | solution.py:1204
  323.5 28.4 %collective-permute-start.50 = (bf16[96,48,128]{2,1,0:T(8,128)(2,1)}, bf16[96,48,128]{2,1,0:T(8,128)(2,1)}, u32[]{:S(2)}, u32[]{:S(2)}) collective-permute-start(bf16[96,48,128]{2,1,0:T(8,128)(2,1)} %get-tuple-element.218), channel_id=1, source_target_pairs={{0,1},{1,0},{2,3},{3,2},{4,5},{5,4},{6,7},{7,6},{8,9},{9,8},{10,11... | collective-permute-start | bytes 3538952 | tf_op jit(solution)/shard_map/ppermute | solution.py:933
  325.0 30.4 %collective-permute-start.52 = (bf16[96,48,128]{2,1,0:T(8,128)(2,1)}, bf16[96,48,128]{2,1,0:T(8,128)(2,1)S(1)}, u32[]{:S(2)}, u32[]{:S(2)}) collective-permute-start(bf16[96,48,128]{2,1,0:T(8,128)(2,1)} %get-tuple-element.230), channel_id=1, source_target_pairs={{0,2},{1,3},{2,0},{3,1},{4,6},{5,7},{6,4},{7,5},{8,10},{9,11},{10,... | collective-permute-start | bytes 3538952 | tf_op jit(solution)/shard_map/ppermute | solution.py:933
  372.7 23.5 %collective-permute-start.57 = (bf16[96,1536]{1,0:T(8,128)(2,1)S(1)}, bf16[96,1536]{1,0:T(8,128)(2,1)S(1)}, u32[]{:S(2)}, u32[]{:S(2)}) collective-permute-start(bf16[96,1536]{1,0:T(8,128)(2,1)S(1)} %get-tuple-element.284), channel_id=1, source_target_pairs={{0,16},{4,20},{8,24},{12,28},{16,0},{20,4},{24,8},{28,12},{1,17},{... | collective-permute-start | bytes 884744 | tf_op jit(solution)/shard_map/ppermute | solution.py:943
  373.6 22.5 %collective-permute-start.56 = (bf16[96,1536]{1,0:T(8,128)(2,1)S(1)}, bf16[96,1536]{1,0:T(8,128)(2,1)}, u32[]{:S(2)}, u32[]{:S(2)}) collective-permute-start(bf16[96,1536]{1,0:T(8,128)(2,1)S(1)} %get-tuple-element.282), channel_id=1, source_target_pairs={{0,24},{4,28},{8,0},{12,4},{16,8},{20,12},{24,16},{28,20},{1,25},{... | collective-permute-start | bytes 884744 | tf_op jit(solution)/shard_map/ppermute | solution.py:943
  381.2 23.2 %collective-permute-start.55 = (bf16[32,48,128]{2,1,0:T(8,128)(2,1)}, bf16[32,48,128]{2,1,0:T(8,128)(2,1)S(1)}, u32[]{:S(2)}, u32[]{:S(2)}) collective-permute-start(bf16[32,48,128]{2,1,0:T(8,128)(2,1)} %get-tuple-element.237), channel_id=1, source_target_pairs={{0,1},{1,0},{2,3},{3,2},{4,5},{5,4},{6,7},{7,6},{8,9},{9,8},{10,11... | collective-permute-start | bytes 1179656 | tf_op jit(solution)/shard_map/ppermute | solution.py:933
  382.7 22.6 %collective-permute-start.60 = (bf16[32,48,128]{2,1,0:T(8,128)(2,1)}, bf16[32,48,128]{2,1,0:T(8,128)(2,1)S(1)}, u32[]{:S(2)}, u32[]{:S(2)}) collective-permute-start(bf16[32,48,128]{2,1,0:T(8,128)(2,1)} %get-tuple-element.244), channel_id=1, source_target_pairs={{0,2},{1,3},{2,0},{3,1},{4,6},{5,7},{6,4},{7,5},{8,10},{9,11},{10,... | collective-permute-start | bytes 1179656 | tf_op jit(solution)/shard_map/ppermute | solution.py:933
  434.8 47.7 %all-to-all-start = ((bf16[32,2,7680]{2,1,0:T(2,128)(2,1)}), bf16[32,2,7680]{2,1,0:T(2,128)(2,1)S(1)}, u32[]{:S(2)}, u32[]{:S(2)}) async-start(bf16[32,2,7680]{2,1,0:T(2,128)(2,1)} %all_to_all.6), calls=%async_computation.2 | async-start | bytes 1966080 | tf_op jit(solution)/shard_map/all_to_all | solution.py:1228
  441.0 66.8 %collective-permute-start.62 = (bf16[256,1536]{1,0:T(8,128)(2,1)}, bf16[256,1536]{1,0:T(8,128)(2,1)S(1)}, u32[]{:S(2)}, u32[]{:S(2)}) collective-permute-start(bf16[256,1536]{1,0:T(8,128)(2,1)} %get-tuple-element.247), channel_id=1, source_target_pairs={{0,1},{1,0},{2,3},{3,2},{4,5},{5,4},{6,7},{7,6},{8,9},{9,8},{10,11... | collective-permute-start | bytes 2359304 | tf_op jit(solution)/shard_map/ppermute | solution.py:933
  442.9 65.0 %collective-permute-start.63 = (bf16[256,1536]{1,0:T(8,128)(2,1)}, bf16[256,1536]{1,0:T(8,128)(2,1)}, u32[]{:S(2)}, u32[]{:S(2)}) collective-permute-start(bf16[256,1536]{1,0:T(8,128)(2,1)} %get-tuple-element.248), channel_id=1, source_target_pairs={{0,2},{1,3},{2,0},{3,1},{4,6},{5,7},{6,4},{7,5},{8,10},{9,11},{10,... | collective-permute-start | bytes 2359304 | tf_op jit(solution)/shard_map/ppermute | solution.py:933
  444.3 63.6 %collective-permute-start.64 = (bf16[256,1536]{1,0:T(8,128)(2,1)}, bf16[256,1536]{1,0:T(8,128)(2,1)}, u32[]{:S(2)}, u32[]{:S(2)}) collective-permute-start(bf16[256,1536]{1,0:T(8,128)(2,1)} %get-tuple-element.249), channel_id=1, source_target_pairs={{0,3},{1,2},{2,1},{3,0},{4,7},{5,6},{6,5},{7,4},{8,11},{9,10},{10,... | collective-permute-start | bytes 2359304 | tf_op jit(solution)/shard_map/ppermute | solution.py:933
  (112 other events, 1421.9 us)
Sparse Core Ops, SparseCore 0:
  47.0 62.4 all-gather.3
  111.7 45.7 all-gather.5
  159.8 37.3 all-gather.7
  255.7 53.5 reduce-scatter.3
  311.4 48.3 reduce-scatter.5
  411.5 78.8 reduce-scatter.7

commit v9 on v8

--- a/solution.py
+++ b/solution.py
@@ -14,7 +14,7 @@
 BR = 192
 BC = 256
 LANES = 128
-UPPER = 128
+UPPER = 144
 
 norm_eps = 1e-06
 beta_one = 0.9
@@ -126,9 +126,10 @@
     piece_refs = refs[micros + 1 : micros + 1 + len(pieces)]
     refs = refs[micros + 1 + len(pieces) :]
     h_ref = refs[0]
-    kv_ref, win_ref, wout_ref, held, held_out, sems, out_sems = refs[1:]
+    kv_refs = refs[1 : 1 + micros]
+    win_ref, wout_ref, held, held_out, sems, out_sems = refs[1 + micros :]
     groups = held.shape[1] // BC
-    kv_groups = kv_ref.shape[-1] // BC
+    kv_groups = kv_refs[0].shape[-1] // BC
     rows = x_refs[0].shape[0]
     ctx, shard = me_ref[0], me_ref[1]
     chip, core = lax.div(ctx, 2), lax.rem(ctx, 2)
@@ -177,7 +178,8 @@
     def _(b):
         across = pl.ds(pl.multiple_of((q_groups + b) * BC, BC), BC)
         made = dot(h_ref[...], held[:, across]).astype(low_type)
-        kv_ref[:, pl.ds(pl.multiple_of(b * BC, BC), BC)] = made
+        for m in range(micros):
+            kv_refs[m][:, pl.ds(pl.multiple_of(b * BC, BC), BC)] = made[m * rows : (m + 1) * rows]
 
     for copy in copies:
         copy.wait()
@@ -195,11 +197,11 @@
         ),
         tuple(
             [shaped((micros * rows, width), low_type)]
-            + [shaped((micros * rows, kv_width), low_type)]
+            + [shaped((rows, kv_width), low_type)] * micros
             + [shaped((width, in_width), low_type), shaped((width, out_width), low_type)]
         ),
         [in_smem, in_smem] + [in_vmem] * (micros + 1) + [in_any] * len(arrays),
-        (in_vmem, in_vmem, in_any, in_any),
+        tuple([in_vmem] * (1 + micros) + [in_any, in_any]),
         [
             pltpu.VMEM((width, in_width), low_type),
             pltpu.VMEM((width, out_width), low_type),
@@ -248,25 +250,12 @@
     )(h, w)
 
 
-def load_keys(kv_ref, micro, rows, held, sem):
-    count = held.shape[0] // rows
-    span = kv_ref.shape[0] // count
-
-    @pl.loop(0, count)
-    def _(i):
-        pltpu.make_async_copy(
-            kv_ref.at[pl.ds(pl.multiple_of(i * span + micro * rows, 16), rows)],
-            held.at[pl.ds(pl.multiple_of(i * rows, 16), rows)],
-            sem,
-        ).start()
-
-
 def attend_kernel(
-    micro, q_ref, rpos_ref, kpos_ref, x_ref, gain_ref, w_ref, all_ref,
+    q_ref, rpos_ref, kpos_ref, x_ref, gain_ref, w_ref, all_ref,
     ob_ref, log_ref, x2_ref, h2_ref, bias, kv_ref, held, sems,
 ):
     rows = q_ref.shape[0]
-    load_keys(all_ref, micro, rows, kv_ref, sems.at[0])
+    pltpu.make_async_copy(all_ref, kv_ref, sems.at[0]).start()
     pltpu.make_async_copy(w_ref, held, sems.at[1]).start()
     bias[...] = jnp.where(kpos_ref[...] <= rpos_ref[...], 0.0, masked_score)
     log_ref[...] = jnp.zeros_like(log_ref)
@@ -299,12 +288,12 @@
     h2_ref[...] = unit_rows(x2_ref[...], gain_ref[1:2])[0].astype(low_type)
 
 
-def attend(micro, q, kv, rows_pos, key_pos, x, gains, w):
+def attend(q, kv, rows_pos, key_pos, x, gains, w):
     rows, width = q.shape
     length = key_pos.shape[1]
     model = x.shape[1]
     return call(
-        functools.partial(attend_kernel, micro),
+        attend_kernel,
         (
             shaped((rows, width), low_type),
             shaped((3 * rows, LANES), jnp.float32),
@@ -702,7 +691,7 @@
 ):
     dq_ref, out_ref, bias, kv_ref, grad_ref, sems = refs[-6:]
     rows = q_ref.shape[0]
-    load_keys(all_ref, micro, rows, kv_ref, sems.at[0])
+    pltpu.make_async_copy(all_ref, kv_ref, sems.at[0]).start()
     length = kv_ref.shape[0]
     bias[...] = jnp.where(kpos_ref[...] <= rpos_ref[...], 0.0, masked_score)
     wait_bytes(kv_ref, sems.at[0])
@@ -755,7 +744,7 @@
     wait_bytes(grad_ref, sems.at[1])
 
 
-def attend_back(micro, q, kv, rows_pos, key_pos, ob, log_total, do, shared):
+def attend_back(micro, micros, q, kv, rows_pos, key_pos, ob, log_total, do, shared):
     rows, width = q.shape
     length = key_pos.shape[1]
     operands = [q, rows_pos, key_pos, ob, log_total, do, kv]
@@ -767,7 +756,10 @@
         in_specs.append(in_any)
     return pl.pallas_call(
         functools.partial(attend_back_kernel, micro),
-        out_shape=(shaped((rows, width), low_type), shaped(kv.shape, low_type)),
+        out_shape=(
+            shaped((rows, width), low_type),
+            shaped((micros * length, kv.shape[1]), low_type),
+        ),
         in_specs=in_specs,
         out_specs=(in_vmem, in_any),
         scratch_shapes=[
@@ -992,6 +984,7 @@
         return got
 
     got = [to_partner(blocks, offset) for offset in range(1, members)]
+    first = got + parts[1:3]
     gate.append(got[0])
     add(blocks, 0, 0, 0)
     for offset in range(1, members):
@@ -1000,11 +993,10 @@
     if chips > 1:
         last = spread(after(parts[1], *last), 1)
         gate[:] = last
-        got = last
     if chips > 2:
         group = after(jnp.concatenate(parts[2:], axis=0), *last)
         spread(group, 2)
-    return got + parts[1:], pieces, arrays
+    return first, pieces, arrays
 
 
 def add_wide(parts):
@@ -1103,7 +1095,7 @@
     here, expert_inverse, router_pad, key_pos, rows_pos = lax.optimization_barrier(
         (me, expert_inverse, router_pad, key_pos, rows_pos)
     )
-    h1, kv, w_in, w_out = project(
+    h1, *kv, w_in, w_out = project(
         pieces,
         arrays,
         chips,
@@ -1117,13 +1109,18 @@
     q = make_queries(h1, w_in, micros)
     h1_other = to_ctx(h1, 1)
     obs, logs, x2s, h2s = [], [], [], []
-    kv_all = lax.all_gather(after(kv, expert_all[0]), "ctx", axis=0, tiled=True)
-    lower = after(expert_low[:, UPPER:], kv_all, q, cot_parts)
-    expert_all.append(lax.all_gather(lower, "ctx", axis=0, tiled=True))
+    kv = after(kv, expert_all[0])
+    kv_all = []
     for m in range(micros):
-        query = after(q[m], *(cot_parts if m == 0 else obs[m - 1 : m]))
+        own = after(kv[m], kv_all, q, cot_parts[1:3]) if m else kv[m]
+        kv_all.append(lax.all_gather(own, "ctx", axis=0, tiled=True))
+    for m in range(micros):
+        if m == micros - 1:
+            lower = after(expert_low[:, UPPER:], kv_all[m], obs, cot_parts)
+            expert_all.append(lax.all_gather(lower, "ctx", axis=0, tiled=True))
+        query = after(q[m], *(cot_parts[1:3] if m == 0 else obs[m - 1 : m]))
         ob, log_total, x2, h2 = attend(
-            m, query, kv_all, rows_pos, key_pos, tokens[m], norm_gains, w_out
+            query, kv_all[m], rows_pos, key_pos, tokens[m], norm_gains, w_out
         )
         obs.append(ob)
         logs.append(log_total)
@@ -1152,15 +1149,17 @@
     expert_terms = outer_blocks(
         after(expert_inverse, *backs[0]), width, (0, 0, 1), [xs, cs], [dgs, dus, zs]
     )
+    outs = produce(after(expert_inverse, *expert_terms), expert_all, zs, shard_count, width)
+    arrived = [to_partner(outs[j], j) for j in range(min(3, shard_count))]
     dxs, das, dqs, stats = [], [], [], []
     dkv_terms = None
     for m in range(micros):
-        here = after(me, expert_terms, backs[-1]) if m == 0 else after(me, dqs[-1])
+        here = after(me, outs, backs[-1]) if m == 0 else after(me, dqs[-1], arrived[1:])
         dx, da, do, stat = merge(
             here, x2s[m], cotangent[m], h2s[m], norm_gains, router_pad, w_out, backs[m]
         )
         dq, dkv_terms = attend_back(
-            m, q[m], kv_all, rows_pos, key_pos, obs[m], logs[m], do, dkv_terms
+            m, micros, q[m], kv_all[m], rows_pos, key_pos, obs[m], logs[m], do, dkv_terms
         )
         dxs.append(dx)
         das.append(da)
@@ -1184,9 +1183,8 @@
         False,
     )
     h1_turned = early[4]
-    outs = produce(after(expert_inverse, early[0]), expert_all, zs, shard_count, width)
     parts_back = query_back(after(w_in, early[0]), dqs)
-    early_rows, early_seen = sum_members(early[:4], (outs, parts_back), shard_count)
+    early_rows, early_seen = sum_members(early[:4], parts_back, shard_count)
     chip = ctx // 2
     early_parts = sum_chips(early_rows, chip, chips)
     late = gradient_pieces(
@@ -1200,9 +1198,10 @@
         after(tokens, late[0]), norm_gains, w_in, dxs, parts_back, dkv
     )
     late_rows, late_seen = sum_members(late[:4], (input_grad, early_parts), shard_count)
-    late_term = after(expert_terms[1], *late_seen)
+    late_term = after(expert_terms[1], dkv)
     expert_sums.append(lax.psum_scatter(late_term, "ctx", scatter_dimension=0, tiled=True))
-    arrived = [to_partner(part, j) for j, part in enumerate(after(list(outs), *late_seen))]
+    last_outs = after(list(outs), *late_seen)
+    arrived += [to_partner(last_outs[j], j) for j in range(3, shard_count)]
     early_sum = add_wide(early_parts).astype(low_type)
     late_sum = add_wide(sum_chips(late_rows, chip, chips)).astype(low_type)
     all_sums = jnp.concatenate([early_sum, late_sum], axis=0)

time: 526 us -> 532 us (1.011)
  waiting for transfers between devices: 190 us -> 203 us
  starting transfers between devices: 74 us -> 64.2 us
    ppermute x9, waiting for transfers between devices: 33.6 us -> 63.2 us  [to_chip(): lax.ppermute(array, 'ctx', [(i, (i + 2 * offset) % count) for i in range(...]
    all_to_all x1, waiting for transfers between devices: 37.9 us -> 22.8 us  [shards(): lax.all_to_all(ordered, ('ctx', 'shard'), split_axis=0, concat_axis=0, ti...]
    ppermute x37, waiting for transfers between devices: 102 us -> 91.2 us  [to_partner(): return lax.ppermute(array, 'shard', [(i, i ^ offset) for i in range(count)])]
    all_gather x1 -> x2, waiting for transfers between devices: 4.67 us -> 13.3 us  [shards(): kv_all.append(lax.all_gather(own, 'ctx', axis=0, tiled=True))]
    reduce_scatter x1, waiting for transfers between devices: 8.34 us -> 0.02 us  [shards(): lax.psum_scatter(first_term, 'ctx', scatter_dimension=0, tiled=True)]
    all_gather x1, waiting for transfers between devices: 0.73 us -> 7.79 us  [shards(): expert_all.append(lax.all_gather(lower, 'ctx', axis=0, tiled=True))]
  transfers between devices with their start and end apart: 75 -> 76, of which waited for: 35 -> 31; matrix products, arithmetic and copies ran while one was open for 6% -> 6% of each run, Pallas kernels for 37% -> 37%
where the time goes in v9:
time: 532 us; the launch traced here: 524 us
  waiting for transfers between devices  203 us (38%)
  Pallas kernels  194 us (36%)
  starting transfers between devices  64.2 us (12%)
  local copies, waits for them, and re-layouts  28 us (5%)
  other arithmetic  18.3 us (3%)
  between operations  15.6 us (3%)
    ppermute x37, waiting for transfers between devices, to_partner(): return lax.ppermute(array, 'shard', [(i, i ^ offset) for i in range(count)])  91.2 us
    ppermute x9, waiting for transfers between devices, to_chip(): lax.ppermute(array, 'ctx', [(i, (i + 2 * offset) % count) for i in range(...  63.2 us
    ppermute x37, starting transfers between devices, to_partner(): return lax.ppermute(array, 'shard', [(i, i ^ offset) for i in range(count)])  41.6 us
    pallas_call x2, Pallas kernels, run_expert(): call(functools.partial(expert_kernel, sources, micro), tuple([shaped((row...  32.4 us
    pallas_call x2, Pallas kernels, attend_back(): pl.pallas_call(functools.partial(attend_back_kernel, micro), out_shape=(s...  31.1 us
    pallas_call x2, Pallas kernels, attend(): call(attend_kernel, (shaped((rows, width), low_type), shaped((3 * rows, L...  25.8 us
    all_to_all x1, waiting for transfers between devices, shards(): lax.all_to_all(ordered, ('ctx', 'shard'), split_axis=0, concat_axis=0, ti...  22.8 us
    pallas_call x2, Pallas kernels, rotate(): pl.pallas_call(rotate_kernel, grid=(count,), out_shape=(shaped(weight.sha...  21.1 us
  transfers between devices with their start and end apart: 76, of which 31 were waited for; matrix products, arithmetic and copies ran while one was open for 6% of the time, Pallas kernels for 37%

profile of v9, /device:TPU:0, one launch (start us, length us, event | category | flops | bytes accessed | tf_op | source)
XLA Modules:
  0.0 524.1 jit_solution(17601190034434631297)
XLA Ops:
  15.0 7.7 %collective-permute-done.7.refs_11_ = bf16[4,192,256]{2,1,0:T(8,128)(2,1)S(1)} collective-permute-done((bf16[4,192,256]{2,1,0:T(8,128)(2,1)S(1)}, bf16[4,192,256]{2,1,0:T(8,128)(2,1)S(1)}, u32[]{:S(2)}, u32[]{:S(2)}) %collective-permute-start.7) | collective-permute-done | bytes 393248 | tf_op jit(solution)/shard_map/ppermute | solution.py:935
  24.6 7.2 %collective-permute-done.3.refs_7_ = bf16[4,192,256]{2,1,0:T(8,128)(2,1)} collective-permute-done((bf16[4,192,256]{2,1,0:T(8,128)(2,1)S(1)}, bf16[4,192,256]{2,1,0:T(8,128)(2,1)}, u32[]{:S(2)}, u32[]{:S(2)}) %collective-permute-start.3) | collective-permute-done | bytes 393248 | tf_op jit(solution)/shard_map/ppermute | solution.py:925
  38.7 9.4 %collective-permute-done.18 = bf16[4,192,256]{2,1,0:T(8,128)(2,1)S(1)} collective-permute-done((bf16[4,192,256]{2,1,0:T(8,128)(2,1)S(1)}, bf16[4,192,256]{2,1,0:T(8,128)(2,1)S(1)}, u32[]{:S(2)}, u32[]{:S(2)}) %collective-permute-start.18) | collective-permute-done | bytes 393248 | tf_op jit(solution)/shard_map/ppermute | solution.py:935
  53.5 14.8 %collective-permute-done.13.refs_17_ = bf16[4,96,256]{2,1,0:T(8,128)(2,1)S(1)} collective-permute-done((bf16[4,96,256]{2,1,0:T(8,128)(2,1)S(1)}, bf16[4,96,256]{2,1,0:T(8,128)(2,1)S(1)}, u32[]{:S(2)}, u32[]{:S(2)}) %collective-permute-start.13) | collective-permute-done | bytes 196640 | tf_op jit(solution)/shard_map/ppermute | solution.py:925
  96.0 12.3 %shard_map.358 = (bf16[256,1536]{1,0:T(8,128)(2,1)}, bf16[128,1024]{1,0:T(8,128)(2,1)}, bf16[128,1024]{1,0:T(8,128)(2,1)}, bf16[1536,2560]{1,0:T(8,128)(2,1)}, bf16[1536,1536]{1,0:T(8,128)(2,1)}) custom-call(s32[128]{0:T(128)} %order_ref.1, s32[2]{0:T(128)} %pad_add_fusion.me_ref, f32[128,1536]{1,0:T(8,128)} %get-tuple-element.281.refs_0_.x_ref, ...), custom_call_target="tpu_custom_call" | custom-call | flops 805306368 | bytes 25165824 | tf_op jit(solution)/shard_map/pallas_call | solution.py:194
  117.1 13.4 %collective-permute-done.28.refs_5_ = bf16[256,1664]{1,0:T(8,128)(2,1)S(1)} collective-permute-done((bf16[256,1664]{1,0:T(8,128)(2,1)S(1)}, bf16[256,1664]{1,0:T(8,128)(2,1)S(1)}, u32[]{:S(2)}, u32[]{:S(2)}) %collective-permute-start.28) | collective-permute-done | bytes 852000 | tf_op jit(solution)/shard_map/ppermute | solution.py:925
  140.6 13.0 %shard_map.360 = (bf16[128,1536]{1,0:T(8,128)(2,1)}, f32[384,128]{1,0:T(8,128)}, f32[128,1536]{1,0:T(8,128)}, bf16[128,1536]{1,0:T(8,128)(2,1)}) custom-call(bf16[128,1536]{1,0:T(8,128)(2,1)} %get-tuple-element.163.q_ref, s32[128,1]{1,0:T(8,128)} %constant_dynamic-slice_fusion.7.rpos_ref, s32[1,1024]{1,0:T(1,128)} %bitcast.63, ...), custom_call_target="tpu_custom_call" | custom-call | flops 3221225472 | bytes 8388608 | tf_op jit(solution)/shard_map/pallas_call | solution.py:295
  158.6 8.0 %all-gather.9.cloned.1.call-done.all_ref = bf16[1024,1024]{1,0:T(8,128)(2,1)} async-done(((bf16[128,1024]{1,0:T(8,128)(2,1)}), bf16[1024,1024]{1,0:T(8,128)(2,1)}) %all-gather.9.cloned.1.call-update) | async-done | bytes 2097168 | tf_op jit(solution)/shard_map/all_gather | solution.py:1116
  170.7 12.8 %shard_map.361 = (bf16[128,1536]{1,0:T(8,128)(2,1)}, f32[384,128]{1,0:T(8,128)}, f32[128,1536]{1,0:T(8,128)}, bf16[128,1536]{1,0:T(8,128)(2,1)}) custom-call(bf16[128,1536]{1,0:T(8,128)(2,1)} %get-tuple-element.175.q_ref, s32[128,1]{1,0:T(8,128)} %constant_dynamic-slice_fusion.7.rpos_ref, s32[1,1024]{1,0:T(1,128)} %bitcast.64, ...), custom_call_target="tpu_custom_call" | custom-call | flops 3221225472 | bytes 8388608 | tf_op jit(solution)/shard_map/pallas_call | solution.py:295
  192.0 7.8 %all-gather.11.cloned.1.call-done.refs_9_.lower_ref = bf16[96,48,256]{2,1,0:T(8,128)(2,1)} async-done(((bf16[12,48,256]{2,1,0:T(8,128)(2,1)}), bf16[96,48,256]{2,1,0:T(8,128)(2,1)}) %all-gather.11.cloned.1.call-update) | async-done | bytes 2359312 | tf_op jit(solution)/shard_map/all_gather | solution.py:1120
  199.8 16.0 %shard_map.362 = (bf16[128,1664]{1,0:T(8,128)(2,1)}, bf16[128,1664]{1,0:T(8,128)(2,1)}, bf16[128,1664]{1,0:T(8,128)(2,1)}, bf16[128,1664]{1,0:T(8,128)(2,1)}, bf...) custom-call(s32[96]{0:T(128)} %select_reduce_fusion.order_ref, ...), custom_call_target="tpu_custom_call" | custom-call | flops 8053063680 | bytes 20971520 | tf_op jit(solution)/shard_map/pallas_call | solution.py:395
  220.1 16.4 %shard_map.363 = (bf16[128,1664]{1,0:T(8,128)(2,1)}, bf16[128,1664]{1,0:T(8,128)(2,1)}, bf16[128,1664]{1,0:T(8,128)(2,1)}, bf16[128,1664]{1,0:T(8,128)(2,1)}, bf...) custom-call(s32[96]{0:T(128)} %select_reduce_fusion.order_ref, ...), custom_call_target="tpu_custom_call" | custom-call | flops 8053063680 | bytes 20971520 | tf_op jit(solution)/shard_map/pallas_call | solution.py:395
  240.1 17.9 %shard_map.364 = (bf16[96,192,128]{2,1,0:T(8,128)(2,1)}, bf16[96,192,128]{2,1,0:T(8,128)(2,1)}) custom-call(s32[96]{0:T(128)} %select_reduce_fusion.order_ref, bf16[512,1536]{1,0:T(8,128)(2,1)} %get-tuple-element.189.refs_0_, bf16[512,1536]{1,0:T(8,128)(2,1)} %get-tuple-element.193.refs_1_, bf16[512,1664]{1,0:T(8,128)(2,1)} %get-tuple-element.194.refs_2_, ...), custom_call_target="tpu_custom_call" | custom-call | flops 9663676416 | bytes 22282240 | tf_op jit(solution)/shard_map/pallas_call | solution.py:510
  260.1 9.1 %shard_map.365 = (bf16[256,1536]{1,0:T(8,128)(2,1)}, bf16[256,1536]{1,0:T(8,128)(2,1)}, bf16[256,1536]{1,0:T(8,128)(2,1)}, bf16[256,1536]{1,0:T(8,128)(2,1)}) custom-call(s32[96]{0:T(128)} %select_reduce_fusion.order_ref, bf16[96,144,256]{2,1,0:T(8,128)(2,1)} %all-gather.5.cloned.1.call-done.refs_8_.upper_ref, ...), custom_call_target="tpu_custom_call" | custom-call | flops 3221225472 | bytes 8388608 | tf_op jit(solution)/shard_map/pallas_call | solution.py:449
  278.0 15.6 %shard_map.367 = (bf16[128,1536]{1,0:T(8,128)(2,1)}, bf16[2048,1024]{1,0:T(8,128)(2,1)}) custom-call(bf16[128,1536]{1,0:T(8,128)(2,1)} %get-tuple-element.163.q_ref, s32[128,1]{1,0:T(8,128)} %constant_dynamic-slice_fusion.7.rpos_ref, s32[1,1024]{1,0:T(1,128)} %bitcast.65, bf16[128,1536]{1,0:T(8,128)(2,1)} %get-tuple-element.174.ob_ref.refs_10_, ...), custom_call_target="tpu_custom_call" | custom-call | flops 8053063680 | bytes 8388608 | tf_op jit(solution)/shard_map/pallas_call | solution.py:757
  300.3 15.6 %shard_map.369 = (bf16[128,1536]{1,0:T(8,128)(2,1)}, bf16[2048,1024]{1,0:T(8,128)(2,1)}) custom-call(bf16[128,1536]{1,0:T(8,128)(2,1)} %get-tuple-element.175.q_ref, s32[128,1]{1,0:T(8,128)} %constant_dynamic-slice_fusion.7.rpos_ref, s32[1,1024]{1,0:T(1,128)} %bitcast.66, ...), custom_call_target="tpu_custom_call", output_to_operand_aliasing={{1}: (7, {})} | custom-call | flops 8053063680 | bytes 8388608 | tf_op jit(solution)/shard_map/pallas_call | solution.py:757
  321.5 8.5 %shard_map.370 = (bf16[96,48,128]{2,1,0:T(8,128)(2,1)}, bf16[96,48,128]{2,1,0:T(8,128)(2,1)}, bf16[96,48,128]{2,1,0:T(8,128)(2,1)}, bf16[96,48,128]{2,1,0:T(8,128)(2,1)}, bf16[1536,512]{1,0:T(8,128)(2,1)}) custom-call(s32[2]{0:T(128)} %pad_add_fusion.me_ref, bf16[256,1536]{1,0:T(8,128)(2,1)} %get-tuple-element.159.h_ref.refs_0_, ...), custom_call_target="tpu_custom_call" | custom-call | flops 2415919104 | bytes 16777216 | tf_op jit(solution)/shard_map/pallas_call | solution.py:615
  337.3 21.0 %collective-permute-done.54 = bf16[96,48,128]{2,1,0:T(8,128)(2,1)} collective-permute-done((bf16[96,48,128]{2,1,0:T(8,128)(2,1)}, bf16[96,48,128]{2,1,0:T(8,128)(2,1)}, u32[]{:S(2)}, u32[]{:S(2)}) %collective-permute-start.54) | collective-permute-done | bytes 1179680 | tf_op jit(solution)/shard_map/ppermute | solution.py:925
  363.8 11.5 %collective-permute-done.55 = bf16[48,48,128]{2,1,0:T(8,128)(2,1)} collective-permute-done((bf16[48,48,128]{2,1,0:T(8,128)(2,1)}, bf16[48,48,128]{2,1,0:T(8,128)(2,1)}, u32[]{:S(2)}, u32[]{:S(2)}) %collective-permute-start.55) | collective-permute-done | bytes 589856 | tf_op jit(solution)/shard_map/ppermute | solution.py:925
  394.2 30.7 %collective-permute-done.59 = bf16[96,1536]{1,0:T(8,128)(2,1)S(1)} collective-permute-done((bf16[96,1536]{1,0:T(8,128)(2,1)S(1)}, bf16[96,1536]{1,0:T(8,128)(2,1)S(1)}, u32[]{:S(2)}, u32[]{:S(2)}) %collective-permute-start.59) | collective-permute-done | bytes 294944 | tf_op jit(solution)/shard_map/ppermute | solution.py:935
  425.1 7.2 %shard_map.373 = (f32[2,128,1536]{2,1,0:T(8,128)}, f32[8,1536]{1,0:T(8,128)}) custom-call(f32[2,128,1536]{2,1,0:T(8,128)} %x_ref, f32[2,1536]{1,0:T(2,128)} %gain_ref.9, bf16[1536,2560]{1,0:T(8,128)(2,1)} %get-tuple-element.228.w_ref, f32[128,1536]{1,0:T(8,128)} %get-tuple-element.242.refs_0_, f32[128,1536]{1,0:T(8,128)} %get-tuple-element.243.refs_1_, ...), custom_call_target="tpu_custom_call" | custom-call | flops 805306368 | bytes 14680064 | tf_op jit(solution)/shard_map/pallas_call | solution.py:844
  449.0 8.7 %collective-permute-done.66 = bf16[32,1536]{1,0:T(8,128)(2,1)S(1)} collective-permute-done((bf16[32,1536]{1,0:T(8,128)(2,1)S(1)}, bf16[32,1536]{1,0:T(8,128)(2,1)S(1)}, u32[]{:S(2)}, u32[]{:S(2)}) %collective-permute-start.66) | collective-permute-done | bytes 98336 | tf_op jit(solution)/shard_map/ppermute | solution.py:935
  465.7 22.8 %all-to-all-done = bf16[32,2,7680]{2,1,0:T(2,128)(2,1)S(1)} async-done(((bf16[32,2,7680]{2,1,0:T(2,128)(2,1)}), bf16[32,2,7680]{2,1,0:T(2,128)(2,1)S(1)}, u32[]{:S(2)}, u32[]{:S(2)}) %all-to-all-start) | async-done | bytes 983072 | tf_op jit(solution)/shard_map/all_to_all | solution.py:1227
  498.6 15.2 %shard_map.375 = (f32[12,192,256]{2,1,0:T(8,128)}, f32[12,192,256]{2,1,0:T(8,128)}, f32[12,192,256]{2,1,0:T(8,128)}, f32[12,192,256]{2,1,0:T(8,128)}) custom-call(f32[12,192,256]{2,1,0:T(8,128)} %bitcast.48, f32[12,192,256]{2,1,0:T(8,128)} %bitcast.52, f32[12,192,256]{2,1,0:T(8,128)} %bitcast.53, f32[12,192,192]{2,1,0:T(8,128)} %bitcast.54, ...), custom_call_target="tpu_custom_call" | custom-call | flops 1056964608 | bytes 25165824 | tf_op jit(solution)/shard_map/pallas_call | solution.py:883
  (339 shorter events, 186.1 us)
Async XLA Ops:
  7.2 101.1 %all-gather.5.cloned.1.call-start = ((), (), s32[]{:S(2)}) async-start(), calls=%async_computation.4 | async-start | bytes 7962624 | tf_op jit(solution)/shard_map/all_gather | solution.py:1086
  35.8 100.6 %all-gather.7.cloned.1.call-start = ((), (), s32[]{:S(2)}) async-start(), calls=%async_computation.5 | async-start | bytes 2359296 | tf_op jit(solution)/shard_map/all_gather | solution.py:1116
  108.4 58.3 %all-gather.9.cloned.1.call-start = ((), (), s32[]{:S(2)}) async-start(), calls=%async_computation.6 | async-start | bytes 2359296 | tf_op jit(solution)/shard_map/all_gather | solution.py:1116
  136.4 63.4 %all-gather.11.cloned.1.call-start = ((), (), s32[]{:S(2)}) async-start(), calls=%async_computation.7 | async-start | bytes 2654208 | tf_op jit(solution)/shard_map/all_gather | solution.py:1120
  136.5 22.2 %collective-permute-start.36 = (bf16[256,1664]{1,0:T(8,128)(2,1)S(1)}, bf16[256,1664]{1,0:T(8,128)(2,1)}, u32[]{:S(2)}, u32[]{:S(2)}) collective-permute-start(bf16[256,1664]{1,0:T(8,128)(2,1)S(1)} %bitcast.58), channel_id=1, source_target_pairs={{0,3},{1,2},{2,1},{3,0},{4,7},{5,6},{6,5},{7,4},{8,11},{9,10},{10,... | collective-permute-start | bytes 2555912 | tf_op jit(solution)/shard_map/ppermute | solution.py:925
  166.6 149.3 %reduce-scatter.4.cloned.1.call-start = ((), (), s32[]{:S(2)}) async-start(), calls=%async_computation.8 | async-start | bytes 5308416 | tf_op jit(solution)/shard_map/reduce_scatter | solution.py:1174
  166.9 23.6 %collective-permute-start.30 = (bf16[256,1536]{1,0:T(8,128)(2,1)S(1)}, bf16[256,1536]{1,0:T(8,128)(2,1)S(1)}, u32[]{:S(2)}, u32[]{:S(2)}) collective-permute-start(bf16[256,1536]{1,0:T(8,128)(2,1)S(1)} %copy-done.19), channel_id=1, source_target_pairs={{0,4},{4,0},{8,12},{12,8},{16,20},{20,16},{24,28},{28,24},{1,5},{5... | collective-permute-start | bytes 2359304 | tf_op jit(solution)/shard_map/ppermute | solution.py:930
  188.4 30.4 %collective-permute-start.40 = (bf16[128,1536]{1,0:T(8,128)(2,1)}, bf16[128,1536]{1,0:T(8,128)(2,1)}, u32[]{:S(2)}, u32[]{:S(2)}) collective-permute-start(bf16[128,1536]{1,0:T(8,128)(2,1)} %get-tuple-element.192.refs_0_.h2_ref), channel_id=1, source_target_pairs={{0,1},{1,0},{2,3},{3,2},{4,5},{5,4},{6,7},{7,6},{8,9},{9,8},{10,11... | collective-permute-start | bytes 1179656 | tf_op jit(solution)/shard_map/ppermute | solution.py:925
  189.6 29.7 %collective-permute-start.41 = (bf16[128,1536]{1,0:T(8,128)(2,1)}, bf16[128,1536]{1,0:T(8,128)(2,1)}, u32[]{:S(2)}, u32[]{:S(2)}) collective-permute-start(bf16[128,1536]{1,0:T(8,128)(2,1)} %get-tuple-element.192.refs_0_.h2_ref), channel_id=1, source_target_pairs={{0,2},{1,3},{2,0},{3,1},{4,6},{5,7},{6,4},{7,5},{8,10},{9,11},{10,... | collective-permute-start | bytes 1179656 | tf_op jit(solution)/shard_map/ppermute | solution.py:925
  190.5 28.9 %collective-permute-start.42 = (bf16[128,1536]{1,0:T(8,128)(2,1)}, bf16[128,1536]{1,0:T(8,128)(2,1)S(1)}, u32[]{:S(2)}, u32[]{:S(2)}) collective-permute-start(bf16[128,1536]{1,0:T(8,128)(2,1)} %get-tuple-element.192.refs_0_.h2_ref), channel_id=1, source_target_pairs={{0,3},{1,2},{2,1},{3,0},{4,7},{5,6},{6,5},{7,4},{8,11},{9,10},{10,... | collective-permute-start | bytes 1179656 | tf_op jit(solution)/shard_map/ppermute | solution.py:925
  215.8 23.8 %collective-permute-start.37 = (bf16[128,1664]{1,0:T(8,128)(2,1)}, bf16[128,1664]{1,0:T(8,128)(2,1)S(1)}, u32[]{:S(2)}, u32[]{:S(2)}) collective-permute-start(bf16[128,1664]{1,0:T(8,128)(2,1)} %get-tuple-element.185), channel_id=1, source_target_pairs={{0,1},{1,0},{2,3},{3,2},{4,5},{5,4},{6,7},{7,6},{8,9},{9,8},{10,11... | collective-permute-start | bytes 1277960 | tf_op jit(solution)/shard_map/ppermute | solution.py:925
  217.4 22.7 %collective-permute-start.38 = (bf16[128,1664]{1,0:T(8,128)(2,1)}, bf16[128,1664]{1,0:T(8,128)(2,1)S(1)}, u32[]{:S(2)}, u32[]{:S(2)}) collective-permute-start(bf16[128,1664]{1,0:T(8,128)(2,1)} %get-tuple-element.186), channel_id=1, source_target_pairs={{0,2},{1,3},{2,0},{3,1},{4,6},{5,7},{6,4},{7,5},{8,10},{9,11},{10,... | collective-permute-start | bytes 1277960 | tf_op jit(solution)/shard_map/ppermute | solution.py:925
  258.8 119.5 %reduce-scatter.6.cloned.1.call-start = ((), (), s32[]{:S(2)}) async-start(), calls=%async_computation.9 | async-start | bytes 4718592 | tf_op jit(solution)/shard_map/reduce_scatter | solution.py:1175
  269.1 24.5 %collective-permute-start.43 = (bf16[256,1536]{1,0:T(8,128)(2,1)}, bf16[256,1536]{1,0:T(8,128)(2,1)S(1)}, u32[]{:S(2)}, u32[]{:S(2)}) collective-permute-start(bf16[256,1536]{1,0:T(8,128)(2,1)} %get-tuple-element.205), channel_id=1, source_target_pairs={{0,1},{1,0},{2,3},{3,2},{4,5},{5,4},{6,7},{7,6},{8,9},{9,8},{10,11... | collective-permute-start | bytes 2359304 | tf_op jit(solution)/shard_map/ppermute | solution.py:925
  270.5 23.2 %collective-permute-start.44 = (bf16[256,1536]{1,0:T(8,128)(2,1)}, bf16[256,1536]{1,0:T(8,128)(2,1)S(1)}, u32[]{:S(2)}, u32[]{:S(2)}) collective-permute-start(bf16[256,1536]{1,0:T(8,128)(2,1)} %get-tuple-element.206), channel_id=1, source_target_pairs={{0,2},{1,3},{2,0},{3,1},{4,6},{5,7},{6,4},{7,5},{8,10},{9,11},{10,... | collective-permute-start | bytes 2359304 | tf_op jit(solution)/shard_map/ppermute | solution.py:925
  316.0 182.6 %reduce-scatter.8.cloned.1.call-start = ((), (), s32[]{:S(2)}) async-start(), calls=%async_computation.10 | async-start | bytes 5308416 | tf_op jit(solution)/shard_map/reduce_scatter | solution.py:1202
  329.9 28.4 %collective-permute-start.54 = (bf16[96,48,128]{2,1,0:T(8,128)(2,1)}, bf16[96,48,128]{2,1,0:T(8,128)(2,1)}, u32[]{:S(2)}, u32[]{:S(2)}) collective-permute-start(bf16[96,48,128]{2,1,0:T(8,128)(2,1)} %get-tuple-element.233), channel_id=1, source_target_pairs={{0,2},{1,3},{2,0},{3,1},{4,6},{5,7},{6,4},{7,5},{8,10},{9,11},{10,... | collective-permute-start | bytes 3538952 | tf_op jit(solution)/shard_map/ppermute | solution.py:925
  330.5 30.4 %collective-permute-start.52 = (bf16[96,48,128]{2,1,0:T(8,128)(2,1)}, bf16[96,48,128]{2,1,0:T(8,128)(2,1)S(1)}, u32[]{:S(2)}, u32[]{:S(2)}) collective-permute-start(bf16[96,48,128]{2,1,0:T(8,128)(2,1)} %get-tuple-element.227), channel_id=1, source_target_pairs={{0,1},{1,0},{2,3},{3,2},{4,5},{5,4},{6,7},{7,6},{8,9},{9,8},{10,11... | collective-permute-start | bytes 3538952 | tf_op jit(solution)/shard_map/ppermute | solution.py:925
  380.9 44.0 %collective-permute-start.59 = (bf16[96,1536]{1,0:T(8,128)(2,1)S(1)}, bf16[96,1536]{1,0:T(8,128)(2,1)S(1)}, u32[]{:S(2)}, u32[]{:S(2)}) collective-permute-start(bf16[96,1536]{1,0:T(8,128)(2,1)S(1)} %get-tuple-element.284), channel_id=1, source_target_pairs={{0,16},{4,20},{8,24},{12,28},{16,0},{20,4},{24,8},{28,12},{1,17},{... | collective-permute-start | bytes 884744 | tf_op jit(solution)/shard_map/ppermute | solution.py:935
  381.7 43.2 %collective-permute-start.60 = (bf16[96,1536]{1,0:T(8,128)(2,1)S(1)}, bf16[96,1536]{1,0:T(8,128)(2,1)S(1)}, u32[]{:S(2)}, u32[]{:S(2)}) collective-permute-start(bf16[96,1536]{1,0:T(8,128)(2,1)S(1)} %get-tuple-element.283), channel_id=1, source_target_pairs={{0,8},{4,12},{8,16},{12,20},{16,24},{20,28},{24,0},{28,4},{1,9},{5... | collective-permute-start | bytes 884744 | tf_op jit(solution)/shard_map/ppermute | solution.py:935
  388.1 45.0 %collective-permute-start.62 = (bf16[32,48,128]{2,1,0:T(8,128)(2,1)}, bf16[32,48,128]{2,1,0:T(8,128)(2,1)S(1)}, u32[]{:S(2)}, u32[]{:S(2)}) collective-permute-start(bf16[32,48,128]{2,1,0:T(8,128)(2,1)} %get-tuple-element.247), channel_id=1, source_target_pairs={{0,2},{1,3},{2,0},{3,1},{4,6},{5,7},{6,4},{7,5},{8,10},{9,11},{10,... | collective-permute-start | bytes 1179656 | tf_op jit(solution)/shard_map/ppermute | solution.py:925
  389.0 45.2 %collective-permute-start.57 = (bf16[32,48,128]{2,1,0:T(8,128)(2,1)}, bf16[32,48,128]{2,1,0:T(8,128)(2,1)S(1)}, u32[]{:S(2)}, u32[]{:S(2)}) collective-permute-start(bf16[32,48,128]{2,1,0:T(8,128)(2,1)} %get-tuple-element.240), channel_id=1, source_target_pairs={{0,1},{1,0},{2,3},{3,2},{4,5},{5,4},{6,7},{7,6},{8,9},{9,8},{10,11... | collective-permute-start | bytes 1179656 | tf_op jit(solution)/shard_map/ppermute | solution.py:925
  460.3 28.1 %all-to-all-start = ((bf16[32,2,7680]{2,1,0:T(2,128)(2,1)}), bf16[32,2,7680]{2,1,0:T(2,128)(2,1)S(1)}, u32[]{:S(2)}, u32[]{:S(2)}) async-start(bf16[32,2,7680]{2,1,0:T(2,128)(2,1)} %all_to_all.6), calls=%async_computation.2 | async-start | bytes 1966080 | tf_op jit(solution)/shard_map/all_to_all | solution.py:1227
  463.0 50.8 %collective-permute-start.64 = (bf16[256,1536]{1,0:T(8,128)(2,1)}, bf16[256,1536]{1,0:T(8,128)(2,1)}, u32[]{:S(2)}, u32[]{:S(2)}) collective-permute-start(bf16[256,1536]{1,0:T(8,128)(2,1)} %get-tuple-element.249), channel_id=1, source_target_pairs={{0,3},{1,2},{2,1},{3,0},{4,7},{5,6},{6,5},{7,4},{8,11},{9,10},{10,... | collective-permute-start | bytes 2359304 | tf_op jit(solution)/shard_map/ppermute | solution.py:925
  (112 other events, 1444.1 us)
Sparse Core Ops, SparseCore 0:
  35.9 70.1 all-gather.4
  108.5 27.8 all-gather.6
  138.0 28.5 all-gather.8
  168.7 31.0 all-gather.10
  258.5 53.8 reduce-scatter.3
  316.1 47.2 reduce-scatter.5
  378.5 71.5 reduce-scatter.7

commit v10 on v8

--- a/solution.py
+++ b/solution.py
@@ -14,7 +14,7 @@
 BR = 192
 BC = 256
 LANES = 128
-UPPER = 128
+UPPER = 144
 
 norm_eps = 1e-06
 beta_one = 0.9
@@ -962,7 +962,7 @@
     return total
 
 
-def gather_weights(blocks, chips, members):
+def gather_weights(blocks, chips, members, small):
     parts = [blocks]
     for _ in range(chips - 1):
         parts.append(to_chip(parts[-1], 1))
@@ -992,6 +992,7 @@
         return got
 
     got = [to_partner(blocks, offset) for offset in range(1, members)]
+    first = got + parts[1:3]
     gate.append(got[0])
     add(blocks, 0, 0, 0)
     for offset in range(1, members):
@@ -1000,11 +1001,10 @@
     if chips > 1:
         last = spread(after(parts[1], *last), 1)
         gate[:] = last
-        got = last
     if chips > 2:
-        group = after(jnp.concatenate(parts[2:], axis=0), *last)
+        group = after(jnp.concatenate(parts[2:], axis=0), *last, *small)
         spread(group, 2)
-    return got + parts[1:], pieces, arrays
+    return first, pieces, arrays
 
 
 def add_wide(parts):
@@ -1089,7 +1089,10 @@
     rows_pos = all_pos[ctx].reshape(rows, 1)
     router_pad = jnp.pad(router.astype(low_type), ((0, 0), (0, LANES - shard_count)))
 
-    far, pieces, arrays = gather_weights(dense_weight.astype(low_type), chips, shard_count)
+    small = (me, expert_inverse, router_pad, key_pos, rows_pos)
+    far, pieces, arrays = gather_weights(
+        dense_weight.astype(low_type), chips, shard_count, small
+    )
     expert_low = after(expert_weight[0].astype(low_type), *far)
     expert_all = [lax.all_gather(expert_low[:, :UPPER], "ctx", axis=0, tiled=True)]
 
@@ -1100,9 +1103,6 @@
     cot_rows = after(cot_rows, *arrays[::2])
     cot_parts = [to_partner(cot_rows, j) for j in range(shard_count)]
 
-    here, expert_inverse, router_pad, key_pos, rows_pos = lax.optimization_barrier(
-        (me, expert_inverse, router_pad, key_pos, rows_pos)
-    )
     h1, kv, w_in, w_out = project(
         pieces,
         arrays,
@@ -1110,7 +1110,7 @@
         shard_count,
         slots,
         dense_order,
-        here,
+        me,
         [tokens[m] for m in range(micros)],
         norm_gains,
     )
@@ -1152,10 +1152,12 @@
     expert_terms = outer_blocks(
         after(expert_inverse, *backs[0]), width, (0, 0, 1), [xs, cs], [dgs, dus, zs]
     )
+    outs = produce(after(expert_inverse, *expert_terms), expert_all, zs, shard_count, width)
+    arrived = [to_partner(outs[j], j) for j in range(min(3, shard_count))]
     dxs, das, dqs, stats = [], [], [], []
     dkv_terms = None
     for m in range(micros):
-        here = after(me, expert_terms, backs[-1]) if m == 0 else after(me, dqs[-1])
+        here = after(me, outs, backs[-1]) if m == 0 else after(me, dqs[-1], arrived[1:])
         dx, da, do, stat = merge(
             here, x2s[m], cotangent[m], h2s[m], norm_gains, router_pad, w_out, backs[m]
         )
@@ -1184,9 +1186,8 @@
         False,
     )
     h1_turned = early[4]
-    outs = produce(after(expert_inverse, early[0]), expert_all, zs, shard_count, width)
     parts_back = query_back(after(w_in, early[0]), dqs)
-    early_rows, early_seen = sum_members(early[:4], (outs, parts_back), shard_count)
+    early_rows, early_seen = sum_members(early[:4], parts_back, shard_count)
     chip = ctx // 2
     early_parts = sum_chips(early_rows, chip, chips)
     late = gradient_pieces(
@@ -1200,9 +1201,10 @@
         after(tokens, late[0]), norm_gains, w_in, dxs, parts_back, dkv
     )
     late_rows, late_seen = sum_members(late[:4], (input_grad, early_parts), shard_count)
-    late_term = after(expert_terms[1], *late_seen)
+    late_term = after(expert_terms[1], dkv)
     expert_sums.append(lax.psum_scatter(late_term, "ctx", scatter_dimension=0, tiled=True))
-    arrived = [to_partner(part, j) for j, part in enumerate(after(list(outs), *late_seen))]
+    last_outs = after(list(outs), *late_seen)
+    arrived += [to_partner(last_outs[j], j) for j in range(3, shard_count)]
     early_sum = add_wide(early_parts).astype(low_type)
     late_sum = add_wide(sum_chips(late_rows, chip, chips)).astype(low_type)
     all_sums = jnp.concatenate([early_sum, late_sum], axis=0)
@@ -1226,7 +1228,10 @@
         axis=1,
     ).reshape(devices * 2, (slots + extra) * piece_width // 2)
     ordered = lax.all_to_all(ordered, ("ctx", "shard"), split_axis=0, concat_axis=0, tiled=True)
-    ordered = ordered.reshape(devices, slots + extra, piece_width)
+    expert_grad, expert_new, expert_moment_new, expert_second_new = rotate(
+        expert_weight[0], expert_sums, expert_moment[0], expert_second[0], expert_left[0], expert_right[0]
+    )
+    ordered = after(ordered, expert_new).reshape(devices, slots + extra, piece_width)
     stat_rows = jnp.sum(wide(ordered[:, slots:]), axis=0).reshape(shard_count + 2, width)
     ordered = ordered[:, :slots].reshape(
         chips, 2, shard_count, slots, BR // (shard_count * chips), LANES
@@ -1235,9 +1240,6 @@
     router_grad = stat_rows[:shard_count].T
     gains_grad = stat_rows[shard_count:]
 
-    expert_grad, expert_new, expert_moment_new, expert_second_new = rotate(
-        expert_weight[0], expert_sums, expert_moment[0], expert_second[0], expert_left[0], expert_right[0]
-    )
     dense_grad, dense_new, dense_moment_new, dense_second_new = rotate(
         dense_weight, [dense_sum], dense_moment, dense_second, dense_left, dense_right
     )

time: 526 us -> 522 us (level)
  waiting for transfers between devices: 190 us -> 202 us
  starting transfers between devices: 74 us -> 63.4 us
    ppermute x9, waiting for transfers between devices: 33.6 us -> 61.4 us  [to_chip(): lax.ppermute(array, 'ctx', [(i, (i + 2 * offset) % count) for i in range(...]
    all_to_all x1, waiting for transfers between devices: 37.9 us -> 22.8 us  [shards(): lax.all_to_all(ordered, ('ctx', 'shard'), split_axis=0, concat_axis=0, ti...]
    all_gather x1, waiting for transfers between devices: 0.02 us -> 9.16 us  [shards(): lax.all_gather(expert_low[:, :UPPER], 'ctx', axis=0, tiled=True)]
    reduce_scatter x1, waiting for transfers between devices: 8.34 us -> 0.02 us  [shards(): lax.psum_scatter(first_term, 'ctx', scatter_dimension=0, tiled=True)]
    ppermute x37, waiting for transfers between devices: 102 us -> 95.9 us  [to_partner(): return lax.ppermute(array, 'shard', [(i, i ^ offset) for i in range(count)])]
  transfers between devices with their start and end apart: 75 -> 75, of which waited for: 35 -> 35; matrix products, arithmetic and copies ran while one was open for 6% -> 5% of each run, Pallas kernels for 37% -> 38%
where the time goes in v10:
time: 522 us; the launch traced here: 516 us
  waiting for transfers between devices  202 us (39%)
  Pallas kernels  194 us (37%)
  starting transfers between devices  63.4 us (12%)
  local copies, waits for them, and re-layouts  23.7 us (5%)
  other arithmetic  17.9 us (3%)
  between operations  15.5 us (3%)
    ppermute x37, waiting for transfers between devices, to_partner(): return lax.ppermute(array, 'shard', [(i, i ^ offset) for i in range(count)])  95.9 us
    ppermute x9, waiting for transfers between devices, to_chip(): lax.ppermute(array, 'ctx', [(i, (i + 2 * offset) % count) for i in range(...  61.4 us
    ppermute x37, starting transfers between devices, to_partner(): return lax.ppermute(array, 'shard', [(i, i ^ offset) for i in range(count)])  40.4 us
    pallas_call x2, Pallas kernels, run_expert(): call(functools.partial(expert_kernel, sources, micro), tuple([shaped((row...  32.2 us
    pallas_call x2, Pallas kernels, attend_back(): pl.pallas_call(functools.partial(attend_back_kernel, micro), out_shape=(s...  31.1 us
    pallas_call x2, Pallas kernels, attend(): call(functools.partial(attend_kernel, micro), (shaped((rows, width), low_...  25.5 us
    all_to_all x1, waiting for transfers between devices, shards(): lax.all_to_all(ordered, ('ctx', 'shard'), split_axis=0, concat_axis=0, ti...  22.8 us
    pallas_call x2, Pallas kernels, rotate(): pl.pallas_call(rotate_kernel, grid=(count,), out_shape=(shaped(weight.sha...  21 us
  transfers between devices with their start and end apart: 75, of which 35 were waited for; matrix products, arithmetic and copies ran while one was open for 5% of the time, Pallas kernels for 38%

profile of v10, /device:TPU:0, one launch (start us, length us, event | category | flops | bytes accessed | tf_op | source)
XLA Modules:
  0.0 516.1 jit_solution(5033571578109480041)
XLA Ops:
  15.0 7.7 %collective-permute-done.7.refs_11_ = bf16[4,192,256]{2,1,0:T(8,128)(2,1)S(1)} collective-permute-done((bf16[4,192,256]{2,1,0:T(8,128)(2,1)S(1)}, bf16[4,192,256]{2,1,0:T(8,128)(2,1)S(1)}, u32[]{:S(2)}, u32[]{:S(2)}) %collective-permute-start.7) | collective-permute-done | bytes 393248 | tf_op jit(solution)/shard_map/ppermute | solution.py:943
  24.7 7.1 %collective-permute-done.3.refs_7_ = bf16[4,192,256]{2,1,0:T(8,128)(2,1)S(1)} collective-permute-done((bf16[4,192,256]{2,1,0:T(8,128)(2,1)S(1)}, bf16[4,192,256]{2,1,0:T(8,128)(2,1)S(1)}, u32[]{:S(2)}, u32[]{:S(2)}) %collective-permute-start.3) | collective-permute-done | bytes 393248 | tf_op jit(solution)/shard_map/ppermute | solution.py:933
  45.4 6.8 %collective-permute-done.18 = bf16[4,192,256]{2,1,0:T(8,128)(2,1)S(1)} collective-permute-done((bf16[4,192,256]{2,1,0:T(8,128)(2,1)S(1)}, bf16[4,192,256]{2,1,0:T(8,128)(2,1)S(1)}, u32[]{:S(2)}, u32[]{:S(2)}) %collective-permute-start.18) | collective-permute-done | bytes 393248 | tf_op jit(solution)/shard_map/ppermute | solution.py:943
  57.0 12.0 %collective-permute-done.22.refs_25_ = bf16[8,192,256]{2,1,0:T(8,128)(2,1)S(1)} collective-permute-done((bf16[8,192,256]{2,1,0:T(8,128)(2,1)S(1)}, bf16[8,192,256]{2,1,0:T(8,128)(2,1)S(1)}, u32[]{:S(2)}, u32[]{:S(2)}) %collective-permute-start.22) | collective-permute-done | bytes 786464 | tf_op jit(solution)/shard_map/ppermute | solution.py:933
  85.8 12.4 %shard_map.358 = (bf16[256,1536]{1,0:T(8,128)(2,1)}, bf16[256,1024]{1,0:T(8,128)(2,1)}, bf16[1536,2560]{1,0:T(8,128)(2,1)}, bf16[1536,1536]{1,0:T(8,128)(2,1)}) custom-call(s32[128]{0:T(128)} %order_ref.1, s32[2]{0:T(128)} %pad_add_fusion.me_ref, f32[128,1536]{1,0:T(8,128)} %get-tuple-element.267.refs_0_.x_ref, ...), custom_call_target="tpu_custom_call" | custom-call | flops 805306368 | bytes 25165824 | tf_op jit(solution)/shard_map/pallas_call | solution.py:192
  98.2 9.2 %all-gather.4.cloned.1.call-done.refs_8_.upper_ref = bf16[96,144,256]{2,1,0:T(8,128)(2,1)} async-done(((bf16[12,144,256]{2,1,0:T(8,128)(2,1)}), bf16[96,144,256]{2,1,0:T(8,128)(2,1)}) %all-gather.4.cloned.1.call-update) | async-done | bytes 7077904 | tf_op jit(solution)/shard_map/all_gather | solution.py:1097
  118.7 11.0 %collective-permute-done.28.refs_5_ = bf16[256,1664]{1,0:T(8,128)(2,1)} collective-permute-done((bf16[256,1664]{1,0:T(8,128)(2,1)S(1)}, bf16[256,1664]{1,0:T(8,128)(2,1)}, u32[]{:S(2)}, u32[]{:S(2)}) %collective-permute-start.28) | collective-permute-done | bytes 852000 | tf_op jit(solution)/shard_map/ppermute | solution.py:933
  129.8 18.3 %collective-permute-done.29.refs_6_ = bf16[256,1664]{1,0:T(8,128)(2,1)} collective-permute-done((bf16[256,1664]{1,0:T(8,128)(2,1)S(1)}, bf16[256,1664]{1,0:T(8,128)(2,1)}, u32[]{:S(2)}, u32[]{:S(2)}) %collective-permute-start.29) | collective-permute-done | bytes 852000 | tf_op jit(solution)/shard_map/ppermute | solution.py:933
  154.9 12.7 %shard_map.360 = (bf16[128,1536]{1,0:T(8,128)(2,1)}, f32[384,128]{1,0:T(8,128)}, f32[128,1536]{1,0:T(8,128)}, bf16[128,1536]{1,0:T(8,128)(2,1)}) custom-call(bf16[128,1536]{1,0:T(8,128)(2,1)} %get-tuple-element.155.q_ref, s32[128,1]{1,0:T(8,128)} %constant_dynamic-slice_fusion.7.rpos_ref, s32[1,1024]{1,0:T(1,128)} %bitcast.63, ...), custom_call_target="tpu_custom_call" | custom-call | flops 3221225472 | bytes 8388608 | tf_op jit(solution)/shard_map/pallas_call | solution.py:306
  171.2 12.8 %shard_map.361 = (bf16[128,1536]{1,0:T(8,128)(2,1)}, f32[384,128]{1,0:T(8,128)}, f32[128,1536]{1,0:T(8,128)}, bf16[128,1536]{1,0:T(8,128)(2,1)}) custom-call(bf16[128,1536]{1,0:T(8,128)(2,1)} %get-tuple-element.163.q_ref, s32[128,1]{1,0:T(8,128)} %constant_dynamic-slice_fusion.7.rpos_ref, s32[1,1024]{1,0:T(1,128)} %bitcast.64, ...), custom_call_target="tpu_custom_call" | custom-call | flops 3221225472 | bytes 8388608 | tf_op jit(solution)/shard_map/pallas_call | solution.py:306
  192.5 16.0 %shard_map.362 = (bf16[128,1664]{1,0:T(8,128)(2,1)}, bf16[128,1664]{1,0:T(8,128)(2,1)}, bf16[128,1664]{1,0:T(8,128)(2,1)}, bf16[128,1664]{1,0:T(8,128)(2,1)}, bf...) custom-call(s32[96]{0:T(128)} %select_reduce_fusion.order_ref, ...), custom_call_target="tpu_custom_call" | custom-call | flops 8053063680 | bytes 20971520 | tf_op jit(solution)/shard_map/pallas_call | solution.py:406
  212.8 16.2 %shard_map.363 = (bf16[128,1664]{1,0:T(8,128)(2,1)}, bf16[128,1664]{1,0:T(8,128)(2,1)}, bf16[128,1664]{1,0:T(8,128)(2,1)}, bf16[128,1664]{1,0:T(8,128)(2,1)}, bf...) custom-call(s32[96]{0:T(128)} %select_reduce_fusion.order_ref, ...), custom_call_target="tpu_custom_call" | custom-call | flops 8053063680 | bytes 20971520 | tf_op jit(solution)/shard_map/pallas_call | solution.py:406
  232.5 17.9 %shard_map.364 = (bf16[96,192,128]{2,1,0:T(8,128)(2,1)}, bf16[96,192,128]{2,1,0:T(8,128)(2,1)}) custom-call(s32[96]{0:T(128)} %select_reduce_fusion.order_ref, bf16[512,1536]{1,0:T(8,128)(2,1)} %get-tuple-element.174.refs_0_, bf16[512,1536]{1,0:T(8,128)(2,1)} %get-tuple-element.178.refs_1_, bf16[512,1664]{1,0:T(8,128)(2,1)} %get-tuple-element.179.refs_2_, ...), custom_call_target="tpu_custom_call" | custom-call | flops 9663676416 | bytes 22282240 | tf_op jit(solution)/shard_map/pallas_call | solution.py:521
  252.5 8.8 %shard_map.365 = (bf16[256,1536]{1,0:T(8,128)(2,1)}, bf16[256,1536]{1,0:T(8,128)(2,1)}, bf16[256,1536]{1,0:T(8,128)(2,1)}, bf16[256,1536]{1,0:T(8,128)(2,1)}) custom-call(s32[96]{0:T(128)} %select_reduce_fusion.order_ref, bf16[96,144,256]{2,1,0:T(8,128)(2,1)} %all-gather.4.cloned.1.call-done.refs_8_.upper_ref, ...), custom_call_target="tpu_custom_call" | custom-call | flops 3221225472 | bytes 8388608 | tf_op jit(solution)/shard_map/pallas_call | solution.py:460
  269.8 15.5 %shard_map.367 = (bf16[128,1536]{1,0:T(8,128)(2,1)}, bf16[2048,1024]{1,0:T(8,128)(2,1)}) custom-call(bf16[128,1536]{1,0:T(8,128)(2,1)} %get-tuple-element.155.q_ref, s32[128,1]{1,0:T(8,128)} %constant_dynamic-slice_fusion.7.rpos_ref, s32[1,1024]{1,0:T(1,128)} %bitcast.65, bf16[128,1536]{1,0:T(8,128)(2,1)} %get-tuple-element.162.ob_ref.refs_10_, ...), custom_call_target="tpu_custom_call" | custom-call | flops 8053063680 | bytes 8388608 | tf_op jit(solution)/shard_map/pallas_call | solution.py:768
  292.0 15.6 %shard_map.369 = (bf16[128,1536]{1,0:T(8,128)(2,1)}, bf16[2048,1024]{1,0:T(8,128)(2,1)}) custom-call(bf16[128,1536]{1,0:T(8,128)(2,1)} %get-tuple-element.163.q_ref, s32[128,1]{1,0:T(8,128)} %constant_dynamic-slice_fusion.7.rpos_ref, s32[1,1024]{1,0:T(1,128)} %bitcast.66, ...), custom_call_target="tpu_custom_call", output_to_operand_aliasing={{1}: (7, {})} | custom-call | flops 8053063680 | bytes 8388608 | tf_op jit(solution)/shard_map/pallas_call | solution.py:768
  313.2 8.5 %shard_map.370 = (bf16[96,48,128]{2,1,0:T(8,128)(2,1)}, bf16[96,48,128]{2,1,0:T(8,128)(2,1)}, bf16[96,48,128]{2,1,0:T(8,128)(2,1)}, bf16[96,48,128]{2,1,0:T(8,128)(2,1)}, bf16[1536,512]{1,0:T(8,128)(2,1)}) custom-call(s32[2]{0:T(128)} %pad_add_fusion.me_ref, bf16[256,1536]{1,0:T(8,128)(2,1)} %get-tuple-element.151.h_ref.refs_0_, ...), custom_call_target="tpu_custom_call" | custom-call | flops 2415919104 | bytes 16777216 | tf_op jit(solution)/shard_map/pallas_call | solution.py:626
  329.4 20.6 %collective-permute-done.54 = bf16[96,48,128]{2,1,0:T(8,128)(2,1)} collective-permute-done((bf16[96,48,128]{2,1,0:T(8,128)(2,1)}, bf16[96,48,128]{2,1,0:T(8,128)(2,1)}, u32[]{:S(2)}, u32[]{:S(2)}) %collective-permute-start.54) | collective-permute-done | bytes 1179680 | tf_op jit(solution)/shard_map/ppermute | solution.py:933
  355.4 10.6 %collective-permute-done.55 = bf16[48,48,128]{2,1,0:T(8,128)(2,1)} collective-permute-done((bf16[48,48,128]{2,1,0:T(8,128)(2,1)S(1)}, bf16[48,48,128]{2,1,0:T(8,128)(2,1)}, u32[]{:S(2)}, u32[]{:S(2)}) %collective-permute-start.55) | collective-permute-done | bytes 589856 | tf_op jit(solution)/shard_map/ppermute | solution.py:933
  386.3 28.8 %collective-permute-done.59 = bf16[96,1536]{1,0:T(8,128)(2,1)S(1)} collective-permute-done((bf16[96,1536]{1,0:T(8,128)(2,1)S(1)}, bf16[96,1536]{1,0:T(8,128)(2,1)S(1)}, u32[]{:S(2)}, u32[]{:S(2)}) %collective-permute-start.59) | collective-permute-done | bytes 294944 | tf_op jit(solution)/shard_map/ppermute | solution.py:943
  415.3 7.2 %shard_map.373 = (f32[2,128,1536]{2,1,0:T(8,128)}, f32[8,1536]{1,0:T(8,128)}) custom-call(f32[2,128,1536]{2,1,0:T(8,128)} %x_ref, f32[2,1536]{1,0:T(2,128)} %gain_ref.9, bf16[1536,2560]{1,0:T(8,128)(2,1)} %get-tuple-element.213.w_ref, f32[128,1536]{1,0:T(8,128)} %get-tuple-element.227.refs_0_, f32[128,1536]{1,0:T(8,128)} %get-tuple-element.228.refs_1_, ...), custom_call_target="tpu_custom_call" | custom-call | flops 805306368 | bytes 14680064 | tf_op jit(solution)/shard_map/pallas_call | solution.py:852
  438.6 10.0 %collective-permute-done.66 = bf16[32,1536]{1,0:T(8,128)(2,1)S(1)} collective-permute-done((bf16[32,1536]{1,0:T(8,128)(2,1)S(1)}, bf16[32,1536]{1,0:T(8,128)(2,1)S(1)}, u32[]{:S(2)}, u32[]{:S(2)}) %collective-permute-start.66) | collective-permute-done | bytes 98336 | tf_op jit(solution)/shard_map/ppermute | solution.py:943
  456.5 22.8 %all-to-all-done = bf16[32,2,7680]{2,1,0:T(2,128)(2,1)S(1)} async-done(((bf16[32,2,7680]{2,1,0:T(2,128)(2,1)}), bf16[32,2,7680]{2,1,0:T(2,128)(2,1)S(1)}, u32[]{:S(2)}, u32[]{:S(2)}) %all-to-all-start) | async-done | bytes 983072 | tf_op jit(solution)/shard_map/all_to_all | solution.py:1230
  479.7 15.1 %shard_map.374 = (f32[12,192,256]{2,1,0:T(8,128)}, f32[12,192,256]{2,1,0:T(8,128)}, f32[12,192,256]{2,1,0:T(8,128)}, f32[12,192,256]{2,1,0:T(8,128)}) custom-call(f32[12,192,256]{2,1,0:T(8,128)} %bitcast.48, f32[12,192,256]{2,1,0:T(8,128)} %bitcast.52, f32[12,192,256]{2,1,0:T(8,128)} %bitcast.53, f32[12,192,192]{2,1,0:T(8,128)} %bitcast.54, ...), custom_call_target="tpu_custom_call" | custom-call | flops 1056964608 | bytes 25165824 | tf_op jit(solution)/shard_map/pallas_call | solution.py:891
  (367 shorter events, 177.2 us)
Async XLA Ops:
  7.2 100.2 %all-gather.4.cloned.1.call-start = ((), (), s32[]{:S(2)}) async-start(), calls=%async_computation.4 | async-start | bytes 7962624 | tf_op jit(solution)/shard_map/all_gather | solution.py:1097
  35.8 118.2 %all-gather.6.cloned.1.call-start = ((), (), s32[]{:S(2)}) async-start(), calls=%async_computation.5 | async-start | bytes 4718592 | tf_op jit(solution)/shard_map/all_gather | solution.py:1120
  107.4 85.0 %all-gather.8.cloned.1.call-start = ((), (), s32[]{:S(2)}) async-start(), calls=%async_computation.6 | async-start | bytes 2654208 | tf_op jit(solution)/shard_map/all_gather | solution.py:1122
  107.8 22.0 %collective-permute-start.28 = (bf16[256,1664]{1,0:T(8,128)(2,1)S(1)}, bf16[256,1664]{1,0:T(8,128)(2,1)}, u32[]{:S(2)}, u32[]{:S(2)}) collective-permute-start(bf16[256,1664]{1,0:T(8,128)(2,1)S(1)} %bitcast.56), channel_id=1, source_target_pairs={{0,1},{1,0},{2,3},{3,2},{4,5},{5,4},{6,7},{7,6},{8,9},{9,8},{10,11... | collective-permute-start | bytes 2555912 | tf_op jit(solution)/shard_map/ppermute | solution.py:933
  108.9 39.2 %collective-permute-start.29 = (bf16[256,1664]{1,0:T(8,128)(2,1)S(1)}, bf16[256,1664]{1,0:T(8,128)(2,1)}, u32[]{:S(2)}, u32[]{:S(2)}) collective-permute-start(bf16[256,1664]{1,0:T(8,128)(2,1)S(1)} %bitcast.57), channel_id=1, source_target_pairs={{0,2},{1,3},{2,0},{3,1},{4,6},{5,7},{6,4},{7,5},{8,10},{9,11},{10,... | collective-permute-start | bytes 2555912 | tf_op jit(solution)/shard_map/ppermute | solution.py:933
  110.4 37.7 %collective-permute-start.30 = (bf16[256,1664]{1,0:T(8,128)(2,1)S(1)}, bf16[256,1664]{1,0:T(8,128)(2,1)}, u32[]{:S(2)}, u32[]{:S(2)}) collective-permute-start(bf16[256,1664]{1,0:T(8,128)(2,1)S(1)} %bitcast.58), channel_id=1, source_target_pairs={{0,3},{1,2},{2,1},{3,0},{4,7},{5,6},{6,5},{7,4},{8,11},{9,10},{10,... | collective-permute-start | bytes 2555912 | tf_op jit(solution)/shard_map/ppermute | solution.py:933
  154.0 153.6 %reduce-scatter.4.cloned.1.call-start = ((), (), s32[]{:S(2)}) async-start(), calls=%async_computation.7 | async-start | bytes 5308416 | tf_op jit(solution)/shard_map/reduce_scatter | solution.py:1177
  154.6 36.4 %collective-permute-start.31 = (bf16[256,1536]{1,0:T(8,128)(2,1)S(1)}, bf16[256,1536]{1,0:T(8,128)(2,1)S(1)}, u32[]{:S(2)}, u32[]{:S(2)}) collective-permute-start(bf16[256,1536]{1,0:T(8,128)(2,1)S(1)} %copy-done.19), channel_id=1, source_target_pairs={{0,4},{4,0},{8,12},{12,8},{16,20},{20,16},{24,28},{28,24},{1,5},{5... | collective-permute-start | bytes 2359304 | tf_op jit(solution)/shard_map/ppermute | solution.py:938
  190.1 21.9 %collective-permute-start.41 = (bf16[128,1536]{1,0:T(8,128)(2,1)}, bf16[128,1536]{1,0:T(8,128)(2,1)}, u32[]{:S(2)}, u32[]{:S(2)}) collective-permute-start(bf16[128,1536]{1,0:T(8,128)(2,1)} %get-tuple-element.177.refs_0_.h2_ref), channel_id=1, source_target_pairs={{0,2},{1,3},{2,0},{3,1},{4,6},{5,7},{6,4},{7,5},{8,10},{9,11},{10,... | collective-permute-start | bytes 1179656 | tf_op jit(solution)/shard_map/ppermute | solution.py:933
  208.5 22.6 %collective-permute-start.37 = (bf16[128,1664]{1,0:T(8,128)(2,1)}, bf16[128,1664]{1,0:T(8,128)(2,1)S(1)}, u32[]{:S(2)}, u32[]{:S(2)}) collective-permute-start(bf16[128,1664]{1,0:T(8,128)(2,1)} %get-tuple-element.170), channel_id=1, source_target_pairs={{0,1},{1,0},{2,3},{3,2},{4,5},{5,4},{6,7},{7,6},{8,9},{9,8},{10,11... | collective-permute-start | bytes 1277960 | tf_op jit(solution)/shard_map/ppermute | solution.py:933
  209.7 22.8 %collective-permute-start.38 = (bf16[128,1664]{1,0:T(8,128)(2,1)}, bf16[128,1664]{1,0:T(8,128)(2,1)S(1)}, u32[]{:S(2)}, u32[]{:S(2)}) collective-permute-start(bf16[128,1664]{1,0:T(8,128)(2,1)} %get-tuple-element.171), channel_id=1, source_target_pairs={{0,2},{1,3},{2,0},{3,1},{4,6},{5,7},{6,4},{7,5},{8,10},{9,11},{10,... | collective-permute-start | bytes 1277960 | tf_op jit(solution)/shard_map/ppermute | solution.py:933
  210.6 22.0 %collective-permute-start.39 = (bf16[128,1664]{1,0:T(8,128)(2,1)}, bf16[128,1664]{1,0:T(8,128)(2,1)S(1)}, u32[]{:S(2)}, u32[]{:S(2)}) collective-permute-start(bf16[128,1664]{1,0:T(8,128)(2,1)} %get-tuple-element.172), channel_id=1, source_target_pairs={{0,3},{1,2},{2,1},{3,0},{4,7},{5,6},{6,5},{7,4},{8,11},{9,10},{10,... | collective-permute-start | bytes 1277960 | tf_op jit(solution)/shard_map/ppermute | solution.py:933
  251.3 118.5 %reduce-scatter.6.cloned.1.call-start = ((), (), s32[]{:S(2)}) async-start(), calls=%async_computation.8 | async-start | bytes 4718592 | tf_op jit(solution)/shard_map/reduce_scatter | solution.py:1178
  261.3 24.0 %collective-permute-start.43 = (bf16[256,1536]{1,0:T(8,128)(2,1)}, bf16[256,1536]{1,0:T(8,128)(2,1)S(1)}, u32[]{:S(2)}, u32[]{:S(2)}) collective-permute-start(bf16[256,1536]{1,0:T(8,128)(2,1)} %get-tuple-element.190), channel_id=1, source_target_pairs={{0,1},{1,0},{2,3},{3,2},{4,5},{5,4},{6,7},{7,6},{8,9},{9,8},{10,11... | collective-permute-start | bytes 2359304 | tf_op jit(solution)/shard_map/ppermute | solution.py:933
  262.8 22.5 %collective-permute-start.44 = (bf16[256,1536]{1,0:T(8,128)(2,1)}, bf16[256,1536]{1,0:T(8,128)(2,1)S(1)}, u32[]{:S(2)}, u32[]{:S(2)}) collective-permute-start(bf16[256,1536]{1,0:T(8,128)(2,1)} %get-tuple-element.191), channel_id=1, source_target_pairs={{0,2},{1,3},{2,0},{3,1},{4,6},{5,7},{6,4},{7,5},{8,10},{9,11},{10,... | collective-permute-start | bytes 2359304 | tf_op jit(solution)/shard_map/ppermute | solution.py:933
  307.7 172.0 %reduce-scatter.8.cloned.1.call-start = ((), (), s32[]{:S(2)}) async-start(), calls=%async_computation.9 | async-start | bytes 5308416 | tf_op jit(solution)/shard_map/reduce_scatter | solution.py:1205
  321.6 28.4 %collective-permute-start.54 = (bf16[96,48,128]{2,1,0:T(8,128)(2,1)}, bf16[96,48,128]{2,1,0:T(8,128)(2,1)}, u32[]{:S(2)}, u32[]{:S(2)}) collective-permute-start(bf16[96,48,128]{2,1,0:T(8,128)(2,1)} %get-tuple-element.218), channel_id=1, source_target_pairs={{0,2},{1,3},{2,0},{3,1},{4,6},{5,7},{6,4},{7,5},{8,10},{9,11},{10,... | collective-permute-start | bytes 3538952 | tf_op jit(solution)/shard_map/ppermute | solution.py:933
  322.6 29.8 %collective-permute-start.52 = (bf16[96,48,128]{2,1,0:T(8,128)(2,1)}, bf16[96,48,128]{2,1,0:T(8,128)(2,1)}, u32[]{:S(2)}, u32[]{:S(2)}) collective-permute-start(bf16[96,48,128]{2,1,0:T(8,128)(2,1)} %get-tuple-element.212), channel_id=1, source_target_pairs={{0,1},{1,0},{2,3},{3,2},{4,5},{5,4},{6,7},{7,6},{8,9},{9,8},{10,11... | collective-permute-start | bytes 3538952 | tf_op jit(solution)/shard_map/ppermute | solution.py:933
  372.0 43.1 %collective-permute-start.59 = (bf16[96,1536]{1,0:T(8,128)(2,1)S(1)}, bf16[96,1536]{1,0:T(8,128)(2,1)S(1)}, u32[]{:S(2)}, u32[]{:S(2)}) collective-permute-start(bf16[96,1536]{1,0:T(8,128)(2,1)S(1)} %get-tuple-element.270), channel_id=1, source_target_pairs={{0,16},{4,20},{8,24},{12,28},{16,0},{20,4},{24,8},{28,12},{1,17},{... | collective-permute-start | bytes 884744 | tf_op jit(solution)/shard_map/ppermute | solution.py:943
  372.2 43.0 %collective-permute-start.60 = (bf16[96,1536]{1,0:T(8,128)(2,1)S(1)}, bf16[96,1536]{1,0:T(8,128)(2,1)S(1)}, u32[]{:S(2)}, u32[]{:S(2)}) collective-permute-start(bf16[96,1536]{1,0:T(8,128)(2,1)S(1)} %get-tuple-element.269), channel_id=1, source_target_pairs={{0,8},{4,12},{8,16},{12,20},{16,24},{20,28},{24,0},{28,4},{1,9},{5... | collective-permute-start | bytes 884744 | tf_op jit(solution)/shard_map/ppermute | solution.py:943
  379.3 44.1 %collective-permute-start.62 = (bf16[32,48,128]{2,1,0:T(8,128)(2,1)}, bf16[32,48,128]{2,1,0:T(8,128)(2,1)S(1)}, u32[]{:S(2)}, u32[]{:S(2)}) collective-permute-start(bf16[32,48,128]{2,1,0:T(8,128)(2,1)} %get-tuple-element.232), channel_id=1, source_target_pairs={{0,2},{1,3},{2,0},{3,1},{4,6},{5,7},{6,4},{7,5},{8,10},{9,11},{10,... | collective-permute-start | bytes 1179656 | tf_op jit(solution)/shard_map/ppermute | solution.py:933
  380.1 43.4 %collective-permute-start.57 = (bf16[32,48,128]{2,1,0:T(8,128)(2,1)}, bf16[32,48,128]{2,1,0:T(8,128)(2,1)S(1)}, u32[]{:S(2)}, u32[]{:S(2)}) collective-permute-start(bf16[32,48,128]{2,1,0:T(8,128)(2,1)} %get-tuple-element.225), channel_id=1, source_target_pairs={{0,1},{1,0},{2,3},{3,2},{4,5},{5,4},{6,7},{7,6},{8,9},{9,8},{10,11... | collective-permute-start | bytes 1179656 | tf_op jit(solution)/shard_map/ppermute | solution.py:933
  451.2 28.1 %all-to-all-start = ((bf16[32,2,7680]{2,1,0:T(2,128)(2,1)}), bf16[32,2,7680]{2,1,0:T(2,128)(2,1)S(1)}, u32[]{:S(2)}, u32[]{:S(2)}) async-start(bf16[32,2,7680]{2,1,0:T(2,128)(2,1)} %all_to_all.8), calls=%async_computation.2 | async-start | bytes 1966080 | tf_op jit(solution)/shard_map/all_to_all | solution.py:1230
  453.9 50.1 %collective-permute-start.64 = (bf16[256,1536]{1,0:T(8,128)(2,1)}, bf16[256,1536]{1,0:T(8,128)(2,1)}, u32[]{:S(2)}, u32[]{:S(2)}) collective-permute-start(bf16[256,1536]{1,0:T(8,128)(2,1)} %get-tuple-element.234), channel_id=1, source_target_pairs={{0,3},{1,2},{2,1},{3,0},{4,7},{5,6},{6,5},{7,4},{8,11},{9,10},{10,... | collective-permute-start | bytes 2359304 | tf_op jit(solution)/shard_map/ppermute | solution.py:933
  (126 other events, 1373.6 us)
Sparse Core Ops, SparseCore 0:
  35.9 71.4 all-gather.3
  109.0 44.9 all-gather.5
  156.2 30.3 all-gather.7
  250.7 52.7 reduce-scatter.3
  307.8 47.4 reduce-scatter.5
  369.9 72.1 reduce-scatter.7

commit v11 on v10

--- a/solution.py
+++ b/solution.py
@@ -14,7 +14,7 @@
 BR = 192
 BC = 256
 LANES = 128
-UPPER = 144
+UPPER = 128
 
 norm_eps = 1e-06
 beta_one = 0.9
@@ -541,14 +541,15 @@
 
 
 def pieces_kernel(members, counts, cols, turned_first, me_ref, *refs):
-    row_groups = 8
     lists = []
     for left_count, right_count in counts:
         lists.append((refs[:left_count], refs[left_count : left_count + right_count]))
         refs = refs[left_count + right_count :]
+    stat_refs = refs[: len(refs) - 8] if turned_first else refs[: len(refs) - 10]
+    refs = refs[len(stat_refs) :]
     outs, refs = refs[:4], refs[4:]
     extra = refs[0] if not turned_first else None
-    turned, rights, stage, sems = refs[0 if turned_first else 1 :]
+    turned, rights, stage, sems = refs[0 if turned_first else 1 :][:4]
     ctx, shard = me_ref[0], me_ref[1]
     core = lax.rem(ctx, 2)
     total = turned.shape[2]
@@ -580,7 +581,24 @@
         extra[...] = turned[0]
     all_cols = sum(cols)
     half_blocks = row_groups // 2 * all_cols
+    counts = [half_blocks + (1 if stat_refs else 0), half_blocks]
     span = BR // members
+    if stat_refs:
+        block = refs[-1]
+        block[...] = jnp.zeros_like(block)
+        up = stat_refs[0].shape[0] - 8
+        for r, row in enumerate(list(range(members)) + [up]):
+            total_row = sum(ref[row : row + 1, :] for ref in stat_refs)
+            for t in range(total_row.shape[1] // BC):
+                place = r * (total_row.shape[1] // BC) + t
+                block[place : place + 1, :] = total_row[:, t * BC : (t + 1) * BC]
+        lane = pl.multiple_of(core * LANES, LANES)
+        for out, hops in zip(outs[:2], xor_plan(members, 1)):
+            for place, hop in enumerate(hops):
+                down = pl.multiple_of(jnp.bitwise_xor(shard, hop) * span, 8)
+                out[place * counts[0] + half_blocks] = block[
+                    pl.ds(down, span), pl.ds(lane, LANES)
+                ].astype(low_type)
     base = 0
     for g in range(len(lists)):
         wide_cols = cols[g] * LANES
@@ -597,13 +615,13 @@
                 for place, hop in enumerate(hops):
                     down = pl.multiple_of(jnp.bitwise_xor(shard, hop) * span, 16 if span % 16 == 0 else 8)
                     for b in range(cols[g]):
-                        out[place * half_blocks + first + b] = stage[
+                        out[place * counts[half] + first + b] = stage[
                             a % 2, pl.ds(down, span), b * LANES : (b + 1) * LANES
                         ].astype(low_type)
         base += cols[g]
 
 
-def gradient_pieces(members, me, groups, cols, turned_first):
+def gradient_pieces(members, me, groups, cols, turned_first, stats):
     counts = tuple((len(left), len(right)) for left, right in groups)
     flat = [part for left, right in groups for part in left + right]
     total = sum(part.shape[0] for part in groups[0][1])
@@ -614,8 +632,9 @@
     stage_type = jnp.float32 if span % 16 else low_type
     outs = []
     for half in range(2):
+        count = half_blocks + (1 if stats and half == 0 else 0)
         for hops in xor_plan(members, 1 - half):
-            outs.append(shaped((len(hops) * half_blocks, span, LANES), low_type))
+            outs.append(shaped((len(hops) * count, span, LANES), low_type))
     out_specs = [in_vmem] * 4
     if not turned_first:
         outs.append(shaped((width, total), low_type))
@@ -623,6 +642,7 @@
     in_specs = [in_smem]
     for left, right in groups:
         in_specs += [in_vmem] * len(left) + [in_any] * len(right)
+    in_specs += [in_vmem] * len(stats)
     return call(
         functools.partial(pieces_kernel, members, counts, tuple(cols), turned_first),
         tuple(outs),
@@ -633,10 +653,11 @@
             pltpu.VMEM((total, sum(cols) * LANES), low_type),
             pltpu.VMEM((2, BR, max(cols) * LANES), stage_type),
             pltpu.SemaphoreType.DMA((len(groups),)),
-        ],
+        ]
+        + ([pltpu.VMEM((BR, BC), jnp.float32)] if stats else []),
         2 * total * width * sum(cols) * LANES,
         16 * MIB,
-    )(me, *flat)
+    )(me, *flat, *stats)
 
 
 def merge_kernel(
@@ -918,11 +939,14 @@
 def piece_places(row_groups, q_groups, kv_groups):
     all_groups = 2 * q_groups + kv_groups
     out_groups = list(range(q_groups)) + list(range(q_groups + kv_groups, all_groups))
-    numbers = [a * all_groups + b for a in range(row_groups) for b in out_groups]
+    half = row_groups // 2
+    numbers = [a * all_groups + b for a in range(half) for b in out_groups] + [None]
+    numbers += [a * all_groups + b for a in range(half, row_groups) for b in out_groups]
     numbers += [a * all_groups + q_groups + b for a in range(row_groups) for b in range(kv_groups)]
-    places = [0] * len(numbers)
+    places = [0] * (len(numbers) - 1)
     for place, number in enumerate(numbers):
-        places[number] = place
+        if number is not None:
+            places[number] = place
     return places
 
 
@@ -1178,12 +1202,14 @@
     dkv = lax.psum_scatter(
         after(dkv_terms, expert_sums[0]), "ctx", scatter_dimension=0, tiled=True
     )
+    stat_sum = add_wide(stats)
     early = gradient_pieces(
         shard_count,
         after(me, dkv_terms),
         [([h1, h1_other], dqs + dq_others), (das + da_others, obs + ob_others)],
         [q_groups, q_groups],
         False,
+        [stat_sum, to_ctx(stat_sum, 1)],
     )
     h1_turned = early[4]
     parts_back = query_back(after(w_in, early[0]), dqs)
@@ -1196,29 +1222,31 @@
         [([h1_turned], [dkv, to_ctx(dkv, 1)])],
         [kv_groups],
         True,
+        [],
     )
     input_grad, gain_stat = input_back(
         after(tokens, late[0]), norm_gains, w_in, dxs, parts_back, dkv
     )
     late_rows, late_seen = sum_members(late[:4], (input_grad, early_parts), shard_count)
-    late_term = after(expert_terms[1], dkv)
+    late_term = after(expert_terms[1], dkv, early_seen)
     expert_sums.append(lax.psum_scatter(late_term, "ctx", scatter_dimension=0, tiled=True))
     last_outs = after(list(outs), *late_seen)
     arrived += [to_partner(last_outs[j], j) for j in range(3, shard_count)]
     early_sum = add_wide(early_parts).astype(low_type)
-    late_sum = add_wide(sum_chips(late_rows, chip, chips)).astype(low_type)
+    expert_grad, expert_new, expert_moment_new, expert_second_new = rotate(
+        expert_weight[0], expert_sums, expert_moment[0], expert_second[0], expert_left[0], expert_right[0]
+    )
+    late_parts = after(sum_chips(late_rows, chip, chips), expert_new)
+    late_sum = add_wide(late_parts).astype(low_type)
     all_sums = jnp.concatenate([early_sum, late_sum], axis=0)
     places = jnp.asarray(piece_places(row_groups, q_groups, kv_groups), jnp.int32)[dense_order]
     chosen = (places[:, None] == jnp.arange(all_sums.shape[0])[None, :]).astype(low_type)
     ordered = jnp.dot(chosen, all_sums, preferred_element_type=jnp.float32).astype(low_type)
     devices = ctx_count * shard_count
     piece_width = ordered.shape[1]
-    experts_up = stats[0].shape[0] - 8
-    stat_rows = add_wide(stats)
-    stat_rows = jnp.concatenate(
-        [stat_rows[:shard_count], gain_stat[:1], stat_rows[experts_up : experts_up + 1]], axis=0
-    )
-    stat_parts = stat_rows.astype(low_type).reshape(-1, piece_width)
+    stat_place = row_groups // 2 * 2 * q_groups
+    gain_parts = gain_stat[:1].astype(low_type).reshape(-1, piece_width)
+    stat_parts = jnp.concatenate([early_sum[stat_place : stat_place + 1], gain_parts], axis=0)
     extra = stat_parts.shape[0]
     ordered = jnp.concatenate(
         [
@@ -1228,17 +1256,18 @@
         axis=1,
     ).reshape(devices * 2, (slots + extra) * piece_width // 2)
     ordered = lax.all_to_all(ordered, ("ctx", "shard"), split_axis=0, concat_axis=0, tiled=True)
-    expert_grad, expert_new, expert_moment_new, expert_second_new = rotate(
-        expert_weight[0], expert_sums, expert_moment[0], expert_second[0], expert_left[0], expert_right[0]
-    )
-    ordered = after(ordered, expert_new).reshape(devices, slots + extra, piece_width)
-    stat_rows = jnp.sum(wide(ordered[:, slots:]), axis=0).reshape(shard_count + 2, width)
+    ordered = ordered.reshape(devices, slots + extra, piece_width)
+    span = BR // (shard_count * chips)
+    stat_block = ordered[:, slots].reshape(chips, 2, shard_count, span, LANES)
+    stat_rows = wide(stat_block.transpose(2, 0, 3, 1, 4).reshape(BR * BC)[: (shard_count + 1) * width])
+    stat_rows = stat_rows.reshape(shard_count + 1, width)
+    gain_row = jnp.sum(wide(ordered[:, slots + 1 :]), axis=0).reshape(width)
     ordered = ordered[:, :slots].reshape(
         chips, 2, shard_count, slots, BR // (shard_count * chips), LANES
     )
     dense_sum = ordered.transpose(3, 2, 0, 4, 1, 5).reshape(slots, BR, BC)
     router_grad = stat_rows[:shard_count].T
-    gains_grad = stat_rows[shard_count:]
+    gains_grad = jnp.stack([gain_row, stat_rows[shard_count]])
 
     dense_grad, dense_new, dense_moment_new, dense_second_new = rotate(
         dense_weight, [dense_sum], dense_moment, dense_second, dense_left, dense_right
@@ -1246,7 +1275,7 @@
     outputs = []
     for m in range(micros):
         total = x2s[m]
-        for part in after(arrived, dense_new, expert_new):
+        for part in after(arrived, expert_new):
             total = total + wide(part[m * rows : (m + 1) * rows])
         outputs.append(total)
 

time: 522 us -> 514 us (0.985)
  waiting for transfers between devices: 202 us -> 192 us
    all_to_all x1, waiting for transfers between devices: 22.8 us -> 14.2 us  [shards(): lax.all_to_all(ordered, ('ctx', 'shard'), split_axis=0, concat_axis=0, ti...]
    all_to_all x1, starting transfers between devices: 2.64 us -> 9.44 us  [shards(): lax.all_to_all(ordered, ('ctx', 'shard'), split_axis=0, concat_axis=0, ti...]
    all_gather x1, waiting for transfers between devices: 9.16 us -> 3 us  [shards(): lax.all_gather(expert_low[:, :UPPER], 'ctx', axis=0, tiled=True)]
    ppermute x37, waiting for transfers between devices: 95.9 us -> 101 us  [to_partner(): return lax.ppermute(array, 'shard', [(i, i ^ offset) for i in range(count)])]
  transfers between devices with their start and end apart: 75 -> 76, of which waited for: 35 -> 33; matrix products, arithmetic and copies ran while one was open for 5% -> 4% of each run, Pallas kernels for 38% -> 37%
where the time goes in v11:
time: 514 us; the launch traced here: 508 us
  Pallas kernels  195 us (38%)
  waiting for transfers between devices  192 us (37%)
  starting transfers between devices  68.5 us (13%)
  local copies, waits for them, and re-layouts  21.7 us (4%)
  between operations  16 us (3%)
  other arithmetic  15.1 us (3%)
    ppermute x37, waiting for transfers between devices, to_partner(): return lax.ppermute(array, 'shard', [(i, i ^ offset) for i in range(count)])  101 us
    ppermute x9, waiting for transfers between devices, to_chip(): lax.ppermute(array, 'ctx', [(i, (i + 2 * offset) % count) for i in range(...  59.7 us
    ppermute x37, starting transfers between devices, to_partner(): return lax.ppermute(array, 'shard', [(i, i ^ offset) for i in range(count)])  40.7 us
    pallas_call x2, Pallas kernels, run_expert(): call(functools.partial(expert_kernel, sources, micro), tuple([shaped((row...  32.4 us
    pallas_call x2, Pallas kernels, attend_back(): pl.pallas_call(functools.partial(attend_back_kernel, micro), out_shape=(s...  31 us
    pallas_call x2, Pallas kernels, attend(): call(functools.partial(attend_kernel, micro), (shaped((rows, width), low_...  25.6 us
    pallas_call x2, Pallas kernels, rotate(): pl.pallas_call(rotate_kernel, grid=(count,), out_shape=(shaped(weight.sha...  20.9 us
    pallas_call x1, Pallas kernels, outer_blocks(): call(functools.partial(outer_kernel, groups, cols // BC), (shaped((blocks...  17.9 us
  transfers between devices with their start and end apart: 76, of which 33 were waited for; matrix products, arithmetic and copies ran while one was open for 4% of the time, Pallas kernels for 37%

profile of v11, /device:TPU:0, one launch (start us, length us, event | category | flops | bytes accessed | tf_op | source)
XLA Modules:
  0.0 508.0 jit_solution(14996271678326664689)
XLA Ops:
  15.0 7.8 %collective-permute-done.7.refs_11_ = bf16[4,192,256]{2,1,0:T(8,128)(2,1)} collective-permute-done((bf16[4,192,256]{2,1,0:T(8,128)(2,1)S(1)}, bf16[4,192,256]{2,1,0:T(8,128)(2,1)}, u32[]{:S(2)}, u32[]{:S(2)}) %collective-permute-start.7) | collective-permute-done | bytes 393248 | tf_op jit(solution)/shard_map/ppermute | solution.py:967
  24.6 7.1 %collective-permute-done.3.refs_7_ = bf16[4,192,256]{2,1,0:T(8,128)(2,1)S(1)} collective-permute-done((bf16[4,192,256]{2,1,0:T(8,128)(2,1)S(1)}, bf16[4,192,256]{2,1,0:T(8,128)(2,1)S(1)}, u32[]{:S(2)}, u32[]{:S(2)}) %collective-permute-start.3) | collective-permute-done | bytes 393248 | tf_op jit(solution)/shard_map/ppermute | solution.py:957
  43.6 7.3 %collective-permute-done.18 = bf16[4,192,256]{2,1,0:T(8,128)(2,1)S(1)} collective-permute-done((bf16[4,192,256]{2,1,0:T(8,128)(2,1)S(1)}, bf16[4,192,256]{2,1,0:T(8,128)(2,1)S(1)}, u32[]{:S(2)}, u32[]{:S(2)}) %collective-permute-start.18) | collective-permute-done | bytes 393248 | tf_op jit(solution)/shard_map/ppermute | solution.py:967
  56.1 12.6 %collective-permute-done.22.refs_25_ = bf16[8,192,256]{2,1,0:T(8,128)(2,1)S(1)} collective-permute-done((bf16[8,192,256]{2,1,0:T(8,128)(2,1)S(1)}, bf16[8,192,256]{2,1,0:T(8,128)(2,1)S(1)}, u32[]{:S(2)}, u32[]{:S(2)}) %collective-permute-start.22) | collective-permute-done | bytes 786464 | tf_op jit(solution)/shard_map/ppermute | solution.py:957
  85.5 12.3 %shard_map.358 = (bf16[256,1536]{1,0:T(8,128)(2,1)}, bf16[256,1024]{1,0:T(8,128)(2,1)}, bf16[1536,2560]{1,0:T(8,128)(2,1)}, bf16[1536,1536]{1,0:T(8,128)(2,1)}) custom-call(s32[128]{0:T(128)} %order_ref.1, s32[2]{0:T(128)} %pad_add_fusion.me_ref, f32[128,1536]{1,0:T(8,128)} %get-tuple-element.273.refs_0_.x_ref, ...), custom_call_target="tpu_custom_call" | custom-call | flops 805306368 | bytes 25165824 | tf_op jit(solution)/shard_map/pallas_call | solution.py:192
  112.7 11.0 %collective-permute-done.28.refs_5_ = bf16[256,1664]{1,0:T(8,128)(2,1)} collective-permute-done((bf16[256,1664]{1,0:T(8,128)(2,1)S(1)}, bf16[256,1664]{1,0:T(8,128)(2,1)}, u32[]{:S(2)}, u32[]{:S(2)}) %collective-permute-start.28) | collective-permute-done | bytes 852000 | tf_op jit(solution)/shard_map/ppermute | solution.py:957
  123.7 18.3 %collective-permute-done.29.refs_6_ = bf16[256,1664]{1,0:T(8,128)(2,1)} collective-permute-done((bf16[256,1664]{1,0:T(8,128)(2,1)S(1)}, bf16[256,1664]{1,0:T(8,128)(2,1)}, u32[]{:S(2)}, u32[]{:S(2)}) %collective-permute-start.29) | collective-permute-done | bytes 852000 | tf_op jit(solution)/shard_map/ppermute | solution.py:957
  148.0 12.8 %shard_map.360 = (bf16[128,1536]{1,0:T(8,128)(2,1)}, f32[384,128]{1,0:T(8,128)}, f32[128,1536]{1,0:T(8,128)}, bf16[128,1536]{1,0:T(8,128)(2,1)}) custom-call(bf16[128,1536]{1,0:T(8,128)(2,1)} %get-tuple-element.158.q_ref, s32[128,1]{1,0:T(8,128)} %constant_dynamic-slice_fusion.4.rpos_ref, s32[1,1024]{1,0:T(1,128)} %bitcast.72, ...), custom_call_target="tpu_custom_call" | custom-call | flops 3221225472 | bytes 8388608 | tf_op jit(solution)/shard_map/pallas_call | solution.py:306
  164.3 12.8 %shard_map.361 = (bf16[128,1536]{1,0:T(8,128)(2,1)}, f32[384,128]{1,0:T(8,128)}, f32[128,1536]{1,0:T(8,128)}, bf16[128,1536]{1,0:T(8,128)(2,1)}) custom-call(bf16[128,1536]{1,0:T(8,128)(2,1)} %get-tuple-element.166.q_ref, s32[128,1]{1,0:T(8,128)} %constant_dynamic-slice_fusion.4.rpos_ref, s32[1,1024]{1,0:T(1,128)} %bitcast.73, ...), custom_call_target="tpu_custom_call" | custom-call | flops 3221225472 | bytes 8388608 | tf_op jit(solution)/shard_map/pallas_call | solution.py:306
  187.1 16.0 %shard_map.362 = (bf16[128,1664]{1,0:T(8,128)(2,1)}, bf16[128,1664]{1,0:T(8,128)(2,1)}, bf16[128,1664]{1,0:T(8,128)(2,1)}, bf16[128,1664]{1,0:T(8,128)(2,1)}, bf...) custom-call(s32[96]{0:T(128)} %select_reduce_fusion.order_ref, ...), custom_call_target="tpu_custom_call" | custom-call | flops 8053063680 | bytes 20971520 | tf_op jit(solution)/shard_map/pallas_call | solution.py:406
  207.4 16.4 %shard_map.363 = (bf16[128,1664]{1,0:T(8,128)(2,1)}, bf16[128,1664]{1,0:T(8,128)(2,1)}, bf16[128,1664]{1,0:T(8,128)(2,1)}, bf16[128,1664]{1,0:T(8,128)(2,1)}, bf...) custom-call(s32[96]{0:T(128)} %select_reduce_fusion.order_ref, ...), custom_call_target="tpu_custom_call" | custom-call | flops 8053063680 | bytes 20971520 | tf_op jit(solution)/shard_map/pallas_call | solution.py:406
  227.4 17.9 %shard_map.364 = (bf16[96,192,128]{2,1,0:T(8,128)(2,1)}, bf16[96,192,128]{2,1,0:T(8,128)(2,1)}) custom-call(s32[96]{0:T(128)} %select_reduce_fusion.order_ref, bf16[512,1536]{1,0:T(8,128)(2,1)} %get-tuple-element.177.refs_0_, bf16[512,1536]{1,0:T(8,128)(2,1)} %get-tuple-element.181.refs_1_, bf16[512,1664]{1,0:T(8,128)(2,1)} %get-tuple-element.182.refs_2_, ...), custom_call_target="tpu_custom_call" | custom-call | flops 9663676416 | bytes 22282240 | tf_op jit(solution)/shard_map/pallas_call | solution.py:521
  247.4 9.1 %shard_map.365 = (bf16[256,1536]{1,0:T(8,128)(2,1)}, bf16[256,1536]{1,0:T(8,128)(2,1)}, bf16[256,1536]{1,0:T(8,128)(2,1)}, bf16[256,1536]{1,0:T(8,128)(2,1)}) custom-call(s32[96]{0:T(128)} %select_reduce_fusion.order_ref, bf16[96,128,256]{2,1,0:T(8,128)(2,1)} %all-gather.4.cloned.1.call-done.refs_8_.upper_ref, ...), custom_call_target="tpu_custom_call" | custom-call | flops 3221225472 | bytes 8388608 | tf_op jit(solution)/shard_map/pallas_call | solution.py:460
  265.5 15.5 %shard_map.367 = (bf16[128,1536]{1,0:T(8,128)(2,1)}, bf16[2048,1024]{1,0:T(8,128)(2,1)}) custom-call(bf16[128,1536]{1,0:T(8,128)(2,1)} %get-tuple-element.158.q_ref, s32[128,1]{1,0:T(8,128)} %constant_dynamic-slice_fusion.4.rpos_ref, s32[1,1024]{1,0:T(1,128)} %bitcast.74, bf16[128,1536]{1,0:T(8,128)(2,1)} %get-tuple-element.165.ob_ref.refs_10_, ...), custom_call_target="tpu_custom_call" | custom-call | flops 8053063680 | bytes 8388608 | tf_op jit(solution)/shard_map/pallas_call | solution.py:789
  287.7 15.6 %shard_map.369 = (bf16[128,1536]{1,0:T(8,128)(2,1)}, bf16[2048,1024]{1,0:T(8,128)(2,1)}) custom-call(bf16[128,1536]{1,0:T(8,128)(2,1)} %get-tuple-element.166.q_ref, s32[128,1]{1,0:T(8,128)} %constant_dynamic-slice_fusion.4.rpos_ref, s32[1,1024]{1,0:T(1,128)} %bitcast.75, ...), custom_call_target="tpu_custom_call", output_to_operand_aliasing={{1}: (7, {})} | custom-call | flops 8053063680 | bytes 8388608 | tf_op jit(solution)/shard_map/pallas_call | solution.py:789
  309.0 9.3 %shard_map.370 = (bf16[98,48,128]{2,1,0:T(8,128)(2,1)}, bf16[98,48,128]{2,1,0:T(8,128)(2,1)}, bf16[96,48,128]{2,1,0:T(8,128)(2,1)}, bf16[96,48,128]{2,1,0:T(8,128)(2,1)}, bf16[1536,512]{1,0:T(8,128)(2,1)}) custom-call(s32[2]{0:T(128)} %pad_add_fusion.me_ref, bf16[256,1536]{1,0:T(8,128)(2,1)} %get-tuple-element.154.h_ref.refs_0_, ...), custom_call_target="tpu_custom_call" | custom-call | flops 2415919104 | bytes 16777216 | tf_op jit(solution)/shard_map/pallas_call | solution.py:646
  325.4 21.4 %collective-permute-done.55 = bf16[96,48,128]{2,1,0:T(8,128)(2,1)} collective-permute-done((bf16[96,48,128]{2,1,0:T(8,128)(2,1)}, bf16[96,48,128]{2,1,0:T(8,128)(2,1)}, u32[]{:S(2)}, u32[]{:S(2)}) %collective-permute-start.55) | collective-permute-done | bytes 1179680 | tf_op jit(solution)/shard_map/ppermute | solution.py:957
  350.3 13.4 %collective-permute-done.56 = bf16[48,48,128]{2,1,0:T(8,128)(2,1)} collective-permute-done((bf16[48,48,128]{2,1,0:T(8,128)(2,1)S(1)}, bf16[48,48,128]{2,1,0:T(8,128)(2,1)}, u32[]{:S(2)}, u32[]{:S(2)}) %collective-permute-start.56) | collective-permute-done | bytes 589856 | tf_op jit(solution)/shard_map/ppermute | solution.py:957
  377.0 7.6 %collective-permute-done.59 = bf16[97,1536]{1,0:T(8,128)(2,1)S(1)} collective-permute-done((bf16[97,1536]{1,0:T(8,128)(2,1)S(1)}, bf16[97,1536]{1,0:T(8,128)(2,1)S(1)}, u32[]{:S(2)}, u32[]{:S(2)}) %collective-permute-start.59) | collective-permute-done | bytes 298016 | tf_op jit(solution)/shard_map/ppermute | solution.py:967
  384.7 33.7 %collective-permute-done.60 = bf16[97,1536]{1,0:T(8,128)(2,1)S(1)} collective-permute-done((bf16[97,1536]{1,0:T(8,128)(2,1)S(1)}, bf16[97,1536]{1,0:T(8,128)(2,1)S(1)}, u32[]{:S(2)}, u32[]{:S(2)}) %collective-permute-start.60) | collective-permute-done | bytes 298016 | tf_op jit(solution)/shard_map/ppermute | solution.py:967
  419.6 7.1 %shard_map.373 = (f32[2,128,1536]{2,1,0:T(8,128)}, f32[8,1536]{1,0:T(8,128)}) custom-call(f32[2,128,1536]{2,1,0:T(8,128)} %x_ref, f32[2,1536]{1,0:T(2,128)} %gain_ref.9, bf16[1536,2560]{1,0:T(8,128)(2,1)} %get-tuple-element.218.w_ref, f32[128,1536]{1,0:T(8,128)} %get-tuple-element.232.refs_0_, f32[128,1536]{1,0:T(8,128)} %get-tuple-element.233.refs_1_, ...), custom_call_target="tpu_custom_call" | custom-call | flops 805306368 | bytes 14680064 | tf_op jit(solution)/shard_map/pallas_call | solution.py:873
  445.6 15.1 %shard_map.374 = (f32[12,192,256]{2,1,0:T(8,128)}, f32[12,192,256]{2,1,0:T(8,128)}, f32[12,192,256]{2,1,0:T(8,128)}, f32[12,192,256]{2,1,0:T(8,128)}) custom-call(f32[12,192,256]{2,1,0:T(8,128)} %bitcast.51, f32[12,192,256]{2,1,0:T(8,128)} %bitcast.59, f32[12,192,256]{2,1,0:T(8,128)} %bitcast.60, f32[12,192,192]{2,1,0:T(8,128)} %bitcast.61, ...), custom_call_target="tpu_custom_call" | custom-call | flops 1056964608 | bytes 25165824 | tf_op jit(solution)/shard_map/pallas_call | solution.py:912
  463.0 9.4 %all-to-all-start = ((bf16[32,2,4608]{2,1,0:T(2,128)(2,1)}), bf16[32,2,4608]{2,1,0:T(2,128)(2,1)S(1)}, u32[]{:S(2)}, u32[]{:S(2)}) async-start(bf16[32,2,4608]{2,1,0:T(2,128)(2,1)} %all_to_all.6), calls=%async_computation.3 | async-start | bytes 1179648 | tf_op jit(solution)/shard_map/all_to_all | solution.py:1258
  475.8 14.2 %all-to-all-done = bf16[32,2,4608]{2,1,0:T(2,128)(2,1)S(1)} async-done(((bf16[32,2,4608]{2,1,0:T(2,128)(2,1)}), bf16[32,2,4608]{2,1,0:T(2,128)(2,1)S(1)}, u32[]{:S(2)}, u32[]{:S(2)}) %all-to-all-start) | async-done | bytes 589856 | tf_op jit(solution)/shard_map/all_to_all | solution.py:1258
  (382 shorter events, 168.5 us)
Async XLA Ops:
  7.2 93.6 %all-gather.4.cloned.1.call-start = ((), (), s32[]{:S(2)}) async-start(), calls=%async_computation.4 | async-start | bytes 7077888 | tf_op jit(solution)/shard_map/all_gather | solution.py:1121
  36.0 111.3 %all-gather.6.cloned.1.call-start = ((), (), s32[]{:S(2)}) async-start(), calls=%async_computation.5 | async-start | bytes 4718592 | tf_op jit(solution)/shard_map/all_gather | solution.py:1144
  100.8 86.3 %all-gather.8.cloned.1.call-start = ((), (), s32[]{:S(2)}) async-start(), calls=%async_computation.6 | async-start | bytes 3538944 | tf_op jit(solution)/shard_map/all_gather | solution.py:1146
  102.8 39.2 %collective-permute-start.29 = (bf16[256,1664]{1,0:T(8,128)(2,1)S(1)}, bf16[256,1664]{1,0:T(8,128)(2,1)}, u32[]{:S(2)}, u32[]{:S(2)}) collective-permute-start(bf16[256,1664]{1,0:T(8,128)(2,1)S(1)} %bitcast.64), channel_id=1, source_target_pairs={{0,2},{1,3},{2,0},{3,1},{4,6},{5,7},{6,4},{7,5},{8,10},{9,11},{10,... | collective-permute-start | bytes 2555912 | tf_op jit(solution)/shard_map/ppermute | solution.py:957
  104.3 37.7 %collective-permute-start.30 = (bf16[256,1664]{1,0:T(8,128)(2,1)S(1)}, bf16[256,1664]{1,0:T(8,128)(2,1)}, u32[]{:S(2)}, u32[]{:S(2)}) collective-permute-start(bf16[256,1664]{1,0:T(8,128)(2,1)S(1)} %bitcast.65), channel_id=1, source_target_pairs={{0,3},{1,2},{2,1},{3,0},{4,7},{5,6},{6,5},{7,4},{8,11},{9,10},{10,... | collective-permute-start | bytes 2555912 | tf_op jit(solution)/shard_map/ppermute | solution.py:957
  147.4 155.9 %reduce-scatter.4.cloned.1.call-start = ((), (), s32[]{:S(2)}) async-start(), calls=%async_computation.7 | async-start | bytes 5308416 | tf_op jit(solution)/shard_map/reduce_scatter | solution.py:1201
  147.7 36.6 %collective-permute-start.31 = (bf16[256,1536]{1,0:T(8,128)(2,1)S(1)}, bf16[256,1536]{1,0:T(8,128)(2,1)S(1)}, u32[]{:S(2)}, u32[]{:S(2)}) collective-permute-start(bf16[256,1536]{1,0:T(8,128)(2,1)S(1)} %copy-done.23), channel_id=1, source_target_pairs={{0,4},{4,0},{8,12},{12,8},{16,20},{20,16},{24,28},{28,24},{1,5},{5... | collective-permute-start | bytes 2359304 | tf_op jit(solution)/shard_map/ppermute | solution.py:962
  182.2 23.9 %collective-permute-start.40 = (bf16[128,1536]{1,0:T(8,128)(2,1)}, bf16[128,1536]{1,0:T(8,128)(2,1)}, u32[]{:S(2)}, u32[]{:S(2)}) collective-permute-start(bf16[128,1536]{1,0:T(8,128)(2,1)} %get-tuple-element.180.refs_0_.h2_ref), channel_id=1, source_target_pairs={{0,1},{1,0},{2,3},{3,2},{4,5},{5,4},{6,7},{7,6},{8,9},{9,8},{10,11... | collective-permute-start | bytes 1179656 | tf_op jit(solution)/shard_map/ppermute | solution.py:957
  183.4 23.2 %collective-permute-start.41 = (bf16[128,1536]{1,0:T(8,128)(2,1)}, bf16[128,1536]{1,0:T(8,128)(2,1)}, u32[]{:S(2)}, u32[]{:S(2)}) collective-permute-start(bf16[128,1536]{1,0:T(8,128)(2,1)} %get-tuple-element.180.refs_0_.h2_ref), channel_id=1, source_target_pairs={{0,2},{1,3},{2,0},{3,1},{4,6},{5,7},{6,4},{7,5},{8,10},{9,11},{10,... | collective-permute-start | bytes 1179656 | tf_op jit(solution)/shard_map/ppermute | solution.py:957
  203.1 23.7 %collective-permute-start.37 = (bf16[128,1664]{1,0:T(8,128)(2,1)}, bf16[128,1664]{1,0:T(8,128)(2,1)S(1)}, u32[]{:S(2)}, u32[]{:S(2)}) collective-permute-start(bf16[128,1664]{1,0:T(8,128)(2,1)} %get-tuple-element.173), channel_id=1, source_target_pairs={{0,1},{1,0},{2,3},{3,2},{4,5},{5,4},{6,7},{7,6},{8,9},{9,8},{10,11... | collective-permute-start | bytes 1277960 | tf_op jit(solution)/shard_map/ppermute | solution.py:957
  204.6 22.8 %collective-permute-start.38 = (bf16[128,1664]{1,0:T(8,128)(2,1)}, bf16[128,1664]{1,0:T(8,128)(2,1)S(1)}, u32[]{:S(2)}, u32[]{:S(2)}) collective-permute-start(bf16[128,1664]{1,0:T(8,128)(2,1)} %get-tuple-element.174), channel_id=1, source_target_pairs={{0,2},{1,3},{2,0},{3,1},{4,6},{5,7},{6,4},{7,5},{8,10},{9,11},{10,... | collective-permute-start | bytes 1277960 | tf_op jit(solution)/shard_map/ppermute | solution.py:957
  246.1 117.5 %reduce-scatter.6.cloned.1.call-start = ((), (), s32[]{:S(2)}) async-start(), calls=%async_computation.8 | async-start | bytes 4718592 | tf_op jit(solution)/shard_map/reduce_scatter | solution.py:1202
  256.5 24.5 %collective-permute-start.43 = (bf16[256,1536]{1,0:T(8,128)(2,1)}, bf16[256,1536]{1,0:T(8,128)(2,1)S(1)}, u32[]{:S(2)}, u32[]{:S(2)}) collective-permute-start(bf16[256,1536]{1,0:T(8,128)(2,1)} %get-tuple-element.193), channel_id=1, source_target_pairs={{0,1},{1,0},{2,3},{3,2},{4,5},{5,4},{6,7},{7,6},{8,9},{9,8},{10,11... | collective-permute-start | bytes 2359304 | tf_op jit(solution)/shard_map/ppermute | solution.py:957
  257.9 23.1 %collective-permute-start.44 = (bf16[256,1536]{1,0:T(8,128)(2,1)}, bf16[256,1536]{1,0:T(8,128)(2,1)S(1)}, u32[]{:S(2)}, u32[]{:S(2)}) collective-permute-start(bf16[256,1536]{1,0:T(8,128)(2,1)} %get-tuple-element.194), channel_id=1, source_target_pairs={{0,2},{1,3},{2,0},{3,1},{4,6},{5,7},{6,4},{7,5},{8,10},{9,11},{10,... | collective-permute-start | bytes 2359304 | tf_op jit(solution)/shard_map/ppermute | solution.py:957
  303.4 142.2 %reduce-scatter.8.cloned.1.call-start = ((), (), s32[]{:S(2)}) async-start(), calls=%async_computation.9 | async-start | bytes 5308416 | tf_op jit(solution)/shard_map/reduce_scatter | solution.py:1232
  318.3 28.8 %collective-permute-start.53 = (bf16[98,48,128]{2,1,0:T(8,128)(2,1)}, bf16[98,48,128]{2,1,0:T(8,128)(2,1)S(1)}, u32[]{:S(2)}, u32[]{:S(2)}) collective-permute-start(bf16[98,48,128]{2,1,0:T(8,128)(2,1)} %get-tuple-element.217), channel_id=1, source_target_pairs={{0,1},{1,0},{2,3},{3,2},{4,5},{5,4},{6,7},{7,6},{8,9},{9,8},{10,11... | collective-permute-start | bytes 3612680 | tf_op jit(solution)/shard_map/ppermute | solution.py:957
  318.6 28.2 %collective-permute-start.55 = (bf16[96,48,128]{2,1,0:T(8,128)(2,1)}, bf16[96,48,128]{2,1,0:T(8,128)(2,1)}, u32[]{:S(2)}, u32[]{:S(2)}) collective-permute-start(bf16[96,48,128]{2,1,0:T(8,128)(2,1)} %get-tuple-element.223), channel_id=1, source_target_pairs={{0,2},{1,3},{2,0},{3,1},{4,6},{5,7},{6,4},{7,5},{8,10},{9,11},{10,... | collective-permute-start | bytes 3538952 | tf_op jit(solution)/shard_map/ppermute | solution.py:957
  368.1 50.2 %collective-permute-start.60 = (bf16[97,1536]{1,0:T(8,128)(2,1)S(1)}, bf16[97,1536]{1,0:T(8,128)(2,1)S(1)}, u32[]{:S(2)}, u32[]{:S(2)}) collective-permute-start(bf16[97,1536]{1,0:T(8,128)(2,1)S(1)} %get-tuple-element.275), channel_id=1, source_target_pairs={{0,16},{4,20},{8,24},{12,28},{16,0},{20,4},{24,8},{28,12},{1,17},{... | collective-permute-start | bytes 893960 | tf_op jit(solution)/shard_map/ppermute | solution.py:967
  368.6 49.8 %collective-permute-start.61 = (bf16[97,1536]{1,0:T(8,128)(2,1)S(1)}, bf16[97,1536]{1,0:T(8,128)(2,1)}, u32[]{:S(2)}, u32[]{:S(2)}) collective-permute-start(bf16[97,1536]{1,0:T(8,128)(2,1)S(1)} %get-tuple-element.276), channel_id=1, source_target_pairs={{0,8},{4,12},{8,16},{12,20},{16,24},{20,28},{24,0},{28,4},{1,9},{5... | collective-permute-start | bytes 893960 | tf_op jit(solution)/shard_map/ppermute | solution.py:967
  375.7 51.9 %collective-permute-start.63 = (bf16[32,48,128]{2,1,0:T(8,128)(2,1)}, bf16[32,48,128]{2,1,0:T(8,128)(2,1)S(1)}, u32[]{:S(2)}, u32[]{:S(2)}) collective-permute-start(bf16[32,48,128]{2,1,0:T(8,128)(2,1)} %get-tuple-element.237), channel_id=1, source_target_pairs={{0,2},{1,3},{2,0},{3,1},{4,6},{5,7},{6,4},{7,5},{8,10},{9,11},{10,... | collective-permute-start | bytes 1179656 | tf_op jit(solution)/shard_map/ppermute | solution.py:957
  436.0 24.7 %collective-permute-start.66 = (bf16[32,1536]{1,0:T(8,128)(2,1)S(1)}, bf16[32,1536]{1,0:T(8,128)(2,1)S(1)}, u32[]{:S(2)}, u32[]{:S(2)}) collective-permute-start(bf16[32,1536]{1,0:T(8,128)(2,1)S(1)} %get-tuple-element.279), channel_id=1, source_target_pairs={{0,24},{4,28},{8,0},{12,4},{16,8},{20,12},{24,16},{28,20},{1,25},{... | collective-permute-start | bytes 294920 | tf_op jit(solution)/shard_map/ppermute | solution.py:967
  436.0 24.7 %collective-permute-start.67 = (bf16[32,1536]{1,0:T(8,128)(2,1)S(1)}, bf16[32,1536]{1,0:T(8,128)(2,1)S(1)}, u32[]{:S(2)}, u32[]{:S(2)}) collective-permute-start(bf16[32,1536]{1,0:T(8,128)(2,1)S(1)} %get-tuple-element.278), channel_id=1, source_target_pairs={{0,16},{4,20},{8,24},{12,28},{16,0},{20,4},{24,8},{28,12},{1,17},{... | collective-permute-start | bytes 294920 | tf_op jit(solution)/shard_map/ppermute | solution.py:967
  443.4 29.1 %collective-permute-start.65 = (bf16[256,1536]{1,0:T(8,128)(2,1)}, bf16[256,1536]{1,0:T(8,128)(2,1)}, u32[]{:S(2)}, u32[]{:S(2)}) collective-permute-start(bf16[256,1536]{1,0:T(8,128)(2,1)} %get-tuple-element.239), channel_id=1, source_target_pairs={{0,3},{1,2},{2,1},{3,0},{4,7},{5,6},{6,5},{7,4},{8,11},{9,10},{10,... | collective-permute-start | bytes 2359304 | tf_op jit(solution)/shard_map/ppermute | solution.py:957
  463.0 27.0 %all-to-all-start = ((bf16[32,2,4608]{2,1,0:T(2,128)(2,1)}), bf16[32,2,4608]{2,1,0:T(2,128)(2,1)S(1)}, u32[]{:S(2)}, u32[]{:S(2)}) async-start(bf16[32,2,4608]{2,1,0:T(2,128)(2,1)} %all_to_all.6), calls=%async_computation.3 | async-start | bytes 1179648 | tf_op jit(solution)/shard_map/all_to_all | solution.py:1258
  (130 other events, 1318.0 us)
Sparse Core Ops, SparseCore 0:
  36.2 64.5 all-gather.3
  102.4 44.9 all-gather.5
  149.6 37.4 all-gather.7
  245.8 53.5 reduce-scatter.3
  303.5 46.7 reduce-scatter.5
  363.8 73.5 reduce-scatter.7

commit v12 on v11

--- a/solution.py
+++ b/solution.py
@@ -1224,19 +1224,20 @@
         True,
         [],
     )
+    last_outs = after(list(outs), early_seen)
+    arrived += [to_partner(last_outs[j], j) for j in range(3, shard_count)]
     input_grad, gain_stat = input_back(
-        after(tokens, late[0]), norm_gains, w_in, dxs, parts_back, dkv
-    )
-    late_rows, late_seen = sum_members(late[:4], (input_grad, early_parts), shard_count)
+        after(tokens, late[0], arrived[3:]), norm_gains, w_in, dxs, parts_back, dkv
+    )
+    late_rows, late_seen = sum_members(late[:4], input_grad, shard_count)
     late_term = after(expert_terms[1], dkv, early_seen)
     expert_sums.append(lax.psum_scatter(late_term, "ctx", scatter_dimension=0, tiled=True))
-    last_outs = after(list(outs), *late_seen)
-    arrived += [to_partner(last_outs[j], j) for j in range(3, shard_count)]
-    early_sum = add_wide(early_parts).astype(low_type)
     expert_grad, expert_new, expert_moment_new, expert_second_new = rotate(
         expert_weight[0], expert_sums, expert_moment[0], expert_second[0], expert_left[0], expert_right[0]
     )
-    late_parts = after(sum_chips(late_rows, chip, chips), expert_new)
+    late_parts = sum_chips(late_rows, chip, chips)
+    early_parts, late_parts = after((early_parts, late_parts), expert_new)
+    early_sum = add_wide(early_parts).astype(low_type)
     late_sum = add_wide(late_parts).astype(low_type)
     all_sums = jnp.concatenate([early_sum, late_sum], axis=0)
     places = jnp.asarray(piece_places(row_groups, q_groups, kv_groups), jnp.int32)[dense_order]

time: 514 us -> 515 us (level)
    ppermute x9, waiting for transfers between devices: 59.7 us -> 17.7 us  [to_chip(): lax.ppermute(array, 'ctx', [(i, (i + 2 * offset) % count) for i in range(...]
    reduce_scatter x1, waiting for transfers between devices: 0.01 us -> 36.9 us  [shards(): lax.psum_scatter(late_term, 'ctx', scatter_dimension=0, tiled=True)]
  transfers between devices with their start and end apart: 76 -> 76, of which waited for: 33 -> 35; matrix products, arithmetic and copies ran while one was open for 4% -> 5% of each run, Pallas kernels for 37% -> 37%
where the time goes in v12:
time: 515 us; the launch traced here: 509 us
  Pallas kernels  194 us (38%)
  waiting for transfers between devices  190 us (37%)
  starting transfers between devices  66.3 us (13%)
  local copies, waits for them, and re-layouts  23.9 us (5%)
  other arithmetic  17.7 us (3%)
  between operations  15.9 us (3%)
    ppermute x37, waiting for transfers between devices, to_partner(): return lax.ppermute(array, 'shard', [(i, i ^ offset) for i in range(count)])  105 us
    ppermute x37, starting transfers between devices, to_partner(): return lax.ppermute(array, 'shard', [(i, i ^ offset) for i in range(count)])  41.9 us
    reduce_scatter x1, waiting for transfers between devices, shards(): lax.psum_scatter(late_term, 'ctx', scatter_dimension=0, tiled=True)  36.9 us
    pallas_call x2, Pallas kernels, run_expert(): call(functools.partial(expert_kernel, sources, micro), tuple([shaped((row...  32.4 us
    pallas_call x2, Pallas kernels, attend_back(): pl.pallas_call(functools.partial(attend_back_kernel, micro), out_shape=(s...  31 us
    pallas_call x2, Pallas kernels, attend(): call(functools.partial(attend_kernel, micro), (shaped((rows, width), low_...  25.5 us
    pallas_call x2, Pallas kernels, rotate(): pl.pallas_call(rotate_kernel, grid=(count,), out_shape=(shaped(weight.sha...  20.9 us
    pallas_call x1, Pallas kernels, outer_blocks(): call(functools.partial(outer_kernel, groups, cols // BC), (shaped((blocks...  17.9 us
  transfers between devices with their start and end apart: 76, of which 35 were waited for; matrix products, arithmetic and copies ran while one was open for 5% of the time, Pallas kernels for 37%

profile of v12, /device:TPU:0, one launch (start us, length us, event | category | flops | bytes accessed | tf_op | source)
XLA Modules:
  0.0 508.8 jit_solution(14943185750277553708)
XLA Ops:
  15.0 7.7 %collective-permute-done.7.refs_11_ = bf16[4,192,256]{2,1,0:T(8,128)(2,1)S(1)} collective-permute-done((bf16[4,192,256]{2,1,0:T(8,128)(2,1)S(1)}, bf16[4,192,256]{2,1,0:T(8,128)(2,1)S(1)}, u32[]{:S(2)}, u32[]{:S(2)}) %collective-permute-start.7) | collective-permute-done | bytes 393248 | tf_op jit(solution)/shard_map/ppermute | solution.py:967
  24.7 7.1 %collective-permute-done.3.refs_7_ = bf16[4,192,256]{2,1,0:T(8,128)(2,1)S(1)} collective-permute-done((bf16[4,192,256]{2,1,0:T(8,128)(2,1)S(1)}, bf16[4,192,256]{2,1,0:T(8,128)(2,1)S(1)}, u32[]{:S(2)}, u32[]{:S(2)}) %collective-permute-start.3) | collective-permute-done | bytes 393248 | tf_op jit(solution)/shard_map/ppermute | solution.py:957
  45.3 7.0 %collective-permute-done.18 = bf16[4,192,256]{2,1,0:T(8,128)(2,1)S(1)} collective-permute-done((bf16[4,192,256]{2,1,0:T(8,128)(2,1)S(1)}, bf16[4,192,256]{2,1,0:T(8,128)(2,1)S(1)}, u32[]{:S(2)}, u32[]{:S(2)}) %collective-permute-start.18) | collective-permute-done | bytes 393248 | tf_op jit(solution)/shard_map/ppermute | solution.py:967
  57.3 11.3 %collective-permute-done.22.refs_25_ = bf16[8,192,256]{2,1,0:T(8,128)(2,1)S(1)} collective-permute-done((bf16[8,192,256]{2,1,0:T(8,128)(2,1)S(1)}, bf16[8,192,256]{2,1,0:T(8,128)(2,1)S(1)}, u32[]{:S(2)}, u32[]{:S(2)}) %collective-permute-start.22) | collective-permute-done | bytes 786464 | tf_op jit(solution)/shard_map/ppermute | solution.py:957
  85.3 12.3 %shard_map.358 = (bf16[256,1536]{1,0:T(8,128)(2,1)}, bf16[256,1024]{1,0:T(8,128)(2,1)}, bf16[1536,2560]{1,0:T(8,128)(2,1)}, bf16[1536,1536]{1,0:T(8,128)(2,1)}) custom-call(s32[128]{0:T(128)} %order_ref.1, s32[2]{0:T(128)} %pad_add_fusion.me_ref, f32[128,1536]{1,0:T(8,128)} %get-tuple-element.279.refs_0_.x_ref, ...), custom_call_target="tpu_custom_call" | custom-call | flops 805306368 | bytes 25165824 | tf_op jit(solution)/shard_map/pallas_call | solution.py:192
  113.0 11.0 %collective-permute-done.28.refs_5_ = bf16[256,1664]{1,0:T(8,128)(2,1)} collective-permute-done((bf16[256,1664]{1,0:T(8,128)(2,1)S(1)}, bf16[256,1664]{1,0:T(8,128)(2,1)}, u32[]{:S(2)}, u32[]{:S(2)}) %collective-permute-start.28) | collective-permute-done | bytes 852000 | tf_op jit(solution)/shard_map/ppermute | solution.py:957
  123.9 18.3 %collective-permute-done.29.refs_6_ = bf16[256,1664]{1,0:T(8,128)(2,1)} collective-permute-done((bf16[256,1664]{1,0:T(8,128)(2,1)S(1)}, bf16[256,1664]{1,0:T(8,128)(2,1)}, u32[]{:S(2)}, u32[]{:S(2)}) %collective-permute-start.29) | collective-permute-done | bytes 852000 | tf_op jit(solution)/shard_map/ppermute | solution.py:957
  148.2 12.7 %shard_map.360 = (bf16[128,1536]{1,0:T(8,128)(2,1)}, f32[384,128]{1,0:T(8,128)}, f32[128,1536]{1,0:T(8,128)}, bf16[128,1536]{1,0:T(8,128)(2,1)}) custom-call(bf16[128,1536]{1,0:T(8,128)(2,1)} %get-tuple-element.162.q_ref, s32[128,1]{1,0:T(8,128)} %constant_dynamic-slice_fusion.4.rpos_ref, s32[1,1024]{1,0:T(1,128)} %bitcast.70, ...), custom_call_target="tpu_custom_call" | custom-call | flops 3221225472 | bytes 8388608 | tf_op jit(solution)/shard_map/pallas_call | solution.py:306
  164.5 12.8 %shard_map.361 = (bf16[128,1536]{1,0:T(8,128)(2,1)}, f32[384,128]{1,0:T(8,128)}, f32[128,1536]{1,0:T(8,128)}, bf16[128,1536]{1,0:T(8,128)(2,1)}) custom-call(bf16[128,1536]{1,0:T(8,128)(2,1)} %get-tuple-element.170.q_ref, s32[128,1]{1,0:T(8,128)} %constant_dynamic-slice_fusion.4.rpos_ref, s32[1,1024]{1,0:T(1,128)} %bitcast.71, ...), custom_call_target="tpu_custom_call" | custom-call | flops 3221225472 | bytes 8388608 | tf_op jit(solution)/shard_map/pallas_call | solution.py:306
  186.9 16.0 %shard_map.362 = (bf16[128,1664]{1,0:T(8,128)(2,1)}, bf16[128,1664]{1,0:T(8,128)(2,1)}, bf16[128,1664]{1,0:T(8,128)(2,1)}, bf16[128,1664]{1,0:T(8,128)(2,1)}, bf...) custom-call(s32[96]{0:T(128)} %select_reduce_fusion.order_ref, ...), custom_call_target="tpu_custom_call" | custom-call | flops 8053063680 | bytes 20971520 | tf_op jit(solution)/shard_map/pallas_call | solution.py:406
  207.2 16.4 %shard_map.363 = (bf16[128,1664]{1,0:T(8,128)(2,1)}, bf16[128,1664]{1,0:T(8,128)(2,1)}, bf16[128,1664]{1,0:T(8,128)(2,1)}, bf16[128,1664]{1,0:T(8,128)(2,1)}, bf...) custom-call(s32[96]{0:T(128)} %select_reduce_fusion.order_ref, ...), custom_call_target="tpu_custom_call" | custom-call | flops 8053063680 | bytes 20971520 | tf_op jit(solution)/shard_map/pallas_call | solution.py:406
  227.2 17.9 %shard_map.364 = (bf16[96,192,128]{2,1,0:T(8,128)(2,1)}, bf16[96,192,128]{2,1,0:T(8,128)(2,1)}) custom-call(s32[96]{0:T(128)} %select_reduce_fusion.order_ref, bf16[512,1536]{1,0:T(8,128)(2,1)} %get-tuple-element.181.refs_0_, bf16[512,1536]{1,0:T(8,128)(2,1)} %get-tuple-element.185.refs_1_, bf16[512,1664]{1,0:T(8,128)(2,1)} %get-tuple-element.186.refs_2_, ...), custom_call_target="tpu_custom_call" | custom-call | flops 9663676416 | bytes 22282240 | tf_op jit(solution)/shard_map/pallas_call | solution.py:521
  247.1 9.0 %shard_map.365 = (bf16[256,1536]{1,0:T(8,128)(2,1)}, bf16[256,1536]{1,0:T(8,128)(2,1)}, bf16[256,1536]{1,0:T(8,128)(2,1)}, bf16[256,1536]{1,0:T(8,128)(2,1)}) custom-call(s32[96]{0:T(128)} %select_reduce_fusion.order_ref, bf16[96,128,256]{2,1,0:T(8,128)(2,1)} %all-gather.4.cloned.1.call-done.refs_8_.upper_ref, ...), custom_call_target="tpu_custom_call" | custom-call | flops 3221225472 | bytes 8388608 | tf_op jit(solution)/shard_map/pallas_call | solution.py:460
  265.2 15.5 %shard_map.367 = (bf16[128,1536]{1,0:T(8,128)(2,1)}, bf16[2048,1024]{1,0:T(8,128)(2,1)}) custom-call(bf16[128,1536]{1,0:T(8,128)(2,1)} %get-tuple-element.162.q_ref, s32[128,1]{1,0:T(8,128)} %constant_dynamic-slice_fusion.4.rpos_ref, s32[1,1024]{1,0:T(1,128)} %bitcast.72, bf16[128,1536]{1,0:T(8,128)(2,1)} %get-tuple-element.169.ob_ref.refs_10_, ...), custom_call_target="tpu_custom_call" | custom-call | flops 8053063680 | bytes 8388608 | tf_op jit(solution)/shard_map/pallas_call | solution.py:789
  287.4 15.5 %shard_map.369 = (bf16[128,1536]{1,0:T(8,128)(2,1)}, bf16[2048,1024]{1,0:T(8,128)(2,1)}) custom-call(bf16[128,1536]{1,0:T(8,128)(2,1)} %get-tuple-element.170.q_ref, s32[128,1]{1,0:T(8,128)} %constant_dynamic-slice_fusion.4.rpos_ref, s32[1,1024]{1,0:T(1,128)} %bitcast.73, ...), custom_call_target="tpu_custom_call", output_to_operand_aliasing={{1}: (7, {})} | custom-call | flops 8053063680 | bytes 8388608 | tf_op jit(solution)/shard_map/pallas_call | solution.py:789
  309.4 9.4 %shard_map.370 = (bf16[98,48,128]{2,1,0:T(8,128)(2,1)}, bf16[98,48,128]{2,1,0:T(8,128)(2,1)}, bf16[96,48,128]{2,1,0:T(8,128)(2,1)}, bf16[96,48,128]{2,1,0:T(8,128)(2,1)}, bf16[1536,512]{1,0:T(8,128)(2,1)}) custom-call(s32[2]{0:T(128)} %pad_add_fusion.me_ref, bf16[256,1536]{1,0:T(8,128)(2,1)} %get-tuple-element.158.h_ref.refs_0_, ...), custom_call_target="tpu_custom_call" | custom-call | flops 2415919104 | bytes 16777216 | tf_op jit(solution)/shard_map/pallas_call | solution.py:646
  325.8 21.6 %collective-permute-done.55 = bf16[96,48,128]{2,1,0:T(8,128)(2,1)} collective-permute-done((bf16[96,48,128]{2,1,0:T(8,128)(2,1)}, bf16[96,48,128]{2,1,0:T(8,128)(2,1)}, u32[]{:S(2)}, u32[]{:S(2)}) %collective-permute-start.55) | collective-permute-done | bytes 1179680 | tf_op jit(solution)/shard_map/ppermute | solution.py:957
  350.8 13.1 %collective-permute-done.56 = bf16[48,48,128]{2,1,0:T(8,128)(2,1)S(1)} collective-permute-done((bf16[48,48,128]{2,1,0:T(8,128)(2,1)S(1)}, bf16[48,48,128]{2,1,0:T(8,128)(2,1)S(1)}, u32[]{:S(2)}, u32[]{:S(2)}) %collective-permute-start.56) | collective-permute-done | bytes 589856 | tf_op jit(solution)/shard_map/ppermute | solution.py:957
  380.6 7.4 %collective-permute-done.57 = bf16[256,1536]{1,0:T(8,128)(2,1)} collective-permute-done((bf16[256,1536]{1,0:T(8,128)(2,1)}, bf16[256,1536]{1,0:T(8,128)(2,1)}, u32[]{:S(2)}, u32[]{:S(2)}) %collective-permute-start.57) | collective-permute-done | bytes 786464 | tf_op jit(solution)/shard_map/ppermute | solution.py:957
  388.0 7.1 %shard_map.374 = (f32[2,128,1536]{2,1,0:T(8,128)}, f32[8,1536]{1,0:T(8,128)}) custom-call(f32[2,128,1536]{2,1,0:T(8,128)} %x_ref, f32[2,1536]{1,0:T(2,128)} %gain_ref.9, bf16[1536,2560]{1,0:T(8,128)(2,1)} %get-tuple-element.222.w_ref, f32[128,1536]{1,0:T(8,128)} %get-tuple-element.242.refs_0_, f32[128,1536]{1,0:T(8,128)} %get-tuple-element.243.refs_1_, ...), custom_call_target="tpu_custom_call" | custom-call | flops 805306368 | bytes 14680064 | tf_op jit(solution)/shard_map/pallas_call | solution.py:873
  407.7 36.9 %reduce-scatter.8.cloned.1.call-done.refs_1_ = bf16[12,192,128]{2,1,0:T(8,128)(2,1)} async-done(((bf16[96,192,128]{2,1,0:T(8,128)(2,1)}), bf16[12,192,128]{2,1,0:T(8,128)(2,1)}) %reduce-scatter.8.cloned.1.call-update) | async-done | bytes 589840 | tf_op jit(solution)/shard_map/reduce_scatter | solution.py:1234
  444.6 15.1 %shard_map.372 = (f32[12,192,256]{2,1,0:T(8,128)}, f32[12,192,256]{2,1,0:T(8,128)}, f32[12,192,256]{2,1,0:T(8,128)}, f32[12,192,256]{2,1,0:T(8,128)}) custom-call(f32[12,192,256]{2,1,0:T(8,128)} %bitcast.51, f32[12,192,256]{2,1,0:T(8,128)} %bitcast.57, f32[12,192,256]{2,1,0:T(8,128)} %bitcast.58, f32[12,192,192]{2,1,0:T(8,128)} %bitcast.59, ...), custom_call_target="tpu_custom_call" | custom-call | flops 1056964608 | bytes 25165824 | tf_op jit(solution)/shard_map/pallas_call | solution.py:912
  462.2 11.0 %all-to-all-start = ((bf16[32,2,4608]{2,1,0:T(2,128)(2,1)}), bf16[32,2,4608]{2,1,0:T(2,128)(2,1)S(1)}, u32[]{:S(2)}, u32[]{:S(2)}) async-start(bf16[32,2,4608]{2,1,0:T(2,128)(2,1)} %all_to_all.6), calls=%async_computation.3 | async-start | bytes 1179648 | tf_op jit(solution)/shard_map/all_to_all | solution.py:1259
  476.6 14.1 %all-to-all-done = bf16[32,2,4608]{2,1,0:T(2,128)(2,1)S(1)} async-done(((bf16[32,2,4608]{2,1,0:T(2,128)(2,1)}), bf16[32,2,4608]{2,1,0:T(2,128)(2,1)S(1)}, u32[]{:S(2)}, u32[]{:S(2)}) %all-to-all-start) | async-done | bytes 589856 | tf_op jit(solution)/shard_map/all_to_all | solution.py:1259
  (376 shorter events, 167.0 us)
Async XLA Ops:
  7.2 93.8 %all-gather.4.cloned.1.call-start = ((), (), s32[]{:S(2)}) async-start(), calls=%async_computation.4 | async-start | bytes 7077888 | tf_op jit(solution)/shard_map/all_gather | solution.py:1121
  35.7 111.9 %all-gather.6.cloned.1.call-start = ((), (), s32[]{:S(2)}) async-start(), calls=%async_computation.5 | async-start | bytes 4718592 | tf_op jit(solution)/shard_map/all_gather | solution.py:1144
  101.1 85.8 %all-gather.8.cloned.1.call-start = ((), (), s32[]{:S(2)}) async-start(), calls=%async_computation.6 | async-start | bytes 3538944 | tf_op jit(solution)/shard_map/all_gather | solution.py:1146
  103.0 39.2 %collective-permute-start.29 = (bf16[256,1664]{1,0:T(8,128)(2,1)S(1)}, bf16[256,1664]{1,0:T(8,128)(2,1)}, u32[]{:S(2)}, u32[]{:S(2)}) collective-permute-start(bf16[256,1664]{1,0:T(8,128)(2,1)S(1)} %bitcast.62), channel_id=1, source_target_pairs={{0,2},{1,3},{2,0},{3,1},{4,6},{5,7},{6,4},{7,5},{8,10},{9,11},{10,... | collective-permute-start | bytes 2555912 | tf_op jit(solution)/shard_map/ppermute | solution.py:957
  104.5 37.7 %collective-permute-start.30 = (bf16[256,1664]{1,0:T(8,128)(2,1)S(1)}, bf16[256,1664]{1,0:T(8,128)(2,1)}, u32[]{:S(2)}, u32[]{:S(2)}) collective-permute-start(bf16[256,1664]{1,0:T(8,128)(2,1)S(1)} %bitcast.63), channel_id=1, source_target_pairs={{0,3},{1,2},{2,1},{3,0},{4,7},{5,6},{6,5},{7,4},{8,11},{9,10},{10,... | collective-permute-start | bytes 2555912 | tf_op jit(solution)/shard_map/ppermute | solution.py:957
  147.6 155.3 %reduce-scatter.4.cloned.1.call-start = ((), (), s32[]{:S(2)}) async-start(), calls=%async_computation.7 | async-start | bytes 5308416 | tf_op jit(solution)/shard_map/reduce_scatter | solution.py:1201
  147.9 36.3 %collective-permute-start.31 = (bf16[256,1536]{1,0:T(8,128)(2,1)S(1)}, bf16[256,1536]{1,0:T(8,128)(2,1)S(1)}, u32[]{:S(2)}, u32[]{:S(2)}) collective-permute-start(bf16[256,1536]{1,0:T(8,128)(2,1)S(1)} %copy-done.20), channel_id=1, source_target_pairs={{0,4},{4,0},{8,12},{12,8},{16,20},{20,16},{24,28},{28,24},{1,5},{5... | collective-permute-start | bytes 2359304 | tf_op jit(solution)/shard_map/ppermute | solution.py:962
  182.2 23.7 %collective-permute-start.40 = (bf16[128,1536]{1,0:T(8,128)(2,1)}, bf16[128,1536]{1,0:T(8,128)(2,1)}, u32[]{:S(2)}, u32[]{:S(2)}) collective-permute-start(bf16[128,1536]{1,0:T(8,128)(2,1)} %get-tuple-element.184.refs_0_.h2_ref), channel_id=1, source_target_pairs={{0,1},{1,0},{2,3},{3,2},{4,5},{5,4},{6,7},{7,6},{8,9},{9,8},{10,11... | collective-permute-start | bytes 1179656 | tf_op jit(solution)/shard_map/ppermute | solution.py:957
  183.4 23.0 %collective-permute-start.41 = (bf16[128,1536]{1,0:T(8,128)(2,1)}, bf16[128,1536]{1,0:T(8,128)(2,1)}, u32[]{:S(2)}, u32[]{:S(2)}) collective-permute-start(bf16[128,1536]{1,0:T(8,128)(2,1)} %get-tuple-element.184.refs_0_.h2_ref), channel_id=1, source_target_pairs={{0,2},{1,3},{2,0},{3,1},{4,6},{5,7},{6,4},{7,5},{8,10},{9,11},{10,... | collective-permute-start | bytes 1179656 | tf_op jit(solution)/shard_map/ppermute | solution.py:957
  202.9 23.7 %collective-permute-start.37 = (bf16[128,1664]{1,0:T(8,128)(2,1)}, bf16[128,1664]{1,0:T(8,128)(2,1)S(1)}, u32[]{:S(2)}, u32[]{:S(2)}) collective-permute-start(bf16[128,1664]{1,0:T(8,128)(2,1)} %get-tuple-element.177), channel_id=1, source_target_pairs={{0,1},{1,0},{2,3},{3,2},{4,5},{5,4},{6,7},{7,6},{8,9},{9,8},{10,11... | collective-permute-start | bytes 1277960 | tf_op jit(solution)/shard_map/ppermute | solution.py:957
  204.4 22.7 %collective-permute-start.38 = (bf16[128,1664]{1,0:T(8,128)(2,1)}, bf16[128,1664]{1,0:T(8,128)(2,1)S(1)}, u32[]{:S(2)}, u32[]{:S(2)}) collective-permute-start(bf16[128,1664]{1,0:T(8,128)(2,1)} %get-tuple-element.178), channel_id=1, source_target_pairs={{0,2},{1,3},{2,0},{3,1},{4,6},{5,7},{6,4},{7,5},{8,10},{9,11},{10,... | collective-permute-start | bytes 1277960 | tf_op jit(solution)/shard_map/ppermute | solution.py:957
  245.9 118.1 %reduce-scatter.6.cloned.1.call-start = ((), (), s32[]{:S(2)}) async-start(), calls=%async_computation.8 | async-start | bytes 4718592 | tf_op jit(solution)/shard_map/reduce_scatter | solution.py:1202
  256.2 24.5 %collective-permute-start.43 = (bf16[256,1536]{1,0:T(8,128)(2,1)}, bf16[256,1536]{1,0:T(8,128)(2,1)S(1)}, u32[]{:S(2)}, u32[]{:S(2)}) collective-permute-start(bf16[256,1536]{1,0:T(8,128)(2,1)} %get-tuple-element.197), channel_id=1, source_target_pairs={{0,1},{1,0},{2,3},{3,2},{4,5},{5,4},{6,7},{7,6},{8,9},{9,8},{10,11... | collective-permute-start | bytes 2359304 | tf_op jit(solution)/shard_map/ppermute | solution.py:957
  257.6 23.1 %collective-permute-start.44 = (bf16[256,1536]{1,0:T(8,128)(2,1)}, bf16[256,1536]{1,0:T(8,128)(2,1)S(1)}, u32[]{:S(2)}, u32[]{:S(2)}) collective-permute-start(bf16[256,1536]{1,0:T(8,128)(2,1)} %get-tuple-element.198), channel_id=1, source_target_pairs={{0,2},{1,3},{2,0},{3,1},{4,6},{5,7},{6,4},{7,5},{8,10},{9,11},{10,... | collective-permute-start | bytes 2359304 | tf_op jit(solution)/shard_map/ppermute | solution.py:957
  303.0 141.6 %reduce-scatter.8.cloned.1.call-start = ((), (), s32[]{:S(2)}) async-start(), calls=%async_computation.9 | async-start | bytes 5308416 | tf_op jit(solution)/shard_map/reduce_scatter | solution.py:1234
  318.8 28.9 %collective-permute-start.53 = (bf16[98,48,128]{2,1,0:T(8,128)(2,1)}, bf16[98,48,128]{2,1,0:T(8,128)(2,1)S(1)}, u32[]{:S(2)}, u32[]{:S(2)}) collective-permute-start(bf16[98,48,128]{2,1,0:T(8,128)(2,1)} %get-tuple-element.221), channel_id=1, source_target_pairs={{0,1},{1,0},{2,3},{3,2},{4,5},{5,4},{6,7},{7,6},{8,9},{9,8},{10,11... | collective-permute-start | bytes 3612680 | tf_op jit(solution)/shard_map/ppermute | solution.py:957
  319.1 28.2 %collective-permute-start.55 = (bf16[96,48,128]{2,1,0:T(8,128)(2,1)}, bf16[96,48,128]{2,1,0:T(8,128)(2,1)}, u32[]{:S(2)}, u32[]{:S(2)}) collective-permute-start(bf16[96,48,128]{2,1,0:T(8,128)(2,1)} %get-tuple-element.227), channel_id=1, source_target_pairs={{0,2},{1,3},{2,0},{3,1},{4,6},{5,7},{6,4},{7,5},{8,10},{9,11},{10,... | collective-permute-start | bytes 3538952 | tf_op jit(solution)/shard_map/ppermute | solution.py:957
  379.1 27.7 %collective-permute-start.59 = (bf16[97,1536]{1,0:T(8,128)(2,1)}, bf16[97,1536]{1,0:T(8,128)(2,1)S(1)}, u32[]{:S(2)}, u32[]{:S(2)}) collective-permute-start(bf16[97,1536]{1,0:T(8,128)(2,1)} %get-tuple-element.282), channel_id=1, source_target_pairs={{0,24},{4,28},{8,0},{12,4},{16,8},{20,12},{24,16},{28,20},{1,25},{... | collective-permute-start | bytes 893960 | tf_op jit(solution)/shard_map/ppermute | solution.py:967
  380.2 79.5 %collective-permute-start.60 = (bf16[97,1536]{1,0:T(8,128)(2,1)}, bf16[97,1536]{1,0:T(8,128)(2,1)S(1)}, u32[]{:S(2)}, u32[]{:S(2)}) collective-permute-start(bf16[97,1536]{1,0:T(8,128)(2,1)} %get-tuple-element.283), channel_id=1, source_target_pairs={{0,16},{4,20},{8,24},{12,28},{16,0},{20,4},{24,8},{28,12},{1,17},{... | collective-permute-start | bytes 893960 | tf_op jit(solution)/shard_map/ppermute | solution.py:967
  387.9 71.7 %collective-permute-start.61 = (bf16[97,1536]{1,0:T(8,128)(2,1)}, bf16[97,1536]{1,0:T(8,128)(2,1)S(1)}, u32[]{:S(2)}, u32[]{:S(2)}) collective-permute-start(bf16[97,1536]{1,0:T(8,128)(2,1)} %get-tuple-element.280), channel_id=1, source_target_pairs={{0,8},{4,12},{8,16},{12,20},{16,24},{20,28},{24,0},{28,4},{1,9},{5... | collective-permute-start | bytes 893960 | tf_op jit(solution)/shard_map/ppermute | solution.py:967
  403.9 55.8 %collective-permute-start.66 = (bf16[32,1536]{1,0:T(8,128)(2,1)S(1)}, bf16[32,1536]{1,0:T(8,128)(2,1)S(1)}, u32[]{:S(2)}, u32[]{:S(2)}) collective-permute-start(bf16[32,1536]{1,0:T(8,128)(2,1)S(1)} %get-tuple-element.286), channel_id=1, source_target_pairs={{0,24},{4,28},{8,0},{12,4},{16,8},{20,12},{24,16},{28,20},{1,25},{... | collective-permute-start | bytes 294920 | tf_op jit(solution)/shard_map/ppermute | solution.py:967
  406.8 52.9 %collective-permute-start.67 = (bf16[32,1536]{1,0:T(8,128)(2,1)S(1)}, bf16[32,1536]{1,0:T(8,128)(2,1)S(1)}, u32[]{:S(2)}, u32[]{:S(2)}) collective-permute-start(bf16[32,1536]{1,0:T(8,128)(2,1)S(1)} %get-tuple-element.285), channel_id=1, source_target_pairs={{0,16},{4,20},{8,24},{12,28},{16,0},{20,4},{24,8},{28,12},{1,17},{... | collective-permute-start | bytes 294920 | tf_op jit(solution)/shard_map/ppermute | solution.py:967
  406.8 52.9 %collective-permute-start.68 = (bf16[32,1536]{1,0:T(8,128)(2,1)S(1)}, bf16[32,1536]{1,0:T(8,128)(2,1)S(1)}, u32[]{:S(2)}, u32[]{:S(2)}) collective-permute-start(bf16[32,1536]{1,0:T(8,128)(2,1)S(1)} %get-tuple-element.284), channel_id=1, source_target_pairs={{0,8},{4,12},{8,16},{12,20},{16,24},{20,28},{24,0},{28,4},{1,9},{5... | collective-permute-start | bytes 294920 | tf_op jit(solution)/shard_map/ppermute | solution.py:967
  462.2 28.5 %all-to-all-start = ((bf16[32,2,4608]{2,1,0:T(2,128)(2,1)}), bf16[32,2,4608]{2,1,0:T(2,128)(2,1)S(1)}, u32[]{:S(2)}, u32[]{:S(2)}) async-start(bf16[32,2,4608]{2,1,0:T(2,128)(2,1)} %all_to_all.6), calls=%async_computation.3 | async-start | bytes 1179648 | tf_op jit(solution)/shard_map/all_to_all | solution.py:1259
  (127 other events, 1387.4 us)
Sparse Core Ops, SparseCore 0:
  35.8 65.1 all-gather.3
  102.6 44.9 all-gather.5
  149.8 36.9 all-gather.7
  245.6 53.5 reduce-scatter.3
  303.1 46.7 reduce-scatter.5
  364.1 80.4 reduce-scatter.7

commit v13 on v12

--- a/solution.py
+++ b/solution.py
@@ -1215,7 +1215,6 @@
     parts_back = query_back(after(w_in, early[0]), dqs)
     early_rows, early_seen = sum_members(early[:4], parts_back, shard_count)
     chip = ctx // 2
-    early_parts = sum_chips(early_rows, chip, chips)
     late = gradient_pieces(
         shard_count,
         after(me, *early_seen),
@@ -1235,11 +1234,9 @@
     expert_grad, expert_new, expert_moment_new, expert_second_new = rotate(
         expert_weight[0], expert_sums, expert_moment[0], expert_second[0], expert_left[0], expert_right[0]
     )
-    late_parts = sum_chips(late_rows, chip, chips)
-    early_parts, late_parts = after((early_parts, late_parts), expert_new)
-    early_sum = add_wide(early_parts).astype(low_type)
-    late_sum = add_wide(late_parts).astype(low_type)
-    all_sums = jnp.concatenate([early_sum, late_sum], axis=0)
+    all_rows = after(jnp.concatenate([early_rows, late_rows], axis=0), expert_sums)
+    all_parts = after(sum_chips(all_rows, chip, chips), expert_new)
+    all_sums = add_wide(all_parts).astype(low_type)
     places = jnp.asarray(piece_places(row_groups, q_groups, kv_groups), jnp.int32)[dense_order]
     chosen = (places[:, None] == jnp.arange(all_sums.shape[0])[None, :]).astype(low_type)
     ordered = jnp.dot(chosen, all_sums, preferred_element_type=jnp.float32).astype(low_type)
@@ -1247,7 +1244,7 @@
     piece_width = ordered.shape[1]
     stat_place = row_groups // 2 * 2 * q_groups
     gain_parts = gain_stat[:1].astype(low_type).reshape(-1, piece_width)
-    stat_parts = jnp.concatenate([early_sum[stat_place : stat_place + 1], gain_parts], axis=0)
+    stat_parts = jnp.concatenate([all_sums[stat_place : stat_place + 1], gain_parts], axis=0)
     extra = stat_parts.shape[0]
     ordered = jnp.concatenate(
         [

time: 515 us -> 503 us (0.977)
  starting transfers between devices: 66.3 us -> 55.6 us
    reduce_scatter x1, waiting for transfers between devices: 36.9 us -> 12.9 us  [shards(): lax.psum_scatter(late_term, 'ctx', scatter_dimension=0, tiled=True)]
    ppermute x9 -> x6, waiting for transfers between devices: 17.7 us -> 35.7 us  [to_chip(): lax.ppermute(array, 'ctx', [(i, (i + 2 * offset) % count) for i in range(...]
    ppermute x37, waiting for transfers between devices: 105 us -> 112 us  [to_partner(): return lax.ppermute(array, 'shard', [(i, i ^ offset) for i in range(count)])]
    all_to_all x1, starting transfers between devices: 11 us -> 5.23 us  [shards(): lax.all_to_all(ordered, ('ctx', 'shard'), split_axis=0, concat_axis=0, ti...]
  transfers between devices with their start and end apart: 76 -> 73, of which waited for: 35 -> 34; matrix products, arithmetic and copies ran while one was open for 5% -> 5% of each run, Pallas kernels for 37% -> 38%
where the time goes in v13:
time: 503 us; the launch traced here: 496 us
  Pallas kernels  194 us (39%)
  waiting for transfers between devices  192 us (38%)
  starting transfers between devices  55.6 us (11%)
  local copies, waits for them, and re-layouts  22.1 us (4%)
  between operations  15.9 us (3%)
  other arithmetic  15.8 us (3%)
    ppermute x37, waiting for transfers between devices, to_partner(): return lax.ppermute(array, 'shard', [(i, i ^ offset) for i in range(count)])  112 us
    ppermute x37, starting transfers between devices, to_partner(): return lax.ppermute(array, 'shard', [(i, i ^ offset) for i in range(count)])  40 us
    ppermute x6, waiting for transfers between devices, to_chip(): lax.ppermute(array, 'ctx', [(i, (i + 2 * offset) % count) for i in range(...  35.7 us
    pallas_call x2, Pallas kernels, run_expert(): call(functools.partial(expert_kernel, sources, micro), tuple([shaped((row...  32.4 us
    pallas_call x2, Pallas kernels, attend_back(): pl.pallas_call(functools.partial(attend_back_kernel, micro), out_shape=(s...  30.9 us
    pallas_call x2, Pallas kernels, attend(): call(functools.partial(attend_kernel, micro), (shaped((rows, width), low_...  25.5 us
    pallas_call x2, Pallas kernels, rotate(): pl.pallas_call(rotate_kernel, grid=(count,), out_shape=(shaped(weight.sha...  20.9 us
    pallas_call x1, Pallas kernels, outer_blocks(): call(functools.partial(outer_kernel, groups, cols // BC), (shaped((blocks...  17.9 us
  transfers between devices with their start and end apart: 73, of which 34 were waited for; matrix products, arithmetic and copies ran while one was open for 5% of the time, Pallas kernels for 38%

profile of v13, /device:TPU:0, one launch (start us, length us, event | category | flops | bytes accessed | tf_op | source)
XLA Modules:
  0.0 496.4 jit_solution(10228867557988515494)
XLA Ops:
  15.0 7.8 %collective-permute-done.7.refs_11_ = bf16[4,192,256]{2,1,0:T(8,128)(2,1)} collective-permute-done((bf16[4,192,256]{2,1,0:T(8,128)(2,1)S(1)}, bf16[4,192,256]{2,1,0:T(8,128)(2,1)}, u32[]{:S(2)}, u32[]{:S(2)}) %collective-permute-start.7) | collective-permute-done | bytes 393248 | tf_op jit(solution)/shard_map/ppermute | solution.py:967
  24.6 7.1 %collective-permute-done.3.refs_7_ = bf16[4,192,256]{2,1,0:T(8,128)(2,1)S(1)} collective-permute-done((bf16[4,192,256]{2,1,0:T(8,128)(2,1)S(1)}, bf16[4,192,256]{2,1,0:T(8,128)(2,1)S(1)}, u32[]{:S(2)}, u32[]{:S(2)}) %collective-permute-start.3) | collective-permute-done | bytes 393248 | tf_op jit(solution)/shard_map/ppermute | solution.py:957
  43.6 7.2 %collective-permute-done.18 = bf16[4,192,256]{2,1,0:T(8,128)(2,1)S(1)} collective-permute-done((bf16[4,192,256]{2,1,0:T(8,128)(2,1)S(1)}, bf16[4,192,256]{2,1,0:T(8,128)(2,1)S(1)}, u32[]{:S(2)}, u32[]{:S(2)}) %collective-permute-start.18) | collective-permute-done | bytes 393248 | tf_op jit(solution)/shard_map/ppermute | solution.py:967
  56.1 12.5 %collective-permute-done.22.refs_25_ = bf16[8,192,256]{2,1,0:T(8,128)(2,1)S(1)} collective-permute-done((bf16[8,192,256]{2,1,0:T(8,128)(2,1)S(1)}, bf16[8,192,256]{2,1,0:T(8,128)(2,1)S(1)}, u32[]{:S(2)}, u32[]{:S(2)}) %collective-permute-start.22) | collective-permute-done | bytes 786464 | tf_op jit(solution)/shard_map/ppermute | solution.py:957
  85.4 12.2 %shard_map.358 = (bf16[256,1536]{1,0:T(8,128)(2,1)}, bf16[256,1024]{1,0:T(8,128)(2,1)}, bf16[1536,2560]{1,0:T(8,128)(2,1)}, bf16[1536,1536]{1,0:T(8,128)(2,1)}) custom-call(s32[128]{0:T(128)} %order_ref.1, s32[2]{0:T(128)} %pad_add_fusion.me_ref, f32[128,1536]{1,0:T(8,128)} %get-tuple-element.277.refs_0_.x_ref, ...), custom_call_target="tpu_custom_call" | custom-call | flops 805306368 | bytes 25165824 | tf_op jit(solution)/shard_map/pallas_call | solution.py:192
  112.3 10.9 %collective-permute-done.28.refs_5_ = bf16[256,1664]{1,0:T(8,128)(2,1)} collective-permute-done((bf16[256,1664]{1,0:T(8,128)(2,1)S(1)}, bf16[256,1664]{1,0:T(8,128)(2,1)}, u32[]{:S(2)}, u32[]{:S(2)}) %collective-permute-start.28) | collective-permute-done | bytes 852000 | tf_op jit(solution)/shard_map/ppermute | solution.py:957
  123.1 18.3 %collective-permute-done.29.refs_6_ = bf16[256,1664]{1,0:T(8,128)(2,1)} collective-permute-done((bf16[256,1664]{1,0:T(8,128)(2,1)S(1)}, bf16[256,1664]{1,0:T(8,128)(2,1)}, u32[]{:S(2)}, u32[]{:S(2)}) %collective-permute-start.29) | collective-permute-done | bytes 852000 | tf_op jit(solution)/shard_map/ppermute | solution.py:957
  148.0 12.7 %shard_map.360 = (bf16[128,1536]{1,0:T(8,128)(2,1)}, f32[384,128]{1,0:T(8,128)}, f32[128,1536]{1,0:T(8,128)}, bf16[128,1536]{1,0:T(8,128)(2,1)}) custom-call(bf16[128,1536]{1,0:T(8,128)(2,1)} %get-tuple-element.159.q_ref, s32[128,1]{1,0:T(8,128)} %constant_dynamic-slice_fusion.4.rpos_ref, s32[1,1024]{1,0:T(1,128)} %bitcast.71, ...), custom_call_target="tpu_custom_call" | custom-call | flops 3221225472 | bytes 8388608 | tf_op jit(solution)/shard_map/pallas_call | solution.py:306
  164.3 12.8 %shard_map.361 = (bf16[128,1536]{1,0:T(8,128)(2,1)}, f32[384,128]{1,0:T(8,128)}, f32[128,1536]{1,0:T(8,128)}, bf16[128,1536]{1,0:T(8,128)(2,1)}) custom-call(bf16[128,1536]{1,0:T(8,128)(2,1)} %get-tuple-element.167.q_ref, s32[128,1]{1,0:T(8,128)} %constant_dynamic-slice_fusion.4.rpos_ref, s32[1,1024]{1,0:T(1,128)} %bitcast.72, ...), custom_call_target="tpu_custom_call" | custom-call | flops 3221225472 | bytes 8388608 | tf_op jit(solution)/shard_map/pallas_call | solution.py:306
  186.6 16.0 %shard_map.362 = (bf16[128,1664]{1,0:T(8,128)(2,1)}, bf16[128,1664]{1,0:T(8,128)(2,1)}, bf16[128,1664]{1,0:T(8,128)(2,1)}, bf16[128,1664]{1,0:T(8,128)(2,1)}, bf...) custom-call(s32[96]{0:T(128)} %select_reduce_fusion.order_ref, ...), custom_call_target="tpu_custom_call" | custom-call | flops 8053063680 | bytes 20971520 | tf_op jit(solution)/shard_map/pallas_call | solution.py:406
  207.0 16.4 %shard_map.363 = (bf16[128,1664]{1,0:T(8,128)(2,1)}, bf16[128,1664]{1,0:T(8,128)(2,1)}, bf16[128,1664]{1,0:T(8,128)(2,1)}, bf16[128,1664]{1,0:T(8,128)(2,1)}, bf...) custom-call(s32[96]{0:T(128)} %select_reduce_fusion.order_ref, ...), custom_call_target="tpu_custom_call" | custom-call | flops 8053063680 | bytes 20971520 | tf_op jit(solution)/shard_map/pallas_call | solution.py:406
  226.9 17.9 %shard_map.364 = (bf16[96,192,128]{2,1,0:T(8,128)(2,1)}, bf16[96,192,128]{2,1,0:T(8,128)(2,1)}) custom-call(s32[96]{0:T(128)} %select_reduce_fusion.order_ref, bf16[512,1536]{1,0:T(8,128)(2,1)} %get-tuple-element.178.refs_0_, bf16[512,1536]{1,0:T(8,128)(2,1)} %get-tuple-element.182.refs_1_, bf16[512,1664]{1,0:T(8,128)(2,1)} %get-tuple-element.183.refs_2_, ...), custom_call_target="tpu_custom_call" | custom-call | flops 9663676416 | bytes 22282240 | tf_op jit(solution)/shard_map/pallas_call | solution.py:521
  246.9 9.0 %shard_map.365 = (bf16[256,1536]{1,0:T(8,128)(2,1)}, bf16[256,1536]{1,0:T(8,128)(2,1)}, bf16[256,1536]{1,0:T(8,128)(2,1)}, bf16[256,1536]{1,0:T(8,128)(2,1)}) custom-call(s32[96]{0:T(128)} %select_reduce_fusion.order_ref, bf16[96,128,256]{2,1,0:T(8,128)(2,1)} %all-gather.4.cloned.1.call-done.refs_8_.upper_ref, ...), custom_call_target="tpu_custom_call" | custom-call | flops 3221225472 | bytes 8388608 | tf_op jit(solution)/shard_map/pallas_call | solution.py:460
  265.0 15.5 %shard_map.367 = (bf16[128,1536]{1,0:T(8,128)(2,1)}, bf16[2048,1024]{1,0:T(8,128)(2,1)}) custom-call(bf16[128,1536]{1,0:T(8,128)(2,1)} %get-tuple-element.159.q_ref, s32[128,1]{1,0:T(8,128)} %constant_dynamic-slice_fusion.4.rpos_ref, s32[1,1024]{1,0:T(1,128)} %bitcast.73, bf16[128,1536]{1,0:T(8,128)(2,1)} %get-tuple-element.166.ob_ref.refs_10_, ...), custom_call_target="tpu_custom_call" | custom-call | flops 8053063680 | bytes 8388608 | tf_op jit(solution)/shard_map/pallas_call | solution.py:789
  286.6 15.4 %shard_map.369 = (bf16[128,1536]{1,0:T(8,128)(2,1)}, bf16[2048,1024]{1,0:T(8,128)(2,1)}) custom-call(bf16[128,1536]{1,0:T(8,128)(2,1)} %get-tuple-element.167.q_ref, s32[128,1]{1,0:T(8,128)} %constant_dynamic-slice_fusion.4.rpos_ref, s32[1,1024]{1,0:T(1,128)} %bitcast.74, ...), custom_call_target="tpu_custom_call", output_to_operand_aliasing={{1}: (7, {})} | custom-call | flops 8053063680 | bytes 8388608 | tf_op jit(solution)/shard_map/pallas_call | solution.py:789
  308.5 9.3 %shard_map.370 = (bf16[98,48,128]{2,1,0:T(8,128)(2,1)}, bf16[98,48,128]{2,1,0:T(8,128)(2,1)}, bf16[96,48,128]{2,1,0:T(8,128)(2,1)}, bf16[96,48,128]{2,1,0:T(8,128)(2,1)}, bf16[1536,512]{1,0:T(8,128)(2,1)}) custom-call(s32[2]{0:T(128)} %pad_add_fusion.me_ref, bf16[256,1536]{1,0:T(8,128)(2,1)} %get-tuple-element.155.h_ref.refs_0_, ...), custom_call_target="tpu_custom_call" | custom-call | flops 2415919104 | bytes 16777216 | tf_op jit(solution)/shard_map/pallas_call | solution.py:646
  324.8 21.5 %collective-permute-done.55 = bf16[96,48,128]{2,1,0:T(8,128)(2,1)} collective-permute-done((bf16[96,48,128]{2,1,0:T(8,128)(2,1)}, bf16[96,48,128]{2,1,0:T(8,128)(2,1)}, u32[]{:S(2)}, u32[]{:S(2)}) %collective-permute-start.55) | collective-permute-done | bytes 1179680 | tf_op jit(solution)/shard_map/ppermute | solution.py:957
  349.9 13.4 %collective-permute-done.56 = bf16[48,48,128]{2,1,0:T(8,128)(2,1)} collective-permute-done((bf16[48,48,128]{2,1,0:T(8,128)(2,1)S(1)}, bf16[48,48,128]{2,1,0:T(8,128)(2,1)}, u32[]{:S(2)}, u32[]{:S(2)}) %collective-permute-start.56) | collective-permute-done | bytes 589856 | tf_op jit(solution)/shard_map/ppermute | solution.py:957
  375.6 10.3 %collective-permute-done.57 = bf16[256,1536]{1,0:T(8,128)(2,1)} collective-permute-done((bf16[256,1536]{1,0:T(8,128)(2,1)}, bf16[256,1536]{1,0:T(8,128)(2,1)}, u32[]{:S(2)}, u32[]{:S(2)}) %collective-permute-start.57) | collective-permute-done | bytes 786464 | tf_op jit(solution)/shard_map/ppermute | solution.py:957
  385.9 7.2 %shard_map.374 = (f32[2,128,1536]{2,1,0:T(8,128)}, f32[8,1536]{1,0:T(8,128)}) custom-call(f32[2,128,1536]{2,1,0:T(8,128)} %x_ref, f32[2,1536]{1,0:T(2,128)} %gain_ref.9, bf16[1536,2560]{1,0:T(8,128)(2,1)} %get-tuple-element.219.w_ref, f32[128,1536]{1,0:T(8,128)} %get-tuple-element.239.refs_0_, f32[128,1536]{1,0:T(8,128)} %get-tuple-element.240.refs_1_, ...), custom_call_target="tpu_custom_call" | custom-call | flops 805306368 | bytes 14680064 | tf_op jit(solution)/shard_map/pallas_call | solution.py:873
  403.1 12.9 %reduce-scatter.8.cloned.1.call-done.refs_1_ = bf16[12,192,128]{2,1,0:T(8,128)(2,1)} async-done(((bf16[96,192,128]{2,1,0:T(8,128)(2,1)}), bf16[12,192,128]{2,1,0:T(8,128)(2,1)}) %reduce-scatter.8.cloned.1.call-update) | async-done | bytes 589840 | tf_op jit(solution)/shard_map/reduce_scatter | solution.py:1233
  420.5 15.1 %shard_map.372 = (f32[12,192,256]{2,1,0:T(8,128)}, f32[12,192,256]{2,1,0:T(8,128)}, f32[12,192,256]{2,1,0:T(8,128)}, f32[12,192,256]{2,1,0:T(8,128)}) custom-call(f32[12,192,256]{2,1,0:T(8,128)} %bitcast.52, f32[12,192,256]{2,1,0:T(8,128)} %bitcast.58, f32[12,192,256]{2,1,0:T(8,128)} %bitcast.59, f32[12,192,192]{2,1,0:T(8,128)} %bitcast.60, ...), custom_call_target="tpu_custom_call" | custom-call | flops 1056964608 | bytes 25165824 | tf_op jit(solution)/shard_map/pallas_call | solution.py:912
  435.6 17.4 %collective-permute-done.64 = bf16[129,1536]{1,0:T(8,128)(2,1)S(1)} collective-permute-done((bf16[129,1536]{1,0:T(8,128)(2,1)S(1)}, bf16[129,1536]{1,0:T(8,128)(2,1)S(1)}, u32[]{:S(2)}, u32[]{:S(2)}) %collective-permute-start.64) | collective-permute-done | bytes 396320 | tf_op jit(solution)/shard_map/ppermute | solution.py:967
  464.1 14.2 %all-to-all-done = bf16[32,2,4608]{2,1,0:T(2,128)(2,1)S(1)} async-done(((bf16[32,2,4608]{2,1,0:T(2,128)(2,1)}), bf16[32,2,4608]{2,1,0:T(2,128)(2,1)S(1)}, u32[]{:S(2)}, u32[]{:S(2)}) %all-to-all-start) | async-done | bytes 589856 | tf_op jit(solution)/shard_map/all_to_all | solution.py:1256
  (372 shorter events, 167.4 us)
Async XLA Ops:
  7.2 93.6 %all-gather.4.cloned.1.call-start = ((), (), s32[]{:S(2)}) async-start(), calls=%async_computation.4 | async-start | bytes 7077888 | tf_op jit(solution)/shard_map/all_gather | solution.py:1121
  36.0 111.3 %all-gather.6.cloned.1.call-start = ((), (), s32[]{:S(2)}) async-start(), calls=%async_computation.5 | async-start | bytes 4718592 | tf_op jit(solution)/shard_map/all_gather | solution.py:1144
  100.8 85.8 %all-gather.8.cloned.1.call-start = ((), (), s32[]{:S(2)}) async-start(), calls=%async_computation.6 | async-start | bytes 3538944 | tf_op jit(solution)/shard_map/all_gather | solution.py:1146
  101.2 21.9 %collective-permute-start.28 = (bf16[256,1664]{1,0:T(8,128)(2,1)S(1)}, bf16[256,1664]{1,0:T(8,128)(2,1)}, u32[]{:S(2)}, u32[]{:S(2)}) collective-permute-start(bf16[256,1664]{1,0:T(8,128)(2,1)S(1)} %bitcast.62), channel_id=1, source_target_pairs={{0,1},{1,0},{2,3},{3,2},{4,5},{5,4},{6,7},{7,6},{8,9},{9,8},{10,11... | collective-permute-start | bytes 2555912 | tf_op jit(solution)/shard_map/ppermute | solution.py:957
  102.2 39.2 %collective-permute-start.29 = (bf16[256,1664]{1,0:T(8,128)(2,1)S(1)}, bf16[256,1664]{1,0:T(8,128)(2,1)}, u32[]{:S(2)}, u32[]{:S(2)}) collective-permute-start(bf16[256,1664]{1,0:T(8,128)(2,1)S(1)} %bitcast.63), channel_id=1, source_target_pairs={{0,2},{1,3},{2,0},{3,1},{4,6},{5,7},{6,4},{7,5},{8,10},{9,11},{10,... | collective-permute-start | bytes 2555912 | tf_op jit(solution)/shard_map/ppermute | solution.py:957
  103.8 37.7 %collective-permute-start.30 = (bf16[256,1664]{1,0:T(8,128)(2,1)S(1)}, bf16[256,1664]{1,0:T(8,128)(2,1)}, u32[]{:S(2)}, u32[]{:S(2)}) collective-permute-start(bf16[256,1664]{1,0:T(8,128)(2,1)S(1)} %bitcast.64), channel_id=1, source_target_pairs={{0,3},{1,2},{2,1},{3,0},{4,7},{5,6},{6,5},{7,4},{8,11},{9,10},{10,... | collective-permute-start | bytes 2555912 | tf_op jit(solution)/shard_map/ppermute | solution.py:957
  147.4 154.7 %reduce-scatter.4.cloned.1.call-start = ((), (), s32[]{:S(2)}) async-start(), calls=%async_computation.7 | async-start | bytes 5308416 | tf_op jit(solution)/shard_map/reduce_scatter | solution.py:1201
  147.7 36.4 %collective-permute-start.31 = (bf16[256,1536]{1,0:T(8,128)(2,1)S(1)}, bf16[256,1536]{1,0:T(8,128)(2,1)S(1)}, u32[]{:S(2)}, u32[]{:S(2)}) collective-permute-start(bf16[256,1536]{1,0:T(8,128)(2,1)S(1)} %copy-done.21), channel_id=1, source_target_pairs={{0,4},{4,0},{8,12},{12,8},{16,20},{20,16},{24,28},{28,24},{1,5},{5... | collective-permute-start | bytes 2359304 | tf_op jit(solution)/shard_map/ppermute | solution.py:962
  182.0 23.7 %collective-permute-start.40 = (bf16[128,1536]{1,0:T(8,128)(2,1)}, bf16[128,1536]{1,0:T(8,128)(2,1)}, u32[]{:S(2)}, u32[]{:S(2)}) collective-permute-start(bf16[128,1536]{1,0:T(8,128)(2,1)} %get-tuple-element.181.refs_0_.h2_ref), channel_id=1, source_target_pairs={{0,1},{1,0},{2,3},{3,2},{4,5},{5,4},{6,7},{7,6},{8,9},{9,8},{10,11... | collective-permute-start | bytes 1179656 | tf_op jit(solution)/shard_map/ppermute | solution.py:957
  183.2 23.0 %collective-permute-start.41 = (bf16[128,1536]{1,0:T(8,128)(2,1)}, bf16[128,1536]{1,0:T(8,128)(2,1)}, u32[]{:S(2)}, u32[]{:S(2)}) collective-permute-start(bf16[128,1536]{1,0:T(8,128)(2,1)} %get-tuple-element.181.refs_0_.h2_ref), channel_id=1, source_target_pairs={{0,2},{1,3},{2,0},{3,1},{4,6},{5,7},{6,4},{7,5},{8,10},{9,11},{10,... | collective-permute-start | bytes 1179656 | tf_op jit(solution)/shard_map/ppermute | solution.py:957
  184.0 22.2 %collective-permute-start.42 = (bf16[128,1536]{1,0:T(8,128)(2,1)}, bf16[128,1536]{1,0:T(8,128)(2,1)S(1)}, u32[]{:S(2)}, u32[]{:S(2)}) collective-permute-start(bf16[128,1536]{1,0:T(8,128)(2,1)} %get-tuple-element.181.refs_0_.h2_ref), channel_id=1, source_target_pairs={{0,3},{1,2},{2,1},{3,0},{4,7},{5,6},{6,5},{7,4},{8,11},{9,10},{10,... | collective-permute-start | bytes 1179656 | tf_op jit(solution)/shard_map/ppermute | solution.py:957
  202.6 23.7 %collective-permute-start.37 = (bf16[128,1664]{1,0:T(8,128)(2,1)}, bf16[128,1664]{1,0:T(8,128)(2,1)S(1)}, u32[]{:S(2)}, u32[]{:S(2)}) collective-permute-start(bf16[128,1664]{1,0:T(8,128)(2,1)} %get-tuple-element.174), channel_id=1, source_target_pairs={{0,1},{1,0},{2,3},{3,2},{4,5},{5,4},{6,7},{7,6},{8,9},{9,8},{10,11... | collective-permute-start | bytes 1277960 | tf_op jit(solution)/shard_map/ppermute | solution.py:957
  204.2 22.8 %collective-permute-start.38 = (bf16[128,1664]{1,0:T(8,128)(2,1)}, bf16[128,1664]{1,0:T(8,128)(2,1)S(1)}, u32[]{:S(2)}, u32[]{:S(2)}) collective-permute-start(bf16[128,1664]{1,0:T(8,128)(2,1)} %get-tuple-element.175), channel_id=1, source_target_pairs={{0,2},{1,3},{2,0},{3,1},{4,6},{5,7},{6,4},{7,5},{8,10},{9,11},{10,... | collective-permute-start | bytes 1277960 | tf_op jit(solution)/shard_map/ppermute | solution.py:957
  245.7 117.6 %reduce-scatter.6.cloned.1.call-start = ((), (), s32[]{:S(2)}) async-start(), calls=%async_computation.8 | async-start | bytes 4718592 | tf_op jit(solution)/shard_map/reduce_scatter | solution.py:1202
  256.0 24.5 %collective-permute-start.43 = (bf16[256,1536]{1,0:T(8,128)(2,1)}, bf16[256,1536]{1,0:T(8,128)(2,1)}, u32[]{:S(2)}, u32[]{:S(2)}) collective-permute-start(bf16[256,1536]{1,0:T(8,128)(2,1)} %get-tuple-element.194), channel_id=1, source_target_pairs={{0,1},{1,0},{2,3},{3,2},{4,5},{5,4},{6,7},{7,6},{8,9},{9,8},{10,11... | collective-permute-start | bytes 2359304 | tf_op jit(solution)/shard_map/ppermute | solution.py:957
  257.4 23.1 %collective-permute-start.44 = (bf16[256,1536]{1,0:T(8,128)(2,1)}, bf16[256,1536]{1,0:T(8,128)(2,1)}, u32[]{:S(2)}, u32[]{:S(2)}) collective-permute-start(bf16[256,1536]{1,0:T(8,128)(2,1)} %get-tuple-element.195), channel_id=1, source_target_pairs={{0,2},{1,3},{2,0},{3,1},{4,6},{5,7},{6,4},{7,5},{8,10},{9,11},{10,... | collective-permute-start | bytes 2359304 | tf_op jit(solution)/shard_map/ppermute | solution.py:957
  302.2 113.9 %reduce-scatter.8.cloned.1.call-start = ((), (), s32[]{:S(2)}) async-start(), calls=%async_computation.9 | async-start | bytes 5308416 | tf_op jit(solution)/shard_map/reduce_scatter | solution.py:1233
  317.9 28.8 %collective-permute-start.53 = (bf16[98,48,128]{2,1,0:T(8,128)(2,1)}, bf16[98,48,128]{2,1,0:T(8,128)(2,1)S(1)}, u32[]{:S(2)}, u32[]{:S(2)}) collective-permute-start(bf16[98,48,128]{2,1,0:T(8,128)(2,1)} %get-tuple-element.218), channel_id=1, source_target_pairs={{0,1},{1,0},{2,3},{3,2},{4,5},{5,4},{6,7},{7,6},{8,9},{9,8},{10,11... | collective-permute-start | bytes 3612680 | tf_op jit(solution)/shard_map/ppermute | solution.py:957
  318.1 28.3 %collective-permute-start.55 = (bf16[96,48,128]{2,1,0:T(8,128)(2,1)}, bf16[96,48,128]{2,1,0:T(8,128)(2,1)}, u32[]{:S(2)}, u32[]{:S(2)}) collective-permute-start(bf16[96,48,128]{2,1,0:T(8,128)(2,1)} %get-tuple-element.224), channel_id=1, source_target_pairs={{0,2},{1,3},{2,0},{3,1},{4,6},{5,7},{6,4},{7,5},{8,10},{9,11},{10,... | collective-permute-start | bytes 3538952 | tf_op jit(solution)/shard_map/ppermute | solution.py:957
  371.0 23.0 %collective-permute-start.59 = (bf16[32,48,128]{2,1,0:T(8,128)(2,1)}, bf16[32,48,128]{2,1,0:T(8,128)(2,1)}, u32[]{:S(2)}, u32[]{:S(2)}) collective-permute-start(bf16[32,48,128]{2,1,0:T(8,128)(2,1)} %get-tuple-element.237), channel_id=1, source_target_pairs={{0,1},{1,0},{2,3},{3,2},{4,5},{5,4},{6,7},{7,6},{8,9},{9,8},{10,11... | collective-permute-start | bytes 1179656 | tf_op jit(solution)/shard_map/ppermute | solution.py:957
  373.6 22.1 %collective-permute-start.61 = (bf16[32,48,128]{2,1,0:T(8,128)(2,1)}, bf16[32,48,128]{2,1,0:T(8,128)(2,1)S(1)}, u32[]{:S(2)}, u32[]{:S(2)}) collective-permute-start(bf16[32,48,128]{2,1,0:T(8,128)(2,1)} %get-tuple-element.245), channel_id=1, source_target_pairs={{0,2},{1,3},{2,0},{3,1},{4,6},{5,7},{6,4},{7,5},{8,10},{9,11},{10,... | collective-permute-start | bytes 1179656 | tf_op jit(solution)/shard_map/ppermute | solution.py:957
  417.0 36.1 %collective-permute-start.64 = (bf16[129,1536]{1,0:T(8,128)(2,1)S(1)}, bf16[129,1536]{1,0:T(8,128)(2,1)S(1)}, u32[]{:S(2)}, u32[]{:S(2)}) collective-permute-start(bf16[129,1536]{1,0:T(8,128)(2,1)S(1)} %get-tuple-element.271), channel_id=1, source_target_pairs={{0,16},{4,20},{8,24},{12,28},{16,0},{20,4},{24,8},{28,12},{1,17},{... | collective-permute-start | bytes 1188872 | tf_op jit(solution)/shard_map/ppermute | solution.py:967
  417.0 36.1 %collective-permute-start.65 = (bf16[129,1536]{1,0:T(8,128)(2,1)S(1)}, bf16[129,1536]{1,0:T(8,128)(2,1)S(1)}, u32[]{:S(2)}, u32[]{:S(2)}) collective-permute-start(bf16[129,1536]{1,0:T(8,128)(2,1)S(1)} %get-tuple-element.270), channel_id=1, source_target_pairs={{0,8},{4,12},{8,16},{12,20},{16,24},{20,28},{24,0},{28,4},{1,9},{5... | collective-permute-start | bytes 1188872 | tf_op jit(solution)/shard_map/ppermute | solution.py:967
  455.5 22.8 %all-to-all-start = ((bf16[32,2,4608]{2,1,0:T(2,128)(2,1)}), bf16[32,2,4608]{2,1,0:T(2,128)(2,1)S(1)}, u32[]{:S(2)}, u32[]{:S(2)}) async-start(bf16[32,2,4608]{2,1,0:T(2,128)(2,1)} %all_to_all.6), calls=%async_computation.3 | async-start | bytes 1179648 | tf_op jit(solution)/shard_map/all_to_all | solution.py:1256
  (126 other events, 1265.1 us)
Sparse Core Ops, SparseCore 0:
  36.2 64.5 all-gather.3
  102.4 44.9 all-gather.5
  149.6 36.9 all-gather.7
  245.3 53.5 reduce-scatter.3
  302.3 47.1 reduce-scatter.5
  363.4 52.6 reduce-scatter.7

commit v14 on v13

--- a/solution.py
+++ b/solution.py
@@ -1039,7 +1039,7 @@
 
 
 def sum_members(made, ready, members):
-    sums, seen = [], []
+    sums, seen, relays = [], [], []
     for half in range(2):
         sent, kept = made[2 * half : 2 * half + 2]
         hops, keeps = xor_plan(members, 1 - half)
@@ -1051,13 +1051,14 @@
             total = total + wide(got[:count])
             relay = (wide(kept[count:]) + wide(got[count:])).astype(low_type)
             second = to_partner(relay, keeps[1])
+            relays.append(relay)
             seen.append(second)
             total = total + wide(second)
         else:
             for place, hop in enumerate(hops):
                 total = total + wide(to_partner(sent[place * count : (place + 1) * count], hop))
         sums.append(total.astype(low_type).reshape(count, -1))
-    return jnp.concatenate(sums, axis=0), seen
+    return jnp.concatenate(sums, axis=0), seen, relays
 
 
 def sum_chips(rows, chip, chips):
@@ -1213,7 +1214,7 @@
     )
     h1_turned = early[4]
     parts_back = query_back(after(w_in, early[0]), dqs)
-    early_rows, early_seen = sum_members(early[:4], parts_back, shard_count)
+    early_rows, early_seen, early_relays = sum_members(early[:4], parts_back, shard_count)
     chip = ctx // 2
     late = gradient_pieces(
         shard_count,
@@ -1228,8 +1229,8 @@
     input_grad, gain_stat = input_back(
         after(tokens, late[0], arrived[3:]), norm_gains, w_in, dxs, parts_back, dkv
     )
-    late_rows, late_seen = sum_members(late[:4], input_grad, shard_count)
-    late_term = after(expert_terms[1], dkv, early_seen)
+    late_rows, _, _ = sum_members(late[:4], input_grad, shard_count)
+    late_term = after(expert_terms[1], dkv, early_relays)
     expert_sums.append(lax.psum_scatter(late_term, "ctx", scatter_dimension=0, tiled=True))
     expert_grad, expert_new, expert_moment_new, expert_second_new = rotate(
         expert_weight[0], expert_sums, expert_moment[0], expert_second[0], expert_left[0], expert_right[0]

time: 503 us -> 492 us (0.978)
  waiting for transfers between devices: 192 us -> 174 us
    reduce_scatter x1, waiting for transfers between devices: 12.9 us -> 0.17 us  [shards(): lax.psum_scatter(late_term, 'ctx', scatter_dimension=0, tiled=True)]
    ppermute x37, waiting for transfers between devices: 112 us -> 107 us  [to_partner(): return lax.ppermute(array, 'shard', [(i, i ^ offset) for i in range(count)])]
  transfers between devices with their start and end apart: 73 -> 73, of which waited for: 34 -> 35; matrix products, arithmetic and copies ran while one was open for 5% -> 5% of each run, Pallas kernels for 38% -> 39%
where the time goes in v14:
time: 492 us; the launch traced here: 486 us
  Pallas kernels  195 us (40%)
  waiting for transfers between devices  174 us (35%)
  starting transfers between devices  57.8 us (12%)
  local copies, waits for them, and re-layouts  25 us (5%)
  other arithmetic  18.4 us (4%)
  between operations  15.8 us (3%)
    ppermute x37, waiting for transfers between devices, to_partner(): return lax.ppermute(array, 'shard', [(i, i ^ offset) for i in range(count)])  107 us
    ppermute x37, starting transfers between devices, to_partner(): return lax.ppermute(array, 'shard', [(i, i ^ offset) for i in range(count)])  42 us
    ppermute x6, waiting for transfers between devices, to_chip(): lax.ppermute(array, 'ctx', [(i, (i + 2 * offset) % count) for i in range(...  35.2 us
    pallas_call x2, Pallas kernels, run_expert(): call(functools.partial(expert_kernel, sources, micro), tuple([shaped((row...  32.4 us
    pallas_call x2, Pallas kernels, attend_back(): pl.pallas_call(functools.partial(attend_back_kernel, micro), out_shape=(s...  31 us
    pallas_call x2, Pallas kernels, attend(): call(functools.partial(attend_kernel, micro), (shaped((rows, width), low_...  25.5 us
    pallas_call x2, Pallas kernels, rotate(): pl.pallas_call(rotate_kernel, grid=(count,), out_shape=(shaped(weight.sha...  20.9 us
    pallas_call x1, Pallas kernels, outer_blocks(): call(functools.partial(outer_kernel, groups, cols // BC), (shaped((blocks...  18 us
  transfers between devices with their start and end apart: 73, of which 35 were waited for; matrix products, arithmetic and copies ran while one was open for 5% of the time, Pallas kernels for 39%

profile of v14, /device:TPU:0, one launch (start us, length us, event | category | flops | bytes accessed | tf_op | source)
XLA Modules:
  0.0 486.0 jit_solution(6672419259510297842)
XLA Ops:
  15.0 7.7 %collective-permute-done.7.refs_11_ = bf16[4,192,256]{2,1,0:T(8,128)(2,1)S(1)} collective-permute-done((bf16[4,192,256]{2,1,0:T(8,128)(2,1)S(1)}, bf16[4,192,256]{2,1,0:T(8,128)(2,1)S(1)}, u32[]{:S(2)}, u32[]{:S(2)}) %collective-permute-start.7) | collective-permute-done | bytes 393248 | tf_op jit(solution)/shard_map/ppermute | solution.py:967
  24.7 7.1 %collective-permute-done.3.refs_7_ = bf16[4,192,256]{2,1,0:T(8,128)(2,1)S(1)} collective-permute-done((bf16[4,192,256]{2,1,0:T(8,128)(2,1)S(1)}, bf16[4,192,256]{2,1,0:T(8,128)(2,1)S(1)}, u32[]{:S(2)}, u32[]{:S(2)}) %collective-permute-start.3) | collective-permute-done | bytes 393248 | tf_op jit(solution)/shard_map/ppermute | solution.py:957
  45.3 7.0 %collective-permute-done.18 = bf16[4,192,256]{2,1,0:T(8,128)(2,1)S(1)} collective-permute-done((bf16[4,192,256]{2,1,0:T(8,128)(2,1)S(1)}, bf16[4,192,256]{2,1,0:T(8,128)(2,1)S(1)}, u32[]{:S(2)}, u32[]{:S(2)}) %collective-permute-start.18) | collective-permute-done | bytes 393248 | tf_op jit(solution)/shard_map/ppermute | solution.py:967
  57.3 11.3 %collective-permute-done.22.refs_25_ = bf16[8,192,256]{2,1,0:T(8,128)(2,1)S(1)} collective-permute-done((bf16[8,192,256]{2,1,0:T(8,128)(2,1)S(1)}, bf16[8,192,256]{2,1,0:T(8,128)(2,1)S(1)}, u32[]{:S(2)}, u32[]{:S(2)}) %collective-permute-start.22) | collective-permute-done | bytes 786464 | tf_op jit(solution)/shard_map/ppermute | solution.py:957
  85.3 12.3 %shard_map.358 = (bf16[256,1536]{1,0:T(8,128)(2,1)}, bf16[256,1024]{1,0:T(8,128)(2,1)}, bf16[1536,2560]{1,0:T(8,128)(2,1)}, bf16[1536,1536]{1,0:T(8,128)(2,1)}) custom-call(s32[128]{0:T(128)} %order_ref.1, s32[2]{0:T(128)} %pad_add_fusion.me_ref, f32[128,1536]{1,0:T(8,128)} %get-tuple-element.277.refs_0_.x_ref, ...), custom_call_target="tpu_custom_call" | custom-call | flops 805306368 | bytes 25165824 | tf_op jit(solution)/shard_map/pallas_call | solution.py:192
  112.5 10.9 %collective-permute-done.28.refs_5_ = bf16[256,1664]{1,0:T(8,128)(2,1)} collective-permute-done((bf16[256,1664]{1,0:T(8,128)(2,1)S(1)}, bf16[256,1664]{1,0:T(8,128)(2,1)}, u32[]{:S(2)}, u32[]{:S(2)}) %collective-permute-start.28) | collective-permute-done | bytes 852000 | tf_op jit(solution)/shard_map/ppermute | solution.py:957
  123.4 18.3 %collective-permute-done.29.refs_6_ = bf16[256,1664]{1,0:T(8,128)(2,1)} collective-permute-done((bf16[256,1664]{1,0:T(8,128)(2,1)S(1)}, bf16[256,1664]{1,0:T(8,128)(2,1)}, u32[]{:S(2)}, u32[]{:S(2)}) %collective-permute-start.29) | collective-permute-done | bytes 852000 | tf_op jit(solution)/shard_map/ppermute | solution.py:957
  148.2 12.7 %shard_map.360 = (bf16[128,1536]{1,0:T(8,128)(2,1)}, f32[384,128]{1,0:T(8,128)}, f32[128,1536]{1,0:T(8,128)}, bf16[128,1536]{1,0:T(8,128)(2,1)}) custom-call(bf16[128,1536]{1,0:T(8,128)(2,1)} %get-tuple-element.159.q_ref, s32[128,1]{1,0:T(8,128)} %constant_dynamic-slice_fusion.4.rpos_ref, s32[1,1024]{1,0:T(1,128)} %bitcast.71, ...), custom_call_target="tpu_custom_call" | custom-call | flops 3221225472 | bytes 8388608 | tf_op jit(solution)/shard_map/pallas_call | solution.py:306
  164.5 12.8 %shard_map.361 = (bf16[128,1536]{1,0:T(8,128)(2,1)}, f32[384,128]{1,0:T(8,128)}, f32[128,1536]{1,0:T(8,128)}, bf16[128,1536]{1,0:T(8,128)(2,1)}) custom-call(bf16[128,1536]{1,0:T(8,128)(2,1)} %get-tuple-element.167.q_ref, s32[128,1]{1,0:T(8,128)} %constant_dynamic-slice_fusion.4.rpos_ref, s32[1,1024]{1,0:T(1,128)} %bitcast.72, ...), custom_call_target="tpu_custom_call" | custom-call | flops 3221225472 | bytes 8388608 | tf_op jit(solution)/shard_map/pallas_call | solution.py:306
  186.9 16.0 %shard_map.362 = (bf16[128,1664]{1,0:T(8,128)(2,1)}, bf16[128,1664]{1,0:T(8,128)(2,1)}, bf16[128,1664]{1,0:T(8,128)(2,1)}, bf16[128,1664]{1,0:T(8,128)(2,1)}, bf...) custom-call(s32[96]{0:T(128)} %select_reduce_fusion.order_ref, ...), custom_call_target="tpu_custom_call" | custom-call | flops 8053063680 | bytes 20971520 | tf_op jit(solution)/shard_map/pallas_call | solution.py:406
  206.7 16.4 %shard_map.363 = (bf16[128,1664]{1,0:T(8,128)(2,1)}, bf16[128,1664]{1,0:T(8,128)(2,1)}, bf16[128,1664]{1,0:T(8,128)(2,1)}, bf16[128,1664]{1,0:T(8,128)(2,1)}, bf...) custom-call(s32[96]{0:T(128)} %select_reduce_fusion.order_ref, ...), custom_call_target="tpu_custom_call" | custom-call | flops 8053063680 | bytes 20971520 | tf_op jit(solution)/shard_map/pallas_call | solution.py:406
  226.6 18.0 %shard_map.364 = (bf16[96,192,128]{2,1,0:T(8,128)(2,1)}, bf16[96,192,128]{2,1,0:T(8,128)(2,1)}) custom-call(s32[96]{0:T(128)} %select_reduce_fusion.order_ref, bf16[512,1536]{1,0:T(8,128)(2,1)} %get-tuple-element.178.refs_0_, bf16[512,1536]{1,0:T(8,128)(2,1)} %get-tuple-element.182.refs_1_, bf16[512,1664]{1,0:T(8,128)(2,1)} %get-tuple-element.183.refs_2_, ...), custom_call_target="tpu_custom_call" | custom-call | flops 9663676416 | bytes 22282240 | tf_op jit(solution)/shard_map/pallas_call | solution.py:521
  246.7 9.0 %shard_map.365 = (bf16[256,1536]{1,0:T(8,128)(2,1)}, bf16[256,1536]{1,0:T(8,128)(2,1)}, bf16[256,1536]{1,0:T(8,128)(2,1)}, bf16[256,1536]{1,0:T(8,128)(2,1)}) custom-call(s32[96]{0:T(128)} %select_reduce_fusion.order_ref, bf16[96,128,256]{2,1,0:T(8,128)(2,1)} %all-gather.4.cloned.1.call-done.refs_8_.upper_ref, ...), custom_call_target="tpu_custom_call" | custom-call | flops 3221225472 | bytes 8388608 | tf_op jit(solution)/shard_map/pallas_call | solution.py:460
  264.5 15.5 %shard_map.367 = (bf16[128,1536]{1,0:T(8,128)(2,1)}, bf16[2048,1024]{1,0:T(8,128)(2,1)}) custom-call(bf16[128,1536]{1,0:T(8,128)(2,1)} %get-tuple-element.159.q_ref, s32[128,1]{1,0:T(8,128)} %constant_dynamic-slice_fusion.4.rpos_ref, s32[1,1024]{1,0:T(1,128)} %bitcast.73, bf16[128,1536]{1,0:T(8,128)(2,1)} %get-tuple-element.166.ob_ref.refs_10_, ...), custom_call_target="tpu_custom_call" | custom-call | flops 8053063680 | bytes 8388608 | tf_op jit(solution)/shard_map/pallas_call | solution.py:789
  280.0 6.6 %shard_map.368 = (f32[128,1536]{1,0:T(8,128)}, bf16[128,1536]{1,0:T(8,128)(2,1)}, bf16[128,1536]{1,0:T(8,128)(2,1)}, f32[16,1536]{1,0:T(8,128)}) custom-call(s32[2]{0:T(128)} %pad_add_fusion.me_ref, f32[128,1536]{1,0:T(8,128)} %get-tuple-element.207.x2_ref, f32[128,1536]{1,0:T(8,128)} %get-tuple-element.274.cot_ref, ...), custom_call_target="tpu_custom_call" | custom-call | flops 603979776 | bytes 10485760 | tf_op jit(solution)/shard_map/pallas_call | solution.py:705
  286.7 15.5 %shard_map.369 = (bf16[128,1536]{1,0:T(8,128)(2,1)}, bf16[2048,1024]{1,0:T(8,128)(2,1)}) custom-call(bf16[128,1536]{1,0:T(8,128)(2,1)} %get-tuple-element.167.q_ref, s32[128,1]{1,0:T(8,128)} %constant_dynamic-slice_fusion.4.rpos_ref, s32[1,1024]{1,0:T(1,128)} %bitcast.74, ...), custom_call_target="tpu_custom_call", output_to_operand_aliasing={{1}: (7, {})} | custom-call | flops 8053063680 | bytes 8388608 | tf_op jit(solution)/shard_map/pallas_call | solution.py:789
  308.8 9.4 %shard_map.370 = (bf16[98,48,128]{2,1,0:T(8,128)(2,1)}, bf16[98,48,128]{2,1,0:T(8,128)(2,1)}, bf16[96,48,128]{2,1,0:T(8,128)(2,1)}, bf16[96,48,128]{2,1,0:T(8,128)(2,1)}, bf16[1536,512]{1,0:T(8,128)(2,1)}) custom-call(s32[2]{0:T(128)} %pad_add_fusion.me_ref, bf16[256,1536]{1,0:T(8,128)(2,1)} %get-tuple-element.155.h_ref.refs_0_, ...), custom_call_target="tpu_custom_call" | custom-call | flops 2415919104 | bytes 16777216 | tf_op jit(solution)/shard_map/pallas_call | solution.py:646
  325.4 21.2 %collective-permute-done.55 = bf16[96,48,128]{2,1,0:T(8,128)(2,1)} collective-permute-done((bf16[96,48,128]{2,1,0:T(8,128)(2,1)}, bf16[96,48,128]{2,1,0:T(8,128)(2,1)}, u32[]{:S(2)}, u32[]{:S(2)}) %collective-permute-start.55) | collective-permute-done | bytes 1179680 | tf_op jit(solution)/shard_map/ppermute | solution.py:957
  352.5 12.2 %collective-permute-done.56 = bf16[48,48,128]{2,1,0:T(8,128)(2,1)S(1)} collective-permute-done((bf16[48,48,128]{2,1,0:T(8,128)(2,1)}, bf16[48,48,128]{2,1,0:T(8,128)(2,1)S(1)}, u32[]{:S(2)}, u32[]{:S(2)}) %collective-permute-start.56) | collective-permute-done | bytes 589856 | tf_op jit(solution)/shard_map/ppermute | solution.py:957
  376.7 11.3 %collective-permute-done.57 = bf16[256,1536]{1,0:T(8,128)(2,1)S(1)} collective-permute-done((bf16[256,1536]{1,0:T(8,128)(2,1)}, bf16[256,1536]{1,0:T(8,128)(2,1)S(1)}, u32[]{:S(2)}, u32[]{:S(2)}) %collective-permute-start.57) | collective-permute-done | bytes 786464 | tf_op jit(solution)/shard_map/ppermute | solution.py:957
  388.0 7.4 %shard_map.374 = (f32[2,128,1536]{2,1,0:T(8,128)}, f32[8,1536]{1,0:T(8,128)}) custom-call(f32[2,128,1536]{2,1,0:T(8,128)} %x_ref, f32[2,1536]{1,0:T(2,128)} %gain_ref.9, bf16[1536,2560]{1,0:T(8,128)(2,1)} %get-tuple-element.219.w_ref, f32[128,1536]{1,0:T(8,128)} %get-tuple-element.239.refs_0_, f32[128,1536]{1,0:T(8,128)} %get-tuple-element.240.refs_1_, ...), custom_call_target="tpu_custom_call" | custom-call | flops 805306368 | bytes 14680064 | tf_op jit(solution)/shard_map/pallas_call | solution.py:873
  411.0 15.1 %shard_map.372 = (f32[12,192,256]{2,1,0:T(8,128)}, f32[12,192,256]{2,1,0:T(8,128)}, f32[12,192,256]{2,1,0:T(8,128)}, f32[12,192,256]{2,1,0:T(8,128)}) custom-call(f32[12,192,256]{2,1,0:T(8,128)} %bitcast.52, f32[12,192,256]{2,1,0:T(8,128)} %bitcast.58, f32[12,192,256]{2,1,0:T(8,128)} %bitcast.59, f32[12,192,192]{2,1,0:T(8,128)} %bitcast.60, ...), custom_call_target="tpu_custom_call" | custom-call | flops 1056964608 | bytes 25165824 | tf_op jit(solution)/shard_map/pallas_call | solution.py:912
  426.1 17.5 %collective-permute-done.64 = bf16[129,1536]{1,0:T(8,128)(2,1)S(1)} collective-permute-done((bf16[129,1536]{1,0:T(8,128)(2,1)S(1)}, bf16[129,1536]{1,0:T(8,128)(2,1)S(1)}, u32[]{:S(2)}, u32[]{:S(2)}) %collective-permute-start.64) | collective-permute-done | bytes 396320 | tf_op jit(solution)/shard_map/ppermute | solution.py:967
  453.8 14.1 %all-to-all-done = bf16[32,2,4608]{2,1,0:T(2,128)(2,1)S(1)} async-done(((bf16[32,2,4608]{2,1,0:T(2,128)(2,1)}), bf16[32,2,4608]{2,1,0:T(2,128)(2,1)S(1)}, u32[]{:S(2)}, u32[]{:S(2)}) %all-to-all-start) | async-done | bytes 589856 | tf_op jit(solution)/shard_map/all_to_all | solution.py:1257
  (380 shorter events, 164.9 us)
Async XLA Ops:
  7.2 93.8 %all-gather.4.cloned.1.call-start = ((), (), s32[]{:S(2)}) async-start(), calls=%async_computation.4 | async-start | bytes 7077888 | tf_op jit(solution)/shard_map/all_gather | solution.py:1122
  35.7 111.9 %all-gather.6.cloned.1.call-start = ((), (), s32[]{:S(2)}) async-start(), calls=%async_computation.5 | async-start | bytes 4718592 | tf_op jit(solution)/shard_map/all_gather | solution.py:1145
  101.1 85.8 %all-gather.8.cloned.1.call-start = ((), (), s32[]{:S(2)}) async-start(), calls=%async_computation.6 | async-start | bytes 3538944 | tf_op jit(solution)/shard_map/all_gather | solution.py:1147
  101.4 21.9 %collective-permute-start.28 = (bf16[256,1664]{1,0:T(8,128)(2,1)S(1)}, bf16[256,1664]{1,0:T(8,128)(2,1)}, u32[]{:S(2)}, u32[]{:S(2)}) collective-permute-start(bf16[256,1664]{1,0:T(8,128)(2,1)S(1)} %bitcast.62), channel_id=1, source_target_pairs={{0,1},{1,0},{2,3},{3,2},{4,5},{5,4},{6,7},{7,6},{8,9},{9,8},{10,11... | collective-permute-start | bytes 2555912 | tf_op jit(solution)/shard_map/ppermute | solution.py:957
  102.5 39.2 %collective-permute-start.29 = (bf16[256,1664]{1,0:T(8,128)(2,1)S(1)}, bf16[256,1664]{1,0:T(8,128)(2,1)}, u32[]{:S(2)}, u32[]{:S(2)}) collective-permute-start(bf16[256,1664]{1,0:T(8,128)(2,1)S(1)} %bitcast.63), channel_id=1, source_target_pairs={{0,2},{1,3},{2,0},{3,1},{4,6},{5,7},{6,4},{7,5},{8,10},{9,11},{10,... | collective-permute-start | bytes 2555912 | tf_op jit(solution)/shard_map/ppermute | solution.py:957
  104.0 37.7 %collective-permute-start.30 = (bf16[256,1664]{1,0:T(8,128)(2,1)S(1)}, bf16[256,1664]{1,0:T(8,128)(2,1)}, u32[]{:S(2)}, u32[]{:S(2)}) collective-permute-start(bf16[256,1664]{1,0:T(8,128)(2,1)S(1)} %bitcast.64), channel_id=1, source_target_pairs={{0,3},{1,2},{2,1},{3,0},{4,7},{5,6},{6,5},{7,4},{8,11},{9,10},{10,... | collective-permute-start | bytes 2555912 | tf_op jit(solution)/shard_map/ppermute | solution.py:957
  147.7 154.6 %reduce-scatter.4.cloned.1.call-start = ((), (), s32[]{:S(2)}) async-start(), calls=%async_computation.7 | async-start | bytes 5308416 | tf_op jit(solution)/shard_map/reduce_scatter | solution.py:1202
  147.9 36.3 %collective-permute-start.31 = (bf16[256,1536]{1,0:T(8,128)(2,1)S(1)}, bf16[256,1536]{1,0:T(8,128)(2,1)S(1)}, u32[]{:S(2)}, u32[]{:S(2)}) collective-permute-start(bf16[256,1536]{1,0:T(8,128)(2,1)S(1)} %copy-done.22), channel_id=1, source_target_pairs={{0,4},{4,0},{8,12},{12,8},{16,20},{20,16},{24,28},{28,24},{1,5},{5... | collective-permute-start | bytes 2359304 | tf_op jit(solution)/shard_map/ppermute | solution.py:962
  182.2 23.6 %collective-permute-start.40 = (bf16[128,1536]{1,0:T(8,128)(2,1)}, bf16[128,1536]{1,0:T(8,128)(2,1)S(1)}, u32[]{:S(2)}, u32[]{:S(2)}) collective-permute-start(bf16[128,1536]{1,0:T(8,128)(2,1)} %get-tuple-element.181.refs_0_.h2_ref), channel_id=1, source_target_pairs={{0,1},{1,0},{2,3},{3,2},{4,5},{5,4},{6,7},{7,6},{8,9},{9,8},{10,11... | collective-permute-start | bytes 1179656 | tf_op jit(solution)/shard_map/ppermute | solution.py:957
  183.4 23.0 %collective-permute-start.41 = (bf16[128,1536]{1,0:T(8,128)(2,1)}, bf16[128,1536]{1,0:T(8,128)(2,1)}, u32[]{:S(2)}, u32[]{:S(2)}) collective-permute-start(bf16[128,1536]{1,0:T(8,128)(2,1)} %get-tuple-element.181.refs_0_.h2_ref), channel_id=1, source_target_pairs={{0,2},{1,3},{2,0},{3,1},{4,6},{5,7},{6,4},{7,5},{8,10},{9,11},{10,... | collective-permute-start | bytes 1179656 | tf_op jit(solution)/shard_map/ppermute | solution.py:957
  184.3 22.2 %collective-permute-start.42 = (bf16[128,1536]{1,0:T(8,128)(2,1)}, bf16[128,1536]{1,0:T(8,128)(2,1)}, u32[]{:S(2)}, u32[]{:S(2)}) collective-permute-start(bf16[128,1536]{1,0:T(8,128)(2,1)} %get-tuple-element.181.refs_0_.h2_ref), channel_id=1, source_target_pairs={{0,3},{1,2},{2,1},{3,0},{4,7},{5,6},{6,5},{7,4},{8,11},{9,10},{10,... | collective-permute-start | bytes 1179656 | tf_op jit(solution)/shard_map/ppermute | solution.py:957
  202.9 23.0 %collective-permute-start.37 = (bf16[128,1664]{1,0:T(8,128)(2,1)}, bf16[128,1664]{1,0:T(8,128)(2,1)S(1)}, u32[]{:S(2)}, u32[]{:S(2)}) collective-permute-start(bf16[128,1664]{1,0:T(8,128)(2,1)} %get-tuple-element.174), channel_id=1, source_target_pairs={{0,1},{1,0},{2,3},{3,2},{4,5},{5,4},{6,7},{7,6},{8,9},{9,8},{10,11... | collective-permute-start | bytes 1277960 | tf_op jit(solution)/shard_map/ppermute | solution.py:957
  204.4 22.2 %collective-permute-start.38 = (bf16[128,1664]{1,0:T(8,128)(2,1)}, bf16[128,1664]{1,0:T(8,128)(2,1)S(1)}, u32[]{:S(2)}, u32[]{:S(2)}) collective-permute-start(bf16[128,1664]{1,0:T(8,128)(2,1)} %get-tuple-element.175), channel_id=1, source_target_pairs={{0,2},{1,3},{2,0},{3,1},{4,6},{5,7},{6,4},{7,5},{8,10},{9,11},{10,... | collective-permute-start | bytes 1277960 | tf_op jit(solution)/shard_map/ppermute | solution.py:957
  245.4 104.0 %reduce-scatter.6.cloned.1.call-start = ((), (), s32[]{:S(2)}) async-start(), calls=%async_computation.8 | async-start | bytes 4718592 | tf_op jit(solution)/shard_map/reduce_scatter | solution.py:1203
  255.7 24.3 %collective-permute-start.43 = (bf16[256,1536]{1,0:T(8,128)(2,1)}, bf16[256,1536]{1,0:T(8,128)(2,1)S(1)}, u32[]{:S(2)}, u32[]{:S(2)}) collective-permute-start(bf16[256,1536]{1,0:T(8,128)(2,1)} %get-tuple-element.194), channel_id=1, source_target_pairs={{0,1},{1,0},{2,3},{3,2},{4,5},{5,4},{6,7},{7,6},{8,9},{9,8},{10,11... | collective-permute-start | bytes 2359304 | tf_op jit(solution)/shard_map/ppermute | solution.py:957
  256.9 23.1 %collective-permute-start.44 = (bf16[256,1536]{1,0:T(8,128)(2,1)}, bf16[256,1536]{1,0:T(8,128)(2,1)S(1)}, u32[]{:S(2)}, u32[]{:S(2)}) collective-permute-start(bf16[256,1536]{1,0:T(8,128)(2,1)} %get-tuple-element.195), channel_id=1, source_target_pairs={{0,2},{1,3},{2,0},{3,1},{4,6},{5,7},{6,4},{7,5},{8,10},{9,11},{10,... | collective-permute-start | bytes 2359304 | tf_op jit(solution)/shard_map/ppermute | solution.py:957
  302.4 102.3 %reduce-scatter.8.cloned.1.call-start = ((), (), s32[]{:S(2)}) async-start(), calls=%async_computation.9 | async-start | bytes 5308416 | tf_op jit(solution)/shard_map/reduce_scatter | solution.py:1234
  318.1 28.5 %collective-permute-start.55 = (bf16[96,48,128]{2,1,0:T(8,128)(2,1)}, bf16[96,48,128]{2,1,0:T(8,128)(2,1)}, u32[]{:S(2)}, u32[]{:S(2)}) collective-permute-start(bf16[96,48,128]{2,1,0:T(8,128)(2,1)} %get-tuple-element.224), channel_id=1, source_target_pairs={{0,2},{1,3},{2,0},{3,1},{4,6},{5,7},{6,4},{7,5},{8,10},{9,11},{10,... | collective-permute-start | bytes 3538952 | tf_op jit(solution)/shard_map/ppermute | solution.py:957
  318.5 30.3 %collective-permute-start.53 = (bf16[98,48,128]{2,1,0:T(8,128)(2,1)}, bf16[98,48,128]{2,1,0:T(8,128)(2,1)S(1)}, u32[]{:S(2)}, u32[]{:S(2)}) collective-permute-start(bf16[98,48,128]{2,1,0:T(8,128)(2,1)} %get-tuple-element.218), channel_id=1, source_target_pairs={{0,1},{1,0},{2,3},{3,2},{4,5},{5,4},{6,7},{7,6},{8,9},{9,8},{10,11... | collective-permute-start | bytes 3612680 | tf_op jit(solution)/shard_map/ppermute | solution.py:957
  372.4 23.0 %collective-permute-start.59 = (bf16[32,48,128]{2,1,0:T(8,128)(2,1)}, bf16[32,48,128]{2,1,0:T(8,128)(2,1)}, u32[]{:S(2)}, u32[]{:S(2)}) collective-permute-start(bf16[32,48,128]{2,1,0:T(8,128)(2,1)} %get-tuple-element.237), channel_id=1, source_target_pairs={{0,1},{1,0},{2,3},{3,2},{4,5},{5,4},{6,7},{7,6},{8,9},{9,8},{10,11... | collective-permute-start | bytes 1179656 | tf_op jit(solution)/shard_map/ppermute | solution.py:957
  375.9 22.3 %collective-permute-start.61 = (bf16[32,48,128]{2,1,0:T(8,128)(2,1)}, bf16[32,48,128]{2,1,0:T(8,128)(2,1)S(1)}, u32[]{:S(2)}, u32[]{:S(2)}) collective-permute-start(bf16[32,48,128]{2,1,0:T(8,128)(2,1)} %get-tuple-element.245), channel_id=1, source_target_pairs={{0,2},{1,3},{2,0},{3,1},{4,6},{5,7},{6,4},{7,5},{8,10},{9,11},{10,... | collective-permute-start | bytes 1179656 | tf_op jit(solution)/shard_map/ppermute | solution.py:957
  406.7 37.0 %collective-permute-start.64 = (bf16[129,1536]{1,0:T(8,128)(2,1)S(1)}, bf16[129,1536]{1,0:T(8,128)(2,1)S(1)}, u32[]{:S(2)}, u32[]{:S(2)}) collective-permute-start(bf16[129,1536]{1,0:T(8,128)(2,1)S(1)} %get-tuple-element.271), channel_id=1, source_target_pairs={{0,16},{4,20},{8,24},{12,28},{16,0},{20,4},{24,8},{28,12},{1,17},{... | collective-permute-start | bytes 1188872 | tf_op jit(solution)/shard_map/ppermute | solution.py:967
  407.3 36.3 %collective-permute-start.65 = (bf16[129,1536]{1,0:T(8,128)(2,1)S(1)}, bf16[129,1536]{1,0:T(8,128)(2,1)S(1)}, u32[]{:S(2)}, u32[]{:S(2)}) collective-permute-start(bf16[129,1536]{1,0:T(8,128)(2,1)S(1)} %get-tuple-element.270), channel_id=1, source_target_pairs={{0,8},{4,12},{8,16},{12,20},{16,24},{20,28},{24,0},{28,4},{1,9},{5... | collective-permute-start | bytes 1188872 | tf_op jit(solution)/shard_map/ppermute | solution.py:967
  446.1 21.8 %all-to-all-start = ((bf16[32,2,4608]{2,1,0:T(2,128)(2,1)}), bf16[32,2,4608]{2,1,0:T(2,128)(2,1)S(1)}, u32[]{:S(2)}, u32[]{:S(2)}) async-start(bf16[32,2,4608]{2,1,0:T(2,128)(2,1)} %all_to_all.6), calls=%async_computation.3 | async-start | bytes 1179648 | tf_op jit(solution)/shard_map/all_to_all | solution.py:1257
  (130 other events, 1307.6 us)
Sparse Core Ops, SparseCore 0:
  35.8 65.1 all-gather.3
  102.6 44.9 all-gather.5
  149.9 36.9 all-gather.7
  244.8 53.6 reduce-scatter.3
  302.5 46.8 reduce-scatter.5
  351.6 53.0 reduce-scatter.7

commit v15 on v14

--- a/solution.py
+++ b/solution.py
@@ -40,14 +40,14 @@
     return lax.dot_general(left_side, right_side, dims, preferred_element_type=jnp.float32)
 
 
-def call(kernel, out_shapes, in_specs, out_specs, scratch, flops, moved):
+def call(kernel, out_shapes, in_specs, out_specs, scratch, flops, moved, limit=VMEM_LIMIT):
     return pl.pallas_call(
         kernel,
         out_shape=out_shapes,
         in_specs=in_specs,
         out_specs=out_specs,
         scratch_shapes=scratch,
-        compiler_params=pltpu.CompilerParams(vmem_limit_bytes=VMEM_LIMIT),
+        compiler_params=pltpu.CompilerParams(vmem_limit_bytes=limit),
         cost_estimate=pl.CostEstimate(flops=flops, bytes_accessed=moved, transcendentals=0),
     )
 
@@ -715,6 +715,7 @@
         [pltpu.VMEM((width, HEADS * HD), low_type), pltpu.SemaphoreType.DMA],
         2 * rows * width * HEADS * HD,
         10 * MIB,
+        24 * MIB,
     )(me, x2, cot, h2, gains, router, w, *backs)
 
 
@@ -798,7 +799,7 @@
             pltpu.SemaphoreType.DMA((2,)),
         ],
         input_output_aliases=aliases,
-        compiler_params=pltpu.CompilerParams(vmem_limit_bytes=VMEM_LIMIT),
+        compiler_params=pltpu.CompilerParams(vmem_limit_bytes=40 * MIB),
         cost_estimate=pl.CostEstimate(
             flops=40 * rows * length * width, bytes_accessed=8 * MIB, transcendentals=0
         ),
@@ -917,7 +918,7 @@
         + [spec(BR, BR), spec(BC, BC)]
         + [spec(BR, part.shape[2]) for part in gradients],
         out_specs=(block,) * 4,
-        compiler_params=pltpu.CompilerParams(vmem_limit_bytes=VMEM_LIMIT),
+        compiler_params=pltpu.CompilerParams(vmem_limit_bytes=VMEM_LIMIT if count > 8 else 16 * MIB),
         cost_estimate=pl.CostEstimate(
             flops=4 * count * BR * BC * (BR + BC),
             bytes_accessed=count * 2 * MIB,

time: 492 us -> 500 us (1.016)
  local copies, waits for them, and re-layouts: 25 us -> 44.6 us
  Pallas kernels: 195 us -> 177 us
    unnamed x165 -> x229, local copies, waits for them, and re-layouts: 8.26 us -> 24 us
    pallas_call x2, Pallas kernels: 31 us -> 22.2 us  [attend_back(): pl.pallas_call(functools.partial(attend_back_kernel, micro), out_shape=(s...]
    pallas_call x2, Pallas kernels: 12.7 us -> 6.25 us  [merge(): call(functools.partial(merge_kernel, sources), (shaped((rows, width), jnp...]
  transfers between devices with their start and end apart: 73 -> 73, of which waited for: 35 -> 32; matrix products, arithmetic and copies ran while one was open for 5% -> 6% of each run, Pallas kernels for 39% -> 35%
where the time goes in v15:
time: 500 us; the launch traced here: 493 us
  Pallas kernels  177 us (35%)
  waiting for transfers between devices  176 us (35%)
  starting transfers between devices  57.1 us (11%)
  local copies, waits for them, and re-layouts  44.6 us (9%)
  other arithmetic  21.8 us (4%)
  between operations  16 us (3%)
    ppermute x37, waiting for transfers between devices, to_partner(): return lax.ppermute(array, 'shard', [(i, i ^ offset) for i in range(count)])  106 us
    ppermute x37, starting transfers between devices, to_partner(): return lax.ppermute(array, 'shard', [(i, i ^ offset) for i in range(count)])  41.5 us
    ppermute x6, waiting for transfers between devices, to_chip(): lax.ppermute(array, 'ctx', [(i, (i + 2 * offset) % count) for i in range(...  35.6 us
    pallas_call x2, Pallas kernels, run_expert(): call(functools.partial(expert_kernel, sources, micro), tuple([shaped((row...  32.4 us
    pallas_call x2, Pallas kernels, attend(): call(functools.partial(attend_kernel, micro), (shaped((rows, width), low_...  25.5 us
    unnamed x229, local copies, waits for them, and re-layouts  24 us
    pallas_call x2, Pallas kernels, attend_back(): pl.pallas_call(functools.partial(attend_back_kernel, micro), out_shape=(s...  22.2 us
    pallas_call x2, Pallas kernels, rotate(): pl.pallas_call(rotate_kernel, grid=(count,), out_shape=(shaped(weight.sha...  18.7 us
  transfers between devices with their start and end apart: 73, of which 32 were waited for; matrix products, arithmetic and copies ran while one was open for 6% of the time, Pallas kernels for 35%

profile of v15, /device:TPU:0, one launch (start us, length us, event | category | flops | bytes accessed | tf_op | source)
XLA Modules:
  0.0 493.1 jit_solution(14826197925215468780)
XLA Ops:
  15.0 7.8 %collective-permute-done.7.refs_11_ = bf16[4,192,256]{2,1,0:T(8,128)(2,1)} collective-permute-done((bf16[4,192,256]{2,1,0:T(8,128)(2,1)S(1)}, bf16[4,192,256]{2,1,0:T(8,128)(2,1)}, u32[]{:S(2)}, u32[]{:S(2)}) %collective-permute-start.7) | collective-permute-done | bytes 393248 | tf_op jit(solution)/shard_map/ppermute | solution.py:968
  24.6 7.1 %collective-permute-done.3.refs_7_ = bf16[4,192,256]{2,1,0:T(8,128)(2,1)S(1)} collective-permute-done((bf16[4,192,256]{2,1,0:T(8,128)(2,1)S(1)}, bf16[4,192,256]{2,1,0:T(8,128)(2,1)S(1)}, u32[]{:S(2)}, u32[]{:S(2)}) %collective-permute-start.3) | collective-permute-done | bytes 393248 | tf_op jit(solution)/shard_map/ppermute | solution.py:958
  43.7 7.3 %collective-permute-done.18 = bf16[4,192,256]{2,1,0:T(8,128)(2,1)} collective-permute-done((bf16[4,192,256]{2,1,0:T(8,128)(2,1)S(1)}, bf16[4,192,256]{2,1,0:T(8,128)(2,1)}, u32[]{:S(2)}, u32[]{:S(2)}) %collective-permute-start.18) | collective-permute-done | bytes 393248 | tf_op jit(solution)/shard_map/ppermute | solution.py:968
  57.4 12.5 %collective-permute-done.22.refs_25_ = bf16[8,192,256]{2,1,0:T(8,128)(2,1)S(1)} collective-permute-done((bf16[8,192,256]{2,1,0:T(8,128)(2,1)S(1)}, bf16[8,192,256]{2,1,0:T(8,128)(2,1)S(1)}, u32[]{:S(2)}, u32[]{:S(2)}) %collective-permute-start.22) | collective-permute-done | bytes 786464 | tf_op jit(solution)/shard_map/ppermute | solution.py:958
  86.7 12.3 %shard_map.358 = (bf16[256,1536]{1,0:T(8,128)(2,1)}, bf16[256,1024]{1,0:T(8,128)(2,1)}, bf16[1536,2560]{1,0:T(8,128)(2,1)}, bf16[1536,1536]{1,0:T(8,128)(2,1)}) custom-call(s32[128]{0:T(128)} %order_ref.1, s32[2]{0:T(128)} %pad_add_fusion.me_ref, f32[128,1536]{1,0:T(8,128)} %get-tuple-element.277.refs_0_.x_ref, ...), custom_call_target="tpu_custom_call" | custom-call | flops 805306368 | bytes 25165824 | tf_op jit(solution)/shard_map/pallas_call | solution.py:192
  111.2 12.0 %collective-permute-done.28.refs_5_ = bf16[256,1664]{1,0:T(8,128)(2,1)} collective-permute-done((bf16[256,1664]{1,0:T(8,128)(2,1)S(1)}, bf16[256,1664]{1,0:T(8,128)(2,1)}, u32[]{:S(2)}, u32[]{:S(2)}) %collective-permute-start.28) | collective-permute-done | bytes 852000 | tf_op jit(solution)/shard_map/ppermute | solution.py:958
  123.2 18.3 %collective-permute-done.29.refs_6_ = bf16[256,1664]{1,0:T(8,128)(2,1)} collective-permute-done((bf16[256,1664]{1,0:T(8,128)(2,1)S(1)}, bf16[256,1664]{1,0:T(8,128)(2,1)}, u32[]{:S(2)}, u32[]{:S(2)}) %collective-permute-start.29) | collective-permute-done | bytes 852000 | tf_op jit(solution)/shard_map/ppermute | solution.py:958
  141.5 6.5 %all-gather.6.cloned.1.call-done.all_ref = bf16[2048,1024]{1,0:T(8,128)(2,1)} async-done(((bf16[256,1024]{1,0:T(8,128)(2,1)}), bf16[2048,1024]{1,0:T(8,128)(2,1)}) %all-gather.6.cloned.1.call-update) | async-done | bytes 4194320 | tf_op jit(solution)/shard_map/all_gather | solution.py:1146
  148.6 12.7 %shard_map.360 = (bf16[128,1536]{1,0:T(8,128)(2,1)}, f32[384,128]{1,0:T(8,128)}, f32[128,1536]{1,0:T(8,128)}, bf16[128,1536]{1,0:T(8,128)(2,1)}) custom-call(bf16[128,1536]{1,0:T(8,128)(2,1)} %get-tuple-element.159.q_ref, s32[128,1]{1,0:T(8,128)} %constant_dynamic-slice_fusion.4.rpos_ref, s32[1,1024]{1,0:T(1,128)} %bitcast.54, ...), custom_call_target="tpu_custom_call" | custom-call | flops 3221225472 | bytes 8388608 | tf_op jit(solution)/shard_map/pallas_call | solution.py:306
  164.9 12.8 %shard_map.361 = (bf16[128,1536]{1,0:T(8,128)(2,1)}, f32[384,128]{1,0:T(8,128)}, f32[128,1536]{1,0:T(8,128)}, bf16[128,1536]{1,0:T(8,128)(2,1)}) custom-call(bf16[128,1536]{1,0:T(8,128)(2,1)} %get-tuple-element.167.q_ref, s32[128,1]{1,0:T(8,128)} %constant_dynamic-slice_fusion.4.rpos_ref, s32[1,1024]{1,0:T(1,128)} %bitcast.55, ...), custom_call_target="tpu_custom_call" | custom-call | flops 3221225472 | bytes 8388608 | tf_op jit(solution)/shard_map/pallas_call | solution.py:306
  187.2 16.0 %shard_map.362 = (bf16[128,1664]{1,0:T(8,128)(2,1)}, bf16[128,1664]{1,0:T(8,128)(2,1)}, bf16[128,1664]{1,0:T(8,128)(2,1)}, bf16[128,1664]{1,0:T(8,128)(2,1)}, bf...) custom-call(s32[96]{0:T(128)} %select_reduce_fusion.order_ref, ...), custom_call_target="tpu_custom_call" | custom-call | flops 8053063680 | bytes 20971520 | tf_op jit(solution)/shard_map/pallas_call | solution.py:406
  207.7 16.4 %shard_map.363 = (bf16[128,1664]{1,0:T(8,128)(2,1)}, bf16[128,1664]{1,0:T(8,128)(2,1)}, bf16[128,1664]{1,0:T(8,128)(2,1)}, bf16[128,1664]{1,0:T(8,128)(2,1)}, bf...) custom-call(s32[96]{0:T(128)} %select_reduce_fusion.order_ref, ...), custom_call_target="tpu_custom_call" | custom-call | flops 8053063680 | bytes 20971520 | tf_op jit(solution)/shard_map/pallas_call | solution.py:406
  227.7 17.9 %shard_map.364 = (bf16[96,192,128]{2,1,0:T(8,128)(2,1)}, bf16[96,192,128]{2,1,0:T(8,128)(2,1)}) custom-call(s32[96]{0:T(128)} %select_reduce_fusion.order_ref, bf16[512,1536]{1,0:T(8,128)(2,1)} %get-tuple-element.178.refs_0_, bf16[512,1536]{1,0:T(8,128)(2,1)} %get-tuple-element.182.refs_1_, bf16[512,1664]{1,0:T(8,128)(2,1)} %get-tuple-element.183.refs_2_, ...), custom_call_target="tpu_custom_call" | custom-call | flops 9663676416 | bytes 22282240 | tf_op jit(solution)/shard_map/pallas_call | solution.py:521
  248.3 8.9 %shard_map.365 = (bf16[256,1536]{1,0:T(8,128)(2,1)}, bf16[256,1536]{1,0:T(8,128)(2,1)}, bf16[256,1536]{1,0:T(8,128)(2,1)}, bf16[256,1536]{1,0:T(8,128)(2,1)}) custom-call(s32[96]{0:T(128)} %select_reduce_fusion.order_ref, bf16[96,128,256]{2,1,0:T(8,128)(2,1)} %all-gather.4.cloned.1.call-done.refs_8_.upper_ref, ...), custom_call_target="tpu_custom_call" | custom-call | flops 3221225472 | bytes 8388608 | tf_op jit(solution)/shard_map/pallas_call | solution.py:460
  270.6 11.0 %shard_map.367 = (bf16[128,1536]{1,0:T(8,128)(2,1)S(1)}, bf16[2048,1024]{1,0:T(8,128)(2,1)S(1)}) custom-call(bf16[128,1536]{1,0:T(8,128)(2,1)S(1)} %copy-done.41, s32[128,1]{1,0:T(8,128)S(1)} %copy-done.32, s32[1,1024]{1,0:T(1,128)S(1)} %bitcast.56, bf16[128,1536]{1,0:T(8,128)(2,1)S(1)} %copy-done.38, f32[384,128]{1,0:T(8,128)S(1)} %copy-done.46, ...), custom_call_target="tpu_custom_call" | custom-call | flops 8053063680 | bytes 8388608 | tf_op jit(solution)/shard_map/pallas_call | solution.py:790
  287.7 11.2 %shard_map.369 = (bf16[128,1536]{1,0:T(8,128)(2,1)S(1)}, bf16[2048,1024]{1,0:T(8,128)(2,1)S(1)}) custom-call(bf16[128,1536]{1,0:T(8,128)(2,1)S(1)} %copy-done.40, s32[128,1]{1,0:T(8,128)S(1)} %copy-done.32, s32[1,1024]{1,0:T(1,128)S(1)} %bitcast.57, bf16[128,1536]{1,0:T(8,128)(2,1)S(1)} %copy-done.39, ...), custom_call_target="tpu_custom_call", output_to_operand_aliasing={{1}: (7, {})} | custom-call | flops 8053063680 | bytes 8388608 | tf_op jit(solution)/shard_map/pallas_call | solution.py:790
  305.9 9.4 %shard_map.370 = (bf16[98,48,128]{2,1,0:T(8,128)(2,1)}, bf16[98,48,128]{2,1,0:T(8,128)(2,1)}, bf16[96,48,128]{2,1,0:T(8,128)(2,1)}, bf16[96,48,128]{2,1,0:T(8,128)(2,1)}, bf16[1536,512]{1,0:T(8,128)(2,1)}) custom-call(s32[2]{0:T(128)} %pad_add_fusion.me_ref, bf16[256,1536]{1,0:T(8,128)(2,1)} %get-tuple-element.155.h_ref.refs_0_, ...), custom_call_target="tpu_custom_call" | custom-call | flops 2415919104 | bytes 16777216 | tf_op jit(solution)/shard_map/pallas_call | solution.py:646
  322.9 20.9 %collective-permute-done.55 = bf16[96,48,128]{2,1,0:T(8,128)(2,1)} collective-permute-done((bf16[96,48,128]{2,1,0:T(8,128)(2,1)}, bf16[96,48,128]{2,1,0:T(8,128)(2,1)}, u32[]{:S(2)}, u32[]{:S(2)}) %collective-permute-start.55) | collective-permute-done | bytes 1179680 | tf_op jit(solution)/shard_map/ppermute | solution.py:958
  353.1 11.4 %collective-permute-done.56 = bf16[48,48,128]{2,1,0:T(8,128)(2,1)S(1)} collective-permute-done((bf16[48,48,128]{2,1,0:T(8,128)(2,1)}, bf16[48,48,128]{2,1,0:T(8,128)(2,1)S(1)}, u32[]{:S(2)}, u32[]{:S(2)}) %collective-permute-start.56) | collective-permute-done | bytes 589856 | tf_op jit(solution)/shard_map/ppermute | solution.py:958
  379.3 8.4 %collective-permute-done.57 = bf16[256,1536]{1,0:T(8,128)(2,1)} collective-permute-done((bf16[256,1536]{1,0:T(8,128)(2,1)}, bf16[256,1536]{1,0:T(8,128)(2,1)}, u32[]{:S(2)}, u32[]{:S(2)}) %collective-permute-start.57) | collective-permute-done | bytes 786464 | tf_op jit(solution)/shard_map/ppermute | solution.py:958
  387.7 7.2 %shard_map.374 = (f32[2,128,1536]{2,1,0:T(8,128)}, f32[8,1536]{1,0:T(8,128)}) custom-call(f32[2,128,1536]{2,1,0:T(8,128)} %x_ref, f32[2,1536]{1,0:T(2,128)} %gain_ref.9, bf16[1536,2560]{1,0:T(8,128)(2,1)} %get-tuple-element.219.w_ref, f32[128,1536]{1,0:T(8,128)} %copy-done.12, f32[128,1536]{1,0:T(8,128)} %copy-done.13, ...), custom_call_target="tpu_custom_call" | custom-call | flops 805306368 | bytes 14680064 | tf_op jit(solution)/shard_map/pallas_call | solution.py:874
  412.3 15.1 %shard_map.372 = (f32[12,192,256]{2,1,0:T(8,128)}, f32[12,192,256]{2,1,0:T(8,128)}, f32[12,192,256]{2,1,0:T(8,128)}, f32[12,192,256]{2,1,0:T(8,128)}) custom-call(f32[12,192,256]{2,1,0:T(8,128)} %bitcast.58, f32[12,192,256]{2,1,0:T(8,128)} %bitcast.64, f32[12,192,256]{2,1,0:T(8,128)} %bitcast.65, f32[12,192,192]{2,1,0:T(8,128)} %bitcast.66, ...), custom_call_target="tpu_custom_call" | custom-call | flops 1056964608 | bytes 25165824 | tf_op jit(solution)/shard_map/pallas_call | solution.py:913
  427.4 17.2 %collective-permute-done.64 = bf16[129,1536]{1,0:T(8,128)(2,1)S(1)} collective-permute-done((bf16[129,1536]{1,0:T(8,128)(2,1)}, bf16[129,1536]{1,0:T(8,128)(2,1)S(1)}, u32[]{:S(2)}, u32[]{:S(2)}) %collective-permute-start.64) | collective-permute-done | bytes 396320 | tf_op jit(solution)/shard_map/ppermute | solution.py:968
  454.8 14.1 %all-to-all-done = bf16[32,2,4608]{2,1,0:T(2,128)(2,1)S(1)} async-done(((bf16[32,2,4608]{2,1,0:T(2,128)(2,1)}), bf16[32,2,4608]{2,1,0:T(2,128)(2,1)S(1)}, u32[]{:S(2)}, u32[]{:S(2)}) %all-to-all-start) | async-done | bytes 589856 | tf_op jit(solution)/shard_map/all_to_all | solution.py:1258
  (445 shorter events, 182.5 us)
Async XLA Ops:
  7.2 93.6 %all-gather.4.cloned.1.call-start = ((), (), s32[]{:S(2)}) async-start(), calls=%async_computation.4 | async-start | bytes 7077888 | tf_op jit(solution)/shard_map/all_gather | solution.py:1123
  36.1 111.9 %all-gather.6.cloned.1.call-start = ((), (), s32[]{:S(2)}) async-start(), calls=%async_computation.5 | async-start | bytes 4718592 | tf_op jit(solution)/shard_map/all_gather | solution.py:1146
  100.9 86.3 %all-gather.8.cloned.1.call-start = ((), (), s32[]{:S(2)}) async-start(), calls=%async_computation.6 | async-start | bytes 3538944 | tf_op jit(solution)/shard_map/all_gather | solution.py:1148
  101.2 21.9 %collective-permute-start.28 = (bf16[256,1664]{1,0:T(8,128)(2,1)S(1)}, bf16[256,1664]{1,0:T(8,128)(2,1)}, u32[]{:S(2)}, u32[]{:S(2)}) collective-permute-start(bf16[256,1664]{1,0:T(8,128)(2,1)S(1)} %bitcast.68), channel_id=1, source_target_pairs={{0,1},{1,0},{2,3},{3,2},{4,5},{5,4},{6,7},{7,6},{8,9},{9,8},{10,11... | collective-permute-start | bytes 2555912 | tf_op jit(solution)/shard_map/ppermute | solution.py:958
  102.3 39.2 %collective-permute-start.29 = (bf16[256,1664]{1,0:T(8,128)(2,1)S(1)}, bf16[256,1664]{1,0:T(8,128)(2,1)}, u32[]{:S(2)}, u32[]{:S(2)}) collective-permute-start(bf16[256,1664]{1,0:T(8,128)(2,1)S(1)} %bitcast.69), channel_id=1, source_target_pairs={{0,2},{1,3},{2,0},{3,1},{4,6},{5,7},{6,4},{7,5},{8,10},{9,11},{10,... | collective-permute-start | bytes 2555912 | tf_op jit(solution)/shard_map/ppermute | solution.py:958
  103.8 37.7 %collective-permute-start.30 = (bf16[256,1664]{1,0:T(8,128)(2,1)S(1)}, bf16[256,1664]{1,0:T(8,128)(2,1)}, u32[]{:S(2)}, u32[]{:S(2)}) collective-permute-start(bf16[256,1664]{1,0:T(8,128)(2,1)S(1)} %bitcast.70), channel_id=1, source_target_pairs={{0,3},{1,2},{2,1},{3,0},{4,7},{5,6},{6,5},{7,4},{8,11},{9,10},{10,... | collective-permute-start | bytes 2555912 | tf_op jit(solution)/shard_map/ppermute | solution.py:958
  148.0 152.9 %reduce-scatter.4.cloned.1.call-start = ((), (), s32[]{:S(2)}) async-start(), calls=%async_computation.7 | async-start | bytes 5308416 | tf_op jit(solution)/shard_map/reduce_scatter | solution.py:1203
  148.3 36.3 %collective-permute-start.31 = (bf16[256,1536]{1,0:T(8,128)(2,1)S(1)}, bf16[256,1536]{1,0:T(8,128)(2,1)S(1)}, u32[]{:S(2)}, u32[]{:S(2)}) collective-permute-start(bf16[256,1536]{1,0:T(8,128)(2,1)S(1)} %copy-done.64), channel_id=1, source_target_pairs={{0,4},{4,0},{8,12},{12,8},{16,20},{20,16},{24,28},{28,24},{1,5},{5... | collective-permute-start | bytes 2359304 | tf_op jit(solution)/shard_map/ppermute | solution.py:963
  182.5 23.7 %collective-permute-start.40 = (bf16[128,1536]{1,0:T(8,128)(2,1)}, bf16[128,1536]{1,0:T(8,128)(2,1)S(1)}, u32[]{:S(2)}, u32[]{:S(2)}) collective-permute-start(bf16[128,1536]{1,0:T(8,128)(2,1)} %get-tuple-element.181.refs_0_.h2_ref), channel_id=1, source_target_pairs={{0,1},{1,0},{2,3},{3,2},{4,5},{5,4},{6,7},{7,6},{8,9},{9,8},{10,11... | collective-permute-start | bytes 1179656 | tf_op jit(solution)/shard_map/ppermute | solution.py:958
  183.7 23.1 %collective-permute-start.41 = (bf16[128,1536]{1,0:T(8,128)(2,1)}, bf16[128,1536]{1,0:T(8,128)(2,1)}, u32[]{:S(2)}, u32[]{:S(2)}) collective-permute-start(bf16[128,1536]{1,0:T(8,128)(2,1)} %get-tuple-element.181.refs_0_.h2_ref), channel_id=1, source_target_pairs={{0,2},{1,3},{2,0},{3,1},{4,6},{5,7},{6,4},{7,5},{8,10},{9,11},{10,... | collective-permute-start | bytes 1179656 | tf_op jit(solution)/shard_map/ppermute | solution.py:958
  203.2 23.8 %collective-permute-start.37 = (bf16[128,1664]{1,0:T(8,128)(2,1)}, bf16[128,1664]{1,0:T(8,128)(2,1)S(1)}, u32[]{:S(2)}, u32[]{:S(2)}) collective-permute-start(bf16[128,1664]{1,0:T(8,128)(2,1)} %get-tuple-element.174), channel_id=1, source_target_pairs={{0,1},{1,0},{2,3},{3,2},{4,5},{5,4},{6,7},{7,6},{8,9},{9,8},{10,11... | collective-permute-start | bytes 1277960 | tf_op jit(solution)/shard_map/ppermute | solution.py:958
  204.7 23.0 %collective-permute-start.38 = (bf16[128,1664]{1,0:T(8,128)(2,1)}, bf16[128,1664]{1,0:T(8,128)(2,1)S(1)}, u32[]{:S(2)}, u32[]{:S(2)}) collective-permute-start(bf16[128,1664]{1,0:T(8,128)(2,1)} %get-tuple-element.175), channel_id=1, source_target_pairs={{0,2},{1,3},{2,0},{3,1},{4,6},{5,7},{6,4},{7,5},{8,10},{9,11},{10,... | collective-permute-start | bytes 1277960 | tf_op jit(solution)/shard_map/ppermute | solution.py:958
  224.2 21.5 %collective-permute-start.45 = (bf16[128,1664]{1,0:T(8,128)(2,1)}, bf16[128,1664]{1,0:T(8,128)(2,1)S(1)}, u32[]{:S(2)}, u32[]{:S(2)}) collective-permute-start(bf16[128,1664]{1,0:T(8,128)(2,1)} %get-tuple-element.200), channel_id=1, source_target_pairs={{0,1},{1,0},{2,3},{3,2},{4,5},{5,4},{6,7},{7,6},{8,9},{9,8},{10,11... | collective-permute-start | bytes 1277960 | tf_op jit(solution)/shard_map/ppermute | solution.py:958
  246.7 103.4 %reduce-scatter.6.cloned.1.call-start = ((), (), s32[]{:S(2)}) async-start(), calls=%async_computation.8 | async-start | bytes 4718592 | tf_op jit(solution)/shard_map/reduce_scatter | solution.py:1204
  257.2 24.4 %collective-permute-start.43 = (bf16[256,1536]{1,0:T(8,128)(2,1)}, bf16[256,1536]{1,0:T(8,128)(2,1)S(1)}, u32[]{:S(2)}, u32[]{:S(2)}) collective-permute-start(bf16[256,1536]{1,0:T(8,128)(2,1)} %get-tuple-element.194), channel_id=1, source_target_pairs={{0,1},{1,0},{2,3},{3,2},{4,5},{5,4},{6,7},{7,6},{8,9},{9,8},{10,11... | collective-permute-start | bytes 2359304 | tf_op jit(solution)/shard_map/ppermute | solution.py:958
  258.7 22.9 %collective-permute-start.44 = (bf16[256,1536]{1,0:T(8,128)(2,1)}, bf16[256,1536]{1,0:T(8,128)(2,1)S(1)}, u32[]{:S(2)}, u32[]{:S(2)}) collective-permute-start(bf16[256,1536]{1,0:T(8,128)(2,1)} %get-tuple-element.195), channel_id=1, source_target_pairs={{0,2},{1,3},{2,0},{3,1},{4,6},{5,7},{6,4},{7,5},{8,10},{9,11},{10,... | collective-permute-start | bytes 2359304 | tf_op jit(solution)/shard_map/ppermute | solution.py:958
  301.0 104.4 %reduce-scatter.8.cloned.1.call-start = ((), (), s32[]{:S(2)}) async-start(), calls=%async_computation.9 | async-start | bytes 5308416 | tf_op jit(solution)/shard_map/reduce_scatter | solution.py:1235
  315.4 28.4 %collective-permute-start.55 = (bf16[96,48,128]{2,1,0:T(8,128)(2,1)}, bf16[96,48,128]{2,1,0:T(8,128)(2,1)}, u32[]{:S(2)}, u32[]{:S(2)}) collective-permute-start(bf16[96,48,128]{2,1,0:T(8,128)(2,1)} %get-tuple-element.224), channel_id=1, source_target_pairs={{0,2},{1,3},{2,0},{3,1},{4,6},{5,7},{6,4},{7,5},{8,10},{9,11},{10,... | collective-permute-start | bytes 3538952 | tf_op jit(solution)/shard_map/ppermute | solution.py:958
  316.3 29.7 %collective-permute-start.53 = (bf16[98,48,128]{2,1,0:T(8,128)(2,1)}, bf16[98,48,128]{2,1,0:T(8,128)(2,1)}, u32[]{:S(2)}, u32[]{:S(2)}) collective-permute-start(bf16[98,48,128]{2,1,0:T(8,128)(2,1)} %get-tuple-element.218), channel_id=1, source_target_pairs={{0,1},{1,0},{2,3},{3,2},{4,5},{5,4},{6,7},{7,6},{8,9},{9,8},{10,11... | collective-permute-start | bytes 3612680 | tf_op jit(solution)/shard_map/ppermute | solution.py:958
  366.1 21.6 %collective-permute-start.57 = (bf16[256,1536]{1,0:T(8,128)(2,1)}, bf16[256,1536]{1,0:T(8,128)(2,1)}, u32[]{:S(2)}, u32[]{:S(2)}) collective-permute-start(bf16[256,1536]{1,0:T(8,128)(2,1)} %get-tuple-element.226), channel_id=1, source_target_pairs={{0,3},{1,2},{2,1},{3,0},{4,7},{5,6},{6,5},{7,4},{8,11},{9,10},{10,... | collective-permute-start | bytes 2359304 | tf_op jit(solution)/shard_map/ppermute | solution.py:958
  372.2 22.7 %collective-permute-start.59 = (bf16[32,48,128]{2,1,0:T(8,128)(2,1)}, bf16[32,48,128]{2,1,0:T(8,128)(2,1)}, u32[]{:S(2)}, u32[]{:S(2)}) collective-permute-start(bf16[32,48,128]{2,1,0:T(8,128)(2,1)} %get-tuple-element.237), channel_id=1, source_target_pairs={{0,1},{1,0},{2,3},{3,2},{4,5},{5,4},{6,7},{7,6},{8,9},{9,8},{10,11... | collective-permute-start | bytes 1179656 | tf_op jit(solution)/shard_map/ppermute | solution.py:958
  407.6 37.1 %collective-permute-start.64 = (bf16[129,1536]{1,0:T(8,128)(2,1)}, bf16[129,1536]{1,0:T(8,128)(2,1)S(1)}, u32[]{:S(2)}, u32[]{:S(2)}) collective-permute-start(bf16[129,1536]{1,0:T(8,128)(2,1)} %get-tuple-element.271), channel_id=1, source_target_pairs={{0,16},{4,20},{8,24},{12,28},{16,0},{20,4},{24,8},{28,12},{1,17},{... | collective-permute-start | bytes 1188872 | tf_op jit(solution)/shard_map/ppermute | solution.py:968
  408.5 36.1 %collective-permute-start.65 = (bf16[129,1536]{1,0:T(8,128)(2,1)}, bf16[129,1536]{1,0:T(8,128)(2,1)S(1)}, u32[]{:S(2)}, u32[]{:S(2)}) collective-permute-start(bf16[129,1536]{1,0:T(8,128)(2,1)} %get-tuple-element.270), channel_id=1, source_target_pairs={{0,8},{4,12},{8,16},{12,20},{16,24},{20,28},{24,0},{28,4},{1,9},{5... | collective-permute-start | bytes 1188872 | tf_op jit(solution)/shard_map/ppermute | solution.py:968
  447.1 21.8 %all-to-all-start = ((bf16[32,2,4608]{2,1,0:T(2,128)(2,1)}), bf16[32,2,4608]{2,1,0:T(2,128)(2,1)S(1)}, u32[]{:S(2)}, u32[]{:S(2)}) async-start(bf16[32,2,4608]{2,1,0:T(2,128)(2,1)} %all_to_all.6), calls=%async_computation.3 | async-start | bytes 1179648 | tf_op jit(solution)/shard_map/all_to_all | solution.py:1258
  (162 other events, 1512.2 us)
Sparse Core Ops, SparseCore 0:
  36.2 64.5 all-gather.3
  103.0 44.9 all-gather.5
  150.2 36.9 all-gather.7
  245.9 53.6 reduce-scatter.3
  301.7 48.3 reduce-scatter.5
  352.2 53.0 reduce-scatter.7
